TPU v7x, 32 devices: a whole 2x2x4 slice. The times are simulated.
32 devices in a mesh: groups: 2 (over x), expert: 16 (over z, y, core).
Axes of the slice: x: 2, y: 2, z: 4, core: 2. Of those that a mesh axis runs over, the one named last changes fastest.
Arguments:
- tokens: bfloat16 [2048, 4096], P(('groups', 'expert')), parts along dimension 0, may hold values from -6 to 6
- out_grad: bfloat16 [2048, 4096], P(('groups', 'expert')), parts along dimension 0, may hold values from -6 to 6
- routes: int32 [2048, 8], P(('groups', 'expert')), parts along dimension 0, may hold values from 0 to 31, all different within a row; in each aligned block of 64 rows (0 to 63, 64 to 127, ...) at most 24 rows name the same one
- route_weight: float32 [2048, 8], P(('groups', 'expert')), parts along dimension 0, may hold values from 0.05 to 1
- example_ids: int32 [32, 64], P(('groups', 'expert')), parts along dimension 0, may hold values from 0 to 3, never falling along the last dimension, each value on 1 to 32 neighbouring positions
- in_proj: bfloat16 [32, 4096, 64], P('expert'), may hold values from -0.09375 to 0.09375
- out_proj: bfloat16 [4096, 64], replicated, may hold values from -0.09375 to 0.09375
- queries: bfloat16 [256, 4096], P('expert'), may hold values from -0.29882812 to 0.29882812
Outputs:
- sketches: float32 [128, 4096], P(('groups', 'expert')), parts along dimension 0
- scores: float32 [128, 256], P(('groups', 'expert')), parts along dimension 0
There are 2 independent parts, one for each index of `groups`. A program takes and returns all parts, laid end to end along the dimension named above; an argument that names none is the same for every part. Nothing has to cross between parts.
Inputs may be any that keep to these rules, and one draw needn't show every extreme that they name: The 8 experts of a token differ. Among the 64 tokens of one device no expert is named by more than 24 routes, a bound that some block reaches. `example_ids`: on each device the ids never fall along the tokens, every id occurs, and one example holds exactly 32 tokens.
All inputs are finite; a program needn't handle non-finite values.
Results may differ from a plain program's by a relative error of at most 0.0042.
Values may be sent and summed in bfloat16 or wider, within the bound.
No kernel may reach another device: no remote copies, remote signals or barrier semaphores. Data moves between devices by JAX's collectives and lax.ppermute only.
A program may use at most 128 MiB of HBM per device.

v0:
```python
import jax
import jax.numpy as jnp
from jax import lax
from jax.sharding import PartitionSpec as P

RANK = 64
EX_DEV = 4


def shards(tokens, out_grad, routes, route_weight, example_ids, in_proj, out_proj, queries):
    token_count, model_width = tokens.shape
    route_count = routes.shape[1]
    owned_experts = in_proj.shape[0]
    devices_axis = lax.axis_size("expert")
    experts_all = owned_experts * devices_axis
    capacity = 3 * token_count * route_count // (2 * experts_all)
    row_count = token_count * route_count
    flat_routes = routes.reshape(row_count)
    expert_member = (
        flat_routes[:, None] == jnp.arange(experts_all, dtype=jnp.int32)[None, :]
    ).astype(jnp.int32)
    slot_index = jnp.sum(jnp.cumsum(expert_member, axis=0) * expert_member, axis=1) - 1
    target = flat_routes * capacity + slot_index
    token_of_row = jnp.arange(row_count, dtype=jnp.int32) // route_count
    send_rows = (
        jnp.zeros((experts_all * capacity, model_width), jnp.bfloat16)
        .at[target]
        .set(tokens[token_of_row])
    )
    grad_side = jnp.dot(out_grad, out_proj, preferred_element_type=jnp.float32)
    weighted = (
        (route_weight[:, :, None] * grad_side[:, None, :])
        .reshape(row_count, RANK)
        .astype(jnp.bfloat16)
    )
    local_ids = example_ids.reshape(token_count)
    member = local_ids[:, None] == jnp.arange(EX_DEV, dtype=jnp.int32)[None, :]
    counts = jnp.sum(member.astype(jnp.float32), axis=0)
    row_member = jnp.repeat(member, route_count, axis=0)
    widened = jnp.where(row_member[:, :, None], weighted[:, None, :], jnp.zeros((), jnp.bfloat16))
    widened = widened.reshape(row_count, EX_DEV * RANK)
    received = lax.all_to_all(
        send_rows.reshape(experts_all, capacity, model_width),
        "expert",
        split_axis=0,
        concat_axis=0,
        tiled=True,
    )
    slot_span = received.shape[1]
    by_owner = received.reshape(-1, owned_experts, slot_span, model_width)
    projected = jnp.einsum("slcd,ldr->slcr", by_owner, in_proj, preferred_element_type=jnp.float32)
    projected = projected.reshape(-1, slot_span, RANK)
    returned = lax.all_to_all(projected, "expert", split_axis=0, concat_axis=0, tiled=True)
    input_side = returned.reshape(experts_all * capacity, RANK)[target]
    block_sum = jnp.dot(
        input_side.T,
        widened.astype(jnp.float32),
        precision=lax.Precision.HIGHEST,
        preferred_element_type=jnp.float32,
    )
    combined = block_sum.reshape(RANK, EX_DEV, RANK).transpose(1, 0, 2).reshape(EX_DEV, RANK * RANK)
    sketches = combined / counts[:, None]
    rounded = sketches.astype(jnp.bfloat16)
    partial_value = lax.dot_general(
        rounded,
        lax.all_gather(queries, "expert", axis=0, tiled=True),
        (((1,), (1,)), ((), ())),
        preferred_element_type=jnp.float32,
    )
    return (sketches, partial_value)


def solution(mesh):
    placed = (
        P(("groups", "expert"), None),
        P(("groups", "expert"), None),
        P(("groups", "expert"), None),
        P(("groups", "expert"), None),
        P(("groups", "expert"), None),
        P("expert", None, None),
        P(),
        P("expert", None),
    )
    return jax.shard_map(
        shards,
        mesh=mesh,
        in_specs=placed,
        out_specs=(P(("groups", "expert"), None), P(("groups", "expert"), None)),
        check_vma=False,
    )
```

profile of v0, /device:TPU:0, one launch (start us, length us, event | category | flops | bytes accessed | tf_op | source)
XLA Modules:
  0.0 222.5 jit_solution(11791615656188488752)
XLA Ops:
  7.2 0.0 copy-start
  7.2 0.9 copy.13
  8.0 0.1 eq.44
  8.1 0.1 eq.40
  8.2 0.7 broadcast_multiply_fusion
  8.9 1.2 reduce-window.6
  10.1 0.2 slice_reduce_fusion
  10.4 0.1 fusion.17
  10.5 0.1 copy.12
  10.6 0.1 mul.43
  10.7 21.4 %scatter_custom_fusion = bf16[768,4096]{1,0:T(8,128)(2,1)} fusion(s32[512]{0:T(512)S(1)} %bitcast.54, bf16[64,4096]{1,0:T(8,128)(2,1)} %param.8, s32[1024]{0:T(1024)S(1)} %pad_clamp_fusion.1, bf16[]{:T(256)} %constant.27.clone.1), kind=kCustom, calls=%fused_computation.5 | custom fusion | bytes 6291968 | tf_op jit(solution)/shard_map/scatter | solution.py:28
  32.1 0.0 copy-start.5
  32.1 0.0 copy-start.4
  32.1 0.0 copy-start.1
  32.1 0.0 copy-start.2
  32.1 7.6 %all-to-all-start = ((bf16[32,24,4096]{2,1,0:T(8,128)(2,1)}), bf16[32,24,4096]{2,1,0:T(8,128)(2,1)}, u32[]{:S(2)}, u32[]{:S(2)}) async-start(bf16[32,24,4096]{2,1,0:T(8,128)(2,1)} %bitcast.51), calls=%async_computation | async-start | bytes 12582912 | tf_op jit(solution)/shard_map/all_to_all | solution.py:42
  39.7 0.0 all-gather.2.cloned.1.call-start
  39.8 0.7 all-gather.2.cloned.1.call-update
  40.5 0.0 copy-done.5
  40.5 0.1 broadcast_in_dim.38
  40.6 0.1 broadcast_in_dim.39
  40.7 0.0 copy-done.4
  40.7 0.1 copy.18
  40.8 0.1 mul.45
  40.9 0.0 copy-done.1
  40.9 0.0 copy-done.2
  40.9 0.3 fusion.22
  41.2 125.4 %all-to-all-done = bf16[32,24,4096]{2,1,0:T(8,128)(2,1)} async-done(((bf16[32,24,4096]{2,1,0:T(8,128)(2,1)}), bf16[32,24,4096]{2,1,0:T(8,128)(2,1)}, u32[]{:S(2)}, u32[]{:S(2)}) %all-to-all-start) | async-done | bytes 6291488 | tf_op jit(solution)/shard_map/all_to_all | solution.py:42
  166.6 0.0 copy-done
  166.6 4.6 %fusion.5 = f32[16,2,24,64]{3,2,0,1:T(8,128)S(1)} fusion(bf16[16,2,24,4096]{3,2,1,0:T(8,128)(2,1)} %bitcast.5, bf16[2,4096,64]{1,2,0:T(8,128)(2,1)S(1)} %copy-done), kind=kOutput, calls=%fused_computation.8 | convolution fusion | flops 402653184 | bytes 7536640 | tf_op jit(solution)/shard_map/slcd,ldr->slcr/dot_general | solution.py:51
  171.2 0.9 reshape.187
  172.1 28.0 %all-to-all-start.1 = ((f32[16,1,3072]{2,1,0:T(1,128)}), f32[16,1,3072]{2,1,0:T(1,128)S(1)}, u32[]{:S(2)}, u32[]{:S(2)}) async-start(f32[16,1,3072]{2,1,0:T(1,128)} %reshape.187), calls=%async_computation.1 | async-start | bytes 393216 | tf_op jit(solution)/shard_map/all_to_all | solution.py:53
  200.1 0.1 fusion.10
  200.3 0.1 copy.19
  200.4 0.1 convert_reduce_fusion
  200.5 8.6 %all-to-all-done.1 = f32[16,1,3072]{2,1,0:T(1,128)S(1)} async-done(((f32[16,1,3072]{2,1,0:T(1,128)}), f32[16,1,3072]{2,1,0:T(1,128)S(1)}, u32[]{:S(2)}, u32[]{:S(2)}) %all-to-all-start.1) | async-done | bytes 196640 | tf_op jit(solution)/shard_map/all_to_all | solution.py:53
  209.1 0.5 broadcast.153
  209.7 1.1 reduce.2
  210.8 0.1 reshape.188
  210.9 1.0 gather_fusion
  211.9 0.6 convolution_bitcast_fusion
  212.6 0.1 reshape.153
  212.7 0.1 broadcast_divide_fusion
  212.8 0.0 copy-start.3
  212.8 0.0 all-gather.2.cloned.1.call-done
  212.8 2.8 %fusion.19 = f32[4,256]{1,0:T(4,128)} fusion(bf16[256,4096]{1,0:T(8,128)(2,1)} %all-gather.2.cloned.1.call-done, f32[4,4096]{1,0:T(4,128)S(1)} %broadcast_divide_fusion), kind=kOutput, calls=%fused_computation.27 | convolution fusion | flops 8404992 | bytes 2166784 | tf_op jit(solution)/shard_map/dot_general | solution.py:64
  215.6 0.0 copy-done.3
  (10 shorter events, 0.1 us)
Async XLA Ops:
  7.2 159.4 %copy-start = (bf16[2,4096,64]{1,2,0:T(8,128)(2,1)S(1)}, bf16[2,4096,64]{1,2,0:T(8,128)(2,1)}, u32[]{:S(2)}) copy-start(bf16[2,4096,64]{1,2,0:T(8,128)(2,1)} %param.13) | copy-start | bytes 3145732
  32.1 8.3 %copy-start.5 = (s32[1,64]{1,0:T(1,128)S(1)}, s32[1,64]{1,0:T(1,128)}, u32[]{:S(2)}) copy-start(s32[1,64]{1,0:T(1,128)} %param.12) | copy-start | bytes 772
  32.1 8.6 %copy-start.4 = (f32[64,8]{0,1:T(8,128)S(1)}, f32[64,8]{0,1:T(8,128)}, u32[]{:S(2)}) copy-start(f32[64,8]{0,1:T(8,128)} %param.11) | copy-start | bytes 6148
  32.1 8.8 %copy-start.1 = (bf16[64,4096]{1,0:T(8,128)(2,1)S(1)}, bf16[64,4096]{1,0:T(8,128)(2,1)}, u32[]{:S(2)}) copy-start(bf16[64,4096]{1,0:T(8,128)(2,1)} %param.9) | copy-start | bytes 1572868
  32.1 8.8 %copy-start.2 = (bf16[4096,64]{0,1:T(8,128)(2,1)S(1)}, bf16[4096,64]{0,1:T(8,128)(2,1)}, u32[]{:S(2)}) copy-start(bf16[4096,64]{0,1:T(8,128)(2,1)} %param.14) | copy-start | bytes 1572868
  32.1 134.4 %all-to-all-start = ((bf16[32,24,4096]{2,1,0:T(8,128)(2,1)}), bf16[32,24,4096]{2,1,0:T(8,128)(2,1)}, u32[]{:S(2)}, u32[]{:S(2)}) async-start(bf16[32,24,4096]{2,1,0:T(8,128)(2,1)} %bitcast.51), calls=%async_computation | async-start | bytes 12582912 | tf_op jit(solution)/shard_map/all_to_all | solution.py:42
  39.7 173.1 %all-gather.2.cloned.1.call-start = ((), (), s32[]{:S(2)}) async-start(), calls=%async_computation.2 | async-start | bytes 2228224 | tf_op jit(solution)/shard_map/all_gather | solution.py:66
  172.1 37.0 %all-to-all-start.1 = ((f32[16,1,3072]{2,1,0:T(1,128)}), f32[16,1,3072]{2,1,0:T(1,128)S(1)}, u32[]{:S(2)}, u32[]{:S(2)}) async-start(f32[16,1,3072]{2,1,0:T(1,128)} %reshape.187), calls=%async_computation.1 | async-start | bytes 393216 | tf_op jit(solution)/shard_map/all_to_all | solution.py:53
  212.8 2.9 %copy-start.3 = (f32[4,4096]{1,0:T(4,128)}, f32[4,4096]{1,0:T(4,128)S(1)}, u32[]{:S(2)}) copy-start(f32[4,4096]{1,0:T(4,128)S(1)} %broadcast_divide_fusion) | copy-start | bytes 196612
Sparse Core Ops, SparseCore 0:
  42.7 109.4 all-gather.1
where the time goes:
time: 223 us; the launch traced here: 222 us
  waiting for transfers between devices  135 us (61%)
  starting transfers between devices  35.7 us (16%)
  local copies, waits for them, and re-layouts  26.1 us (12%)
  between operations  14.2 us (6%)
  matrix products  8.31 us (4%)
  other arithmetic  3.49 us (2%)
    all_to_all x1, waiting for transfers between devices, shards(): lax.all_to_all(send_rows.reshape(experts_all, capacity, model_width), 'ex...  125 us
    all_to_all x1, starting transfers between devices, shards(): lax.all_to_all(projected, 'expert', split_axis=0, concat_axis=0, tiled=True)  28 us
    scatter x1, local copies, waits for them, and re-layouts, shards(): send_rows = jnp.zeros((experts_all * capacity, model_width), jnp.bfloat16...  21.4 us
    all_to_all x1, waiting for transfers between devices, shards(): lax.all_to_all(projected, 'expert', split_axis=0, concat_axis=0, tiled=True)  8.63 us
    all_to_all x1, starting transfers between devices, shards(): lax.all_to_all(send_rows.reshape(experts_all, capacity, model_width), 'ex...  7.57 us
    dot_general x1, matrix products, shards(): jnp.einsum('slcd,ldr->slcr', by_owner, in_proj, preferred_element_type=jn...  4.56 us
  transfers between devices with their start and end apart: 3, of which 2 were waited for; matrix products, arithmetic and copies ran while one was open for 5% of the time, Pallas kernels for 0%

commit v1 on v0

v1 whole, which is shorter than its diff:
```python
import jax
import jax.numpy as jnp
from jax import lax
from jax.sharding import PartitionSpec as P

RANK = 64
EX_DEV = 4


def shards(tokens, out_grad, routes, route_weight, example_ids, in_proj, out_proj, queries):
    token_count, model_width = tokens.shape
    owned = in_proj.shape[0]
    n = lax.axis_size("expert")
    experts_all = owned * n
    everyone = lax.all_gather(tokens, "expert", axis=0, tiled=True)
    all_queries = lax.all_gather(queries, "expert", axis=0, tiled=True)
    weights = jnp.swapaxes(in_proj, 1, 2).reshape(owned * RANK, model_width)
    projected = lax.dot_general(
        everyone, weights, (((1,), (1,)), ((), ())), preferred_element_type=jnp.float32
    ).astype(jnp.bfloat16)
    returned = lax.all_to_all(
        projected.reshape(n, token_count, owned * RANK), "expert", split_axis=0, concat_axis=0, tiled=True
    )
    grad_side = jnp.dot(out_grad, out_proj, preferred_element_type=jnp.float32)
    hit = routes[:, :, None] == jnp.arange(experts_all, dtype=jnp.int32)[None, None, :]
    gate = jnp.sum(jnp.where(hit, route_weight[:, :, None], 0.0), axis=1)
    local_ids = example_ids.reshape(token_count)
    member = (local_ids[:, None] == jnp.arange(EX_DEV, dtype=jnp.int32)[None, :]).astype(jnp.float32)
    counts = jnp.sum(member, axis=0)
    weighted = (gate.T[:, :, None] * grad_side[None, :, :]).astype(jnp.bfloat16)
    widened = jnp.where(member.T[None, :, :, None].transpose(0, 2, 1, 3) > 0, weighted[:, :, None, :], jnp.zeros((), jnp.bfloat16))
    widened = widened.reshape(experts_all * token_count, EX_DEV * RANK)
    sides = returned.reshape(n, token_count, owned, RANK).transpose(0, 2, 1, 3).reshape(experts_all * token_count, RANK)
    block_sum = lax.dot_general(
        sides, widened, (((0,), (0,)), ((), ())), preferred_element_type=jnp.float32
    )
    combined = block_sum.reshape(RANK, EX_DEV, RANK).transpose(1, 0, 2).reshape(EX_DEV, RANK * RANK)
    sketches = combined / counts[:, None]
    scores = lax.dot_general(
        sketches.astype(jnp.bfloat16), all_queries, (((1,), (1,)), ((), ())), preferred_element_type=jnp.float32
    )
    return (sketches, scores)


def solution(mesh):
    placed = (
        P(("groups", "expert"), None),
        P(("groups", "expert"), None),
        P(("groups", "expert"), None),
        P(("groups", "expert"), None),
        P(("groups", "expert"), None),
        P("expert", None, None),
        P(),
        P("expert", None),
    )
    return jax.shard_map(
        shards,
        mesh=mesh,
        in_specs=placed,
        out_specs=(P(("groups", "expert"), None), P(("groups", "expert"), None)),
        check_vma=False,
    )
```

time: 223 us -> 141 us (0.63)
  starting transfers between devices: 35.7 us -> 3.61 us
  waiting for transfers between devices: 135 us -> 104 us
  local copies, waits for them, and re-layouts: 26.1 us -> 4.62 us
  matrix products: 8.31 us -> 11.4 us
    all_to_all x2 -> x1, waiting for transfers between devices: 134 us -> 8.67 us  [shards(): lax.all_to_all(projected.reshape(n, token_count, owned * RANK), 'expert',...]
    all_gather x1 -> x2, waiting for transfers between devices: 0.02 us -> 94.1 us  [the longest x1 76 us: shards(): everyone = lax.all_gather(tokens, 'expert', axis=0, tiled=True)]
    all_to_all x2 -> x1, starting transfers between devices: 35.6 us -> 3.53 us  [shards(): lax.all_to_all(projected.reshape(n, token_count, owned * RANK), 'expert',...]
    scatter x1 -> x0, local copies, waits for them, and re-layouts: 21.4 us -> none  [shards(): send_rows = jnp.zeros((experts_all * capacity, model_width), jnp.bfloat16...]
    select_n x0 -> x1, local copies, waits for them, and re-layouts: none -> 2.43 us  [shards(): jnp.where(member.T[None, :, :, None].transpose(0, 2, 1, 3) > 0, weighted[...]
  transfers between devices with their start and end apart: 3 -> 3, of which waited for: 2 -> 3; matrix products, arithmetic and copies ran while one was open for 5% -> 12% of each run, Pallas kernels for 0% -> 0%
where the time goes in v1:
time: 141 us
  waiting for transfers between devices  104 us (74%)
  between operations  14.1 us (10%)
  matrix products  11.4 us (8%)
  local copies, waits for them, and re-layouts  4.62 us (3%)
  starting transfers between devices  3.61 us (3%)
  other arithmetic  3.08 us (2%)
    all_gather x1, waiting for transfers between devices, shards(): everyone = lax.all_gather(tokens, 'expert', axis=0, tiled=True)  76 us
    all_gather x1, waiting for transfers between devices, shards(): all_queries = lax.all_gather(queries, 'expert', axis=0, tiled=True)  18.1 us
    all_to_all x1, waiting for transfers between devices, shards(): lax.all_to_all(projected.reshape(n, token_count, owned * RANK), 'expert',...  8.67 us
    dot_general x1, matrix products, shards(): lax.dot_general(everyone, weights, (((1,), (1,)), ((), ())), preferred_el...  6.44 us
    all_to_all x1, starting transfers between devices, shards(): lax.all_to_all(projected.reshape(n, token_count, owned * RANK), 'expert',...  3.53 us
    dot_general x1, matrix products, shards(): lax.dot_general(sketches.astype(jnp.bfloat16), all_queries, (((1,), (1,))...  2.84 us
  transfers between devices with their start and end apart: 3, of which 3 were waited for; matrix products, arithmetic and copies ran while one was open for 12% of the time, Pallas kernels for 0%

profile of v1, /device:TPU:0, one launch (start us, length us, event | category | flops | bytes accessed | tf_op | source)
XLA Modules:
  0.0 141.0 jit_solution(17492686935054161711)
XLA Ops:
  7.2 0.0 copy-start
  7.2 0.0 all-gather.3.cloned.1.call-start
  7.2 0.7 all-gather.3.cloned.1.call-update
  7.9 0.0 all-gather.5.cloned.1.call-start
  8.0 0.7 all-gather.5.cloned.1.call-update
  8.7 0.7 select_reduce_fusion
  9.4 1.5 %fusion.3 = f32[64,64]{0,1:T(8,128)S(1)} fusion(bf16[64,4096]{1,0:T(8,128)(2,1)} %param.9, bf16[4096,64]{0,1:T(8,128)(2,1)} %param.14), kind=kOutput, calls=%fused_computation.14 | convolution fusion | flops 33554432 | bytes 1064960 | tf_op jit(solution)/shard_map/dot_general | solution.py:24
  10.9 0.9 multiply_convert_fusion
  11.8 76.0 %all-gather.3.cloned.1.call-done = bf16[1024,4096]{1,0:T(8,128)(2,1)} async-done(((bf16[64,4096]{1,0:T(8,128)(2,1)}), bf16[1024,4096]{1,0:T(8,128)(2,1)}) %all-gather.3.cloned.1.call-update) | async-done | bytes 8388624 | tf_op jit(solution)/shard_map/all_gather | solution.py:15
  87.8 0.0 copy-done
  87.8 0.0 copy-start.3
  87.8 6.4 %convolution_convert_fusion = bf16[1024,128]{1,0:T(8,128)(2,1)} fusion(bf16[1024,4096]{1,0:T(8,128)(2,1)} %all-gather.3.cloned.1.call-done, bf16[128,4096]{1,0:T(8,128)(2,1)S(1)} %bitcast.29), kind=kOutput, calls=%fused_computation.1 | convolution fusion | flops 1073872896 | bytes 9699328 | tf_op jit(solution)/shard_map/dot_general | solution.py:18
  94.3 3.5 %all-to-all-start = ((bf16[16,64,128]{2,1,0:T(8,128)(2,1)}), bf16[16,64,128]{2,1,0:T(8,128)(2,1)S(1)}, u32[]{:S(2)}, u32[]{:S(2)}) async-start(bf16[16,64,128]{2,1,0:T(8,128)(2,1)} %bitcast.2), calls=%async_computation | async-start | bytes 524288 | tf_op jit(solution)/shard_map/all_to_all | solution.py:21
  97.8 0.0 copy-done.3
  97.8 1.2 broadcast_select_fusion
  99.0 2.4 %select_n.14 = bf16[2048,256]{0,1:T(8,128)(2,1)} reshape(bf16[32,64,4,64]{1,0,3,2:T(8,128)(2,1)S(1)} %broadcast_select_fusion) | data formatting | bytes 2097152 | tf_op jit(solution)/shard_map/jit(_where)/select_n | solution.py:31
  101.5 0.0 copy-start.1
  101.5 0.1 convert_reduce_fusion
  101.6 8.7 %all-to-all-done = bf16[16,64,128]{2,1,0:T(8,128)(2,1)S(1)} async-done(((bf16[16,64,128]{2,1,0:T(8,128)(2,1)}), bf16[16,64,128]{2,1,0:T(8,128)(2,1)S(1)}, u32[]{:S(2)}, u32[]{:S(2)}) %all-to-all-start) | async-done | bytes 262176 | tf_op jit(solution)/shard_map/all_to_all | solution.py:21
  110.3 0.2 reshape.82
  110.5 1.4 copy.14
  111.9 0.5 reshape.85
  112.3 0.0 copy-done.1
  112.3 0.6 convolution_bitcast_fusion
  113.0 0.1 reshape.84
  113.1 0.1 broadcast_divide_fusion
  113.2 0.0 copy-start.2
  113.2 18.1 %all-gather.5.cloned.1.call-done = bf16[256,4096]{1,0:T(8,128)(2,1)} async-done(((bf16[16,4096]{1,0:T(8,128)(2,1)}), bf16[256,4096]{1,0:T(8,128)(2,1)}) %all-gather.5.cloned.1.call-update) | async-done | bytes 2097168 | tf_op jit(solution)/shard_map/all_gather | solution.py:16
  131.3 2.8 %fusion = f32[4,256]{1,0:T(4,128)} fusion(bf16[256,4096]{1,0:T(8,128)(2,1)} %all-gather.5.cloned.1.call-done, f32[4,4096]{1,0:T(4,128)S(1)} %broadcast_divide_fusion), kind=kOutput, calls=%fused_computation.6 | convolution fusion | flops 8404992 | bytes 2166784 | tf_op jit(solution)/shard_map/dot_general | solution.py:39
  134.1 0.0 copy-done.2
  (1 shorter events, 0.0 us)
Async XLA Ops:
  7.2 80.6 %copy-start = (bf16[2,4096,64]{1,2,0:T(8,128)(2,1)S(1)}, bf16[2,4096,64]{1,2,0:T(8,128)(2,1)}, u32[]{:S(2)}) copy-start(bf16[2,4096,64]{1,2,0:T(8,128)(2,1)} %param.13) | copy-start | bytes 3145732
  7.2 80.6 %all-gather.3.cloned.1.call-start = ((), (), s32[]{:S(2)}) async-start(), calls=%async_computation.1 | async-start | bytes 8912896 | tf_op jit(solution)/shard_map/all_gather | solution.py:15
  7.9 123.4 %all-gather.5.cloned.1.call-start = ((), (), s32[]{:S(2)}) async-start(), calls=%async_computation.2 | async-start | bytes 2228224 | tf_op jit(solution)/shard_map/all_gather | solution.py:16
  87.8 10.0 %copy-start.3 = (s32[1,64]{1,0:T(1,128)S(1)}, s32[1,64]{1,0:T(1,128)}, u32[]{:S(2)}) copy-start(s32[1,64]{1,0:T(1,128)} %param.12) | copy-start | bytes 772
  94.3 16.0 %all-to-all-start = ((bf16[16,64,128]{2,1,0:T(8,128)(2,1)}), bf16[16,64,128]{2,1,0:T(8,128)(2,1)S(1)}, u32[]{:S(2)}, u32[]{:S(2)}) async-start(bf16[16,64,128]{2,1,0:T(8,128)(2,1)} %bitcast.2), calls=%async_computation | async-start | bytes 524288 | tf_op jit(solution)/shard_map/all_to_all | solution.py:21
  101.5 10.9 %copy-start.1 = (bf16[2048,256]{0,1:T(8,128)(2,1)S(1)}, bf16[2048,256]{0,1:T(8,128)(2,1)}, u32[]{:S(2)}) copy-start(bf16[2048,256]{0,1:T(8,128)(2,1)} %select_n.14) | copy-start | bytes 3145732
  113.2 21.0 %copy-start.2 = (f32[4,4096]{1,0:T(4,128)}, f32[4,4096]{1,0:T(4,128)S(1)}, u32[]{:S(2)}) copy-start(f32[4,4096]{1,0:T(4,128)S(1)} %broadcast_divide_fusion) | copy-start | bytes 196612
Sparse Core Ops, SparseCore 0:
  10.2 77.5 all-gather.2
  90.0 41.2 all-gather.4

commit v2 on v1

v2 whole, which is shorter than its diff:
```python
import functools

import jax
import jax.numpy as jnp
from jax import lax
from jax.experimental import pallas as pl
from jax.experimental.pallas import tpu as pltpu
from jax.sharding import PartitionSpec as P

RANK = 64
EX_DEV = 4
QUAD = 4

NT = (((1,), (1,)), ((), ()))
TN = (((0,), (0,)), ((), ()))


def combine_kernel(blocks, experts, first, last, *refs):
    sides, wide = refs[:blocks], refs[blocks]
    total = jnp.zeros((RANK, EX_DEV * RANK), jnp.float32) if first else refs[blocks + 1][...]
    out = refs[-1]
    for b in range(blocks):
        for e in range(experts):
            total += lax.dot_general(
                sides[b][:, e * RANK : (e + 1) * RANK],
                wide[b * experts + e],
                TN,
                preferred_element_type=jnp.float32,
            )
    if last:
        counts = refs[-2]
        for x in range(EX_DEV):
            out[x] = total[:, x * RANK : (x + 1) * RANK] / counts[x : x + 1, :]
    else:
        out[...] = total


def combine(sides, wide, total=None, counts=None):
    experts = wide.shape[0] // len(sides)
    extra = [a for a in (total, counts) if a is not None]
    shape = (RANK, EX_DEV * RANK) if counts is None else (EX_DEV, RANK, RANK)
    return pl.pallas_call(
        functools.partial(combine_kernel, len(sides), experts, total is None, counts is not None),
        out_shape=jax.ShapeDtypeStruct(shape, jnp.float32),
        in_specs=[pl.BlockSpec(memory_space=pltpu.VMEM)] * (len(sides) + 1 + len(extra)),
        out_specs=pl.BlockSpec(memory_space=pltpu.VMEM),
        compiler_params=pltpu.CompilerParams(vmem_limit_bytes=32 << 20),
        name="combine",
    )(*sides, wide, *extra)


def shards(tokens, out_grad, routes, route_weight, example_ids, in_proj, out_proj, queries):
    token_count, model_width = tokens.shape
    owned = in_proj.shape[0]
    n = lax.axis_size("expert")
    planes = n // QUAD
    me = lax.axis_index("expert")
    plane, spot = me // QUAD, me % QUAD

    def move(array, hops):
        pairs = [(a * QUAD + q, b * QUAD + q) for a, b in hops for q in range(QUAD)]
        return lax.ppermute(array, "expert", pairs)

    def swap(array, bit):
        return lax.ppermute(array, "expert", [(i, i ^ bit) for i in range(n)])

    weights = jnp.swapaxes(in_proj, 1, 2).reshape(owned * RANK, model_width)

    up, down = tokens, tokens
    arrived = []
    over_y = swap(weights, 2)
    for s in range(1, planes):
        up_hops = [(p, p + 1) for p in range(s - 1, planes - 1)]
        down_hops = [(p, p - 1) for p in range(1, planes - s + 1)]
        up_ok, down_ok = plane >= s, plane < planes - s
        up_home = [(p, p - s) for p in range(s, planes)]
        down_home = [(p, p + s) for p in range(planes - s)]
        if 2 * s > planes + 1:
            up = down = move(up, up_hops + down_hops)
        else:
            up, down = move(up, up_hops), move(down, down_hops)
            if 2 * s >= planes:
                up = down = up + down
        if 2 * s >= planes:
            origin = jnp.where(up_ok, plane - s, jnp.where(down_ok, plane + s, -1))
            arrived.append((up, origin, up_home + down_home))
        else:
            arrived.append((up, jnp.where(up_ok, plane - s, -1), up_home))
            arrived.append((down, jnp.where(down_ok, plane + s, -1), down_home))
    over_core = swap(weights, 1)
    across = swap(over_y, 1)
    all_queries = lax.all_gather(queries, "expert", axis=0, tiled=True)
    quad_weights = jnp.concatenate([weights, over_core, over_y, across], axis=0)

    def project(block):
        return lax.dot_general(block, quad_weights, NT, preferred_element_type=jnp.float32).astype(jnp.bfloat16)

    returned, homes = [], []
    own = project(tokens)
    for block, origin, home in arrived:
        returned.append(move(project(block), home))
        back = -jnp.ones((), jnp.int32)
        for a, b in home:
            back = jnp.where(plane == b, a, back)
        homes.append(back)

    grad_side = jnp.dot(out_grad, out_proj, preferred_element_type=jnp.float32)
    rel = jnp.arange(QUAD, dtype=jnp.int32)
    inner = ((spot ^ rel)[:, None] * owned + jnp.arange(owned, dtype=jnp.int32)[None, :]).reshape(-1)
    place = jnp.stack([plane] + homes)
    expert_ids = jnp.where(place[:, None] >= 0, place[:, None] * (QUAD * owned) + inner[None, :], -1).reshape(-1)
    gate = jnp.sum(
        jnp.where(routes.T[None, :, :] == expert_ids[:, None, None], route_weight.T[None, :, :], 0.0), axis=1
    )
    local_ids = example_ids.reshape(token_count)
    member = local_ids[:, None] == jnp.arange(EX_DEV, dtype=jnp.int32)[None, :]
    counts = jnp.sum(member.astype(jnp.float32), axis=0)
    counts = jnp.broadcast_to(counts[:, None], (EX_DEV, RANK))
    repeated = jnp.concatenate([grad_side] * EX_DEV, axis=1)
    widely = jnp.repeat(member, RANK, axis=1)
    wide = jnp.where(
        widely[None], (gate[:, :, None] * repeated[None]).astype(jnp.bfloat16), jnp.zeros((), jnp.bfloat16)
    )
    experts = QUAD * owned
    early = combine([own] + returned[:-1], wide[:-experts])
    sketches = combine([returned[-1]], wide[-experts:], early, counts)
    sketches = sketches.reshape(EX_DEV, RANK * RANK)
    scores = lax.dot_general(sketches.astype(jnp.bfloat16), all_queries, NT, preferred_element_type=jnp.float32)
    return (sketches, scores)


def solution(mesh):
    placed = (
        P(("groups", "expert"), None),
        P(("groups", "expert"), None),
        P(("groups", "expert"), None),
        P(("groups", "expert"), None),
        P(("groups", "expert"), None),
        P("expert", None, None),
        P(),
        P("expert", None),
    )
    return jax.shard_map(
        shards,
        mesh=mesh,
        in_specs=placed,
        out_specs=(P(("groups", "expert"), None), P(("groups", "expert"), None)),
        check_vma=False,
    )
```

time: 141 us -> 113 us (0.80)
  waiting for transfers between devices: 104 us -> 56.7 us
  starting transfers between devices: 3.61 us -> 22.4 us
  local copies, waits for them, and re-layouts: 4.62 us -> 0.83 us
  other arithmetic: 3.08 us -> 5.45 us
    all_gather x1 -> x0, waiting for transfers between devices: 76 us -> none  [shards(): everyone = lax.all_gather(tokens, 'expert', axis=0, tiled=True)]
    ppermute x0 -> x12, waiting for transfers between devices: none -> 56.6 us  [the longest x9 38.6 us: move(): return lax.ppermute(array, 'expert', pairs)]
    ppermute x0 -> x12, starting transfers between devices: none -> 22.4 us  [the longest x9 19.3 us: move(): return lax.ppermute(array, 'expert', pairs)]
    all_gather x1, waiting for transfers between devices: 18.1 us -> 0.02 us  [shards(): all_queries = lax.all_gather(queries, 'expert', axis=0, tiled=True)]
    all_to_all x1 -> x0, waiting for transfers between devices: 8.67 us -> none  [shards(): lax.all_to_all(projected.reshape(n, token_count, owned * RANK), 'expert',...]
    all_to_all x1 -> x0, starting transfers between devices: 3.53 us -> none  [shards(): lax.all_to_all(projected.reshape(n, token_count, owned * RANK), 'expert',...]
    select_n x1, local copies, waits for them, and re-layouts: 2.43 us -> 0.08 us  [shards(): jnp.where(place[:, None] >= 0, place[:, None] * (QUAD * owned) + inner[No...]
    reshape x4 -> x1, local copies, waits for them, and re-layouts: 2.17 us -> 0.11 us  [shards(): sketches = sketches.reshape(EX_DEV, RANK * RANK)]
  transfers between devices with their start and end apart: 3 -> 13, of which waited for: 3 -> 4; matrix products, arithmetic and copies ran while one was open for 12% -> 14% of each run, Pallas kernels for 0% -> 1%
where the time goes in v2:
time: 113 us
  waiting for transfers between devices  56.7 us (50%)
  starting transfers between devices  22.4 us (20%)
  between operations  14.3 us (13%)
  matrix products  12.2 us (11%)
  other arithmetic  5.45 us (5%)
    ppermute x9, waiting for transfers between devices, move(): return lax.ppermute(array, 'expert', pairs)  38.6 us
    ppermute x9, starting transfers between devices, move(): return lax.ppermute(array, 'expert', pairs)  19.3 us
    ppermute x3, waiting for transfers between devices, swap(): return lax.ppermute(array, 'expert', [(i, i ^ bit) for i in range(n)])  18.1 us
    dot_general x5, matrix products, project(): lax.dot_general(block, quad_weights, NT, preferred_element_type=jnp.float32)  7.99 us
    ppermute x3, starting transfers between devices, swap(): return lax.ppermute(array, 'expert', [(i, i ^ bit) for i in range(n)])  3.11 us
    dot_general x1, matrix products, shards(): lax.dot_general(sketches.astype(jnp.bfloat16), all_queries, NT, preferred...  2.84 us
  transfers between devices with their start and end apart: 13, of which 4 were waited for; matrix products, arithmetic and copies ran while one was open for 14% of the time, Pallas kernels for 1%

profile of v2, /device:TPU:0, one launch (start us, length us, event | category | flops | bytes accessed | tf_op | source)
XLA Modules:
  0.0 112.9 jit_solution(258550720749533009)
XLA Ops:
  7.2 0.0 copy-start
  7.2 0.0 copy-start.4
  7.2 0.0 all-gather.2.cloned.1.call-start
  7.2 3.0 %collective-permute-start.6 = (bf16[128,4096]{1,0:T(8,128)(2,1)}, bf16[128,4096]{1,0:T(8,128)(2,1)S(1)}, u32[]{:S(2)}, u32[]{:S(2)}) collective-permute-start(bf16[128,4096]{1,0:T(8,128)(2,1)} %bitcast.30), channel_id=1, source_target_pairs={{0,2},{1,3},{2,0},{3,1},{4,6},{5,7},{6,4},{7,5},{8,10},{9,11},{10,... | collective-permute-start | bytes 3145736 | tf_op jit(solution)/shard_map/ppermute | solution.py:65
  10.3 4.3 %collective-permute-start = (bf16[64,4096]{1,0:T(8,128)(2,1)}, bf16[64,4096]{1,0:T(8,128)(2,1)}, u32[]{:S(2)}, u32[]{:S(2)}) collective-permute-start(bf16[64,4096]{1,0:T(8,128)(2,1)} %param.8), channel_id=1, source_target_pairs={{0,4},{1,5},{2,6},{3,7},{4,8},{5,9},{6,10},{7,11},{8,12},{9,13},{1... | collective-permute-start | bytes 1572872 | tf_op jit(solution)/shard_map/ppermute | solution.py:62
  14.6 1.3 %collective-permute-start.2 = (bf16[64,4096]{1,0:T(8,128)(2,1)}, bf16[64,4096]{1,0:T(8,128)(2,1)S(1)}, u32[]{:S(2)}, u32[]{:S(2)}) collective-permute-start(bf16[64,4096]{1,0:T(8,128)(2,1)} %param.8), channel_id=1, source_target_pairs={{4,0},{5,1},{6,2},{7,3},{8,4},{9,5},{10,6},{11,7},{12,8},{13,9},{1... | collective-permute-start | bytes 1572872 | tf_op jit(solution)/shard_map/ppermute | solution.py:62
  15.8 0.1 collective-permute-start.5
  15.9 0.0 all-gather.2.cloned.1.call-update
  16.0 0.1 stack.23
  16.1 0.1 iota_add_fusion
  16.2 0.7 iota_compare_fusion
  16.9 0.1 add.52
  17.0 18.0 %collective-permute-done.6 = bf16[128,4096]{1,0:T(8,128)(2,1)S(1)} collective-permute-done((bf16[128,4096]{1,0:T(8,128)(2,1)}, bf16[128,4096]{1,0:T(8,128)(2,1)S(1)}, u32[]{:S(2)}, u32[]{:S(2)}) %collective-permute-start.6) | collective-permute-done | bytes 1048608 | tf_op jit(solution)/shard_map/ppermute | solution.py:65
  35.1 0.1 add_select_fusion
  35.1 1.3 %fusion.6 = f32[64,64]{1,0:T(8,128)S(1)} fusion(bf16[64,4096]{1,0:T(8,128)(2,1)S(1)} %copy-done, bf16[4096,64]{0,1:T(8,128)(2,1)} %param.14), kind=kOutput, calls=%fused_computation.22 | convolution fusion | flops 33554432 | bytes 1064960 | tf_op jit(solution)/shard_map/dot_general | solution.py:107
  36.5 1.5 %collective-permute-start.1 = (bf16[64,4096]{1,0:T(8,128)(2,1)}, bf16[64,4096]{1,0:T(8,128)(2,1)}, u32[]{:S(2)}, u32[]{:S(2)}) collective-permute-start(bf16[64,4096]{1,0:T(8,128)(2,1)} %collective-permute-done), channel_id=1, source_target_pairs={{4,8},{5,9},{6,10},{7,11},{8,12},{9,13},{10,14},{11,15},{20,24},{2... | collective-permute-start | bytes 1572872 | tf_op jit(solution)/shard_map/ppermute | solution.py:62
  37.9 1.3 %collective-permute-start.3 = (bf16[64,4096]{1,0:T(8,128)(2,1)S(1)}, bf16[64,4096]{1,0:T(8,128)(2,1)}, u32[]{:S(2)}, u32[]{:S(2)}) collective-permute-start(bf16[64,4096]{1,0:T(8,128)(2,1)S(1)} %collective-permute-done.2), channel_id=1, source_target_pairs={{4,0},{5,1},{6,2},{7,3},{8,4},{9,5},{10,6},{11,7},{20,16},{21,17},... | collective-permute-start | bytes 1572872 | tf_op jit(solution)/shard_map/ppermute | solution.py:62
  39.2 0.1 pad_maximum_fusion.1
  39.3 0.1 select_n.82
  39.4 0.1 broadcast_in_dim.56
  39.5 0.1 broadcast_in_dim.57
  39.7 0.8 select_reduce_fusion
  40.5 0.4 fusion
  40.9 0.1 slice.9.refs_4_
  41.1 0.1 convert_reduce_fusion
  41.2 23.7 %collective-permute-done.3 = bf16[64,4096]{1,0:T(8,128)(2,1)} collective-permute-done((bf16[64,4096]{1,0:T(8,128)(2,1)S(1)}, bf16[64,4096]{1,0:T(8,128)(2,1)}, u32[]{:S(2)}, u32[]{:S(2)}) %collective-permute-start.3) | collective-permute-done | bytes 524320 | tf_op jit(solution)/shard_map/ppermute | solution.py:62
  64.8 1.3 %add.46 = bf16[64,4096]{1,0:T(8,128)(2,1)S(1)} add(bf16[64,4096]{1,0:T(8,128)(2,1)} %collective-permute-done.1, bf16[64,4096]{1,0:T(8,128)(2,1)} %collective-permute-done.3) | non-fusion elementwise | flops 262144 | bytes 1572864 | tf_op jit(solution)/shard_map/add | solution.py:83
  66.2 1.3 %collective-permute-start.4 = (bf16[64,4096]{1,0:T(8,128)(2,1)S(1)}, bf16[64,4096]{1,0:T(8,128)(2,1)S(1)}, u32[]{:S(2)}, u32[]{:S(2)}) collective-permute-start(bf16[64,4096]{1,0:T(8,128)(2,1)S(1)} %add.46), channel_id=1, source_target_pairs={{8,12},{9,13},{10,14},{11,15},{4,0},{5,1},{6,2},{7,3},{24,28},{25,... | collective-permute-start | bytes 1572872 | tf_op jit(solution)/shard_map/ppermute | solution.py:62
  67.5 1.8 %pad_maximum_fusion = bf16[512,4096]{1,0:T(8,128)(2,1)S(1)} fusion(bf16[128,4096]{1,0:T(8,128)(2,1)} %collective-permute-done.7, bf16[128,4096]{1,0:T(8,128)(2,1)S(1)} %collective-permute-done.6, bf16[128,4096]{1,0:T(8,128)(2,1)} %collective-permute-done.5, bf16[128,4096]{1,0:T(8,128)(2,1)S(1)} %bitcast.32), kind=kLoop, calls=%fused_computation | loop fusion | flops 16777216 | bytes 8388608 | tf_op jit(solution)/shard_map/concatenate | solution.py:93
  69.3 12.6 %collective-permute-done.4 = bf16[64,4096]{1,0:T(8,128)(2,1)S(1)} collective-permute-done((bf16[64,4096]{1,0:T(8,128)(2,1)S(1)}, bf16[64,4096]{1,0:T(8,128)(2,1)S(1)}, u32[]{:S(2)}, u32[]{:S(2)}) %collective-permute-start.4) | collective-permute-done | bytes 524320 | tf_op jit(solution)/shard_map/ppermute | solution.py:62
  81.9 1.4 %convolution_convert_fusion.4 = bf16[64,512]{1,0:T(8,128)(2,1)S(1)} fusion(bf16[64,4096]{1,0:T(8,128)(2,1)S(1)} %collective-permute-done.4, bf16[512,4096]{1,0:T(8,128)(2,1)S(1)} %pad_maximum_fusion), kind=kOutput, calls=%fused_computation.7 | convolution fusion | flops 268468224 | bytes 4784128 | tf_op jit(solution)/shard_map/dot_general | solution.py:96
  83.3 2.0 %collective-permute-start.8 = (bf16[64,512]{1,0:T(8,128)(2,1)S(1)}, bf16[64,512]{1,0:T(8,128)(2,1)S(1)}, u32[]{:S(2)}, u32[]{:S(2)}) collective-permute-start(bf16[64,512]{1,0:T(8,128)(2,1)S(1)} %convolution_convert_fusion.4), channel_id=1, source_target_pairs={{12,0},{13,1},{14,2},{15,3},{0,12},{1,13},{2,14},{3,15},{28,16},{2... | collective-permute-start | bytes 196616 | tf_op jit(solution)/shard_map/ppermute | solution.py:62
  85.4 2.4 %fusion.2 = bf16[64,512]{1,0:T(8,128)(2,1)S(1)} fusion(bf16[512,4096]{1,0:T(8,128)(2,1)S(1)} %pad_maximum_fusion, bf16[64,4096]{1,0:T(8,128)(2,1)} %collective-permute-done), kind=kOutput, calls=%fused_computation.9 | convolution fusion | flops 268468224 | bytes 4784128 | tf_op jit(solution)/shard_map/dot_general | solution.py:96
  87.8 0.0 copy-start.2
  87.8 1.4 %collective-permute-start.9 = (bf16[64,512]{1,0:T(8,128)(2,1)S(1)}, bf16[64,512]{1,0:T(8,128)(2,1)S(1)}, u32[]{:S(2)}, u32[]{:S(2)}) collective-permute-start(bf16[64,512]{1,0:T(8,128)(2,1)S(1)} %fusion.2), channel_id=1, source_target_pairs={{4,0},{5,1},{6,2},{7,3},{8,4},{9,5},{10,6},{11,7},{12,8},{13,9},{1... | collective-permute-start | bytes 196616 | tf_op jit(solution)/shard_map/ppermute | solution.py:62
  89.2 1.4 %fusion.3 = bf16[64,512]{1,0:T(8,128)(2,1)S(1)} fusion(bf16[512,4096]{1,0:T(8,128)(2,1)S(1)} %pad_maximum_fusion, bf16[64,4096]{1,0:T(8,128)(2,1)S(1)} %collective-permute-done.2), kind=kOutput, calls=%fused_computation.10 | convolution fusion | flops 268468224 | bytes 4784128 | tf_op jit(solution)/shard_map/dot_general | solution.py:96
  90.6 4.5 %collective-permute-start.10 = (bf16[64,512]{1,0:T(8,128)(2,1)S(1)}, bf16[64,512]{1,0:T(8,128)(2,1)S(1)}, u32[]{:S(2)}, u32[]{:S(2)}) collective-permute-start(bf16[64,512]{1,0:T(8,128)(2,1)S(1)} %fusion.3), channel_id=1, source_target_pairs={{0,4},{1,5},{2,6},{3,7},{4,8},{5,9},{6,10},{7,11},{8,12},{9,13},{1... | collective-permute-start | bytes 196616 | tf_op jit(solution)/shard_map/ppermute | solution.py:62
  95.2 1.4 %convolution_convert_fusion = bf16[64,512]{1,0:T(8,128)(2,1)S(1)} fusion(bf16[64,4096]{1,0:T(8,128)(2,1)S(1)} %add.46, bf16[512,4096]{1,0:T(8,128)(2,1)S(1)} %pad_maximum_fusion), kind=kOutput, calls=%fused_computation.3 | convolution fusion | flops 268468224 | bytes 4784128 | tf_op jit(solution)/shard_map/dot_general | solution.py:96
  96.6 1.7 %collective-permute-start.11 = (bf16[64,512]{1,0:T(8,128)(2,1)S(1)}, bf16[64,512]{1,0:T(8,128)(2,1)S(1)}, u32[]{:S(2)}, u32[]{:S(2)}) collective-permute-start(bf16[64,512]{1,0:T(8,128)(2,1)S(1)} %convolution_convert_fusion), channel_id=1, source_target_pairs={{8,0},{9,1},{10,2},{11,3},{12,4},{13,5},{14,6},{15,7},{0,8},{1,9},... | collective-permute-start | bytes 196616 | tf_op jit(solution)/shard_map/ppermute | solution.py:62
  98.3 1.4 %fusion.1.refs_0_ = bf16[64,512]{1,0:T(8,128)(2,1)S(1)} fusion(bf16[512,4096]{1,0:T(8,128)(2,1)S(1)} %pad_maximum_fusion, bf16[64,4096]{1,0:T(8,128)(2,1)S(1)} %copy-done.2), kind=kOutput, calls=%fused_computation.8 | convolution fusion | flops 268468224 | bytes 4784128 | tf_op jit(solution)/shard_map/dot_general | solution.py:96
  99.7 2.3 %collective-permute-done.11.refs_3_ = bf16[64,512]{1,0:T(8,128)(2,1)S(1)} collective-permute-done((bf16[64,512]{1,0:T(8,128)(2,1)S(1)}, bf16[64,512]{1,0:T(8,128)(2,1)S(1)}, u32[]{:S(2)}, u32[]{:S(2)}) %collective-permute-start.11) | collective-permute-done | bytes 65568 | tf_op jit(solution)/shard_map/ppermute | solution.py:62
  101.9 0.7 combine.2.refs_2_
  102.7 0.1 broadcast_in_dim.64.refs_3_
  102.7 0.4 combine.3
  103.1 0.1 reshape.145
  103.2 0.0 copy-start.3
  103.2 0.0 all-gather.2.cloned.1.call-done
  103.2 2.8 %fusion.4 = f32[4,256]{1,0:T(4,128)} fusion(bf16[256,4096]{1,0:T(8,128)(2,1)} %all-gather.2.cloned.1.call-done, f32[4,4096]{1,0:T(4,128)S(1)} %reshape.145), kind=kOutput, calls=%fused_computation.13 | convolution fusion | flops 8404992 | bytes 2166784 | tf_op jit(solution)/shard_map/dot_general | solution.py:128
  (19 shorter events, 0.1 us)
Async XLA Ops:
  7.2 28.0 %copy-start = (bf16[64,4096]{1,0:T(8,128)(2,1)S(1)}, bf16[64,4096]{1,0:T(8,128)(2,1)}, u32[]{:S(2)}) copy-start(bf16[64,4096]{1,0:T(8,128)(2,1)} %param.9) | copy-start | bytes 1572868
  7.2 60.3 %copy-start.1 = (bf16[2,4096,64]{1,2,0:T(8,128)(2,1)S(1)}, bf16[2,4096,64]{1,2,0:T(8,128)(2,1)}, u32[]{:S(2)}) copy-start(bf16[2,4096,64]{1,2,0:T(8,128)(2,1)} %param.13) | copy-start | bytes 3145732
  7.2 33.9 %copy-start.4 = (s32[1,64]{1,0:T(1,128)S(1)}, s32[1,64]{1,0:T(1,128)}, u32[]{:S(2)}) copy-start(s32[1,64]{1,0:T(1,128)} %param.12) | copy-start | bytes 772
  7.2 96.0 %all-gather.2.cloned.1.call-start = ((), (), s32[]{:S(2)}) async-start(), calls=%async_computation | async-start | bytes 2228224 | tf_op jit(solution)/shard_map/all_gather | solution.py:92
  7.2 27.8 %collective-permute-start.6 = (bf16[128,4096]{1,0:T(8,128)(2,1)}, bf16[128,4096]{1,0:T(8,128)(2,1)S(1)}, u32[]{:S(2)}, u32[]{:S(2)}) collective-permute-start(bf16[128,4096]{1,0:T(8,128)(2,1)} %bitcast.30), channel_id=1, source_target_pairs={{0,2},{1,3},{2,0},{3,1},{4,6},{5,7},{6,4},{7,5},{8,10},{9,11},{10,... | collective-permute-start | bytes 3145736 | tf_op jit(solution)/shard_map/ppermute | solution.py:65
  10.3 26.2 %collective-permute-start = (bf16[64,4096]{1,0:T(8,128)(2,1)}, bf16[64,4096]{1,0:T(8,128)(2,1)}, u32[]{:S(2)}, u32[]{:S(2)}) collective-permute-start(bf16[64,4096]{1,0:T(8,128)(2,1)} %param.8), channel_id=1, source_target_pairs={{0,4},{1,5},{2,6},{3,7},{4,8},{5,9},{6,10},{7,11},{8,12},{9,13},{1... | collective-permute-start | bytes 1572872 | tf_op jit(solution)/shard_map/ppermute | solution.py:62
  14.6 23.4 %collective-permute-start.2 = (bf16[64,4096]{1,0:T(8,128)(2,1)}, bf16[64,4096]{1,0:T(8,128)(2,1)S(1)}, u32[]{:S(2)}, u32[]{:S(2)}) collective-permute-start(bf16[64,4096]{1,0:T(8,128)(2,1)} %param.8), channel_id=1, source_target_pairs={{4,0},{5,1},{6,2},{7,3},{8,4},{9,5},{10,6},{11,7},{12,8},{13,9},{1... | collective-permute-start | bytes 1572872 | tf_op jit(solution)/shard_map/ppermute | solution.py:62
  15.8 51.6 %collective-permute-start.5 = (bf16[128,4096]{1,0:T(8,128)(2,1)}, bf16[128,4096]{1,0:T(8,128)(2,1)}, u32[]{:S(2)}, u32[]{:S(2)}) collective-permute-start(bf16[128,4096]{1,0:T(8,128)(2,1)} %bitcast.31), channel_id=1, source_target_pairs={{0,1},{1,0},{2,3},{3,2},{4,5},{5,4},{6,7},{7,6},{8,9},{9,8},{10,11... | collective-permute-start | bytes 3145736 | tf_op jit(solution)/shard_map/ppermute | solution.py:65
  35.1 32.4 %collective-permute-start.7 = (bf16[128,4096]{1,0:T(8,128)(2,1)S(1)}, bf16[128,4096]{1,0:T(8,128)(2,1)}, u32[]{:S(2)}, u32[]{:S(2)}) collective-permute-start(bf16[128,4096]{1,0:T(8,128)(2,1)S(1)} %collective-permute-done.6), channel_id=1, source_target_pairs={{0,1},{1,0},{2,3},{3,2},{4,5},{5,4},{6,7},{7,6},{8,9},{9,8},{10,11... | collective-permute-start | bytes 3145736 | tf_op jit(solution)/shard_map/ppermute | solution.py:65
  36.5 4.7 %collective-permute-start.1 = (bf16[64,4096]{1,0:T(8,128)(2,1)}, bf16[64,4096]{1,0:T(8,128)(2,1)}, u32[]{:S(2)}, u32[]{:S(2)}) collective-permute-start(bf16[64,4096]{1,0:T(8,128)(2,1)} %collective-permute-done), channel_id=1, source_target_pairs={{4,8},{5,9},{6,10},{7,11},{8,12},{9,13},{10,14},{11,15},{20,24},{2... | collective-permute-start | bytes 1572872 | tf_op jit(solution)/shard_map/ppermute | solution.py:62
  37.9 26.9 %collective-permute-start.3 = (bf16[64,4096]{1,0:T(8,128)(2,1)S(1)}, bf16[64,4096]{1,0:T(8,128)(2,1)}, u32[]{:S(2)}, u32[]{:S(2)}) collective-permute-start(bf16[64,4096]{1,0:T(8,128)(2,1)S(1)} %collective-permute-done.2), channel_id=1, source_target_pairs={{4,0},{5,1},{6,2},{7,3},{8,4},{9,5},{10,6},{11,7},{20,16},{21,17},... | collective-permute-start | bytes 1572872 | tf_op jit(solution)/shard_map/ppermute | solution.py:62
  66.2 15.8 %collective-permute-start.4 = (bf16[64,4096]{1,0:T(8,128)(2,1)S(1)}, bf16[64,4096]{1,0:T(8,128)(2,1)S(1)}, u32[]{:S(2)}, u32[]{:S(2)}) collective-permute-start(bf16[64,4096]{1,0:T(8,128)(2,1)S(1)} %add.46), channel_id=1, source_target_pairs={{8,12},{9,13},{10,14},{11,15},{4,0},{5,1},{6,2},{7,3},{24,28},{25,... | collective-permute-start | bytes 1572872 | tf_op jit(solution)/shard_map/ppermute | solution.py:62
  83.3 19.3 %collective-permute-start.8 = (bf16[64,512]{1,0:T(8,128)(2,1)S(1)}, bf16[64,512]{1,0:T(8,128)(2,1)S(1)}, u32[]{:S(2)}, u32[]{:S(2)}) collective-permute-start(bf16[64,512]{1,0:T(8,128)(2,1)S(1)} %convolution_convert_fusion.4), channel_id=1, source_target_pairs={{12,0},{13,1},{14,2},{15,3},{0,12},{1,13},{2,14},{3,15},{28,16},{2... | collective-permute-start | bytes 196616 | tf_op jit(solution)/shard_map/ppermute | solution.py:62
  87.8 10.5 %copy-start.2 = (bf16[64,4096]{1,0:T(8,128)(2,1)S(1)}, bf16[64,4096]{1,0:T(8,128)(2,1)}, u32[]{:S(2)}) copy-start(bf16[64,4096]{1,0:T(8,128)(2,1)} %param.8) | copy-start | bytes 1572868
  87.8 11.9 %collective-permute-start.9 = (bf16[64,512]{1,0:T(8,128)(2,1)S(1)}, bf16[64,512]{1,0:T(8,128)(2,1)S(1)}, u32[]{:S(2)}, u32[]{:S(2)}) collective-permute-start(bf16[64,512]{1,0:T(8,128)(2,1)S(1)} %fusion.2), channel_id=1, source_target_pairs={{4,0},{5,1},{6,2},{7,3},{8,4},{9,5},{10,6},{11,7},{12,8},{13,9},{1... | collective-permute-start | bytes 196616 | tf_op jit(solution)/shard_map/ppermute | solution.py:62
  90.6 9.1 %collective-permute-start.10 = (bf16[64,512]{1,0:T(8,128)(2,1)S(1)}, bf16[64,512]{1,0:T(8,128)(2,1)S(1)}, u32[]{:S(2)}, u32[]{:S(2)}) collective-permute-start(bf16[64,512]{1,0:T(8,128)(2,1)S(1)} %fusion.3), channel_id=1, source_target_pairs={{0,4},{1,5},{2,6},{3,7},{4,8},{5,9},{6,10},{7,11},{8,12},{9,13},{1... | collective-permute-start | bytes 196616 | tf_op jit(solution)/shard_map/ppermute | solution.py:62
  96.6 5.4 %collective-permute-start.11 = (bf16[64,512]{1,0:T(8,128)(2,1)S(1)}, bf16[64,512]{1,0:T(8,128)(2,1)S(1)}, u32[]{:S(2)}, u32[]{:S(2)}) collective-permute-start(bf16[64,512]{1,0:T(8,128)(2,1)S(1)} %convolution_convert_fusion), channel_id=1, source_target_pairs={{8,0},{9,1},{10,2},{11,3},{12,4},{13,5},{14,6},{15,7},{0,8},{1,9},... | collective-permute-start | bytes 196616 | tf_op jit(solution)/shard_map/ppermute | solution.py:62
  103.2 2.9 %copy-start.3 = (f32[4,4096]{1,0:T(4,128)}, f32[4,4096]{1,0:T(4,128)S(1)}, u32[]{:S(2)}) copy-start(f32[4,4096]{1,0:T(4,128)S(1)} %reshape.145) | copy-start | bytes 196612
Sparse Core Ops, SparseCore 0:
  16.1 44.3 all-gather.1

commit v3 on v2

--- a/solution.py
+++ b/solution.py
@@ -49,12 +49,45 @@
     )(*sides, wide, *extra)
 
 
+def assemble_kernel(planes, groups, here_ref, mine_ref, over_y_ref, rest_ref, out_ref):
+    span = mine_ref.shape[0]
+    rows, columns = span // planes, out_ref.shape[1] // groups
+    sources = (mine_ref, rest_ref, over_y_ref, rest_ref)
+    for rel in range(QUAD):
+        base = span if rel == 3 else 0
+        for d in range(planes):
+            home = lax.rem(here_ref[0] + (planes - d), planes) * QUAD + (here_ref[1] ^ rel)
+            row = pl.multiple_of(home * rows, rows)
+            for k in range(groups):
+                column = pl.multiple_of(lax.rem(here_ref[2] + (groups - k), groups) * columns, columns)
+                out_ref[pl.ds(row, rows), pl.ds(column, columns)] = sources[rel][
+                    base + d * rows : base + (d + 1) * rows, k * columns : (k + 1) * columns
+                ]
+
+
+def assemble(here, mine, over_y, rest, planes, groups):
+    span, width = mine.shape
+    vmem = pl.BlockSpec(memory_space=pltpu.VMEM)
+    return pl.pallas_call(
+        functools.partial(assemble_kernel, planes, groups),
+        out_shape=jax.ShapeDtypeStruct((span * QUAD, width), mine.dtype),
+        in_specs=[pl.BlockSpec(memory_space=pltpu.SMEM), vmem, vmem, vmem],
+        out_specs=vmem,
+        compiler_params=pltpu.CompilerParams(vmem_limit_bytes=32 << 20),
+        name="assemble",
+    )(here, mine, over_y, rest)
+
+
+def after(array, *others):
+    return lax.optimization_barrier((array, *others))[0]
+
+
 def shards(tokens, out_grad, routes, route_weight, example_ids, in_proj, out_proj, queries):
     token_count, model_width = tokens.shape
     owned = in_proj.shape[0]
-    n = lax.axis_size("expert")
+    n, groups = lax.axis_size("expert"), lax.axis_size("groups")
     planes = n // QUAD
-    me = lax.axis_index("expert")
+    me, group = lax.axis_index("expert"), lax.axis_index("groups")
     plane, spot = me // QUAD, me % QUAD
 
     def move(array, hops):
@@ -64,15 +97,11 @@
     def swap(array, bit):
         return lax.ppermute(array, "expert", [(i, i ^ bit) for i in range(n)])
 
-    weights = jnp.swapaxes(in_proj, 1, 2).reshape(owned * RANK, model_width)
-
     up, down = tokens, tokens
-    arrived = []
-    over_y = swap(weights, 2)
+    arrived, steps = [], []
     for s in range(1, planes):
         up_hops = [(p, p + 1) for p in range(s - 1, planes - 1)]
         down_hops = [(p, p - 1) for p in range(1, planes - s + 1)]
-        up_ok, down_ok = plane >= s, plane < planes - s
         up_home = [(p, p - s) for p in range(s, planes)]
         down_home = [(p, p + s) for p in range(planes - s)]
         if 2 * s > planes + 1:
@@ -81,29 +110,37 @@
             up, down = move(up, up_hops), move(down, down_hops)
             if 2 * s >= planes:
                 up = down = up + down
+        steps.append(up)
         if 2 * s >= planes:
-            origin = jnp.where(up_ok, plane - s, jnp.where(down_ok, plane + s, -1))
-            arrived.append((up, origin, up_home + down_home))
+            arrived.append((up, up_home + down_home))
         else:
-            arrived.append((up, jnp.where(up_ok, plane - s, -1), up_home))
-            arrived.append((down, jnp.where(down_ok, plane + s, -1), down_home))
+            arrived.extend([(up, up_home), (down, down_home)])
+
+    weights = jnp.swapaxes(in_proj, 1, 2).reshape(owned * RANK, model_width)
+    over_y = swap(weights, 2)
     over_core = swap(weights, 1)
-    across = swap(over_y, 1)
-    all_queries = lax.all_gather(queries, "expert", axis=0, tiled=True)
+    across = swap(after(over_y, steps[1]), 1)
     quad_weights = jnp.concatenate([weights, over_core, over_y, across], axis=0)
 
-    def project(block):
-        return lax.dot_general(block, quad_weights, NT, preferred_element_type=jnp.float32).astype(jnp.bfloat16)
+    width = queries.shape[1] // groups
+    part = lax.dynamic_slice_in_dim(queries, group * width, width, axis=1)
+    lined = [part] + [move(part, [(p, (p + d) % planes) for p in range(planes)]) for d in range(1, planes)]
+    lined = after(jnp.concatenate(lined, axis=0), steps[0])
+    ranged = [lined] + [
+        lax.ppermute(lined, "groups", [(g, (g + k) % groups) for g in range(groups)]) for k in range(1, groups)
+    ]
+    mine = after(jnp.concatenate(ranged, axis=1), steps[1])
+    mine_over_y = swap(mine, 2)
+    rest = swap(jnp.concatenate([mine, mine_over_y], axis=0), 1)
+    here = jnp.stack([plane, spot, group]).astype(jnp.int32)
+    all_queries = assemble(here, mine, mine_over_y, rest, planes, groups)
 
-    returned, homes = [], []
-    own = project(tokens)
-    for block, origin, home in arrived:
-        returned.append(move(project(block), home))
+    homes = []
+    for _, home in arrived:
         back = -jnp.ones((), jnp.int32)
         for a, b in home:
             back = jnp.where(plane == b, a, back)
         homes.append(back)
-
     grad_side = jnp.dot(out_grad, out_proj, preferred_element_type=jnp.float32)
     rel = jnp.arange(QUAD, dtype=jnp.int32)
     inner = ((spot ^ rel)[:, None] * owned + jnp.arange(owned, dtype=jnp.int32)[None, :]).reshape(-1)
@@ -121,9 +158,16 @@
     wide = jnp.where(
         widely[None], (gate[:, :, None] * repeated[None]).astype(jnp.bfloat16), jnp.zeros((), jnp.bfloat16)
     )
+
+    def project(block):
+        return lax.dot_general(block, quad_weights, NT, preferred_element_type=jnp.float32).astype(jnp.bfloat16)
+
     experts = QUAD * owned
-    early = combine([own] + returned[:-1], wide[:-experts])
-    sketches = combine([returned[-1]], wide[-experts:], early, counts)
+    returned = [move(project(block), home) for block, home in arrived[:-1]]
+    early = combine([project(tokens)] + returned, wide[:-experts])
+    block, home = arrived[-1]
+    late = move(project(after(block, early)), home)
+    sketches = combine([late], wide[-experts:], early, counts)
     sketches = sketches.reshape(EX_DEV, RANK * RANK)
     scores = lax.dot_general(sketches.astype(jnp.bfloat16), all_queries, NT, preferred_element_type=jnp.float32)
     return (sketches, scores)

time: 113 us -> 94.3 us (0.83)
  between operations: 14.3 us -> 1.02 us
  waiting for transfers between devices: 56.7 us -> 44.1 us
  starting transfers between devices: 22.4 us -> 30.5 us
  matrix products: 12.2 us -> 9.55 us
    ppermute x9 -> x12, waiting for transfers between devices: 38.6 us -> 28.5 us  [move(): return lax.ppermute(array, 'expert', pairs)]
    ppermute x3 -> x5, waiting for transfers between devices: 18.1 us -> 10.5 us  [swap(): return lax.ppermute(array, 'expert', [(i, i ^ bit) for i in range(n)])]
    ppermute x9 -> x12, starting transfers between devices: 19.3 us -> 25.9 us  [move(): return lax.ppermute(array, 'expert', pairs)]
    ppermute x0 -> x1, waiting for transfers between devices: none -> 5.05 us  [shards(): lax.ppermute(lined, 'groups', [(g, (g + k) % groups) for g in range(group...]
    dot_general x1, matrix products: 2.84 us -> 1.25 us  [shards(): lax.dot_general(sketches.astype(jnp.bfloat16), all_queries, NT, preferred...]
    ppermute x0 -> x1, starting transfers between devices: none -> 1.56 us  [shards(): lax.ppermute(lined, 'groups', [(g, (g + k) % groups) for g in range(group...]
    add x1, other arithmetic: 1.32 us -> 0.12 us  [shards(): up = down = up + down]
    ppermute x3 -> x5, starting transfers between devices: 3.11 us -> 3.05 us  [swap(): return lax.ppermute(array, 'expert', [(i, i ^ bit) for i in range(n)])]
  transfers between devices with their start and end apart: 13 -> 18, of which waited for: 4 -> 8; matrix products, arithmetic and copies ran while one was open for 14% -> 16% of each run, Pallas kernels for 1% -> 1%
where the time goes in v3:
time: 94.3 us; the launch traced here: 93.9 us
  waiting for transfers between devices  44.1 us (47%)
  starting transfers between devices  30.5 us (32%)
  matrix products  9.55 us (10%)
  other arithmetic  5.41 us (6%)
  Pallas kernels  1.75 us (2%)
  local copies, waits for them, and re-layouts  1.69 us (2%)
  between operations  1.02 us (1%)
    ppermute x12, waiting for transfers between devices, move(): return lax.ppermute(array, 'expert', pairs)  28.5 us
    ppermute x12, starting transfers between devices, move(): return lax.ppermute(array, 'expert', pairs)  25.9 us
    ppermute x5, waiting for transfers between devices, swap(): return lax.ppermute(array, 'expert', [(i, i ^ bit) for i in range(n)])  10.5 us
    dot_general x5, matrix products, project(): lax.dot_general(block, quad_weights, NT, preferred_element_type=jnp.float32)  6.97 us
    ppermute x1, waiting for transfers between devices, shards(): lax.ppermute(lined, 'groups', [(g, (g + k) % groups) for g in range(group...  5.05 us
    ppermute x5, starting transfers between devices, swap(): return lax.ppermute(array, 'expert', [(i, i ^ bit) for i in range(n)])  3.05 us
    concatenate x1, other arithmetic, shards(): quad_weights = jnp.concatenate([weights, over_core, over_y, across], axis=0)  2.48 us
  transfers between devices with their start and end apart: 18, of which 8 were waited for; matrix products, arithmetic and copies ran while one was open for 16% of the time, Pallas kernels for 1%

profile of v3, /device:TPU:0, one launch (start us, length us, event | category | flops | bytes accessed | tf_op | source)
XLA Modules:
  0.0 93.9 jit_solution(2532541842442893728)
XLA Ops:
  0.7 5.1 %collective-permute-start = (bf16[64,4096]{1,0:T(8,128)(2,1)}, bf16[64,4096]{1,0:T(8,128)(2,1)S(1)}, u32[]{:S(2)}, u32[]{:S(2)}) collective-permute-start(bf16[64,4096]{1,0:T(8,128)(2,1)} %param.8), channel_id=1, source_target_pairs={{0,4},{1,5},{2,6},{3,7},{4,8},{5,9},{6,10},{7,11},{8,12},{9,13},{1... | collective-permute-start | bytes 1572872 | tf_op jit(solution)/shard_map/ppermute | solution.py:95
  5.8 1.3 %collective-permute-start.2 = (bf16[64,4096]{1,0:T(8,128)(2,1)}, bf16[64,4096]{1,0:T(8,128)(2,1)S(1)}, u32[]{:S(2)}, u32[]{:S(2)}) collective-permute-start(bf16[64,4096]{1,0:T(8,128)(2,1)} %param.8), channel_id=1, source_target_pairs={{4,0},{5,1},{6,2},{7,3},{8,4},{9,5},{10,6},{11,7},{12,8},{13,9},{1... | collective-permute-start | bytes 1572872 | tf_op jit(solution)/shard_map/ppermute | solution.py:95
  7.1 0.8 constant_dynamic-slice_fusion
  7.9 4.7 %collective-permute-start.14 = (bf16[16,2048]{1,0:T(8,128)(2,1)S(1)}, bf16[16,2048]{1,0:T(8,128)(2,1)S(1)}, u32[]{:S(2)}, u32[]{:S(2)}) collective-permute-start(bf16[16,2048]{1,0:T(8,128)(2,1)S(1)} %constant_dynamic-slice_fusion), channel_id=1, source_target_pairs={{0,12},{1,13},{2,14},{3,15},{4,0},{5,1},{6,2},{7,3},{8,4},{9,5},{1... | collective-permute-start | bytes 196616 | tf_op jit(solution)/shard_map/ppermute | solution.py:95
  12.6 1.0 %collective-permute-start.12 = (bf16[16,2048]{1,0:T(8,128)(2,1)S(1)}, bf16[16,2048]{1,0:T(8,128)(2,1)S(1)}, u32[]{:S(2)}, u32[]{:S(2)}) collective-permute-start(bf16[16,2048]{1,0:T(8,128)(2,1)S(1)} %constant_dynamic-slice_fusion), channel_id=1, source_target_pairs={{0,4},{1,5},{2,6},{3,7},{4,8},{5,9},{6,10},{7,11},{8,12},{9,13},{1... | collective-permute-start | bytes 196616 | tf_op jit(solution)/shard_map/ppermute | solution.py:95
  13.6 0.7 iota_compare_fusion
  14.3 1.3 %fusion.6 = f32[64,64]{1,0:T(8,128)S(1)} fusion(bf16[64,4096]{1,0:T(8,128)(2,1)S(1)} %copy-done, bf16[4096,64]{0,1:T(8,128)(2,1)} %param.14), kind=kOutput, calls=%fused_computation.27 | convolution fusion | flops 33554432 | bytes 1064960 | tf_op jit(solution)/shard_map/dot_general | solution.py:144
  15.7 0.1 stack.33
  15.8 7.3 %collective-permute-done.14 = bf16[16,2048]{1,0:T(8,128)(2,1)S(1)} collective-permute-done((bf16[16,2048]{1,0:T(8,128)(2,1)S(1)}, bf16[16,2048]{1,0:T(8,128)(2,1)S(1)}, u32[]{:S(2)}, u32[]{:S(2)}) %collective-permute-start.14) | collective-permute-done | bytes 65568 | tf_op jit(solution)/shard_map/ppermute | solution.py:95
  23.1 1.5 %collective-permute-start.6 = (bf16[128,4096]{1,0:T(8,128)(2,1)}, bf16[128,4096]{1,0:T(8,128)(2,1)}, u32[]{:S(2)}, u32[]{:S(2)}) collective-permute-start(bf16[128,4096]{1,0:T(8,128)(2,1)} %bitcast.32), channel_id=1, source_target_pairs={{0,2},{1,3},{2,0},{3,1},{4,6},{5,7},{6,4},{7,5},{8,10},{9,11},{10,... | collective-permute-start | bytes 3145736 | tf_op jit(solution)/shard_map/ppermute | solution.py:98
  24.7 3.2 %collective-permute-done.13 = bf16[16,2048]{1,0:T(8,128)(2,1)S(1)} collective-permute-done((bf16[16,2048]{1,0:T(8,128)(2,1)S(1)}, bf16[16,2048]{1,0:T(8,128)(2,1)S(1)}, u32[]{:S(2)}, u32[]{:S(2)}) %collective-permute-start.13) | collective-permute-done | bytes 65568 | tf_op jit(solution)/shard_map/ppermute | solution.py:95
  27.9 1.6 %collective-permute-start.15 = (bf16[64,2048]{1,0:T(8,128)(2,1)S(1)}, bf16[64,2048]{1,0:T(8,128)(2,1)S(1)}, u32[]{:S(2)}, u32[]{:S(2)}) collective-permute-start(bf16[64,2048]{1,0:T(8,128)(2,1)S(1)} %pad_maximum_fusion.3), channel_id=1, source_target_pairs={{0,16},{16,0},{1,17},{17,1},{2,18},{18,2},{3,19},{19,3},{4,20},{20... | collective-permute-start | bytes 786440 | tf_op jit(solution)/shard_map/ppermute | solution.py:130
  29.5 0.1 add.55
  29.6 0.7 collective-permute-start.1
  30.3 1.3 %collective-permute-start.3 = (bf16[64,4096]{1,0:T(8,128)(2,1)S(1)}, bf16[64,4096]{1,0:T(8,128)(2,1)S(1)}, u32[]{:S(2)}, u32[]{:S(2)}) collective-permute-start(bf16[64,4096]{1,0:T(8,128)(2,1)S(1)} %collective-permute-done.2), channel_id=1, source_target_pairs={{4,0},{5,1},{6,2},{7,3},{8,4},{9,5},{10,6},{11,7},{20,16},{21,17},... | collective-permute-start | bytes 1572872 | tf_op jit(solution)/shard_map/ppermute | solution.py:95
  31.6 5.1 %collective-permute-done.15 = bf16[64,2048]{1,0:T(8,128)(2,1)S(1)} collective-permute-done((bf16[64,2048]{1,0:T(8,128)(2,1)S(1)}, bf16[64,2048]{1,0:T(8,128)(2,1)S(1)}, u32[]{:S(2)}, u32[]{:S(2)}) %collective-permute-start.15) | collective-permute-done | bytes 262176 | tf_op jit(solution)/shard_map/ppermute | solution.py:130
  36.8 9.5 %collective-permute-done.3 = bf16[64,4096]{1,0:T(8,128)(2,1)S(1)} collective-permute-done((bf16[64,4096]{1,0:T(8,128)(2,1)S(1)}, bf16[64,4096]{1,0:T(8,128)(2,1)S(1)}, u32[]{:S(2)}, u32[]{:S(2)}) %collective-permute-start.3) | collective-permute-done | bytes 524320 | tf_op jit(solution)/shard_map/ppermute | solution.py:95
  46.3 0.1 add.49
  46.4 0.3 collective-permute-done.6
  46.7 1.5 %collective-permute-start.16 = (bf16[64,4096]{1,0:T(8,128)(2,1)S(1)}, bf16[64,4096]{1,0:T(8,128)(2,1)S(1)}, u32[]{:S(2)}, u32[]{:S(2)}) collective-permute-start(bf16[64,4096]{1,0:T(8,128)(2,1)S(1)} %pad_maximum_fusion.2.mine_ref), channel_id=1, source_target_pairs={{0,2},{1,3},{2,0},{3,1},{4,6},{5,7},{6,4},{7,5},{8,10},{9,11},{10,... | collective-permute-start | bytes 1572872 | tf_op jit(solution)/shard_map/ppermute | solution.py:98
  48.2 0.1 pad_maximum_fusion.4
  48.3 0.1 select_n.85
  48.4 0.1 broadcast_in_dim.56
  48.5 0.1 broadcast_in_dim.57
  48.7 0.1 select_reduce_fusion
  48.8 0.4 fusion
  49.2 0.1 slice.8.refs_4_
  49.4 0.1 convert_reduce_fusion
  49.5 1.3 %collective-permute-start.4 = (bf16[64,4096]{1,0:T(8,128)(2,1)S(1)}, bf16[64,4096]{1,0:T(8,128)(2,1)S(1)}, u32[]{:S(2)}, u32[]{:S(2)}) collective-permute-start(bf16[64,4096]{1,0:T(8,128)(2,1)S(1)} %add.49), channel_id=1, source_target_pairs={{8,12},{9,13},{10,14},{11,15},{4,0},{5,1},{6,2},{7,3},{24,28},{25,... | collective-permute-start | bytes 1572872 | tf_op jit(solution)/shard_map/ppermute | solution.py:95
  50.7 10.3 %collective-permute-done.16.over_y_ref = bf16[64,4096]{1,0:T(8,128)(2,1)S(1)} collective-permute-done((bf16[64,4096]{1,0:T(8,128)(2,1)S(1)}, bf16[64,4096]{1,0:T(8,128)(2,1)S(1)}, u32[]{:S(2)}, u32[]{:S(2)}) %collective-permute-start.16) | collective-permute-done | bytes 524320 | tf_op jit(solution)/shard_map/ppermute | solution.py:98
  61.0 1.1 %pad_maximum_fusion.1 = bf16[128,4096]{1,0:T(8,128)(2,1)} fusion(bf16[64,4096]{1,0:T(8,128)(2,1)S(1)} %collective-permute-done.16.over_y_ref, bf16[64,4096]{1,0:T(8,128)(2,1)S(1)} %pad_maximum_fusion.2.mine_ref), kind=kLoop, calls=%fused_computation.11 | loop fusion | flops 2097152 | bytes 2097152 | tf_op jit(solution)/shard_map/concatenate | solution.py:134
  62.1 2.5 %pad_maximum_fusion = bf16[512,4096]{1,0:T(8,128)(2,1)S(1)} fusion(bf16[128,4096]{1,0:T(8,128)(2,1)} %collective-permute-done.7, bf16[128,4096]{1,0:T(8,128)(2,1)} %collective-permute-done.6, bf16[128,4096]{1,0:T(8,128)(2,1)} %collective-permute-done.5, bf16[128,4096]{1,0:T(8,128)(2,1)} %bitcast.34), kind=kLoop, calls=%fused_computation | loop fusion | flops 16777216 | bytes 8388608 | tf_op jit(solution)/shard_map/concatenate | solution.py:123
  64.6 1.4 %fusion.2 = bf16[64,512]{1,0:T(8,128)(2,1)S(1)} fusion(bf16[512,4096]{1,0:T(8,128)(2,1)S(1)} %pad_maximum_fusion, bf16[64,4096]{1,0:T(8,128)(2,1)S(1)} %copy-done.5), kind=kOutput, calls=%fused_computation.9 | convolution fusion | flops 268468224 | bytes 4784128 | tf_op jit(solution)/shard_map/dot_general | solution.py:163
  66.0 1.4 %collective-permute-start.8 = (bf16[64,512]{1,0:T(8,128)(2,1)S(1)}, bf16[64,512]{1,0:T(8,128)(2,1)S(1)}, u32[]{:S(2)}, u32[]{:S(2)}) collective-permute-start(bf16[64,512]{1,0:T(8,128)(2,1)S(1)} %fusion.2), channel_id=1, source_target_pairs={{4,0},{5,1},{6,2},{7,3},{8,4},{9,5},{10,6},{11,7},{12,8},{13,9},{1... | collective-permute-start | bytes 196616 | tf_op jit(solution)/shard_map/ppermute | solution.py:95
  67.5 1.4 %fusion.3 = bf16[64,512]{1,0:T(8,128)(2,1)S(1)} fusion(bf16[512,4096]{1,0:T(8,128)(2,1)S(1)} %pad_maximum_fusion, bf16[64,4096]{1,0:T(8,128)(2,1)S(1)} %copy-done.3), kind=kOutput, calls=%fused_computation.10 | convolution fusion | flops 268468224 | bytes 4784128 | tf_op jit(solution)/shard_map/dot_general | solution.py:163
  68.9 4.5 %collective-permute-start.9 = (bf16[64,512]{1,0:T(8,128)(2,1)S(1)}, bf16[64,512]{1,0:T(8,128)(2,1)S(1)}, u32[]{:S(2)}, u32[]{:S(2)}) collective-permute-start(bf16[64,512]{1,0:T(8,128)(2,1)S(1)} %fusion.3), channel_id=1, source_target_pairs={{0,4},{1,5},{2,6},{3,7},{4,8},{5,9},{6,10},{7,11},{8,12},{9,13},{1... | collective-permute-start | bytes 196616 | tf_op jit(solution)/shard_map/ppermute | solution.py:95
  73.4 1.4 %convolution_convert_fusion.1 = bf16[64,512]{1,0:T(8,128)(2,1)S(1)} fusion(bf16[64,4096]{1,0:T(8,128)(2,1)S(1)} %add.49, bf16[512,4096]{1,0:T(8,128)(2,1)S(1)} %pad_maximum_fusion), kind=kOutput, calls=%fused_computation.4 | convolution fusion | flops 268468224 | bytes 4784128 | tf_op jit(solution)/shard_map/dot_general | solution.py:163
  74.8 2.6 %collective-permute-start.10 = (bf16[64,512]{1,0:T(8,128)(2,1)S(1)}, bf16[64,512]{1,0:T(8,128)(2,1)S(1)}, u32[]{:S(2)}, u32[]{:S(2)}) collective-permute-start(bf16[64,512]{1,0:T(8,128)(2,1)S(1)} %convolution_convert_fusion.1), channel_id=1, source_target_pairs={{8,0},{9,1},{10,2},{11,3},{12,4},{13,5},{14,6},{15,7},{0,8},{1,9},... | collective-permute-start | bytes 196616 | tf_op jit(solution)/shard_map/ppermute | solution.py:95
  77.4 1.4 %fusion.1.refs_0_ = bf16[64,512]{1,0:T(8,128)(2,1)S(1)} fusion(bf16[512,4096]{1,0:T(8,128)(2,1)S(1)} %pad_maximum_fusion, bf16[64,4096]{1,0:T(8,128)(2,1)S(1)} %copy-done.1), kind=kOutput, calls=%fused_computation.8 | convolution fusion | flops 268468224 | bytes 4784128 | tf_op jit(solution)/shard_map/dot_general | solution.py:163
  78.9 2.5 %collective-permute-done.10.refs_3_ = bf16[64,512]{1,0:T(8,128)(2,1)S(1)} collective-permute-done((bf16[64,512]{1,0:T(8,128)(2,1)S(1)}, bf16[64,512]{1,0:T(8,128)(2,1)S(1)}, u32[]{:S(2)}, u32[]{:S(2)}) %collective-permute-start.10) | collective-permute-done | bytes 65568 | tf_op jit(solution)/shard_map/ppermute | solution.py:95
  81.4 0.7 combine.2.refs_2_
  82.1 1.4 %convolution_convert_fusion = bf16[64,512]{1,0:T(8,128)(2,1)S(1)} fusion(bf16[64,4096]{1,0:T(8,128)(2,1)S(1)} %collective-permute-done.4, bf16[512,4096]{1,0:T(8,128)(2,1)S(1)} %pad_maximum_fusion), kind=kOutput, calls=%fused_computation.3 | convolution fusion | flops 268468224 | bytes 4784128 | tf_op jit(solution)/shard_map/dot_general | solution.py:163
  83.5 2.0 %collective-permute-start.11 = (bf16[64,512]{1,0:T(8,128)(2,1)S(1)}, bf16[64,512]{1,0:T(8,128)(2,1)S(1)}, u32[]{:S(2)}, u32[]{:S(2)}) collective-permute-start(bf16[64,512]{1,0:T(8,128)(2,1)S(1)} %convolution_convert_fusion), channel_id=1, source_target_pairs={{12,0},{13,1},{14,2},{15,3},{0,12},{1,13},{2,14},{3,15},{28,16},{2... | collective-permute-start | bytes 196616 | tf_op jit(solution)/shard_map/ppermute | solution.py:95
  85.5 5.9 %collective-permute-done.11.refs_0_ = bf16[64,512]{1,0:T(8,128)(2,1)S(1)} collective-permute-done((bf16[64,512]{1,0:T(8,128)(2,1)S(1)}, bf16[64,512]{1,0:T(8,128)(2,1)S(1)}, u32[]{:S(2)}, u32[]{:S(2)}) %collective-permute-start.11) | collective-permute-done | bytes 65568 | tf_op jit(solution)/shard_map/ppermute | solution.py:95
  91.5 0.4 combine.3
  91.9 0.1 reshape.145
  92.0 0.7 assemble.1
  92.7 1.2 %fusion.4 = f32[4,256]{1,0:T(4,128)} fusion(bf16[256,4096]{1,0:T(8,128)(2,1)S(1)} %assemble.1, f32[4,4096]{1,0:T(4,128)S(1)} %reshape.145), kind=kOutput, calls=%fused_computation.16 | convolution fusion | flops 8404992 | bytes 2166784 | tf_op jit(solution)/shard_map/dot_general | solution.py:172
  (44 shorter events, 0.5 us)
Async XLA Ops:
  0.6 13.7 %copy-start = (bf16[64,4096]{1,0:T(8,128)(2,1)S(1)}, bf16[64,4096]{1,0:T(8,128)(2,1)}, u32[]{:S(2)}) copy-start(bf16[64,4096]{1,0:T(8,128)(2,1)} %param.9) | copy-start | bytes 1572868
  0.6 48.0 %copy-start.7 = (f32[64,8]{0,1:T(8,128)S(1)}, f32[64,8]{0,1:T(8,128)}, u32[]{:S(2)}) copy-start(f32[64,8]{0,1:T(8,128)} %param.11) | copy-start | bytes 6148
  0.7 48.0 %copy-start.8 = (s32[64,8]{0,1:T(8,128)S(1)}, s32[64,8]{0,1:T(8,128)}, u32[]{:S(2)}) copy-start(s32[64,8]{0,1:T(8,128)} %param.10) | copy-start | bytes 6148
  0.7 27.2 %collective-permute-start = (bf16[64,4096]{1,0:T(8,128)(2,1)}, bf16[64,4096]{1,0:T(8,128)(2,1)S(1)}, u32[]{:S(2)}, u32[]{:S(2)}) collective-permute-start(bf16[64,4096]{1,0:T(8,128)(2,1)} %param.8), channel_id=1, source_target_pairs={{0,4},{1,5},{2,6},{3,7},{4,8},{5,9},{6,10},{7,11},{8,12},{9,13},{1... | collective-permute-start | bytes 1572872 | tf_op jit(solution)/shard_map/ppermute | solution.py:95
  5.8 24.5 %collective-permute-start.2 = (bf16[64,4096]{1,0:T(8,128)(2,1)}, bf16[64,4096]{1,0:T(8,128)(2,1)S(1)}, u32[]{:S(2)}, u32[]{:S(2)}) collective-permute-start(bf16[64,4096]{1,0:T(8,128)(2,1)} %param.8), channel_id=1, source_target_pairs={{4,0},{5,1},{6,2},{7,3},{8,4},{9,5},{10,6},{11,7},{12,8},{13,9},{1... | collective-permute-start | bytes 1572872 | tf_op jit(solution)/shard_map/ppermute | solution.py:95
  7.9 15.2 %collective-permute-start.14 = (bf16[16,2048]{1,0:T(8,128)(2,1)S(1)}, bf16[16,2048]{1,0:T(8,128)(2,1)S(1)}, u32[]{:S(2)}, u32[]{:S(2)}) collective-permute-start(bf16[16,2048]{1,0:T(8,128)(2,1)S(1)} %constant_dynamic-slice_fusion), channel_id=1, source_target_pairs={{0,12},{1,13},{2,14},{3,15},{4,0},{5,1},{6,2},{7,3},{8,4},{9,5},{1... | collective-permute-start | bytes 196616 | tf_op jit(solution)/shard_map/ppermute | solution.py:95
  12.6 15.3 %collective-permute-start.13 = (bf16[16,2048]{1,0:T(8,128)(2,1)S(1)}, bf16[16,2048]{1,0:T(8,128)(2,1)S(1)}, u32[]{:S(2)}, u32[]{:S(2)}) collective-permute-start(bf16[16,2048]{1,0:T(8,128)(2,1)S(1)} %constant_dynamic-slice_fusion), channel_id=1, source_target_pairs={{0,8},{1,9},{2,10},{3,11},{4,12},{5,13},{6,14},{7,15},{8,0},{9,1},... | collective-permute-start | bytes 196616 | tf_op jit(solution)/shard_map/ppermute | solution.py:95
  12.6 15.3 %collective-permute-start.12 = (bf16[16,2048]{1,0:T(8,128)(2,1)S(1)}, bf16[16,2048]{1,0:T(8,128)(2,1)S(1)}, u32[]{:S(2)}, u32[]{:S(2)}) collective-permute-start(bf16[16,2048]{1,0:T(8,128)(2,1)S(1)} %constant_dynamic-slice_fusion), channel_id=1, source_target_pairs={{0,4},{1,5},{2,6},{3,7},{4,8},{5,9},{6,10},{7,11},{8,12},{9,13},{1... | collective-permute-start | bytes 196616 | tf_op jit(solution)/shard_map/ppermute | solution.py:95
  14.3 35.0 %copy-start.9 = (s32[1,64]{1,0:T(1,128)S(1)}, s32[1,64]{1,0:T(1,128)}, u32[]{:S(2)}) copy-start(s32[1,64]{1,0:T(1,128)} %param.12) | copy-start | bytes 772
  23.1 23.5 %collective-permute-start.6 = (bf16[128,4096]{1,0:T(8,128)(2,1)}, bf16[128,4096]{1,0:T(8,128)(2,1)}, u32[]{:S(2)}, u32[]{:S(2)}) collective-permute-start(bf16[128,4096]{1,0:T(8,128)(2,1)} %bitcast.32), channel_id=1, source_target_pairs={{0,2},{1,3},{2,0},{3,1},{4,6},{5,7},{6,4},{7,5},{8,10},{9,11},{10,... | collective-permute-start | bytes 3145736 | tf_op jit(solution)/shard_map/ppermute | solution.py:98
  27.9 34.2 %collective-permute-start.5 = (bf16[128,4096]{1,0:T(8,128)(2,1)}, bf16[128,4096]{1,0:T(8,128)(2,1)}, u32[]{:S(2)}, u32[]{:S(2)}) collective-permute-start(bf16[128,4096]{1,0:T(8,128)(2,1)} %bitcast.33), channel_id=1, source_target_pairs={{0,1},{1,0},{2,3},{3,2},{4,5},{5,4},{6,7},{7,6},{8,9},{9,8},{10,11... | collective-permute-start | bytes 3145736 | tf_op jit(solution)/shard_map/ppermute | solution.py:98
  27.9 8.8 %copy-start.4 = (bf16[64,4096]{1,0:T(8,128)(2,1)}, bf16[64,4096]{1,0:T(8,128)(2,1)S(1)}, u32[]{:S(2)}) copy-start(bf16[64,4096]{1,0:T(8,128)(2,1)S(1)} %collective-permute-done) | copy-start | bytes 1572868
  27.9 8.8 %collective-permute-start.15 = (bf16[64,2048]{1,0:T(8,128)(2,1)S(1)}, bf16[64,2048]{1,0:T(8,128)(2,1)S(1)}, u32[]{:S(2)}, u32[]{:S(2)}) collective-permute-start(bf16[64,2048]{1,0:T(8,128)(2,1)S(1)} %pad_maximum_fusion.3), channel_id=1, source_target_pairs={{0,16},{16,0},{1,17},{17,1},{2,18},{18,2},{3,19},{19,3},{4,20},{20... | collective-permute-start | bytes 786440 | tf_op jit(solution)/shard_map/ppermute | solution.py:130
  29.6 7.2 %collective-permute-start.1 = (bf16[64,4096]{1,0:T(8,128)(2,1)S(1)}, bf16[64,4096]{1,0:T(8,128)(2,1)S(1)}, u32[]{:S(2)}, u32[]{:S(2)}) collective-permute-start(bf16[64,4096]{1,0:T(8,128)(2,1)S(1)} %collective-permute-done), channel_id=1, source_target_pairs={{4,8},{5,9},{6,10},{7,11},{8,12},{9,13},{10,14},{11,15},{20,24},{2... | collective-permute-start | bytes 1572872 | tf_op jit(solution)/shard_map/ppermute | solution.py:95
  30.3 6.5 %copy-start.2 = (bf16[64,4096]{1,0:T(8,128)(2,1)}, bf16[64,4096]{1,0:T(8,128)(2,1)S(1)}, u32[]{:S(2)}) copy-start(bf16[64,4096]{1,0:T(8,128)(2,1)S(1)} %collective-permute-done.2) | copy-start | bytes 1572868
  30.3 16.0 %collective-permute-start.3 = (bf16[64,4096]{1,0:T(8,128)(2,1)S(1)}, bf16[64,4096]{1,0:T(8,128)(2,1)S(1)}, u32[]{:S(2)}, u32[]{:S(2)}) collective-permute-start(bf16[64,4096]{1,0:T(8,128)(2,1)S(1)} %collective-permute-done.2), channel_id=1, source_target_pairs={{4,0},{5,1},{6,2},{7,3},{8,4},{9,5},{10,6},{11,7},{20,16},{21,17},... | collective-permute-start | bytes 1572872 | tf_op jit(solution)/shard_map/ppermute | solution.py:95
  46.7 15.4 %collective-permute-start.7 = (bf16[128,4096]{1,0:T(8,128)(2,1)}, bf16[128,4096]{1,0:T(8,128)(2,1)}, u32[]{:S(2)}, u32[]{:S(2)}) collective-permute-start(bf16[128,4096]{1,0:T(8,128)(2,1)} %collective-permute-done.6), channel_id=1, source_target_pairs={{0,1},{1,0},{2,3},{3,2},{4,5},{5,4},{6,7},{7,6},{8,9},{9,8},{10,11... | collective-permute-start | bytes 3145736 | tf_op jit(solution)/shard_map/ppermute | solution.py:98
  46.7 14.3 %collective-permute-start.16 = (bf16[64,4096]{1,0:T(8,128)(2,1)S(1)}, bf16[64,4096]{1,0:T(8,128)(2,1)S(1)}, u32[]{:S(2)}, u32[]{:S(2)}) collective-permute-start(bf16[64,4096]{1,0:T(8,128)(2,1)S(1)} %pad_maximum_fusion.2.mine_ref), channel_id=1, source_target_pairs={{0,2},{1,3},{2,0},{3,1},{4,6},{5,7},{6,4},{7,5},{8,10},{9,11},{10,... | collective-permute-start | bytes 1572872 | tf_op jit(solution)/shard_map/ppermute | solution.py:98
  49.5 32.6 %collective-permute-start.4 = (bf16[64,4096]{1,0:T(8,128)(2,1)S(1)}, bf16[64,4096]{1,0:T(8,128)(2,1)S(1)}, u32[]{:S(2)}, u32[]{:S(2)}) collective-permute-start(bf16[64,4096]{1,0:T(8,128)(2,1)S(1)} %add.49), channel_id=1, source_target_pairs={{8,12},{9,13},{10,14},{11,15},{4,0},{5,1},{6,2},{7,3},{24,28},{25,... | collective-permute-start | bytes 1572872 | tf_op jit(solution)/shard_map/ppermute | solution.py:95
  62.1 2.5 %copy-start.5 = (bf16[64,4096]{1,0:T(8,128)(2,1)S(1)}, bf16[64,4096]{1,0:T(8,128)(2,1)}, u32[]{:S(2)}) copy-start(bf16[64,4096]{1,0:T(8,128)(2,1)} %copy-done.4) | copy-start | bytes 1572868
  62.1 29.9 %collective-permute-start.17 = (bf16[128,4096]{1,0:T(8,128)(2,1)}, bf16[128,4096]{1,0:T(8,128)(2,1)S(1)}, u32[]{:S(2)}, u32[]{:S(2)}) collective-permute-start(bf16[128,4096]{1,0:T(8,128)(2,1)} %pad_maximum_fusion.1), channel_id=1, source_target_pairs={{0,1},{1,0},{2,3},{3,2},{4,5},{5,4},{6,7},{7,6},{8,9},{9,8},{10,11... | collective-permute-start | bytes 3145736 | tf_op jit(solution)/shard_map/ppermute | solution.py:98
  64.6 2.8 %copy-start.3 = (bf16[64,4096]{1,0:T(8,128)(2,1)S(1)}, bf16[64,4096]{1,0:T(8,128)(2,1)}, u32[]{:S(2)}) copy-start(bf16[64,4096]{1,0:T(8,128)(2,1)} %copy-done.2) | copy-start | bytes 1572868
  66.0 11.4 %copy-start.1 = (bf16[64,4096]{1,0:T(8,128)(2,1)S(1)}, bf16[64,4096]{1,0:T(8,128)(2,1)}, u32[]{:S(2)}) copy-start(bf16[64,4096]{1,0:T(8,128)(2,1)} %param.8) | copy-start | bytes 1572868
  66.0 12.8 %collective-permute-start.8 = (bf16[64,512]{1,0:T(8,128)(2,1)S(1)}, bf16[64,512]{1,0:T(8,128)(2,1)S(1)}, u32[]{:S(2)}, u32[]{:S(2)}) collective-permute-start(bf16[64,512]{1,0:T(8,128)(2,1)S(1)} %fusion.2), channel_id=1, source_target_pairs={{4,0},{5,1},{6,2},{7,3},{8,4},{9,5},{10,6},{11,7},{12,8},{13,9},{1... | collective-permute-start | bytes 196616 | tf_op jit(solution)/shard_map/ppermute | solution.py:95
  68.9 10.0 %collective-permute-start.9 = (bf16[64,512]{1,0:T(8,128)(2,1)S(1)}, bf16[64,512]{1,0:T(8,128)(2,1)S(1)}, u32[]{:S(2)}, u32[]{:S(2)}) collective-permute-start(bf16[64,512]{1,0:T(8,128)(2,1)S(1)} %fusion.3), channel_id=1, source_target_pairs={{0,4},{1,5},{2,6},{3,7},{4,8},{5,9},{6,10},{7,11},{8,12},{9,13},{1... | collective-permute-start | bytes 196616 | tf_op jit(solution)/shard_map/ppermute | solution.py:95
  74.8 6.5 %collective-permute-start.10 = (bf16[64,512]{1,0:T(8,128)(2,1)S(1)}, bf16[64,512]{1,0:T(8,128)(2,1)S(1)}, u32[]{:S(2)}, u32[]{:S(2)}) collective-permute-start(bf16[64,512]{1,0:T(8,128)(2,1)S(1)} %convolution_convert_fusion.1), channel_id=1, source_target_pairs={{8,0},{9,1},{10,2},{11,3},{12,4},{13,5},{14,6},{15,7},{0,8},{1,9},... | collective-permute-start | bytes 196616 | tf_op jit(solution)/shard_map/ppermute | solution.py:95
  83.5 8.0 %collective-permute-start.11 = (bf16[64,512]{1,0:T(8,128)(2,1)S(1)}, bf16[64,512]{1,0:T(8,128)(2,1)S(1)}, u32[]{:S(2)}, u32[]{:S(2)}) collective-permute-start(bf16[64,512]{1,0:T(8,128)(2,1)S(1)} %convolution_convert_fusion), channel_id=1, source_target_pairs={{12,0},{13,1},{14,2},{15,3},{0,12},{1,13},{2,14},{3,15},{28,16},{2... | collective-permute-start | bytes 196616 | tf_op jit(solution)/shard_map/ppermute | solution.py:95
  92.0 2.0 %copy-start.6 = (f32[4,4096]{1,0:T(4,128)}, f32[4,4096]{1,0:T(4,128)S(1)}, u32[]{:S(2)}) copy-start(f32[4,4096]{1,0:T(4,128)S(1)} %reshape.145) | copy-start | bytes 196612

commit v4 on v3

--- a/solution.py
+++ b/solution.py
@@ -10,6 +10,8 @@
 RANK = 64
 EX_DEV = 4
 QUAD = 4
+
+SMALL = pl.CostEstimate(flops=1024, bytes_accessed=1024, transcendentals=0)
 
 NT = (((1,), (1,)), ((), ()))
 TN = (((0,), (0,)), ((), ()))
@@ -44,9 +46,43 @@
         out_shape=jax.ShapeDtypeStruct(shape, jnp.float32),
         in_specs=[pl.BlockSpec(memory_space=pltpu.VMEM)] * (len(sides) + 1 + len(extra)),
         out_specs=pl.BlockSpec(memory_space=pltpu.VMEM),
+        cost_estimate=SMALL,
         compiler_params=pltpu.CompilerParams(vmem_limit_bytes=32 << 20),
         name="combine",
     )(*sides, wide, *extra)
+
+
+def project_kernel(blocks, *refs):
+    parts, weights = refs[:blocks], refs[blocks : blocks + QUAD]
+    outs, total = refs[blocks + QUAD : -1], refs[-1]
+    rows = parts[0].shape[0]
+    depth = 1024
+    total[...] = jnp.zeros_like(total)
+
+    @pl.loop(0, parts[0].shape[1] // depth)
+    def _(i):
+        span = pl.ds(pl.multiple_of(i * depth, depth), depth)
+        left = jnp.concatenate([p[:, span] for p in parts], axis=0)
+        right = jnp.concatenate([w[:, span] for w in weights], axis=0)
+        total[...] += lax.dot_general(left, right, NT, preferred_element_type=jnp.float32)
+
+    for b in range(blocks):
+        outs[b][...] = total[b * rows : (b + 1) * rows].astype(jnp.bfloat16)
+
+
+def project(parts, weights):
+    rows, width = parts[0].shape[0], QUAD * weights[0].shape[0]
+    vmem = pl.BlockSpec(memory_space=pltpu.VMEM)
+    return pl.pallas_call(
+        functools.partial(project_kernel, len(parts)),
+        out_shape=[jax.ShapeDtypeStruct((rows, width), jnp.bfloat16)] * len(parts),
+        in_specs=[vmem] * (len(parts) + QUAD),
+        out_specs=[vmem] * len(parts),
+        scratch_shapes=[pltpu.VMEM((rows * len(parts), width), jnp.float32)],
+        cost_estimate=SMALL,
+        compiler_params=pltpu.CompilerParams(vmem_limit_bytes=40 << 20),
+        name="project",
+    )(*parts, *weights)
 
 
 def assemble_kernel(planes, groups, here_ref, mine_ref, over_y_ref, rest_ref, out_ref):
@@ -56,7 +92,7 @@
     for rel in range(QUAD):
         base = span if rel == 3 else 0
         for d in range(planes):
-            home = lax.rem(here_ref[0] + (planes - d), planes) * QUAD + (here_ref[1] ^ rel)
+            home = (here_ref[0] ^ d) * QUAD + (here_ref[1] ^ rel)
             row = pl.multiple_of(home * rows, rows)
             for k in range(groups):
                 column = pl.multiple_of(lax.rem(here_ref[2] + (groups - k), groups) * columns, columns)
@@ -73,6 +109,7 @@
         out_shape=jax.ShapeDtypeStruct((span * QUAD, width), mine.dtype),
         in_specs=[pl.BlockSpec(memory_space=pltpu.SMEM), vmem, vmem, vmem],
         out_specs=vmem,
+        cost_estimate=SMALL,
         compiler_params=pltpu.CompilerParams(vmem_limit_bytes=32 << 20),
         name="assemble",
     )(here, mine, over_y, rest)
@@ -97,46 +134,27 @@
     def swap(array, bit):
         return lax.ppermute(array, "expert", [(i, i ^ bit) for i in range(n)])
 
-    up, down = tokens, tokens
-    arrived, steps = [], []
+    weights = jnp.swapaxes(in_proj, 1, 2).reshape(owned * RANK, model_width)
+    half = weights.shape[0] // 2
+
+    width = queries.shape[1] // groups
+    lined = lax.dynamic_slice_in_dim(queries, group * width, width, axis=1)
+    lined = jnp.concatenate([lined, swap(lined, QUAD)], axis=0)
+    first = after(tokens, lined)
+    over_core = swap(weights, 1)
+    bit = 2 * QUAD
+    while bit < n:
+        lined = jnp.concatenate([lined, swap(lined, bit)], axis=0)
+        bit *= 2
+
+    ways_home = []
     for s in range(1, planes):
-        up_hops = [(p, p + 1) for p in range(s - 1, planes - 1)]
-        down_hops = [(p, p - 1) for p in range(1, planes - s + 1)]
         up_home = [(p, p - s) for p in range(s, planes)]
         down_home = [(p, p + s) for p in range(planes - s)]
-        if 2 * s > planes + 1:
-            up = down = move(up, up_hops + down_hops)
-        else:
-            up, down = move(up, up_hops), move(down, down_hops)
-            if 2 * s >= planes:
-                up = down = up + down
-        steps.append(up)
-        if 2 * s >= planes:
-            arrived.append((up, up_home + down_home))
-        else:
-            arrived.extend([(up, up_home), (down, down_home)])
-
-    weights = jnp.swapaxes(in_proj, 1, 2).reshape(owned * RANK, model_width)
-    over_y = swap(weights, 2)
-    over_core = swap(weights, 1)
-    across = swap(after(over_y, steps[1]), 1)
-    quad_weights = jnp.concatenate([weights, over_core, over_y, across], axis=0)
-
-    width = queries.shape[1] // groups
-    part = lax.dynamic_slice_in_dim(queries, group * width, width, axis=1)
-    lined = [part] + [move(part, [(p, (p + d) % planes) for p in range(planes)]) for d in range(1, planes)]
-    lined = after(jnp.concatenate(lined, axis=0), steps[0])
-    ranged = [lined] + [
-        lax.ppermute(lined, "groups", [(g, (g + k) % groups) for g in range(groups)]) for k in range(1, groups)
-    ]
-    mine = after(jnp.concatenate(ranged, axis=1), steps[1])
-    mine_over_y = swap(mine, 2)
-    rest = swap(jnp.concatenate([mine, mine_over_y], axis=0), 1)
-    here = jnp.stack([plane, spot, group]).astype(jnp.int32)
-    all_queries = assemble(here, mine, mine_over_y, rest, planes, groups)
+        ways_home.extend([up_home + down_home] if 2 * s >= planes else [up_home, down_home])
 
     homes = []
-    for _, home in arrived:
+    for home in ways_home:
         back = -jnp.ones((), jnp.int32)
         for a, b in home:
             back = jnp.where(plane == b, a, back)
@@ -159,14 +177,45 @@
         widely[None], (gate[:, :, None] * repeated[None]).astype(jnp.bfloat16), jnp.zeros((), jnp.bfloat16)
     )
 
-    def project(block):
-        return lax.dot_general(block, quad_weights, NT, preferred_element_type=jnp.float32).astype(jnp.bfloat16)
+    over_y = swap(weights[:half], 2)
+    up, down = first, first
+    arrived, steps = [], []
+    for s in range(1, planes):
+        up_hops = [(p, p + 1) for p in range(s - 1, planes - 1)]
+        down_hops = [(p, p - 1) for p in range(1, planes - s + 1)]
+        if s == 2:
+            up, down = after(up, lined, wide), after(down, lined, wide)
+            ranged = [lined] + [
+                lax.ppermute(after(lined, over_y, up, down), "groups", [(g, (g + k) % groups) for g in range(groups)])
+                for k in range(1, groups)
+            ]
+        elif s == 3:
+            up, down = after(up, *ranged), after(down, *ranged)
+        if 2 * s > planes + 1:
+            up = down = move(up, up_hops + down_hops)
+        else:
+            up, down = move(up, up_hops), move(down, down_hops)
+            if 2 * s >= planes:
+                up = down = up + down
+        steps.append(up)
+        arrived.extend([up] if 2 * s >= planes else [up, down])
+
+    over_y_late = swap(after(weights[half:], arrived[0]), 2)
+    over_y_all = jnp.concatenate([over_y, over_y_late], axis=0)
+    across = swap(after(over_y_all, steps[1]), 1)
+    quad_weights = [weights, over_core, over_y_all, across]
 
     experts = QUAD * owned
-    returned = [move(project(block), home) for block, home in arrived[:-1]]
-    early = combine([project(tokens)] + returned, wide[:-experts])
-    block, home = arrived[-1]
-    late = move(project(after(block, early)), home)
+    own, *sides = project([tokens] + arrived[:-1], quad_weights)
+    returned = [move(side, home) for side, home in zip(sides, ways_home[:-1])]
+    mine = after(jnp.concatenate(ranged, axis=1), over_y_all, steps[1])
+    mine_over_y = swap(mine, 2)
+    side = project([after(arrived[-1], *returned)], quad_weights)[0]
+    late = move(side, ways_home[-1])
+    early = combine([own] + returned, wide[:-experts])
+    rest = swap(after(jnp.concatenate([mine, mine_over_y], axis=0), side), 1)
+    here = jnp.stack([plane, spot, group]).astype(jnp.int32)
+    all_queries = assemble(here, mine, mine_over_y, rest, planes, groups)
     sketches = combine([late], wide[-experts:], early, counts)
     sketches = sketches.reshape(EX_DEV, RANK * RANK)
     scores = lax.dot_general(sketches.astype(jnp.bfloat16), all_queries, NT, preferred_element_type=jnp.float32)

time: 94.3 us -> 85.5 us (0.907)
  matrix products: 9.55 us -> 2.58 us
  waiting for transfers between devices: 44.1 us -> 38.3 us
  Pallas kernels: 1.75 us -> 6.67 us
  local copies, waits for them, and re-layouts: 1.69 us -> 5.23 us
  other arithmetic: 5.41 us -> 2.38 us
  starting transfers between devices: 30.5 us -> 28.9 us
    ppermute x12 -> x9, starting transfers between devices: 25.9 us -> 18 us  [move(): return lax.ppermute(array, 'expert', pairs)]
    dot_general x5 -> x0, matrix products: 6.97 us -> none  [project(): lax.dot_general(block, quad_weights, NT, preferred_element_type=jnp.float32)]
    ppermute x5 -> x8, starting transfers between devices: 3.05 us -> 9.38 us  [swap(): return lax.ppermute(array, 'expert', [(i, i ^ bit) for i in range(n)])]
    ppermute x1, waiting for transfers between devices: 5.05 us -> 0.01 us  [shards(): lax.ppermute(after(lined, over_y, up, down), 'groups', [(g, (g + k) % gro...]
    pallas_call x0 -> x2, Pallas kernels: none -> 4.92 us  [project(): pl.pallas_call(functools.partial(project_kernel, len(parts)), out_shape=[...]
    ppermute x12 -> x9, waiting for transfers between devices: 28.5 us -> 24.6 us  [move(): return lax.ppermute(array, 'expert', pairs)]
    ppermute x5 -> x8, waiting for transfers between devices: 10.5 us -> 13.8 us  [swap(): return lax.ppermute(array, 'expert', [(i, i ^ bit) for i in range(n)])]
    concatenate x4, other arithmetic: 3.6 us -> 1.23 us  [the longest x1 1.16 us: shards(): rest = swap(after(jnp.concatenate([mine, mine_over_y], axis=0), side), 1)]
  transfers between devices with their start and end apart: 18 -> 18, of which waited for: 8 -> 8; matrix products, arithmetic and copies ran while one was open for 16% -> 9% of each run, Pallas kernels for 1% -> 5%
where the time goes in v4:
time: 85.5 us; the launch traced here: 85.1 us
  waiting for transfers between devices  38.3 us (45%)
  starting transfers between devices  28.9 us (34%)
  Pallas kernels  6.67 us (8%)
  local copies, waits for them, and re-layouts  5.23 us (6%)
  matrix products  2.58 us (3%)
  other arithmetic  2.38 us (3%)
  between operations  1.01 us (1%)
    ppermute x9, waiting for transfers between devices, move(): return lax.ppermute(array, 'expert', pairs)  24.6 us
    ppermute x9, starting transfers between devices, move(): return lax.ppermute(array, 'expert', pairs)  18 us
    ppermute x8, waiting for transfers between devices, swap(): return lax.ppermute(array, 'expert', [(i, i ^ bit) for i in range(n)])  13.8 us
    ppermute x8, starting transfers between devices, swap(): return lax.ppermute(array, 'expert', [(i, i ^ bit) for i in range(n)])  9.38 us
    pallas_call x2, Pallas kernels, project(): pl.pallas_call(functools.partial(project_kernel, len(parts)), out_shape=[...  4.92 us
    slice x1, local copies, waits for them, and re-layouts, shards(): over_y_late = swap(after(weights[half:], arrived[0]), 2)  2.28 us
  transfers between devices with their start and end apart: 18, of which 8 were waited for; matrix products, arithmetic and copies ran while one was open for 9% of the time, Pallas kernels for 5%

profile of v4, /device:TPU:0, one launch (start us, length us, event | category | flops | bytes accessed | tf_op | source)
XLA Modules:
  0.0 85.1 jit_solution(15312135414623062355)
XLA Ops:
  0.7 1.0 %constant_dynamic-slice_fusion = bf16[16,2048]{1,0:T(8,128)(2,1)S(1)} fusion(bf16[16,4096]{1,0:T(8,128)(2,1)} %param.15, s32[]{:T(128)S(6)} %select_n.70), kind=kLoop, calls=%fused_computation.22 | loop fusion | bytes 131076 | tf_op jit(solution)/shard_map/dynamic_slice | solution.py:141
  1.7 3.0 %collective-permute-start = (bf16[16,2048]{1,0:T(8,128)(2,1)S(1)}, bf16[16,2048]{1,0:T(8,128)(2,1)S(1)}, u32[]{:S(2)}, u32[]{:S(2)}) collective-permute-start(bf16[16,2048]{1,0:T(8,128)(2,1)S(1)} %constant_dynamic-slice_fusion), channel_id=1, source_target_pairs={{0,4},{1,5},{2,6},{3,7},{4,0},{5,1},{6,2},{7,3},{8,12},{9,13},{10,... | collective-permute-start | bytes 196616 | tf_op jit(solution)/shard_map/ppermute | solution.py:135
  4.7 2.3 %slice_bitcast_fusion = (bf16[64,4096]{1,0:T(8,128)(2,1)}, bf16[64,4096]{1,0:T(8,128)(2,1)}) fusion(bf16[2,64,4096]{2,1,0:T(8,128)(2,1)} %bitcast.20), kind=kLoop, calls=%fused_computation.3 | loop fusion | bytes 2097152 | tf_op jit(solution)/shard_map/slice | solution.py:203
  7.0 1.5 %collective-permute-start.6 = (bf16[64,4096]{1,0:T(8,128)(2,1)}, bf16[64,4096]{1,0:T(8,128)(2,1)}, u32[]{:S(2)}, u32[]{:S(2)}) collective-permute-start(bf16[64,4096]{1,0:T(8,128)(2,1)} %get-tuple-element.31), channel_id=1, source_target_pairs={{0,2},{1,3},{2,0},{3,1},{4,6},{5,7},{6,4},{7,5},{8,10},{9,11},{10,... | collective-permute-start | bytes 1572872 | tf_op jit(solution)/shard_map/ppermute | solution.py:135
  8.5 0.1 iota_add_fusion
  8.6 0.1 stack.33
  8.7 0.1 iota_compare_fusion
  8.8 1.3 %fusion.3 = f32[64,64]{1,0:T(8,128)S(1)} fusion(bf16[64,4096]{1,0:T(8,128)(2,1)S(1)} %copy-done, bf16[4096,64]{0,1:T(8,128)(2,1)} %param.14), kind=kOutput, calls=%fused_computation.23 | convolution fusion | flops 33554432 | bytes 1064960 | tf_op jit(solution)/shard_map/dot_general | solution.py:162
  10.1 0.1 add.55
  10.2 3.2 %collective-permute-start.1 = (bf16[64,4096]{1,0:T(8,128)(2,1)S(1)}, bf16[64,4096]{1,0:T(8,128)(2,1)}, u32[]{:S(2)}, u32[]{:S(2)}) collective-permute-start(bf16[64,4096]{1,0:T(8,128)(2,1)S(1)} %copy-done.4), channel_id=1, source_target_pairs={{0,4},{1,5},{2,6},{3,7},{4,8},{5,9},{6,10},{7,11},{8,12},{9,13},{1... | collective-permute-start | bytes 1572872 | tf_op jit(solution)/shard_map/ppermute | solution.py:132
  13.5 0.1 select_n.86
  13.6 0.1 select_reduce_fusion
  13.7 1.3 %collective-permute-start.4 = (bf16[64,4096]{1,0:T(8,128)(2,1)S(1)}, bf16[64,4096]{1,0:T(8,128)(2,1)}, u32[]{:S(2)}, u32[]{:S(2)}) collective-permute-start(bf16[64,4096]{1,0:T(8,128)(2,1)S(1)} %copy-done.4), channel_id=1, source_target_pairs={{4,0},{5,1},{6,2},{7,3},{8,4},{9,5},{10,6},{11,7},{12,8},{13,9},{1... | collective-permute-start | bytes 1572872 | tf_op jit(solution)/shard_map/ppermute | solution.py:132
  15.0 0.1 pad_maximum_fusion.4
  15.1 0.1 broadcast_in_dim.56
  15.2 0.1 broadcast_in_dim.57
  15.4 4.0 %collective-permute-start.2 = (bf16[32,2048]{1,0:T(8,128)(2,1)S(1)}, bf16[32,2048]{1,0:T(8,128)(2,1)S(1)}, u32[]{:S(2)}, u32[]{:S(2)}) collective-permute-start(bf16[32,2048]{1,0:T(8,128)(2,1)S(1)} %pad_maximum_fusion.3), channel_id=1, source_target_pairs={{0,8},{1,9},{2,10},{3,11},{4,12},{5,13},{6,14},{7,15},{8,0},{9,1},... | collective-permute-start | bytes 393224 | tf_op jit(solution)/shard_map/ppermute | solution.py:135
  19.4 0.4 fusion
  19.8 5.0 %collective-permute-done.1.refs_1_ = bf16[64,4096]{1,0:T(8,128)(2,1)} collective-permute-done((bf16[64,4096]{1,0:T(8,128)(2,1)S(1)}, bf16[64,4096]{1,0:T(8,128)(2,1)}, u32[]{:S(2)}, u32[]{:S(2)}) %collective-permute-start.1) | collective-permute-done | bytes 524320 | tf_op jit(solution)/shard_map/ppermute | solution.py:132
  24.9 11.7 %collective-permute-done.2 = bf16[32,2048]{1,0:T(8,128)(2,1)S(1)} collective-permute-done((bf16[32,2048]{1,0:T(8,128)(2,1)S(1)}, bf16[32,2048]{1,0:T(8,128)(2,1)S(1)}, u32[]{:S(2)}, u32[]{:S(2)}) %collective-permute-start.2) | collective-permute-done | bytes 131104 | tf_op jit(solution)/shard_map/ppermute | solution.py:135
  36.6 0.7 collective-permute-start.3
  37.3 1.3 %collective-permute-start.5 = (bf16[64,4096]{1,0:T(8,128)(2,1)}, bf16[64,4096]{1,0:T(8,128)(2,1)S(1)}, u32[]{:S(2)}, u32[]{:S(2)}) collective-permute-start(bf16[64,4096]{1,0:T(8,128)(2,1)} %collective-permute-done.4.refs_2_), channel_id=1, source_target_pairs={{4,0},{5,1},{6,2},{7,3},{8,4},{9,5},{10,6},{11,7},{20,16},{21,17},... | collective-permute-start | bytes 1572872 | tf_op jit(solution)/shard_map/ppermute | solution.py:132
  38.7 1.1 %constant_dynamic-update-slice_fusion.1 = bf16[128,4096]{1,0:T(8,128)(2,1)S(1)} fusion(bf16[64,4096]{1,0:T(8,128)(2,1)} %collective-permute-done.6), kind=kLoop, calls=%fused_computation.15 | loop fusion | bytes 1048576
  39.7 1.6 %collective-permute-start.7 = (bf16[64,2048]{1,0:T(8,128)(2,1)S(1)}, bf16[64,2048]{1,0:T(8,128)(2,1)S(1)}, u32[]{:S(2)}, u32[]{:S(2)}) collective-permute-start(bf16[64,2048]{1,0:T(8,128)(2,1)S(1)} %pad_maximum_fusion.2), channel_id=1, source_target_pairs={{0,16},{16,0},{1,17},{17,1},{2,18},{18,2},{3,19},{19,3},{4,20},{20... | collective-permute-start | bytes 786440 | tf_op jit(solution)/shard_map/ppermute | solution.py:189
  41.4 11.3 %collective-permute-done.5 = bf16[64,4096]{1,0:T(8,128)(2,1)S(1)} collective-permute-done((bf16[64,4096]{1,0:T(8,128)(2,1)}, bf16[64,4096]{1,0:T(8,128)(2,1)S(1)}, u32[]{:S(2)}, u32[]{:S(2)}) %collective-permute-start.5) | collective-permute-done | bytes 524320 | tf_op jit(solution)/shard_map/ppermute | solution.py:132
  52.7 0.1 add.58.refs_3_
  52.9 0.6 collective-permute-start.16
  53.5 1.3 %collective-permute-start.8 = (bf16[64,4096]{1,0:T(8,128)(2,1)S(1)}, bf16[64,4096]{1,0:T(8,128)(2,1)S(1)}, u32[]{:S(2)}, u32[]{:S(2)}) collective-permute-start(bf16[64,4096]{1,0:T(8,128)(2,1)S(1)} %add.58.refs_3_), channel_id=1, source_target_pairs={{8,12},{9,13},{10,14},{11,15},{4,0},{5,1},{6,2},{7,3},{24,28},{25,... | collective-permute-start | bytes 1572872 | tf_op jit(solution)/shard_map/ppermute | solution.py:132
  54.8 0.7 collective-permute-done.11.refs_7_.refs_4_
  55.5 3.1 %project.2 = (bf16[64,512]{1,0:T(8,128)(2,1)S(1)}, bf16[64,512]{1,0:T(8,128)(2,1)S(1)}, bf16[64,512]{1,0:T(8,128)(2,1)S(1)}, bf16[64,512]{1,0:T(8,128)(2,1)S(1)}) custom-call(bf16[64,4096]{1,0:T(8,128)(2,1)S(1)} %copy-done.5, bf16[64,4096]{1,0:T(8,128)(2,1)} %collective-permute-done.1.refs_1_, bf16[64,4096]{1,0:T(8,128)(2,1)} %collective-permute-done.4.refs_2_, ...), custom_call_target="tpu_custom_call" | custom-call | flops 1024 | bytes 1024 | tf_op jit(solution)/shard_map/project/pallas_call | solution.py:76
  58.7 1.3 %collective-permute-start.12 = (bf16[64,512]{1,0:T(8,128)(2,1)S(1)}, bf16[64,512]{1,0:T(8,128)(2,1)S(1)}, u32[]{:S(2)}, u32[]{:S(2)}) collective-permute-start(bf16[64,512]{1,0:T(8,128)(2,1)S(1)} %get-tuple-element.23), channel_id=1, source_target_pairs={{4,0},{5,1},{6,2},{7,3},{8,4},{9,5},{10,6},{11,7},{12,8},{13,9},{1... | collective-permute-start | bytes 196616 | tf_op jit(solution)/shard_map/ppermute | solution.py:132
  60.0 4.5 %collective-permute-start.13 = (bf16[64,512]{1,0:T(8,128)(2,1)S(1)}, bf16[64,512]{1,0:T(8,128)(2,1)S(1)}, u32[]{:S(2)}, u32[]{:S(2)}) collective-permute-start(bf16[64,512]{1,0:T(8,128)(2,1)S(1)} %get-tuple-element.24), channel_id=1, source_target_pairs={{0,4},{1,5},{2,6},{3,7},{4,8},{5,9},{6,10},{7,11},{8,12},{9,13},{1... | collective-permute-start | bytes 196616 | tf_op jit(solution)/shard_map/ppermute | solution.py:132
  64.5 1.5 %collective-permute-start.14 = (bf16[64,512]{1,0:T(8,128)(2,1)S(1)}, bf16[64,512]{1,0:T(8,128)(2,1)S(1)}, u32[]{:S(2)}, u32[]{:S(2)}) collective-permute-start(bf16[64,512]{1,0:T(8,128)(2,1)S(1)} %get-tuple-element.25), channel_id=1, source_target_pairs={{8,0},{9,1},{10,2},{11,3},{12,4},{13,5},{14,6},{15,7},{0,8},{1,9},... | collective-permute-start | bytes 196616 | tf_op jit(solution)/shard_map/ppermute | solution.py:132
  66.0 1.3 %collective-permute-done.16.over_y_ref = bf16[64,4096]{1,0:T(8,128)(2,1)S(1)} collective-permute-done((bf16[64,4096]{1,0:T(8,128)(2,1)S(1)}, bf16[64,4096]{1,0:T(8,128)(2,1)S(1)}, u32[]{:S(2)}, u32[]{:S(2)}) %collective-permute-start.16) | collective-permute-done | bytes 524320 | tf_op jit(solution)/shard_map/ppermute | solution.py:135
  67.3 1.2 %pad_maximum_fusion = bf16[128,4096]{1,0:T(8,128)(2,1)} fusion(bf16[64,4096]{1,0:T(8,128)(2,1)S(1)} %collective-permute-done.16.over_y_ref, bf16[64,4096]{1,0:T(8,128)(2,1)S(1)} %pad_maximum_fusion.1.mine_ref), kind=kLoop, calls=%fused_computation.2 | loop fusion | flops 2097152 | bytes 2097152 | tf_op jit(solution)/shard_map/concatenate | solution.py:216
  68.5 3.0 %collective-permute-done.8.refs_0_ = bf16[64,4096]{1,0:T(8,128)(2,1)S(1)} collective-permute-done((bf16[64,4096]{1,0:T(8,128)(2,1)S(1)}, bf16[64,4096]{1,0:T(8,128)(2,1)S(1)}, u32[]{:S(2)}, u32[]{:S(2)}) %collective-permute-start.8) | collective-permute-done | bytes 524320 | tf_op jit(solution)/shard_map/ppermute | solution.py:132
  71.5 0.7 collective-permute-done.12.refs_1_
  72.2 1.8 %project.3 = bf16[64,512]{1,0:T(8,128)(2,1)S(1)} custom-call(bf16[64,4096]{1,0:T(8,128)(2,1)S(1)} %collective-permute-done.8.refs_0_, bf16[128,4096]{1,0:T(8,128)(2,1)S(1)} %bitcast.23, bf16[128,4096]{1,0:T(8,128)(2,1)S(1)} %collective-permute-done.9.refs_5_.refs_2_, bf16[128,4096]{1,0:T(8,128)(2,1)S(1)} %constant_dynamic-update-slice_fusion.refs_6_.refs_3_, ...), custom_call_target="tpu_custom_call" | custom-call | flops 1024 | bytes 1024 | tf_op jit(solution)/shard_map/project/pallas_call | solution.py:76
  74.2 0.1 slice.27.refs_4_
  74.3 0.1 convert_reduce_fusion
  74.4 2.9 %collective-permute-start.15 = (bf16[64,512]{1,0:T(8,128)(2,1)S(1)}, bf16[64,512]{1,0:T(8,128)(2,1)S(1)}, u32[]{:S(2)}, u32[]{:S(2)}) collective-permute-start(bf16[64,512]{1,0:T(8,128)(2,1)S(1)} %project.3), channel_id=1, source_target_pairs={{12,0},{13,1},{14,2},{15,3},{0,12},{1,13},{2,14},{3,15},{28,16},{2... | collective-permute-start | bytes 196616 | tf_op jit(solution)/shard_map/ppermute | solution.py:132
  77.3 0.1 pad_add_fusion.here_ref
  77.4 0.7 combine.2.refs_2_
  78.1 4.5 %collective-permute-done.15.refs_0_ = bf16[64,512]{1,0:T(8,128)(2,1)S(1)} collective-permute-done((bf16[64,512]{1,0:T(8,128)(2,1)S(1)}, bf16[64,512]{1,0:T(8,128)(2,1)S(1)}, u32[]{:S(2)}, u32[]{:S(2)}) %collective-permute-start.15) | collective-permute-done | bytes 65568 | tf_op jit(solution)/shard_map/ppermute | solution.py:132
  82.6 0.4 combine.3
  83.0 0.1 reshape.147
  83.1 0.7 assemble.1
  83.8 1.3 %fusion.1 = f32[4,256]{1,0:T(4,128)} fusion(bf16[256,4096]{1,0:T(8,128)(2,1)S(1)} %assemble.1, f32[4,4096]{1,0:T(4,128)S(1)} %reshape.147), kind=kOutput, calls=%fused_computation.10 | convolution fusion | flops 8404992 | bytes 2166784 | tf_op jit(solution)/shard_map/dot_general | solution.py:221
  (44 shorter events, 0.6 us)
Async XLA Ops:
  0.6 8.1 %copy-start = (bf16[64,4096]{1,0:T(8,128)(2,1)S(1)}, bf16[64,4096]{1,0:T(8,128)(2,1)}, u32[]{:S(2)}) copy-start(bf16[64,4096]{1,0:T(8,128)(2,1)} %param.9) | copy-start | bytes 1572868
  0.6 7.9 %copy-start.1 = (bf16[2,4096,64]{1,2,0:T(8,128)(2,1)S(1)}, bf16[2,4096,64]{1,2,0:T(8,128)(2,1)}, u32[]{:S(2)}) copy-start(bf16[2,4096,64]{1,2,0:T(8,128)(2,1)} %param.13) | copy-start | bytes 3145732
  0.7 8.0 %copy-start.9 = (s32[1,64]{1,0:T(1,128)S(1)}, s32[1,64]{1,0:T(1,128)}, u32[]{:S(2)}) copy-start(s32[1,64]{1,0:T(1,128)} %param.12) | copy-start | bytes 772
  0.7 9.6 %copy-start.4 = (bf16[64,4096]{1,0:T(8,128)(2,1)S(1)}, bf16[64,4096]{1,0:T(8,128)(2,1)}, u32[]{:S(2)}) copy-start(bf16[64,4096]{1,0:T(8,128)(2,1)} %refs_0_.1) | copy-start | bytes 1572868
  0.7 12.9 %copy-start.7 = (f32[64,8]{0,1:T(8,128)S(1)}, f32[64,8]{0,1:T(8,128)}, u32[]{:S(2)}) copy-start(f32[64,8]{0,1:T(8,128)} %param.11) | copy-start | bytes 6148
  0.7 12.9 %copy-start.8 = (s32[64,8]{0,1:T(8,128)S(1)}, s32[64,8]{0,1:T(8,128)}, u32[]{:S(2)}) copy-start(s32[64,8]{0,1:T(8,128)} %param.10) | copy-start | bytes 6148
  1.7 8.5 %collective-permute-start = (bf16[16,2048]{1,0:T(8,128)(2,1)S(1)}, bf16[16,2048]{1,0:T(8,128)(2,1)S(1)}, u32[]{:S(2)}, u32[]{:S(2)}) collective-permute-start(bf16[16,2048]{1,0:T(8,128)(2,1)S(1)} %constant_dynamic-slice_fusion), channel_id=1, source_target_pairs={{0,4},{1,5},{2,6},{3,7},{4,0},{5,1},{6,2},{7,3},{8,12},{9,13},{10,... | collective-permute-start | bytes 196616 | tf_op jit(solution)/shard_map/ppermute | solution.py:135
  7.0 31.6 %collective-permute-start.6 = (bf16[64,4096]{1,0:T(8,128)(2,1)}, bf16[64,4096]{1,0:T(8,128)(2,1)}, u32[]{:S(2)}, u32[]{:S(2)}) collective-permute-start(bf16[64,4096]{1,0:T(8,128)(2,1)} %get-tuple-element.31), channel_id=1, source_target_pairs={{0,2},{1,3},{2,0},{3,1},{4,6},{5,7},{6,4},{7,5},{8,10},{9,11},{10,... | collective-permute-start | bytes 1572872 | tf_op jit(solution)/shard_map/ppermute | solution.py:135
  8.5 46.3 %collective-permute-start.9 = (bf16[128,4096]{1,0:T(8,128)(2,1)S(1)}, bf16[128,4096]{1,0:T(8,128)(2,1)S(1)}, u32[]{:S(2)}, u32[]{:S(2)}) collective-permute-start(bf16[128,4096]{1,0:T(8,128)(2,1)S(1)} %bitcast.21), channel_id=1, source_target_pairs={{0,1},{1,0},{2,3},{3,2},{4,5},{5,4},{6,7},{7,6},{8,9},{9,8},{10,11... | collective-permute-start | bytes 3145736 | tf_op jit(solution)/shard_map/ppermute | solution.py:135
  10.2 14.6 %collective-permute-start.1 = (bf16[64,4096]{1,0:T(8,128)(2,1)S(1)}, bf16[64,4096]{1,0:T(8,128)(2,1)}, u32[]{:S(2)}, u32[]{:S(2)}) collective-permute-start(bf16[64,4096]{1,0:T(8,128)(2,1)S(1)} %copy-done.4), channel_id=1, source_target_pairs={{0,4},{1,5},{2,6},{3,7},{4,8},{5,9},{6,10},{7,11},{8,12},{9,13},{1... | collective-permute-start | bytes 1572872 | tf_op jit(solution)/shard_map/ppermute | solution.py:132
  13.7 23.6 %collective-permute-start.4 = (bf16[64,4096]{1,0:T(8,128)(2,1)S(1)}, bf16[64,4096]{1,0:T(8,128)(2,1)}, u32[]{:S(2)}, u32[]{:S(2)}) collective-permute-start(bf16[64,4096]{1,0:T(8,128)(2,1)S(1)} %copy-done.4), channel_id=1, source_target_pairs={{4,0},{5,1},{6,2},{7,3},{8,4},{9,5},{10,6},{11,7},{12,8},{13,9},{1... | collective-permute-start | bytes 1572872 | tf_op jit(solution)/shard_map/ppermute | solution.py:132
  15.4 21.2 %collective-permute-start.2 = (bf16[32,2048]{1,0:T(8,128)(2,1)S(1)}, bf16[32,2048]{1,0:T(8,128)(2,1)S(1)}, u32[]{:S(2)}, u32[]{:S(2)}) collective-permute-start(bf16[32,2048]{1,0:T(8,128)(2,1)S(1)} %pad_maximum_fusion.3), channel_id=1, source_target_pairs={{0,8},{1,9},{2,10},{3,11},{4,12},{5,13},{6,14},{7,15},{8,0},{9,1},... | collective-permute-start | bytes 393224 | tf_op jit(solution)/shard_map/ppermute | solution.py:135
  24.8 16.5 %collective-permute-start.10 = (bf16[64,4096]{1,0:T(8,128)(2,1)}, bf16[64,4096]{1,0:T(8,128)(2,1)S(1)}, u32[]{:S(2)}, u32[]{:S(2)}) collective-permute-start(bf16[64,4096]{1,0:T(8,128)(2,1)} %get-tuple-element.21), channel_id=1, source_target_pairs={{0,2},{1,3},{2,0},{3,1},{4,6},{5,7},{6,4},{7,5},{8,10},{9,11},{10,... | collective-permute-start | bytes 1572872 | tf_op jit(solution)/shard_map/ppermute | solution.py:135
  36.6 4.7 %collective-permute-start.3 = (bf16[64,4096]{1,0:T(8,128)(2,1)}, bf16[64,4096]{1,0:T(8,128)(2,1)S(1)}, u32[]{:S(2)}, u32[]{:S(2)}) collective-permute-start(bf16[64,4096]{1,0:T(8,128)(2,1)} %collective-permute-done.1.refs_1_), channel_id=1, source_target_pairs={{4,8},{5,9},{6,10},{7,11},{8,12},{9,13},{10,14},{11,15},{20,24},{2... | collective-permute-start | bytes 1572872 | tf_op jit(solution)/shard_map/ppermute | solution.py:132
  37.3 15.3 %collective-permute-start.5 = (bf16[64,4096]{1,0:T(8,128)(2,1)}, bf16[64,4096]{1,0:T(8,128)(2,1)S(1)}, u32[]{:S(2)}, u32[]{:S(2)}) collective-permute-start(bf16[64,4096]{1,0:T(8,128)(2,1)} %collective-permute-done.4.refs_2_), channel_id=1, source_target_pairs={{4,0},{5,1},{6,2},{7,3},{8,4},{9,5},{10,6},{11,7},{20,16},{21,17},... | collective-permute-start | bytes 1572872 | tf_op jit(solution)/shard_map/ppermute | solution.py:132
  39.7 15.8 %copy-start.5 = (bf16[64,4096]{1,0:T(8,128)(2,1)S(1)}, bf16[64,4096]{1,0:T(8,128)(2,1)}, u32[]{:S(2)}) copy-start(bf16[64,4096]{1,0:T(8,128)(2,1)} %refs_0_.1) | copy-start | bytes 1572868
  39.7 13.1 %collective-permute-start.7 = (bf16[64,2048]{1,0:T(8,128)(2,1)S(1)}, bf16[64,2048]{1,0:T(8,128)(2,1)S(1)}, u32[]{:S(2)}, u32[]{:S(2)}) collective-permute-start(bf16[64,2048]{1,0:T(8,128)(2,1)S(1)} %pad_maximum_fusion.2), channel_id=1, source_target_pairs={{0,16},{16,0},{1,17},{17,1},{2,18},{18,2},{3,19},{19,3},{4,20},{20... | collective-permute-start | bytes 786440 | tf_op jit(solution)/shard_map/ppermute | solution.py:189
  52.8 2.7 %collective-permute-start.11 = (bf16[128,4096]{1,0:T(8,128)(2,1)S(1)}, bf16[128,4096]{1,0:T(8,128)(2,1)S(1)}, u32[]{:S(2)}, u32[]{:S(2)}) collective-permute-start(bf16[128,4096]{1,0:T(8,128)(2,1)S(1)} %constant_dynamic-update-slice_fusion.refs_6_.refs_3_), channel_id=1, source_target_pairs={{0,1},{1,0},{2,3},{3,2},{4,5},{5,4},{6,7},{7,6},{8,9},{9,8},{10,11... | collective-permute-start | bytes 3145736 | tf_op jit(solution)/shard_map/ppermute | solution.py:135
  52.9 14.4 %collective-permute-start.16 = (bf16[64,4096]{1,0:T(8,128)(2,1)S(1)}, bf16[64,4096]{1,0:T(8,128)(2,1)S(1)}, u32[]{:S(2)}, u32[]{:S(2)}) collective-permute-start(bf16[64,4096]{1,0:T(8,128)(2,1)S(1)} %pad_maximum_fusion.1.mine_ref), channel_id=1, source_target_pairs={{0,2},{1,3},{2,0},{3,1},{4,6},{5,7},{6,4},{7,5},{8,10},{9,11},{10,... | collective-permute-start | bytes 1572872 | tf_op jit(solution)/shard_map/ppermute | solution.py:135
  53.5 18.0 %collective-permute-start.8 = (bf16[64,4096]{1,0:T(8,128)(2,1)S(1)}, bf16[64,4096]{1,0:T(8,128)(2,1)S(1)}, u32[]{:S(2)}, u32[]{:S(2)}) collective-permute-start(bf16[64,4096]{1,0:T(8,128)(2,1)S(1)} %add.58.refs_3_), channel_id=1, source_target_pairs={{8,12},{9,13},{10,14},{11,15},{4,0},{5,1},{6,2},{7,3},{24,28},{25,... | collective-permute-start | bytes 1572872 | tf_op jit(solution)/shard_map/ppermute | solution.py:132
  58.7 13.6 %collective-permute-start.12 = (bf16[64,512]{1,0:T(8,128)(2,1)S(1)}, bf16[64,512]{1,0:T(8,128)(2,1)S(1)}, u32[]{:S(2)}, u32[]{:S(2)}) collective-permute-start(bf16[64,512]{1,0:T(8,128)(2,1)S(1)} %get-tuple-element.23), channel_id=1, source_target_pairs={{4,0},{5,1},{6,2},{7,3},{8,4},{9,5},{10,6},{11,7},{12,8},{13,9},{1... | collective-permute-start | bytes 196616 | tf_op jit(solution)/shard_map/ppermute | solution.py:132
  60.0 12.3 %collective-permute-start.13 = (bf16[64,512]{1,0:T(8,128)(2,1)S(1)}, bf16[64,512]{1,0:T(8,128)(2,1)S(1)}, u32[]{:S(2)}, u32[]{:S(2)}) collective-permute-start(bf16[64,512]{1,0:T(8,128)(2,1)S(1)} %get-tuple-element.24), channel_id=1, source_target_pairs={{0,4},{1,5},{2,6},{3,7},{4,8},{5,9},{6,10},{7,11},{8,12},{9,13},{1... | collective-permute-start | bytes 196616 | tf_op jit(solution)/shard_map/ppermute | solution.py:132
  64.5 7.7 %collective-permute-start.14 = (bf16[64,512]{1,0:T(8,128)(2,1)S(1)}, bf16[64,512]{1,0:T(8,128)(2,1)S(1)}, u32[]{:S(2)}, u32[]{:S(2)}) collective-permute-start(bf16[64,512]{1,0:T(8,128)(2,1)S(1)} %get-tuple-element.25), channel_id=1, source_target_pairs={{8,0},{9,1},{10,2},{11,3},{12,4},{13,5},{14,6},{15,7},{0,8},{1,9},... | collective-permute-start | bytes 196616 | tf_op jit(solution)/shard_map/ppermute | solution.py:132
  67.3 6.7 %copy-start.2 = (bf16[64,4096]{1,0:T(8,128)(2,1)}, bf16[64,4096]{1,0:T(8,128)(2,1)S(1)}, u32[]{:S(2)}) copy-start(bf16[64,4096]{1,0:T(8,128)(2,1)S(1)} %collective-permute-done.16.over_y_ref) | copy-start | bytes 1572868
  74.0 9.1 %collective-permute-start.17 = (bf16[128,4096]{1,0:T(8,128)(2,1)}, bf16[128,4096]{1,0:T(8,128)(2,1)S(1)}, u32[]{:S(2)}, u32[]{:S(2)}) collective-permute-start(bf16[128,4096]{1,0:T(8,128)(2,1)} %pad_maximum_fusion), channel_id=1, source_target_pairs={{0,1},{1,0},{2,3},{3,2},{4,5},{5,4},{6,7},{7,6},{8,9},{9,8},{10,11... | collective-permute-start | bytes 3145736 | tf_op jit(solution)/shard_map/ppermute | solution.py:135
  74.2 9.0 %copy-start.3 = (bf16[64,4096]{1,0:T(8,128)(2,1)S(1)}, bf16[64,4096]{1,0:T(8,128)(2,1)}, u32[]{:S(2)}) copy-start(bf16[64,4096]{1,0:T(8,128)(2,1)} %copy-done.2) | copy-start | bytes 1572868
  74.4 8.2 %collective-permute-start.15 = (bf16[64,512]{1,0:T(8,128)(2,1)S(1)}, bf16[64,512]{1,0:T(8,128)(2,1)S(1)}, u32[]{:S(2)}, u32[]{:S(2)}) collective-permute-start(bf16[64,512]{1,0:T(8,128)(2,1)S(1)} %project.3), channel_id=1, source_target_pairs={{12,0},{13,1},{14,2},{15,3},{0,12},{1,13},{2,14},{3,15},{28,16},{2... | collective-permute-start | bytes 196616 | tf_op jit(solution)/shard_map/ppermute | solution.py:132
  83.1 0.7 copy-start.6

commit v5 on v4

v5 whole, which is shorter than its diff:
```python
import functools

import jax
import jax.numpy as jnp
from jax import lax
from jax.experimental import pallas as pl
from jax.experimental.pallas import tpu as pltpu
from jax.sharding import PartitionSpec as P

RANK = 64
EX_DEV = 4
QUAD = 4
SLAB = 16

SMALL = pl.CostEstimate(flops=1024, bytes_accessed=1024, transcendentals=0)

NT = (((1,), (1,)), ((), ()))
TN = (((0,), (0,)), ((), ()))


def combine_kernel(blocks, experts, first, last, *refs):
    sides, wide = refs[:blocks], refs[blocks]
    total = jnp.zeros((RANK, EX_DEV * RANK), jnp.float32) if first else refs[blocks + 1][...]
    out = refs[-1]
    span = experts * RANK
    for b in range(blocks):
        slabs = [sides[b][:, g * span : (g + 1) * span] for g in range(wide.shape[1] // SLAB)]
        side = jnp.concatenate(slabs, axis=0)
        for e in range(experts):
            total += lax.dot_general(
                side[:, e * RANK : (e + 1) * RANK],
                wide[b * experts + e],
                TN,
                preferred_element_type=jnp.float32,
            )
    if last:
        counts = refs[-2]
        for x in range(EX_DEV):
            out[x] = total[:, x * RANK : (x + 1) * RANK] / counts[x : x + 1, :]
    else:
        out[...] = total


def combine(sides, wide, total=None, counts=None):
    experts = wide.shape[0] // len(sides)
    extra = [a for a in (total, counts) if a is not None]
    shape = (RANK, EX_DEV * RANK) if counts is None else (EX_DEV, RANK, RANK)
    return pl.pallas_call(
        functools.partial(combine_kernel, len(sides), experts, total is None, counts is not None),
        out_shape=jax.ShapeDtypeStruct(shape, jnp.float32),
        in_specs=[pl.BlockSpec(memory_space=pltpu.VMEM)] * (len(sides) + 1 + len(extra)),
        out_specs=pl.BlockSpec(memory_space=pltpu.VMEM),
        cost_estimate=SMALL,
        compiler_params=pltpu.CompilerParams(vmem_limit_bytes=32 << 20),
        name="combine",
    )(*sides, wide, *extra)


def project_kernel(blocks, rows, *refs):
    parts, weights = refs[:blocks], refs[blocks : blocks + QUAD]
    outs, total = refs[blocks + QUAD : -1], refs[-1]
    depth = 1024
    total[...] = jnp.zeros_like(total)

    @pl.loop(0, parts[0].shape[1] // depth)
    def _(i):
        span = pl.ds(pl.multiple_of(i * depth, depth), depth)
        left = jnp.concatenate([p[:rows, span] for p in parts], axis=0)
        right = jnp.concatenate([w[:, span] for w in weights], axis=0)
        total[...] += lax.dot_general(left, right, NT, preferred_element_type=jnp.float32)

    width = total.shape[1]
    for b in range(blocks):
        for g in range(rows // SLAB):
            top = b * rows + g * SLAB
            outs[b][:, g * width : (g + 1) * width] = total[top : top + SLAB].astype(jnp.bfloat16)
        used = rows // SLAB * width
        if outs[b].shape[1] > used:
            outs[b][:, used:] = parts[-1][rows:, :]


def project(parts, rows, weights, riders=()):
    width = QUAD * weights[0].shape[0]
    vmem = pl.BlockSpec(memory_space=pltpu.VMEM)
    sizes = [rows // SLAB * width + (parts[-1].shape[1] if b in riders else 0) for b in range(len(parts))]
    return pl.pallas_call(
        functools.partial(project_kernel, len(parts), rows),
        out_shape=[jax.ShapeDtypeStruct((SLAB, size), jnp.bfloat16) for size in sizes],
        in_specs=[vmem] * (len(parts) + QUAD),
        out_specs=[vmem] * len(parts),
        scratch_shapes=[pltpu.VMEM((rows * len(parts), width), jnp.float32)],
        cost_estimate=SMALL,
        compiler_params=pltpu.CompilerParams(vmem_limit_bytes=40 << 20),
        name="project",
    )(*parts, *weights)


def assemble_kernel(blocks, where_ref, held_ref, late_ref, over_y_ref, late_over_y_ref, across_ref, out_ref):
    rows = late_ref.shape[0]
    span = blocks * rows
    sources = (
        ((held_ref, 0), (late_ref, 0)),
        ((across_ref, 0), (across_ref, 2 * span)),
        ((over_y_ref, 0), (late_over_y_ref, 0)),
        ((across_ref, span), (across_ref, 2 * span + rows)),
    )
    for b in range(blocks + 1):

        @pl.when(where_ref[b] >= 0)
        def _():
            for rel in range(QUAD):
                source, base = sources[rel][b // blocks]
                top = base + b % blocks * rows
                home = where_ref[b] * QUAD + (where_ref[blocks + 1] ^ rel)
                out_ref[pl.ds(pl.multiple_of(home * rows, rows), rows), :] = source[top : top + rows, :]


def assemble(where, total, *held):
    vmem = pl.BlockSpec(memory_space=pltpu.VMEM)
    return pl.pallas_call(
        functools.partial(assemble_kernel, where.shape[0] - 2),
        out_shape=jax.ShapeDtypeStruct((total, held[0].shape[1]), held[0].dtype),
        in_specs=[pl.BlockSpec(memory_space=pltpu.SMEM)] + [vmem] * len(held),
        out_specs=vmem,
        cost_estimate=SMALL,
        compiler_params=pltpu.CompilerParams(vmem_limit_bytes=40 << 20),
        name="assemble",
    )(where, *held)


def after(array, *others):
    return lax.optimization_barrier((array, *others))[0]


def shards(tokens, out_grad, routes, route_weight, example_ids, in_proj, out_proj, queries):
    token_count, model_width = tokens.shape
    owned = in_proj.shape[0]
    n = lax.axis_size("expert")
    planes = n // QUAD
    me = lax.axis_index("expert")
    plane, spot = me // QUAD, me % QUAD

    def move(array, hops):
        pairs = [(a * QUAD + q, b * QUAD + q) for a, b in hops for q in range(QUAD)]
        return lax.ppermute(array, "expert", pairs)

    def swap(array, bit):
        return lax.ppermute(array, "expert", [(i, i ^ bit) for i in range(n)])

    weights = jnp.swapaxes(in_proj, 1, 2).reshape(owned * RANK, model_width)

    origins, ways_home = [plane], []
    for s in range(1, planes):
        up_home = [(p, p - s) for p in range(s, planes)]
        down_home = [(p, p + s) for p in range(planes - s)]
        from_up = jnp.where(plane >= s, plane - s, -1)
        from_down = jnp.where(plane + s < planes, plane + s, -1)
        if 2 * s >= planes:
            origins.append(jnp.maximum(from_up, from_down))
            ways_home.append(up_home + down_home)
        else:
            origins.extend([from_up, from_down])
            ways_home.extend([up_home, down_home])

    homes = []
    for home in ways_home:
        back = -jnp.ones((), jnp.int32)
        for a, b in home:
            back = jnp.where(plane == b, a, back)
        homes.append(back)
    grad_side = jnp.dot(out_grad, out_proj, preferred_element_type=jnp.float32)
    rel = jnp.arange(QUAD, dtype=jnp.int32)
    inner = ((spot ^ rel)[:, None] * owned + jnp.arange(owned, dtype=jnp.int32)[None, :]).reshape(-1)
    place = jnp.stack([plane] + homes)
    expert_ids = jnp.where(place[:, None] >= 0, place[:, None] * (QUAD * owned) + inner[None, :], -1).reshape(-1)
    gate = jnp.sum(
        jnp.where(routes.T[None, :, :] == expert_ids[:, None, None], route_weight.T[None, :, :], 0.0), axis=1
    )
    local_ids = example_ids.reshape(token_count)
    member = local_ids[:, None] == jnp.arange(EX_DEV, dtype=jnp.int32)[None, :]
    counts = jnp.sum(member.astype(jnp.float32), axis=0)
    counts = jnp.broadcast_to(counts[:, None], (EX_DEV, RANK))
    repeated = jnp.concatenate([grad_side] * EX_DEV, axis=1)
    widely = jnp.repeat(member, RANK, axis=1)
    wide = jnp.where(
        widely[None], (gate[:, :, None] * repeated[None]).astype(jnp.bfloat16), jnp.zeros((), jnp.bfloat16)
    )

    mine = jnp.concatenate([tokens, queries], axis=0)
    up, down = mine, mine
    arrived = []
    for s in range(1, planes):
        up_hops = [(p, p + 1) for p in range(s - 1, planes - 1)]
        down_hops = [(p, p - 1) for p in range(1, planes - s + 1)]
        if s == 2:
            up, down = after(up, wide), after(down, wide)
        if s == planes - 1:
            up, down = up[:token_count], down[:token_count]
        if 2 * s > planes + 1:
            up = down = move(up, up_hops + down_hops)
        else:
            up, down = move(up, up_hops), move(down, down_hops)
            if 2 * s >= planes:
                up = down = up + down
        arrived.extend([up] if 2 * s >= planes else [up, down])
    last = arrived.pop()

    over_core = swap(weights, 1)
    over_y = swap(weights, 2)
    across = swap(after(over_y, arrived[-1]), 1)
    quad_weights = [weights, over_core, over_y, across]

    experts = QUAD * owned
    own, *sides = project([tokens] + arrived, token_count, quad_weights, riders=(1, 2))
    returned = [move(side, home) for side, home in zip(sides, ways_home)]
    side = project([after(last, *returned)], token_count, quad_weights)[0]
    late = move(side, ways_home[-1])
    early = combine([own] + returned, wide[:-experts])

    held = jnp.concatenate([after(queries, arrived[0])] + [block[token_count:] for block in arrived], axis=0)
    held_late = jnp.where(plane == 0, returned[0][:, own.shape[1] :], returned[1][:, own.shape[1] :])
    over_y = swap(held, 2)
    late_over_y = swap(held_late, 2)
    across = swap(jnp.concatenate(after((held, over_y, held_late, late_over_y), side), axis=0), 1)
    where = jnp.stack(origins + [spot]).astype(jnp.int32)
    all_queries = assemble(where, n * queries.shape[0], held, held_late, over_y, late_over_y, across)
    sketches = combine([late], wide[-experts:], early, counts)
    sketches = sketches.reshape(EX_DEV, RANK * RANK)
    scores = lax.dot_general(sketches.astype(jnp.bfloat16), all_queries, NT, preferred_element_type=jnp.float32)
    return (sketches, scores)


def solution(mesh):
    placed = (
        P(("groups", "expert"), None),
        P(("groups", "expert"), None),
        P(("groups", "expert"), None),
        P(("groups", "expert"), None),
        P(("groups", "expert"), None),
        P("expert", None, None),
        P(),
        P("expert", None),
    )
    return jax.shard_map(
        shards,
        mesh=mesh,
        in_specs=placed,
        out_specs=(P(("groups", "expert"), None), P(("groups", "expert"), None)),
        check_vma=False,
    )
```

time: 85.5 us -> 92.3 us (1.080)
  waiting for transfers between devices: 38.3 us -> 31.7 us
  local copies, waits for them, and re-layouts: 5.23 us -> 11.1 us
  starting transfers between devices: 28.9 us -> 33.5 us
  other arithmetic: 2.38 us -> 4.07 us
    ppermute x8 -> x6, waiting for transfers between devices: 13.8 us -> 0.78 us  [swap(): return lax.ppermute(array, 'expert', [(i, i ^ bit) for i in range(n)])]
    ppermute x9, starting transfers between devices: 18 us -> 28.3 us  [move(): return lax.ppermute(array, 'expert', pairs)]
    ppermute x9, waiting for transfers between devices: 24.6 us -> 30.9 us  [move(): return lax.ppermute(array, 'expert', pairs)]
    unnamed x21 -> x37, local copies, waits for them, and re-layouts: 1.13 us -> 5.26 us
    ppermute x8 -> x6, starting transfers between devices: 9.38 us -> 5.27 us  [swap(): return lax.ppermute(array, 'expert', [(i, i ^ bit) for i in range(n)])]
    ppermute x1 -> x0, starting transfers between devices: 1.56 us -> none  [shards(): lax.ppermute(after(lined, over_y, up, down), 'groups', [(g, (g + k) % gro...]
    slice x1, local copies, waits for them, and re-layouts: 0.1 us -> 1.35 us  [shards(): early = combine([own] + returned, wide[:-experts])]
    select_n x1, other arithmetic: 0.4 us -> 1.49 us  [shards(): jnp.where(widely[None], (gate[:, :, None] * repeated[None]).astype(jnp.bf...]
  transfers between devices with their start and end apart: 18 -> 15, of which waited for: 8 -> 7; matrix products, arithmetic and copies ran while one was open for 9% -> 10% of each run, Pallas kernels for 5% -> 3%
where the time goes in v5:
time: 92.3 us; the launch traced here: 91.7 us
  starting transfers between devices  33.5 us (36%)
  waiting for transfers between devices  31.7 us (34%)
  local copies, waits for them, and re-layouts  11.1 us (12%)
  Pallas kernels  7.59 us (8%)
  other arithmetic  4.07 us (4%)
  matrix products  2.58 us (3%)
  between operations  1.13 us (1%)
    ppermute x9, waiting for transfers between devices, move(): return lax.ppermute(array, 'expert', pairs)  30.9 us
    ppermute x9, starting transfers between devices, move(): return lax.ppermute(array, 'expert', pairs)  28.3 us
    ppermute x6, starting transfers between devices, swap(): return lax.ppermute(array, 'expert', [(i, i ^ bit) for i in range(n)])  5.27 us
    unnamed x37, local copies, waits for them, and re-layouts  5.26 us
    pallas_call x2, Pallas kernels, project(): pl.pallas_call(functools.partial(project_kernel, len(parts), rows), out_s...  5.02 us
  transfers between devices with their start and end apart: 15, of which 7 were waited for; matrix products, arithmetic and copies ran while one was open for 10% of the time, Pallas kernels for 3%

profile of v5, /device:TPU:0, one launch (start us, length us, event | category | flops | bytes accessed | tf_op | source)
XLA Modules:
  0.0 91.7 jit_solution(3786494357842855497)
XLA Ops:
  0.7 1.2 %constant_dynamic-update-slice_fusion.1 = bf16[80,4096]{1,0:T(8,128)(2,1)S(1)} fusion(bf16[64,4096]{1,0:T(8,128)(2,1)} %refs_0_.1), kind=kLoop, calls=%fused_computation.12 | loop fusion | bytes 1048576
  1.9 0.9 constant_dynamic-update-slice_fusion
  2.8 1.3 %collective-permute-start.2 = (bf16[80,4096]{1,0:T(8,128)(2,1)S(1)}, bf16[80,4096]{1,0:T(8,128)(2,1)}, u32[]{:S(2)}, u32[]{:S(2)}) collective-permute-start(bf16[80,4096]{1,0:T(8,128)(2,1)S(1)} %constant_dynamic-update-slice_fusion), channel_id=1, source_target_pairs={{4,0},{5,1},{6,2},{7,3},{8,4},{9,5},{10,6},{11,7},{12,8},{13,9},{1... | collective-permute-start | bytes 1966088 | tf_op jit(solution)/shard_map/ppermute | solution.py:145
  4.1 6.4 %collective-permute-start = (bf16[80,4096]{1,0:T(8,128)(2,1)S(1)}, bf16[80,4096]{1,0:T(8,128)(2,1)}, u32[]{:S(2)}, u32[]{:S(2)}) collective-permute-start(bf16[80,4096]{1,0:T(8,128)(2,1)S(1)} %constant_dynamic-update-slice_fusion), channel_id=1, source_target_pairs={{0,4},{1,5},{2,6},{3,7},{4,8},{5,9},{6,10},{7,11},{8,12},{9,13},{1... | collective-permute-start | bytes 1966088 | tf_op jit(solution)/shard_map/ppermute | solution.py:145
  10.5 2.0 %collective-permute-start.6 = (bf16[128,4096]{1,0:T(8,128)(2,1)}, bf16[128,4096]{1,0:T(8,128)(2,1)S(1)}, u32[]{:S(2)}, u32[]{:S(2)}) collective-permute-start(bf16[128,4096]{1,0:T(8,128)(2,1)} %bitcast.19), channel_id=1, source_target_pairs={{0,2},{1,3},{2,0},{3,1},{4,6},{5,7},{6,4},{7,5},{8,10},{9,11},{10,... | collective-permute-start | bytes 3145736 | tf_op jit(solution)/shard_map/ppermute | solution.py:148
  12.6 0.1 add.66
  12.7 0.7 iota_compare_fusion
  13.5 1.3 %fusion.3 = f32[64,64]{1,0:T(8,128)S(1)} fusion(bf16[64,4096]{1,0:T(8,128)(2,1)S(1)} %copy-done, bf16[4096,64]{0,1:T(8,128)(2,1)} %param.14), kind=kOutput, calls=%fused_computation.18 | convolution fusion | flops 33554432 | bytes 1064960 | tf_op jit(solution)/shard_map/dot_general | solution.py:171
  14.9 0.1 pad_maximum_fusion.2
  15.1 0.1 broadcast_in_dim.56
  15.2 0.1 broadcast_in_dim.57
  15.4 0.1 select_reduce_fusion
  15.5 1.5 %fusion = bf16[40,64,256]{2,1,0:T(8,128)(2,1)} fusion(f32[64,256]{1,0:T(8,128)S(1)} %pad_maximum_fusion.2, f32[40,64]{1,0:T(8,128)S(1)} %select_reduce_fusion, pred[64,256]{1,0:T(8,128)(4,1)S(1)} %broadcast_in_dim.57), kind=kLoop, calls=%fused_computation.1 | loop fusion | flops 1966080 | bytes 1402880 | tf_op jit(solution)/shard_map/jit(_where)/select_n | solution.py:185
  17.0 5.6 %collective-permute-done.2.refs_2_ = bf16[80,4096]{1,0:T(8,128)(2,1)} collective-permute-done((bf16[80,4096]{1,0:T(8,128)(2,1)S(1)}, bf16[80,4096]{1,0:T(8,128)(2,1)}, u32[]{:S(2)}, u32[]{:S(2)}) %collective-permute-start.2) | collective-permute-done | bytes 655392 | tf_op jit(solution)/shard_map/ppermute | solution.py:145
  22.6 1.3 %collective-permute-start.3 = (bf16[80,4096]{1,0:T(8,128)(2,1)}, bf16[80,4096]{1,0:T(8,128)(2,1)S(1)}, u32[]{:S(2)}, u32[]{:S(2)}) collective-permute-start(bf16[80,4096]{1,0:T(8,128)(2,1)} %collective-permute-done.2.refs_2_), channel_id=1, source_target_pairs={{4,0},{5,1},{6,2},{7,3},{8,4},{9,5},{10,6},{11,7},{20,16},{21,17},... | collective-permute-start | bytes 1966088 | tf_op jit(solution)/shard_map/ppermute | solution.py:145
  23.9 0.7 collective-permute-start.1
  24.7 15.9 %collective-permute-done.3 = bf16[80,4096]{1,0:T(8,128)(2,1)S(1)} collective-permute-done((bf16[80,4096]{1,0:T(8,128)(2,1)}, bf16[80,4096]{1,0:T(8,128)(2,1)S(1)}, u32[]{:S(2)}, u32[]{:S(2)}) %collective-permute-start.3) | collective-permute-done | bytes 655392 | tf_op jit(solution)/shard_map/ppermute | solution.py:145
  40.6 0.2 add.69.refs_3_
  40.8 0.9 slice.35
  41.7 0.9 slice.36
  42.7 0.8 collective-permute-done.7.refs_7_.refs_4_
  43.5 3.2 %project.2 = (bf16[16,2048]{1,0:T(8,128)(2,1)S(1)}, bf16[16,6144]{1,0:T(8,128)(2,1)S(1)}, bf16[16,6144]{1,0:T(8,128)(2,1)S(1)}, bf16[16,2048]{1,0:T(8,128)(2,1)S(1)}) custom-call(bf16[64,4096]{1,0:T(8,128)(2,1)S(1)} %copy-done.4, bf16[80,4096]{1,0:T(8,128)(2,1)} %collective-permute-done.refs_1_, bf16[80,4096]{1,0:T(8,128)(2,1)} %collective-permute-done.2.refs_2_, ...), custom_call_target="tpu_custom_call" | custom-call | flops 1024 | bytes 1024 | tf_op jit(solution)/shard_map/project/pallas_call | solution.py:86
  46.7 0.6 copy-done.9
  47.3 1.3 %collective-permute-start.8 = (bf16[16,6144]{1,0:T(8,128)(2,1)S(1)}, bf16[16,6144]{1,0:T(8,128)(2,1)S(1)}, u32[]{:S(2)}, u32[]{:S(2)}) collective-permute-start(bf16[16,6144]{1,0:T(8,128)(2,1)S(1)} %get-tuple-element.18), channel_id=1, source_target_pairs={{4,0},{5,1},{6,2},{7,3},{8,4},{9,5},{10,6},{11,7},{12,8},{13,9},{1... | collective-permute-start | bytes 589832 | tf_op jit(solution)/shard_map/ppermute | solution.py:145
  48.6 5.3 %collective-permute-start.9 = (bf16[16,6144]{1,0:T(8,128)(2,1)S(1)}, bf16[16,6144]{1,0:T(8,128)(2,1)S(1)}, u32[]{:S(2)}, u32[]{:S(2)}) collective-permute-start(bf16[16,6144]{1,0:T(8,128)(2,1)S(1)} %get-tuple-element.19), channel_id=1, source_target_pairs={{0,4},{1,5},{2,6},{3,7},{4,8},{5,9},{6,10},{7,11},{8,12},{9,13},{1... | collective-permute-start | bytes 589832 | tf_op jit(solution)/shard_map/ppermute | solution.py:145
  54.0 1.6 %collective-permute-start.12 = (bf16[64,4096]{1,0:T(8,128)(2,1)S(1)}, bf16[64,4096]{1,0:T(8,128)(2,1)S(1)}, u32[]{:S(2)}, u32[]{:S(2)}) collective-permute-start(bf16[64,4096]{1,0:T(8,128)(2,1)S(1)} %pad_maximum_fusion.1.held_ref), channel_id=1, source_target_pairs={{0,2},{1,3},{2,0},{3,1},{4,6},{5,7},{6,4},{7,5},{8,10},{9,11},{10,... | collective-permute-start | bytes 1572872 | tf_op jit(solution)/shard_map/ppermute | solution.py:148
  55.6 1.3 %collective-permute-start.4 = (bf16[64,4096]{1,0:T(8,128)(2,1)S(1)}, bf16[64,4096]{1,0:T(8,128)(2,1)S(1)}, u32[]{:S(2)}, u32[]{:S(2)}) collective-permute-start(bf16[64,4096]{1,0:T(8,128)(2,1)S(1)} %slice.32), channel_id=1, source_target_pairs={{8,12},{9,13},{10,14},{11,15},{4,0},{5,1},{6,2},{7,3},{24,28},{25,... | collective-permute-start | bytes 1572872 | tf_op jit(solution)/shard_map/ppermute | solution.py:145
  56.9 0.3 collective-permute-done.8.refs_1_
  57.2 1.2 %collective-permute-done.9.refs_2_ = bf16[16,6144]{1,0:T(8,128)(2,1)S(1)} collective-permute-done((bf16[16,6144]{1,0:T(8,128)(2,1)S(1)}, bf16[16,6144]{1,0:T(8,128)(2,1)S(1)}, u32[]{:S(2)}, u32[]{:S(2)}) %collective-permute-start.9) | collective-permute-done | bytes 196640 | tf_op jit(solution)/shard_map/ppermute | solution.py:145
  58.4 1.6 %collective-permute-start.13 = (bf16[16,4096]{1,0:T(8,128)(2,1)S(1)}, bf16[16,4096]{1,0:T(8,128)(2,1)S(1)}, u32[]{:S(2)}, u32[]{:S(2)}) collective-permute-start(bf16[16,4096]{1,0:T(8,128)(2,1)S(1)} %slice_select_fusion.late_ref), channel_id=1, source_target_pairs={{0,2},{1,3},{2,0},{3,1},{4,6},{5,7},{6,4},{7,5},{8,10},{9,11},{10,... | collective-permute-start | bytes 393224 | tf_op jit(solution)/shard_map/ppermute | solution.py:148
  60.0 4.7 %collective-permute-start.10 = (bf16[16,2048]{1,0:T(8,128)(2,1)S(1)}, bf16[16,2048]{1,0:T(8,128)(2,1)S(1)}, u32[]{:S(2)}, u32[]{:S(2)}) collective-permute-start(bf16[16,2048]{1,0:T(8,128)(2,1)S(1)} %get-tuple-element.20), channel_id=1, source_target_pairs={{8,0},{9,1},{10,2},{11,3},{12,4},{13,5},{14,6},{15,7},{0,8},{1,9},... | collective-permute-start | bytes 196616 | tf_op jit(solution)/shard_map/ppermute | solution.py:145
  64.6 7.7 %collective-permute-done.4.refs_0_ = bf16[64,4096]{1,0:T(8,128)(2,1)S(1)} collective-permute-done((bf16[64,4096]{1,0:T(8,128)(2,1)S(1)}, bf16[64,4096]{1,0:T(8,128)(2,1)S(1)}, u32[]{:S(2)}, u32[]{:S(2)}) %collective-permute-start.4) | collective-permute-done | bytes 524320 | tf_op jit(solution)/shard_map/ppermute | solution.py:145
  72.3 1.8 %project.3 = bf16[16,2048]{1,0:T(8,128)(2,1)S(1)} custom-call(bf16[64,4096]{1,0:T(8,128)(2,1)S(1)} %collective-permute-done.4.refs_0_, bf16[128,4096]{1,0:T(8,128)(2,1)S(1)} %bitcast.22, bf16[128,4096]{1,0:T(8,128)(2,1)S(1)} %collective-permute-done.5.refs_5_.refs_2_, bf16[128,4096]{1,0:T(8,128)(2,1)S(1)} %collective-permute-done.6.refs_6_.refs_3_, ...), custom_call_target="tpu_custom_call" | custom-call | flops 1024 | bytes 1024 | tf_op jit(solution)/shard_map/project/pallas_call | solution.py:86
  74.2 1.2 %pad_maximum_fusion = bf16[160,4096]{1,0:T(8,128)(2,1)} fusion(bf16[16,4096]{1,0:T(8,128)(2,1)S(1)} %collective-permute-done.13.late_over_y_ref, bf16[16,4096]{1,0:T(8,128)(2,1)S(1)} %slice_select_fusion.late_ref, bf16[64,4096]{1,0:T(8,128)(2,1)S(1)} %collective-permute-done.12.over_y_ref, bf16[64,4096]{1,0:T(8,128)(2,1)S(1)} %pad_maximum_fusion.1.held_ref), kind=kLoop, calls=%fused_computation.2 | loop fusion | flops 5242880 | bytes 2621440 | tf_op jit(solution)/shard_map/concatenate | solution.py:224
  75.4 0.8 copy-done.2
  76.2 1.4 %slice.34.refs_4_ = bf16[32,64,256]{2,1,0:T(8,128)(2,1)S(1)} slice(bf16[40,64,256]{2,1,0:T(8,128)(2,1)} %fusion), slice={[0:32], [0:64], [0:256]} | slice | bytes 2097152 | tf_op jit(solution)/shard_map/slice | solution.py:218
  77.5 1.0 %slice.33.refs_1_ = bf16[8,64,256]{2,1,0:T(8,128)(2,1)S(1)} slice(bf16[40,64,256]{2,1,0:T(8,128)(2,1)} %fusion), slice={[32:40], [0:64], [0:256]} | slice | bytes 524288 | tf_op jit(solution)/shard_map/slice | solution.py:227
  78.6 6.1 %collective-permute-start.11 = (bf16[16,2048]{1,0:T(8,128)(2,1)S(1)}, bf16[16,2048]{1,0:T(8,128)(2,1)S(1)}, u32[]{:S(2)}, u32[]{:S(2)}) collective-permute-start(bf16[16,2048]{1,0:T(8,128)(2,1)S(1)} %project.3), channel_id=1, source_target_pairs={{12,0},{13,1},{14,2},{15,3},{0,12},{1,13},{2,14},{3,15},{28,16},{2... | collective-permute-start | bytes 196616 | tf_op jit(solution)/shard_map/ppermute | solution.py:145
  84.7 0.1 convert_reduce_fusion
  84.8 0.8 copy-done.10
  85.6 0.8 copy-done.12
  86.5 0.7 combine.2.refs_2_
  87.2 0.3 collective-permute-done.11.refs_0_
  87.5 0.4 combine.3
  87.9 0.1 reshape.145
  88.0 0.9 copy-done.8
  88.9 1.5 %assemble.1 = bf16[256,4096]{1,0:T(8,128)(2,1)S(1)} custom-call(s32[6]{0:T(128)S(1)} %stack.48.where_ref, bf16[64,4096]{1,0:T(8,128)(2,1)S(1)} %pad_maximum_fusion.1.held_ref, bf16[16,4096]{1,0:T(8,128)(2,1)S(1)} %slice_select_fusion.late_ref, bf16[64,4096]{1,0:T(8,128)(2,1)S(1)} %copy-done.3, bf16[16,4096]{1,0:T(8,128)(2,1)S(1)} %copy-done.8, ...), custom_call_target="tpu_custom_call" | custom-call | flops 1024 | bytes 1024 | tf_op jit(solution)/shard_map/assemble/pallas_call | solution.py:120
  90.5 1.2 %fusion.1 = f32[4,256]{1,0:T(4,128)} fusion(bf16[256,4096]{1,0:T(8,128)(2,1)S(1)} %assemble.1, f32[4,4096]{1,0:T(4,128)S(1)} %reshape.145), kind=kOutput, calls=%fused_computation.7 | convolution fusion | flops 8404992 | bytes 2166784 | tf_op jit(solution)/shard_map/dot_general | solution.py:229
  (55 shorter events, 0.8 us)
Async XLA Ops:
  0.6 12.8 %copy-start = (bf16[64,4096]{1,0:T(8,128)(2,1)S(1)}, bf16[64,4096]{1,0:T(8,128)(2,1)}, u32[]{:S(2)}) copy-start(bf16[64,4096]{1,0:T(8,128)(2,1)} %param.9) | copy-start | bytes 1572868
  0.6 23.9 %copy-start.1 = (bf16[2,4096,64]{1,2,0:T(8,128)(2,1)S(1)}, bf16[2,4096,64]{1,2,0:T(8,128)(2,1)}, u32[]{:S(2)}) copy-start(bf16[2,4096,64]{1,2,0:T(8,128)(2,1)} %param.13) | copy-start | bytes 3145732
  0.7 14.7 %copy-start.16 = (s32[64,8]{0,1:T(8,128)S(1)}, s32[64,8]{0,1:T(8,128)}, u32[]{:S(2)}) copy-start(s32[64,8]{0,1:T(8,128)} %param.10) | copy-start | bytes 6148
  0.7 14.7 %copy-start.15 = (f32[64,8]{0,1:T(8,128)S(1)}, f32[64,8]{0,1:T(8,128)}, u32[]{:S(2)}) copy-start(f32[64,8]{0,1:T(8,128)} %param.11) | copy-start | bytes 6148
  2.8 19.8 %collective-permute-start.2 = (bf16[80,4096]{1,0:T(8,128)(2,1)S(1)}, bf16[80,4096]{1,0:T(8,128)(2,1)}, u32[]{:S(2)}, u32[]{:S(2)}) collective-permute-start(bf16[80,4096]{1,0:T(8,128)(2,1)S(1)} %constant_dynamic-update-slice_fusion), channel_id=1, source_target_pairs={{4,0},{5,1},{6,2},{7,3},{8,4},{9,5},{10,6},{11,7},{12,8},{13,9},{1... | collective-permute-start | bytes 1966088 | tf_op jit(solution)/shard_map/ppermute | solution.py:145
  4.1 19.8 %collective-permute-start = (bf16[80,4096]{1,0:T(8,128)(2,1)S(1)}, bf16[80,4096]{1,0:T(8,128)(2,1)}, u32[]{:S(2)}, u32[]{:S(2)}) collective-permute-start(bf16[80,4096]{1,0:T(8,128)(2,1)S(1)} %constant_dynamic-update-slice_fusion), channel_id=1, source_target_pairs={{0,4},{1,5},{2,6},{3,7},{4,8},{5,9},{6,10},{7,11},{8,12},{9,13},{1... | collective-permute-start | bytes 1966088 | tf_op jit(solution)/shard_map/ppermute | solution.py:145
  10.5 30.2 %collective-permute-start.6 = (bf16[128,4096]{1,0:T(8,128)(2,1)}, bf16[128,4096]{1,0:T(8,128)(2,1)S(1)}, u32[]{:S(2)}, u32[]{:S(2)}) collective-permute-start(bf16[128,4096]{1,0:T(8,128)(2,1)} %bitcast.19), channel_id=1, source_target_pairs={{0,2},{1,3},{2,0},{3,1},{4,6},{5,7},{6,4},{7,5},{8,10},{9,11},{10,... | collective-permute-start | bytes 3145736 | tf_op jit(solution)/shard_map/ppermute | solution.py:148
  15.3 28.1 %copy-start.4 = (bf16[64,4096]{1,0:T(8,128)(2,1)S(1)}, bf16[64,4096]{1,0:T(8,128)(2,1)}, u32[]{:S(2)}) copy-start(bf16[64,4096]{1,0:T(8,128)(2,1)} %refs_0_.1) | copy-start | bytes 1572868
  22.6 18.0 %collective-permute-start.3 = (bf16[80,4096]{1,0:T(8,128)(2,1)}, bf16[80,4096]{1,0:T(8,128)(2,1)S(1)}, u32[]{:S(2)}, u32[]{:S(2)}) collective-permute-start(bf16[80,4096]{1,0:T(8,128)(2,1)} %collective-permute-done.2.refs_2_), channel_id=1, source_target_pairs={{4,0},{5,1},{6,2},{7,3},{8,4},{9,5},{10,6},{11,7},{20,16},{21,17},... | collective-permute-start | bytes 1966088 | tf_op jit(solution)/shard_map/ppermute | solution.py:145
  23.9 16.7 %collective-permute-start.1 = (bf16[80,4096]{1,0:T(8,128)(2,1)}, bf16[80,4096]{1,0:T(8,128)(2,1)S(1)}, u32[]{:S(2)}, u32[]{:S(2)}) collective-permute-start(bf16[80,4096]{1,0:T(8,128)(2,1)} %collective-permute-done.refs_1_), channel_id=1, source_target_pairs={{4,8},{5,9},{6,10},{7,11},{8,12},{9,13},{10,14},{11,15},{20,24},{2... | collective-permute-start | bytes 1966088 | tf_op jit(solution)/shard_map/ppermute | solution.py:145
  24.6 18.1 %collective-permute-start.5 = (bf16[128,4096]{1,0:T(8,128)(2,1)S(1)}, bf16[128,4096]{1,0:T(8,128)(2,1)S(1)}, u32[]{:S(2)}, u32[]{:S(2)}) collective-permute-start(bf16[128,4096]{1,0:T(8,128)(2,1)S(1)} %bitcast.20), channel_id=1, source_target_pairs={{0,1},{1,0},{2,3},{3,2},{4,5},{5,4},{6,7},{7,6},{8,9},{9,8},{10,11... | collective-permute-start | bytes 3145736 | tf_op jit(solution)/shard_map/ppermute | solution.py:148
  40.7 2.7 %collective-permute-start.7 = (bf16[128,4096]{1,0:T(8,128)(2,1)S(1)}, bf16[128,4096]{1,0:T(8,128)(2,1)S(1)}, u32[]{:S(2)}, u32[]{:S(2)}) collective-permute-start(bf16[128,4096]{1,0:T(8,128)(2,1)S(1)} %collective-permute-done.6.refs_6_.refs_3_), channel_id=1, source_target_pairs={{0,1},{1,0},{2,3},{3,2},{4,5},{5,4},{6,7},{7,6},{8,9},{9,8},{10,11... | collective-permute-start | bytes 3145736 | tf_op jit(solution)/shard_map/ppermute | solution.py:148
  42.7 11.3 %copy-start.13 = (bf16[16,4096]{1,0:T(8,128)(2,1)S(1)}, bf16[16,4096]{1,0:T(8,128)(2,1)}, u32[]{:S(2)}) copy-start(bf16[16,4096]{1,0:T(8,128)(2,1)} %param.15) | copy-start | bytes 393220
  46.7 0.6 copy-start.9
  47.3 9.8 %collective-permute-start.8 = (bf16[16,6144]{1,0:T(8,128)(2,1)S(1)}, bf16[16,6144]{1,0:T(8,128)(2,1)S(1)}, u32[]{:S(2)}, u32[]{:S(2)}) collective-permute-start(bf16[16,6144]{1,0:T(8,128)(2,1)S(1)} %get-tuple-element.18), channel_id=1, source_target_pairs={{4,0},{5,1},{6,2},{7,3},{8,4},{9,5},{10,6},{11,7},{12,8},{13,9},{1... | collective-permute-start | bytes 589832 | tf_op jit(solution)/shard_map/ppermute | solution.py:145
  48.6 9.7 %collective-permute-start.9 = (bf16[16,6144]{1,0:T(8,128)(2,1)S(1)}, bf16[16,6144]{1,0:T(8,128)(2,1)S(1)}, u32[]{:S(2)}, u32[]{:S(2)}) collective-permute-start(bf16[16,6144]{1,0:T(8,128)(2,1)S(1)} %get-tuple-element.19), channel_id=1, source_target_pairs={{0,4},{1,5},{2,6},{3,7},{4,8},{5,9},{6,10},{7,11},{8,12},{9,13},{1... | collective-permute-start | bytes 589832 | tf_op jit(solution)/shard_map/ppermute | solution.py:145
  54.0 20.1 %collective-permute-start.12 = (bf16[64,4096]{1,0:T(8,128)(2,1)S(1)}, bf16[64,4096]{1,0:T(8,128)(2,1)S(1)}, u32[]{:S(2)}, u32[]{:S(2)}) collective-permute-start(bf16[64,4096]{1,0:T(8,128)(2,1)S(1)} %pad_maximum_fusion.1.held_ref), channel_id=1, source_target_pairs={{0,2},{1,3},{2,0},{3,1},{4,6},{5,7},{6,4},{7,5},{8,10},{9,11},{10,... | collective-permute-start | bytes 1572872 | tf_op jit(solution)/shard_map/ppermute | solution.py:148
  55.6 16.7 %collective-permute-start.4 = (bf16[64,4096]{1,0:T(8,128)(2,1)S(1)}, bf16[64,4096]{1,0:T(8,128)(2,1)S(1)}, u32[]{:S(2)}, u32[]{:S(2)}) collective-permute-start(bf16[64,4096]{1,0:T(8,128)(2,1)S(1)} %slice.32), channel_id=1, source_target_pairs={{8,12},{9,13},{10,14},{11,15},{4,0},{5,1},{6,2},{7,3},{24,28},{25,... | collective-permute-start | bytes 1572872 | tf_op jit(solution)/shard_map/ppermute | solution.py:145
  58.4 15.8 %copy-start.5 = (bf16[16,6144]{1,0:T(8,128)(2,1)}, bf16[16,6144]{1,0:T(8,128)(2,1)S(1)}, u32[]{:S(2)}) copy-start(bf16[16,6144]{1,0:T(8,128)(2,1)S(1)} %collective-permute-done.9.refs_2_) | copy-start | bytes 589828
  58.4 15.8 %collective-permute-start.13 = (bf16[16,4096]{1,0:T(8,128)(2,1)S(1)}, bf16[16,4096]{1,0:T(8,128)(2,1)S(1)}, u32[]{:S(2)}, u32[]{:S(2)}) collective-permute-start(bf16[16,4096]{1,0:T(8,128)(2,1)S(1)} %slice_select_fusion.late_ref), channel_id=1, source_target_pairs={{0,2},{1,3},{2,0},{3,1},{4,6},{5,7},{6,4},{7,5},{8,10},{9,11},{10,... | collective-permute-start | bytes 393224 | tf_op jit(solution)/shard_map/ppermute | solution.py:148
  60.0 12.3 %collective-permute-start.10 = (bf16[16,2048]{1,0:T(8,128)(2,1)S(1)}, bf16[16,2048]{1,0:T(8,128)(2,1)S(1)}, u32[]{:S(2)}, u32[]{:S(2)}) collective-permute-start(bf16[16,2048]{1,0:T(8,128)(2,1)S(1)} %get-tuple-element.20), channel_id=1, source_target_pairs={{8,0},{9,1},{10,2},{11,3},{12,4},{13,5},{14,6},{15,7},{0,8},{1,9},... | collective-permute-start | bytes 196616 | tf_op jit(solution)/shard_map/ppermute | solution.py:145
  72.3 1.8 %copy-start.11 = (bf16[16,2048]{1,0:T(8,128)(2,1)}, bf16[16,2048]{1,0:T(8,128)(2,1)S(1)}, u32[]{:S(2)}) copy-start(bf16[16,2048]{1,0:T(8,128)(2,1)S(1)} %collective-permute-done.10.refs_3_) | copy-start | bytes 196612
  74.1 10.5 %copy-start.17 = (s32[1,64]{1,0:T(1,128)S(1)}, s32[1,64]{1,0:T(1,128)}, u32[]{:S(2)}) copy-start(s32[1,64]{1,0:T(1,128)} %param.12) | copy-start | bytes 772
  74.1 10.6 %copy-start.6 = (bf16[16,6144]{1,0:T(8,128)(2,1)S(1)}, bf16[16,6144]{1,0:T(8,128)(2,1)}, u32[]{:S(2)}) copy-start(bf16[16,6144]{1,0:T(8,128)(2,1)} %copy-done.5) | copy-start | bytes 589828
  74.2 1.2 %copy-start.7 = (bf16[16,4096]{1,0:T(8,128)(2,1)}, bf16[16,4096]{1,0:T(8,128)(2,1)S(1)}, u32[]{:S(2)}) copy-start(bf16[16,4096]{1,0:T(8,128)(2,1)S(1)} %collective-permute-done.13.late_over_y_ref) | copy-start | bytes 393220
  75.4 0.8 copy-start.2
  76.2 11.8 %collective-permute-start.14 = (bf16[160,4096]{1,0:T(8,128)(2,1)}, bf16[160,4096]{1,0:T(8,128)(2,1)}, u32[]{:S(2)}, u32[]{:S(2)}) collective-permute-start(bf16[160,4096]{1,0:T(8,128)(2,1)} %pad_maximum_fusion), channel_id=1, source_target_pairs={{0,1},{1,0},{2,3},{3,2},{4,5},{5,4},{6,7},{7,6},{8,9},{9,8},{10,11... | collective-permute-start | bytes 3932168 | tf_op jit(solution)/shard_map/ppermute | solution.py:148
  76.2 11.8 %copy-start.3 = (bf16[64,4096]{1,0:T(8,128)(2,1)S(1)}, bf16[64,4096]{1,0:T(8,128)(2,1)}, u32[]{:S(2)}) copy-start(bf16[64,4096]{1,0:T(8,128)(2,1)} %copy-done.2) | copy-start | bytes 1572868
  78.6 8.8 %collective-permute-start.11 = (bf16[16,2048]{1,0:T(8,128)(2,1)S(1)}, bf16[16,2048]{1,0:T(8,128)(2,1)S(1)}, u32[]{:S(2)}, u32[]{:S(2)}) collective-permute-start(bf16[16,2048]{1,0:T(8,128)(2,1)S(1)} %project.3), channel_id=1, source_target_pairs={{12,0},{13,1},{14,2},{15,3},{0,12},{1,13},{2,14},{3,15},{28,16},{2... | collective-permute-start | bytes 196616 | tf_op jit(solution)/shard_map/ppermute | solution.py:145
  84.8 0.8 copy-start.10
  85.6 0.8 copy-start.12
  88.0 2.5 %copy-start.14 = (f32[4,4096]{1,0:T(4,128)}, f32[4,4096]{1,0:T(4,128)S(1)}, u32[]{:S(2)}) copy-start(f32[4,4096]{1,0:T(4,128)S(1)} %reshape.145) | copy-start | bytes 196612
  88.0 0.9 %copy-start.8 = (bf16[16,4096]{1,0:T(8,128)(2,1)S(1)}, bf16[16,4096]{1,0:T(8,128)(2,1)}, u32[]{:S(2)}) copy-start(bf16[16,4096]{1,0:T(8,128)(2,1)} %copy-done.7) | copy-start | bytes 393220

commit v6 on v5

--- a/solution.py
+++ b/solution.py
@@ -1,4 +1,5 @@
 import functools
+import math
 
 import jax
 import jax.numpy as jnp
@@ -16,6 +17,10 @@
 
 NT = (((1,), (1,)), ((), ()))
 TN = (((0,), (0,)), ((), ()))
+
+
+def room(*arrays):
+    return sum(math.prod(a.shape) * jnp.dtype(a.dtype).itemsize for a in arrays) + (6 << 20)
 
 
 def combine_kernel(blocks, experts, first, last, *refs):
@@ -51,7 +56,7 @@
         in_specs=[pl.BlockSpec(memory_space=pltpu.VMEM)] * (len(sides) + 1 + len(extra)),
         out_specs=pl.BlockSpec(memory_space=pltpu.VMEM),
         cost_estimate=SMALL,
-        compiler_params=pltpu.CompilerParams(vmem_limit_bytes=32 << 20),
+        compiler_params=pltpu.CompilerParams(vmem_limit_bytes=room(*sides, wide)),
         name="combine",
     )(*sides, wide, *extra)
 
@@ -74,56 +79,49 @@
         for g in range(rows // SLAB):
             top = b * rows + g * SLAB
             outs[b][:, g * width : (g + 1) * width] = total[top : top + SLAB].astype(jnp.bfloat16)
-        used = rows // SLAB * width
-        if outs[b].shape[1] > used:
-            outs[b][:, used:] = parts[-1][rows:, :]
-
-
-def project(parts, rows, weights, riders=()):
+
+
+def project(parts, rows, weights):
     width = QUAD * weights[0].shape[0]
     vmem = pl.BlockSpec(memory_space=pltpu.VMEM)
-    sizes = [rows // SLAB * width + (parts[-1].shape[1] if b in riders else 0) for b in range(len(parts))]
+    total = jax.ShapeDtypeStruct((rows * len(parts), width), jnp.float32)
     return pl.pallas_call(
         functools.partial(project_kernel, len(parts), rows),
-        out_shape=[jax.ShapeDtypeStruct((SLAB, size), jnp.bfloat16) for size in sizes],
+        out_shape=[jax.ShapeDtypeStruct((SLAB, rows // SLAB * width), jnp.bfloat16)] * len(parts),
         in_specs=[vmem] * (len(parts) + QUAD),
         out_specs=[vmem] * len(parts),
-        scratch_shapes=[pltpu.VMEM((rows * len(parts), width), jnp.float32)],
+        scratch_shapes=[pltpu.VMEM(total.shape, total.dtype)],
         cost_estimate=SMALL,
-        compiler_params=pltpu.CompilerParams(vmem_limit_bytes=40 << 20),
+        compiler_params=pltpu.CompilerParams(vmem_limit_bytes=room(*parts, *weights, total, total)),
         name="project",
     )(*parts, *weights)
 
 
-def assemble_kernel(blocks, where_ref, held_ref, late_ref, over_y_ref, late_over_y_ref, across_ref, out_ref):
-    rows = late_ref.shape[0]
-    span = blocks * rows
-    sources = (
-        ((held_ref, 0), (late_ref, 0)),
-        ((across_ref, 0), (across_ref, 2 * span)),
-        ((over_y_ref, 0), (late_over_y_ref, 0)),
-        ((across_ref, span), (across_ref, 2 * span + rows)),
-    )
-    for b in range(blocks + 1):
+def assemble_kernel(early, blocks, rows, where_ref, *refs):
+    out_ref = refs[-1]
+    for b in range(blocks):
+        late, at, length = (3, b - early, blocks - early) if b >= early else (0, b, early)
+        mine_ref, over_y_ref, across_ref = refs[late : late + 3]
+        sources = ((mine_ref, at), (across_ref, at), (over_y_ref, at), (across_ref, length + at))
 
         @pl.when(where_ref[b] >= 0)
         def _():
             for rel in range(QUAD):
-                source, base = sources[rel][b // blocks]
-                top = base + b % blocks * rows
-                home = where_ref[b] * QUAD + (where_ref[blocks + 1] ^ rel)
-                out_ref[pl.ds(pl.multiple_of(home * rows, rows), rows), :] = source[top : top + rows, :]
-
-
-def assemble(where, total, *held):
+                source, at = sources[rel]
+                home = where_ref[b] * QUAD + (where_ref[blocks] ^ rel)
+                out_ref[pl.ds(pl.multiple_of(home * rows, rows), rows), :] = source[at * rows : (at + 1) * rows, :]
+
+
+def assemble(where, total, rows, *held):
     vmem = pl.BlockSpec(memory_space=pltpu.VMEM)
+    out = jax.ShapeDtypeStruct((total, held[0].shape[1]), held[0].dtype)
     return pl.pallas_call(
-        functools.partial(assemble_kernel, where.shape[0] - 2),
-        out_shape=jax.ShapeDtypeStruct((total, held[0].shape[1]), held[0].dtype),
+        functools.partial(assemble_kernel, held[0].shape[0] // rows, where.shape[0] - 1, rows),
+        out_shape=out,
         in_specs=[pl.BlockSpec(memory_space=pltpu.SMEM)] + [vmem] * len(held),
         out_specs=vmem,
         cost_estimate=SMALL,
-        compiler_params=pltpu.CompilerParams(vmem_limit_bytes=40 << 20),
+        compiler_params=pltpu.CompilerParams(vmem_limit_bytes=room(out, *held)),
         name="assemble",
     )(where, *held)
 
@@ -186,44 +184,61 @@
         widely[None], (gate[:, :, None] * repeated[None]).astype(jnp.bfloat16), jnp.zeros((), jnp.bfloat16)
     )
 
+    over_core = swap(weights, 1)
+    over_y = swap(weights, 2)
+
+    middle = (planes + 1) // 2
+    experts = QUAD * owned
     mine = jnp.concatenate([tokens, queries], axis=0)
     up, down = mine, mine
-    arrived = []
-    for s in range(1, planes):
+    first = []
+    for s in range(1, middle):
+        if s > 1:
+            up, down = after(up, wide), after(down, wide)
+        up, down = move(up, [(p, p + 1) for p in range(s - 1, planes - 1)]), move(
+            down, [(p, p - 1) for p in range(1, planes - s + 1)]
+        )
+        first.extend([up, down])
+    across = swap(after(over_y, *first), 1)
+    quad_weights = [weights, over_core, over_y, across]
+    own, *sides = project([tokens] + first, token_count, quad_weights)
+    returned = [move(side, home) for side, home in zip(sides, ways_home)]
+    held = jnp.concatenate([queries] + [block[token_count:] for block in first], axis=0)
+    held_over_y = swap(held, 2)
+
+    rider = jnp.where(plane == middle, down[token_count:], up[token_count:])
+    up, down = after(up, wide), after(down, wide)
+    held_late = []
+    for s in range(middle, planes):
         up_hops = [(p, p + 1) for p in range(s - 1, planes - 1)]
         down_hops = [(p, p - 1) for p in range(1, planes - s + 1)]
-        if s == 2:
-            up, down = after(up, wide), after(down, wide)
         if s == planes - 1:
-            up, down = up[:token_count], down[:token_count]
-        if 2 * s > planes + 1:
+            up = down = up[:token_count]
+        if s == middle:
+            up, down = move(up, up_hops), move(down, down_hops)
+            up = down = up + after(down, held_over_y, *sides)
+        else:
             up = down = move(up, up_hops + down_hops)
-        else:
-            up, down = move(up, up_hops), move(down, down_hops)
-            if 2 * s >= planes:
-                up = down = up + down
-        arrived.extend([up] if 2 * s >= planes else [up, down])
-    last = arrived.pop()
-
-    over_core = swap(weights, 1)
-    over_y = swap(weights, 2)
-    across = swap(after(over_y, arrived[-1]), 1)
-    quad_weights = [weights, over_core, over_y, across]
-
-    experts = QUAD * owned
-    own, *sides = project([tokens] + arrived, token_count, quad_weights, riders=(1, 2))
-    returned = [move(side, home) for side, home in zip(sides, ways_home)]
-    side = project([after(last, *returned)], token_count, quad_weights)[0]
-    late = move(side, ways_home[-1])
+        if s == middle:
+            held_across = swap(jnp.concatenate(after((held, held_over_y), up), axis=0), 1)
+        wait = returned if s == planes - 1 else [held_across]
+        (side,) = project([after(up, *wait)], token_count, quad_weights)
+        if s == middle:
+            side = jnp.concatenate([side, rider], axis=1)
+        returned.append(move(side, ways_home[len(returned)]))
+        if s == middle:
+            rider = returned[-1][:, own.shape[1] :]
+        if s < planes - 1:
+            held_late.append(up[token_count:])
+    late = returned.pop()
     early = combine([own] + returned, wide[:-experts])
 
-    held = jnp.concatenate([after(queries, arrived[0])] + [block[token_count:] for block in arrived], axis=0)
-    held_late = jnp.where(plane == 0, returned[0][:, own.shape[1] :], returned[1][:, own.shape[1] :])
-    over_y = swap(held, 2)
+    held_late = after(jnp.concatenate(held_late + [rider], axis=0), side)
     late_over_y = swap(held_late, 2)
-    across = swap(jnp.concatenate(after((held, over_y, held_late, late_over_y), side), axis=0), 1)
+    late_across = swap(after(jnp.concatenate([held_late, late_over_y], axis=0), late), 1)
+    spread = (held, held_over_y, held_across, held_late, late_over_y, late_across)
     where = jnp.stack(origins + [spot]).astype(jnp.int32)
-    all_queries = assemble(where, n * queries.shape[0], held, held_late, over_y, late_over_y, across)
+    all_queries = assemble(where, n * queries.shape[0], queries.shape[0], *spread)
     sketches = combine([late], wide[-experts:], early, counts)
     sketches = sketches.reshape(EX_DEV, RANK * RANK)
     scores = lax.dot_general(sketches.astype(jnp.bfloat16), all_queries, NT, preferred_element_type=jnp.float32)

time: 92.3 us -> 95.3 us (1.033)
  Pallas kernels: 7.59 us -> 12.3 us
  starting transfers between devices: 33.5 us -> 29.5 us
  other arithmetic: 4.07 us -> 5.81 us
  waiting for transfers between devices: 31.7 us -> 33 us
    ppermute x6 -> x7, waiting for transfers between devices: 0.78 us -> 12.6 us  [swap(): return lax.ppermute(array, 'expert', [(i, i ^ bit) for i in range(n)])]
    ppermute x9, waiting for transfers between devices: 30.9 us -> 20.4 us  [move(): return lax.ppermute(array, 'expert', pairs)]
    pallas_call x2 -> x3, Pallas kernels: 5.02 us -> 10 us  [project(): pl.pallas_call(functools.partial(project_kernel, len(parts), rows), out_s...]
    ppermute x9, starting transfers between devices: 28.3 us -> 24.7 us  [move(): return lax.ppermute(array, 'expert', pairs)]
    slice x4 -> x3, local copies, waits for them, and re-layouts: 1.88 us -> 0.06 us  [the longest x1 0.04 us: shards(): up = down = up[:token_count]]
    select_n x1, other arithmetic: 0.02 us -> 1 us  [shards(): rider = jnp.where(plane == middle, down[token_count:], up[token_count:])]
    ppermute x6 -> x7, starting transfers between devices: 5.27 us -> 4.83 us  [swap(): return lax.ppermute(array, 'expert', [(i, i ^ bit) for i in range(n)])]
    unnamed x37 -> x35, local copies, waits for them, and re-layouts: 5.26 us -> 5.58 us
  transfers between devices with their start and end apart: 15 -> 16, of which waited for: 7 -> 7; matrix products, arithmetic and copies ran while one was open for 10% -> 11% of each run, Pallas kernels for 3% -> 9%
where the time goes in v6:
time: 95.3 us; the launch traced here: 94.6 us
  waiting for transfers between devices  33 us (35%)
  starting transfers between devices  29.5 us (31%)
  Pallas kernels  12.3 us (13%)
  local copies, waits for them, and re-layouts  10.3 us (11%)
  other arithmetic  5.81 us (6%)
  matrix products  2.58 us (3%)
  between operations  1.1 us (1%)
    ppermute x9, starting transfers between devices, move(): return lax.ppermute(array, 'expert', pairs)  24.7 us
    ppermute x9, waiting for transfers between devices, move(): return lax.ppermute(array, 'expert', pairs)  20.4 us
    ppermute x7, waiting for transfers between devices, swap(): return lax.ppermute(array, 'expert', [(i, i ^ bit) for i in range(n)])  12.6 us
    pallas_call x3, Pallas kernels, project(): pl.pallas_call(functools.partial(project_kernel, len(parts), rows), out_s...  10 us
    unnamed x35, local copies, waits for them, and re-layouts  5.58 us
    ppermute x7, starting transfers between devices, swap(): return lax.ppermute(array, 'expert', [(i, i ^ bit) for i in range(n)])  4.83 us
  transfers between devices with their start and end apart: 16, of which 7 were waited for; matrix products, arithmetic and copies ran while one was open for 11% of the time, Pallas kernels for 9%

profile of v6, /device:TPU:0, one launch (start us, length us, event | category | flops | bytes accessed | tf_op | source)
XLA Modules:
  0.0 94.6 jit_solution(3238066370687574684)
XLA Ops:
  0.7 1.9 %constant_dynamic-update-slice_fusion.1 = bf16[80,4096]{1,0:T(8,128)(2,1)} fusion(bf16[64,4096]{1,0:T(8,128)(2,1)} %refs_0_.1), kind=kLoop, calls=%fused_computation.15 | loop fusion | bytes 1048576
  2.6 1.6 %constant_dynamic-update-slice_fusion = bf16[80,4096]{1,0:T(8,128)(2,1)} fusion(bf16[80,4096]{1,0:T(8,128)(2,1)} %constant_dynamic-update-slice_fusion.1, bf16[16,4096]{1,0:T(8,128)(2,1)} %param.15), kind=kLoop, calls=%fused_computation.14 | loop fusion | bytes 262144 | tf_op jit(solution)/shard_map/concatenate | solution.py:192
  4.1 5.8 %collective-permute-start = (bf16[80,4096]{1,0:T(8,128)(2,1)}, bf16[80,4096]{1,0:T(8,128)(2,1)}, u32[]{:S(2)}, u32[]{:S(2)}) collective-permute-start(bf16[80,4096]{1,0:T(8,128)(2,1)} %constant_dynamic-update-slice_fusion), channel_id=1, source_target_pairs={{0,4},{1,5},{2,6},{3,7},{4,8},{5,9},{6,10},{7,11},{8,12},{9,13},{1... | collective-permute-start | bytes 1966088 | tf_op jit(solution)/shard_map/ppermute | solution.py:143
  9.9 1.3 %collective-permute-start.2 = (bf16[80,4096]{1,0:T(8,128)(2,1)}, bf16[80,4096]{1,0:T(8,128)(2,1)}, u32[]{:S(2)}, u32[]{:S(2)}) collective-permute-start(bf16[80,4096]{1,0:T(8,128)(2,1)} %constant_dynamic-update-slice_fusion), channel_id=1, source_target_pairs={{4,0},{5,1},{6,2},{7,3},{8,4},{9,5},{10,6},{11,7},{12,8},{13,9},{1... | collective-permute-start | bytes 1966088 | tf_op jit(solution)/shard_map/ppermute | solution.py:143
  11.2 1.6 %collective-permute-start.6 = (bf16[128,4096]{1,0:T(8,128)(2,1)}, bf16[128,4096]{1,0:T(8,128)(2,1)S(1)}, u32[]{:S(2)}, u32[]{:S(2)}) collective-permute-start(bf16[128,4096]{1,0:T(8,128)(2,1)} %bitcast.19), channel_id=1, source_target_pairs={{0,2},{1,3},{2,0},{3,1},{4,6},{5,7},{6,4},{7,5},{8,10},{9,11},{10,... | collective-permute-start | bytes 3145736 | tf_op jit(solution)/shard_map/ppermute | solution.py:146
  13.2 0.9 iota_compare_fusion
  14.1 0.1 broadcast_in_dim.56
  14.2 0.1 broadcast_in_dim.57
  14.4 1.3 %fusion.3 = f32[64,64]{1,0:T(8,128)S(1)} fusion(bf16[64,4096]{1,0:T(8,128)(2,1)S(1)} %copy-done, bf16[4096,64]{0,1:T(8,128)(2,1)} %param.14), kind=kOutput, calls=%fused_computation.21 | convolution fusion | flops 33554432 | bytes 1064960 | tf_op jit(solution)/shard_map/dot_general | solution.py:169
  15.7 0.1 pad_maximum_fusion.5
  15.8 0.1 select_reduce_fusion
  15.9 1.5 %fusion = bf16[40,64,256]{2,1,0:T(8,128)(2,1)} fusion(f32[64,256]{1,0:T(8,128)S(1)} %pad_maximum_fusion.5, f32[40,64]{1,0:T(8,128)S(1)} %select_reduce_fusion, pred[64,256]{1,0:T(8,128)(4,1)S(1)} %broadcast_in_dim.57), kind=kLoop, calls=%fused_computation.1 | loop fusion | flops 1966080 | bytes 1402880 | tf_op jit(solution)/shard_map/jit(_where)/select_n | solution.py:183
  17.4 10.9 %collective-permute-done.2.refs_2_ = bf16[80,4096]{1,0:T(8,128)(2,1)} collective-permute-done((bf16[80,4096]{1,0:T(8,128)(2,1)}, bf16[80,4096]{1,0:T(8,128)(2,1)}, u32[]{:S(2)}, u32[]{:S(2)}) %collective-permute-start.2) | collective-permute-done | bytes 655392 | tf_op jit(solution)/shard_map/ppermute | solution.py:143
  28.3 1.3 %collective-permute-start.3 = (bf16[80,4096]{1,0:T(8,128)(2,1)}, bf16[80,4096]{1,0:T(8,128)(2,1)S(1)}, u32[]{:S(2)}, u32[]{:S(2)}) collective-permute-start(bf16[80,4096]{1,0:T(8,128)(2,1)} %collective-permute-done.2.refs_2_), channel_id=1, source_target_pairs={{4,0},{5,1},{6,2},{7,3},{8,4},{9,5},{10,6},{11,7},{20,16},{21,17},... | collective-permute-start | bytes 1966088 | tf_op jit(solution)/shard_map/ppermute | solution.py:143
  29.6 0.7 collective-permute-start.1
  30.3 5.8 %collective-permute-done.6.refs_5_.refs_3_ = bf16[128,4096]{1,0:T(8,128)(2,1)S(1)} collective-permute-done((bf16[128,4096]{1,0:T(8,128)(2,1)}, bf16[128,4096]{1,0:T(8,128)(2,1)S(1)}, u32[]{:S(2)}, u32[]{:S(2)}) %collective-permute-start.6) | collective-permute-done | bytes 1048608 | tf_op jit(solution)/shard_map/ppermute | solution.py:146
  36.1 1.0 %broadcast_select_fusion = (bf16[16,4096]{1,0:T(8,128)(2,1)S(1)}, bf16[16,4096]{1,0:T(8,128)(2,1)S(1)}, bf16[16,4096]{1,0:T(8,128)(2,1)S(1)}) fusion(pred[]{:T(512)S(6)} %eq.56, bf16[80,4096]{1,0:T(8,128)(2,1)} %collective-permute-done.2.refs_2_, bf16[80,4096]{1,0:T(8,128)(2,1)} %collective-permute-done.refs_1_), kind=kLoop, calls=%fused_computation.8 | loop fusion | flops 65536 | bytes 655361 | tf_op jit(solution)/shard_map/jit(_where)/select_n | solution.py:209
  37.1 0.9 pad_maximum_fusion.2.refs_0_
  38.0 1.6 %collective-permute-start.4 = (bf16[48,4096]{1,0:T(8,128)(2,1)S(1)}, bf16[48,4096]{1,0:T(8,128)(2,1)S(1)}, u32[]{:S(2)}, u32[]{:S(2)}) collective-permute-start(bf16[48,4096]{1,0:T(8,128)(2,1)S(1)} %pad_maximum_fusion.2.refs_0_), channel_id=1, source_target_pairs={{0,2},{1,3},{2,0},{3,1},{4,6},{5,7},{6,4},{7,5},{8,10},{9,11},{10,... | collective-permute-start | bytes 1179656 | tf_op jit(solution)/shard_map/ppermute | solution.py:146
  39.6 3.7 %project.3 = (bf16[16,2048]{1,0:T(8,128)(2,1)S(1)}, bf16[16,2048]{1,0:T(8,128)(2,1)S(1)}, bf16[16,2048]{1,0:T(8,128)(2,1)S(1)}) custom-call(bf16[64,4096]{1,0:T(8,128)(2,1)S(1)} %copy-done.2, bf16[80,4096]{1,0:T(8,128)(2,1)} %collective-permute-done.refs_1_, bf16[80,4096]{1,0:T(8,128)(2,1)} %collective-permute-done.2.refs_2_, ...), custom_call_target="tpu_custom_call" | custom-call | flops 1024 | bytes 1024 | tf_op jit(solution)/shard_map/project/pallas_call | solution.py:88
  43.3 6.3 %collective-permute-done.4.refs_1_ = bf16[48,4096]{1,0:T(8,128)(2,1)S(1)} collective-permute-done((bf16[48,4096]{1,0:T(8,128)(2,1)S(1)}, bf16[48,4096]{1,0:T(8,128)(2,1)S(1)}, u32[]{:S(2)}, u32[]{:S(2)}) %collective-permute-start.4) | collective-permute-done | bytes 393248 | tf_op jit(solution)/shard_map/ppermute | solution.py:146
  49.6 0.2 add.69.refs_0_
  50.0 0.4 copy-done.3
  50.4 1.3 %collective-permute-start.8 = (bf16[64,4096]{1,0:T(8,128)(2,1)S(1)}, bf16[64,4096]{1,0:T(8,128)(2,1)S(1)}, u32[]{:S(2)}, u32[]{:S(2)}) collective-permute-start(bf16[64,4096]{1,0:T(8,128)(2,1)S(1)} %slice.32), channel_id=1, source_target_pairs={{8,12},{9,13},{10,14},{11,15},{4,0},{5,1},{6,2},{7,3},{24,28},{25,... | collective-permute-start | bytes 1572872 | tf_op jit(solution)/shard_map/ppermute | solution.py:143
  51.7 0.6 collective-permute-done.11.refs_2_
  52.2 3.3 %project.4 = bf16[16,2048]{1,0:T(8,128)(2,1)S(1)} custom-call(bf16[80,4096]{1,0:T(8,128)(2,1)S(1)} %add.69.refs_0_, bf16[128,4096]{1,0:T(8,128)(2,1)S(1)} %bitcast.22, bf16[128,4096]{1,0:T(8,128)(2,1)} %collective-permute-done.5.refs_4_.refs_2_, bf16[128,4096]{1,0:T(8,128)(2,1)S(1)} %collective-permute-done.6.refs_5_.refs_3_, ...), custom_call_target="tpu_custom_call" | custom-call | flops 1024 | bytes 1024 | tf_op jit(solution)/shard_map/project/pallas_call | solution.py:88
  55.5 5.1 %collective-permute-start.12 = (bf16[16,6144]{1,0:T(8,128)(2,1)S(1)}, bf16[16,6144]{1,0:T(8,128)(2,1)S(1)}, u32[]{:S(2)}, u32[]{:S(2)}) collective-permute-start(bf16[16,6144]{1,0:T(8,128)(2,1)S(1)} %pad_maximum_fusion.4), channel_id=1, source_target_pairs={{8,0},{9,1},{10,2},{11,3},{12,4},{13,5},{14,6},{15,7},{0,8},{1,9},... | collective-permute-start | bytes 589832 | tf_op jit(solution)/shard_map/ppermute | solution.py:143
  60.6 1.8 %collective-permute-start.10 = (bf16[16,2048]{1,0:T(8,128)(2,1)S(1)}, bf16[16,2048]{1,0:T(8,128)(2,1)S(1)}, u32[]{:S(2)}, u32[]{:S(2)}) collective-permute-start(bf16[16,2048]{1,0:T(8,128)(2,1)S(1)} %get-tuple-element.19), channel_id=1, source_target_pairs={{0,4},{1,5},{2,6},{3,7},{4,8},{5,9},{6,10},{7,11},{8,12},{9,13},{1... | collective-permute-start | bytes 196616 | tf_op jit(solution)/shard_map/ppermute | solution.py:143
  62.4 1.3 %collective-permute-start.9 = (bf16[16,2048]{1,0:T(8,128)(2,1)S(1)}, bf16[16,2048]{1,0:T(8,128)(2,1)S(1)}, u32[]{:S(2)}, u32[]{:S(2)}) collective-permute-start(bf16[16,2048]{1,0:T(8,128)(2,1)S(1)} %get-tuple-element.18), channel_id=1, source_target_pairs={{4,0},{5,1},{6,2},{7,3},{8,4},{9,5},{10,6},{11,7},{12,8},{13,9},{1... | collective-permute-start | bytes 196616 | tf_op jit(solution)/shard_map/ppermute | solution.py:143
  63.7 2.5 %collective-permute-done.10.refs_2_ = bf16[16,2048]{1,0:T(8,128)(2,1)S(1)} collective-permute-done((bf16[16,2048]{1,0:T(8,128)(2,1)S(1)}, bf16[16,2048]{1,0:T(8,128)(2,1)S(1)}, u32[]{:S(2)}, u32[]{:S(2)}) %collective-permute-start.10) | collective-permute-done | bytes 65568 | tf_op jit(solution)/shard_map/ppermute | solution.py:143
  66.3 5.6 %collective-permute-done.9.refs_1_ = bf16[16,2048]{1,0:T(8,128)(2,1)S(1)} collective-permute-done((bf16[16,2048]{1,0:T(8,128)(2,1)S(1)}, bf16[16,2048]{1,0:T(8,128)(2,1)S(1)}, u32[]{:S(2)}, u32[]{:S(2)}) %collective-permute-start.9) | collective-permute-done | bytes 65568 | tf_op jit(solution)/shard_map/ppermute | solution.py:143
  71.8 0.6 copy-done.9
  72.5 3.0 %project.5 = bf16[16,2048]{1,0:T(8,128)(2,1)S(1)} custom-call(bf16[64,4096]{1,0:T(8,128)(2,1)S(1)} %collective-permute-done.8.refs_0_, bf16[128,4096]{1,0:T(8,128)(2,1)S(1)} %bitcast.23, bf16[128,4096]{1,0:T(8,128)(2,1)} %collective-permute-done.5.refs_4_.refs_2_, bf16[128,4096]{1,0:T(8,128)(2,1)S(1)} %collective-permute-done.6.refs_5_.refs_3_, ...), custom_call_target="tpu_custom_call" | custom-call | flops 1024 | bytes 1024 | tf_op jit(solution)/shard_map/project/pallas_call | solution.py:88
  75.5 1.6 %collective-permute-start.14 = (bf16[32,4096]{1,0:T(8,128)(2,1)S(1)}, bf16[32,4096]{1,0:T(8,128)(2,1)S(1)}, u32[]{:S(2)}, u32[]{:S(2)}) collective-permute-start(bf16[32,4096]{1,0:T(8,128)(2,1)S(1)} %pad_maximum_fusion.3.refs_3_), channel_id=1, source_target_pairs={{0,2},{1,3},{2,0},{3,1},{4,6},{5,7},{6,4},{7,5},{8,10},{9,11},{10,... | collective-permute-start | bytes 786440 | tf_op jit(solution)/shard_map/ppermute | solution.py:146
  77.1 6.3 %collective-permute-start.13 = (bf16[16,2048]{1,0:T(8,128)(2,1)S(1)}, bf16[16,2048]{1,0:T(8,128)(2,1)S(1)}, u32[]{:S(2)}, u32[]{:S(2)}) collective-permute-start(bf16[16,2048]{1,0:T(8,128)(2,1)S(1)} %project.5), channel_id=1, source_target_pairs={{12,0},{13,1},{14,2},{15,3},{0,12},{1,13},{2,14},{3,15},{28,16},{2... | collective-permute-start | bytes 196616 | tf_op jit(solution)/shard_map/ppermute | solution.py:143
  83.4 0.8 pad_maximum_fusion.1
  84.2 1.4 %collective-permute-done.13.refs_0_ = bf16[16,2048]{1,0:T(8,128)(2,1)S(1)} collective-permute-done((bf16[16,2048]{1,0:T(8,128)(2,1)S(1)}, bf16[16,2048]{1,0:T(8,128)(2,1)S(1)}, u32[]{:S(2)}, u32[]{:S(2)}) %collective-permute-start.13) | collective-permute-done | bytes 65568 | tf_op jit(solution)/shard_map/ppermute | solution.py:143
  85.6 0.6 copy-done.11
  86.3 1.3 %slice.34.refs_4_ = bf16[32,64,256]{2,1,0:T(8,128)(2,1)S(1)} slice(bf16[40,64,256]{2,1,0:T(8,128)(2,1)} %fusion), slice={[0:32], [0:64], [0:256]} | slice | bytes 2097152 | tf_op jit(solution)/shard_map/slice | solution.py:234
  87.6 1.0 %slice.33.refs_1_ = bf16[8,64,256]{2,1,0:T(8,128)(2,1)S(1)} slice(bf16[40,64,256]{2,1,0:T(8,128)(2,1)} %fusion), slice={[32:40], [0:64], [0:256]} | slice | bytes 524288 | tf_op jit(solution)/shard_map/slice | solution.py:242
  88.7 0.1 convert_reduce_fusion
  88.8 0.7 combine.2.refs_2_
  89.6 0.8 copy-done.12
  90.4 0.4 combine.3
  90.8 0.1 reshape.145
  90.9 1.1 %copy-done.6 = bf16[96,4096]{1,0:T(8,128)(2,1)S(1)} copy-done((bf16[96,4096]{1,0:T(8,128)(2,1)S(1)}, bf16[96,4096]{1,0:T(8,128)(2,1)}, u32[]{:S(2)}) %copy-start.6) | copy-done | bytes 786456
  92.1 1.2 %assemble.1 = bf16[256,4096]{1,0:T(8,128)(2,1)S(1)} custom-call(s32[6]{0:T(128)S(1)} %stack.48.where_ref, bf16[48,4096]{1,0:T(8,128)(2,1)S(1)} %pad_maximum_fusion.2.refs_0_, bf16[48,4096]{1,0:T(8,128)(2,1)S(1)} %copy-done.4, bf16[96,4096]{1,0:T(8,128)(2,1)S(1)} %copy-done.6, bf16[32,4096]{1,0:T(8,128)(2,1)S(1)} %pad_maximum_fusion.3.refs_3_, ...), custom_call_target="tpu_custom_call" | custom-call | flops 1024 | bytes 1024 | tf_op jit(solution)/shard_map/assemble/pallas_call | solution.py:118
  93.3 1.3 %fusion.1 = f32[4,256]{1,0:T(4,128)} fusion(bf16[256,4096]{1,0:T(8,128)(2,1)S(1)} %assemble.1, f32[4,4096]{1,0:T(4,128)S(1)} %reshape.145), kind=kOutput, calls=%fused_computation.10 | convolution fusion | flops 8404992 | bytes 2166784 | tf_op jit(solution)/shard_map/dot_general | solution.py:244
  (58 shorter events, 0.9 us)
Async XLA Ops:
  0.6 13.7 %copy-start = (bf16[64,4096]{1,0:T(8,128)(2,1)S(1)}, bf16[64,4096]{1,0:T(8,128)(2,1)}, u32[]{:S(2)}) copy-start(bf16[64,4096]{1,0:T(8,128)(2,1)} %param.9) | copy-start | bytes 1572868
  0.6 15.2 %copy-start.15 = (s32[64,8]{0,1:T(8,128)S(1)}, s32[64,8]{0,1:T(8,128)}, u32[]{:S(2)}) copy-start(s32[64,8]{0,1:T(8,128)} %param.10) | copy-start | bytes 6148
  0.7 15.2 %copy-start.14 = (f32[64,8]{0,1:T(8,128)S(1)}, f32[64,8]{0,1:T(8,128)}, u32[]{:S(2)}) copy-start(f32[64,8]{0,1:T(8,128)} %param.11) | copy-start | bytes 6148
  4.1 25.4 %collective-permute-start = (bf16[80,4096]{1,0:T(8,128)(2,1)}, bf16[80,4096]{1,0:T(8,128)(2,1)}, u32[]{:S(2)}, u32[]{:S(2)}) collective-permute-start(bf16[80,4096]{1,0:T(8,128)(2,1)} %constant_dynamic-update-slice_fusion), channel_id=1, source_target_pairs={{0,4},{1,5},{2,6},{3,7},{4,8},{5,9},{6,10},{7,11},{8,12},{9,13},{1... | collective-permute-start | bytes 1966088 | tf_op jit(solution)/shard_map/ppermute | solution.py:143
  9.9 18.4 %collective-permute-start.2 = (bf16[80,4096]{1,0:T(8,128)(2,1)}, bf16[80,4096]{1,0:T(8,128)(2,1)}, u32[]{:S(2)}, u32[]{:S(2)}) collective-permute-start(bf16[80,4096]{1,0:T(8,128)(2,1)} %constant_dynamic-update-slice_fusion), channel_id=1, source_target_pairs={{4,0},{5,1},{6,2},{7,3},{8,4},{9,5},{10,6},{11,7},{12,8},{13,9},{1... | collective-permute-start | bytes 1966088 | tf_op jit(solution)/shard_map/ppermute | solution.py:143
  11.2 24.9 %collective-permute-start.6 = (bf16[128,4096]{1,0:T(8,128)(2,1)}, bf16[128,4096]{1,0:T(8,128)(2,1)S(1)}, u32[]{:S(2)}, u32[]{:S(2)}) collective-permute-start(bf16[128,4096]{1,0:T(8,128)(2,1)} %bitcast.19), channel_id=1, source_target_pairs={{0,2},{1,3},{2,0},{3,1},{4,6},{5,7},{6,4},{7,5},{8,10},{9,11},{10,... | collective-permute-start | bytes 3145736 | tf_op jit(solution)/shard_map/ppermute | solution.py:146
  12.8 26.8 %collective-permute-start.5 = (bf16[128,4096]{1,0:T(8,128)(2,1)}, bf16[128,4096]{1,0:T(8,128)(2,1)}, u32[]{:S(2)}, u32[]{:S(2)}) collective-permute-start(bf16[128,4096]{1,0:T(8,128)(2,1)} %bitcast.20), channel_id=1, source_target_pairs={{0,1},{1,0},{2,3},{3,2},{4,5},{5,4},{6,7},{7,6},{8,9},{9,8},{10,11... | collective-permute-start | bytes 3145736 | tf_op jit(solution)/shard_map/ppermute | solution.py:146
  12.9 26.7 %copy-start.1 = (bf16[2,4096,64]{1,2,0:T(8,128)(2,1)S(1)}, bf16[2,4096,64]{1,2,0:T(8,128)(2,1)}, u32[]{:S(2)}) copy-start(bf16[2,4096,64]{1,2,0:T(8,128)(2,1)} %param.13) | copy-start | bytes 3145732
  12.9 26.7 %copy-start.2 = (bf16[64,4096]{1,0:T(8,128)(2,1)S(1)}, bf16[64,4096]{1,0:T(8,128)(2,1)}, u32[]{:S(2)}) copy-start(bf16[64,4096]{1,0:T(8,128)(2,1)} %refs_0_.1) | copy-start | bytes 1572868
  28.3 21.3 %collective-permute-start.3 = (bf16[80,4096]{1,0:T(8,128)(2,1)}, bf16[80,4096]{1,0:T(8,128)(2,1)S(1)}, u32[]{:S(2)}, u32[]{:S(2)}) collective-permute-start(bf16[80,4096]{1,0:T(8,128)(2,1)} %collective-permute-done.2.refs_2_), channel_id=1, source_target_pairs={{4,0},{5,1},{6,2},{7,3},{8,4},{9,5},{10,6},{11,7},{20,16},{21,17},... | collective-permute-start | bytes 1966088 | tf_op jit(solution)/shard_map/ppermute | solution.py:143
  29.6 20.0 %collective-permute-start.1 = (bf16[80,4096]{1,0:T(8,128)(2,1)}, bf16[80,4096]{1,0:T(8,128)(2,1)S(1)}, u32[]{:S(2)}, u32[]{:S(2)}) collective-permute-start(bf16[80,4096]{1,0:T(8,128)(2,1)} %collective-permute-done.refs_1_), channel_id=1, source_target_pairs={{4,8},{5,9},{6,10},{7,11},{8,12},{9,13},{10,14},{11,15},{20,24},{2... | collective-permute-start | bytes 1966088 | tf_op jit(solution)/shard_map/ppermute | solution.py:143
  36.1 3.5 %collective-permute-start.7 = (bf16[128,4096]{1,0:T(8,128)(2,1)S(1)}, bf16[128,4096]{1,0:T(8,128)(2,1)S(1)}, u32[]{:S(2)}, u32[]{:S(2)}) collective-permute-start(bf16[128,4096]{1,0:T(8,128)(2,1)S(1)} %collective-permute-done.6.refs_5_.refs_3_), channel_id=1, source_target_pairs={{0,1},{1,0},{2,3},{3,2},{4,5},{5,4},{6,7},{7,6},{8,9},{9,8},{10,11... | collective-permute-start | bytes 3145736 | tf_op jit(solution)/shard_map/ppermute | solution.py:146
  38.0 11.6 %collective-permute-start.4 = (bf16[48,4096]{1,0:T(8,128)(2,1)S(1)}, bf16[48,4096]{1,0:T(8,128)(2,1)S(1)}, u32[]{:S(2)}, u32[]{:S(2)}) collective-permute-start(bf16[48,4096]{1,0:T(8,128)(2,1)S(1)} %pad_maximum_fusion.2.refs_0_), channel_id=1, source_target_pairs={{0,2},{1,3},{2,0},{3,1},{4,6},{5,7},{6,4},{7,5},{8,10},{9,11},{10,... | collective-permute-start | bytes 1179656 | tf_op jit(solution)/shard_map/ppermute | solution.py:146
  43.3 6.7 %copy-start.7 = (bf16[16,2048]{1,0:T(8,128)(2,1)}, bf16[16,2048]{1,0:T(8,128)(2,1)S(1)}, u32[]{:S(2)}) copy-start(bf16[16,2048]{1,0:T(8,128)(2,1)S(1)} %get-tuple-element.25.refs_0_) | copy-start | bytes 196612
  49.6 0.7 copy-start.3
  49.9 2.4 %collective-permute-start.11 = (bf16[96,4096]{1,0:T(8,128)(2,1)S(1)}, bf16[96,4096]{1,0:T(8,128)(2,1)S(1)}, u32[]{:S(2)}, u32[]{:S(2)}) collective-permute-start(bf16[96,4096]{1,0:T(8,128)(2,1)S(1)} %pad_maximum_fusion), channel_id=1, source_target_pairs={{0,1},{1,0},{2,3},{3,2},{4,5},{5,4},{6,7},{7,6},{8,9},{9,8},{10,11... | collective-permute-start | bytes 2359304 | tf_op jit(solution)/shard_map/ppermute | solution.py:146
  50.4 22.1 %collective-permute-start.8 = (bf16[64,4096]{1,0:T(8,128)(2,1)S(1)}, bf16[64,4096]{1,0:T(8,128)(2,1)S(1)}, u32[]{:S(2)}, u32[]{:S(2)}) collective-permute-start(bf16[64,4096]{1,0:T(8,128)(2,1)S(1)} %slice.32), channel_id=1, source_target_pairs={{8,12},{9,13},{10,14},{11,15},{4,0},{5,1},{6,2},{7,3},{24,28},{25,... | collective-permute-start | bytes 1572872 | tf_op jit(solution)/shard_map/ppermute | solution.py:143
  52.2 3.3 %copy-start.5 = (bf16[96,4096]{1,0:T(8,128)(2,1)}, bf16[96,4096]{1,0:T(8,128)(2,1)S(1)}, u32[]{:S(2)}) copy-start(bf16[96,4096]{1,0:T(8,128)(2,1)S(1)} %collective-permute-done.11.refs_2_) | copy-start | bytes 2359300
  55.5 16.9 %collective-permute-start.12 = (bf16[16,6144]{1,0:T(8,128)(2,1)S(1)}, bf16[16,6144]{1,0:T(8,128)(2,1)S(1)}, u32[]{:S(2)}, u32[]{:S(2)}) collective-permute-start(bf16[16,6144]{1,0:T(8,128)(2,1)S(1)} %pad_maximum_fusion.4), channel_id=1, source_target_pairs={{8,0},{9,1},{10,2},{11,3},{12,4},{13,5},{14,6},{15,7},{0,8},{1,9},... | collective-permute-start | bytes 589832 | tf_op jit(solution)/shard_map/ppermute | solution.py:143
  60.6 5.6 %collective-permute-start.10 = (bf16[16,2048]{1,0:T(8,128)(2,1)S(1)}, bf16[16,2048]{1,0:T(8,128)(2,1)S(1)}, u32[]{:S(2)}, u32[]{:S(2)}) collective-permute-start(bf16[16,2048]{1,0:T(8,128)(2,1)S(1)} %get-tuple-element.19), channel_id=1, source_target_pairs={{0,4},{1,5},{2,6},{3,7},{4,8},{5,9},{6,10},{7,11},{8,12},{9,13},{1... | collective-permute-start | bytes 196616 | tf_op jit(solution)/shard_map/ppermute | solution.py:143
  62.4 9.4 %collective-permute-start.9 = (bf16[16,2048]{1,0:T(8,128)(2,1)S(1)}, bf16[16,2048]{1,0:T(8,128)(2,1)S(1)}, u32[]{:S(2)}, u32[]{:S(2)}) collective-permute-start(bf16[16,2048]{1,0:T(8,128)(2,1)S(1)} %get-tuple-element.18), channel_id=1, source_target_pairs={{4,0},{5,1},{6,2},{7,3},{8,4},{9,5},{10,6},{11,7},{12,8},{13,9},{1... | collective-permute-start | bytes 196616 | tf_op jit(solution)/shard_map/ppermute | solution.py:143
  71.8 0.6 copy-start.9
  75.5 13.2 %copy-start.16 = (s32[1,64]{1,0:T(1,128)S(1)}, s32[1,64]{1,0:T(1,128)}, u32[]{:S(2)}) copy-start(s32[1,64]{1,0:T(1,128)} %param.12) | copy-start | bytes 772
  75.5 13.3 %copy-start.8 = (bf16[16,2048]{1,0:T(8,128)(2,1)S(1)}, bf16[16,2048]{1,0:T(8,128)(2,1)}, u32[]{:S(2)}) copy-start(bf16[16,2048]{1,0:T(8,128)(2,1)} %copy-done.7) | copy-start | bytes 196612
  75.5 13.3 %copy-start.10 = (bf16[16,2048]{1,0:T(8,128)(2,1)S(1)}, bf16[16,2048]{1,0:T(8,128)(2,1)}, u32[]{:S(2)}) copy-start(bf16[16,2048]{1,0:T(8,128)(2,1)} %copy-done.9) | copy-start | bytes 196612
  75.5 7.8 %collective-permute-start.14 = (bf16[32,4096]{1,0:T(8,128)(2,1)S(1)}, bf16[32,4096]{1,0:T(8,128)(2,1)S(1)}, u32[]{:S(2)}, u32[]{:S(2)}) collective-permute-start(bf16[32,4096]{1,0:T(8,128)(2,1)S(1)} %pad_maximum_fusion.3.refs_3_), channel_id=1, source_target_pairs={{0,2},{1,3},{2,0},{3,1},{4,6},{5,7},{6,4},{7,5},{8,10},{9,11},{10,... | collective-permute-start | bytes 786440 | tf_op jit(solution)/shard_map/ppermute | solution.py:146
  77.1 8.5 %collective-permute-start.13 = (bf16[16,2048]{1,0:T(8,128)(2,1)S(1)}, bf16[16,2048]{1,0:T(8,128)(2,1)S(1)}, u32[]{:S(2)}, u32[]{:S(2)}) collective-permute-start(bf16[16,2048]{1,0:T(8,128)(2,1)S(1)} %project.5), channel_id=1, source_target_pairs={{12,0},{13,1},{14,2},{15,3},{0,12},{1,13},{2,14},{3,15},{28,16},{2... | collective-permute-start | bytes 196616 | tf_op jit(solution)/shard_map/ppermute | solution.py:143
  85.6 0.6 copy-start.11
  86.2 4.7 %collective-permute-start.15 = (bf16[64,4096]{1,0:T(8,128)(2,1)}, bf16[64,4096]{1,0:T(8,128)(2,1)}, u32[]{:S(2)}, u32[]{:S(2)}) collective-permute-start(bf16[64,4096]{1,0:T(8,128)(2,1)} %pad_maximum_fusion.1), channel_id=1, source_target_pairs={{0,1},{1,0},{2,3},{3,2},{4,5},{5,4},{6,7},{7,6},{8,9},{9,8},{10,11... | collective-permute-start | bytes 1572872 | tf_op jit(solution)/shard_map/ppermute | solution.py:146
  86.3 4.7 %copy-start.4 = (bf16[48,4096]{1,0:T(8,128)(2,1)S(1)}, bf16[48,4096]{1,0:T(8,128)(2,1)}, u32[]{:S(2)}) copy-start(bf16[48,4096]{1,0:T(8,128)(2,1)} %copy-done.3) | copy-start | bytes 1179652
  89.6 0.8 copy-start.12
  90.9 2.4 %copy-start.13 = (f32[4,4096]{1,0:T(4,128)}, f32[4,4096]{1,0:T(4,128)S(1)}, u32[]{:S(2)}) copy-start(f32[4,4096]{1,0:T(4,128)S(1)} %reshape.145) | copy-start | bytes 196612
  90.9 1.1 %copy-start.6 = (bf16[96,4096]{1,0:T(8,128)(2,1)S(1)}, bf16[96,4096]{1,0:T(8,128)(2,1)}, u32[]{:S(2)}) copy-start(bf16[96,4096]{1,0:T(8,128)(2,1)} %copy-done.5) | copy-start | bytes 2359300

commit v7 on v4

--- a/solution.py
+++ b/solution.py
@@ -1,4 +1,5 @@
 import functools
+import math
 
 import jax
 import jax.numpy as jnp
@@ -10,21 +11,29 @@
 RANK = 64
 EX_DEV = 4
 QUAD = 4
+SLAB = 16
 
 SMALL = pl.CostEstimate(flops=1024, bytes_accessed=1024, transcendentals=0)
 
 NT = (((1,), (1,)), ((), ()))
 TN = (((0,), (0,)), ((), ()))
+
+
+def room(*arrays):
+    return sum(math.prod(a.shape) * jnp.dtype(a.dtype).itemsize for a in arrays) + (6 << 20)
 
 
 def combine_kernel(blocks, experts, first, last, *refs):
     sides, wide = refs[:blocks], refs[blocks]
     total = jnp.zeros((RANK, EX_DEV * RANK), jnp.float32) if first else refs[blocks + 1][...]
     out = refs[-1]
+    span = experts * RANK
     for b in range(blocks):
+        slabs = [sides[b][:, g * span : (g + 1) * span] for g in range(wide.shape[1] // SLAB)]
+        side = jnp.concatenate(slabs, axis=0)
         for e in range(experts):
             total += lax.dot_general(
-                sides[b][:, e * RANK : (e + 1) * RANK],
+                side[:, e * RANK : (e + 1) * RANK],
                 wide[b * experts + e],
                 TN,
                 preferred_element_type=jnp.float32,
@@ -47,40 +56,43 @@
         in_specs=[pl.BlockSpec(memory_space=pltpu.VMEM)] * (len(sides) + 1 + len(extra)),
         out_specs=pl.BlockSpec(memory_space=pltpu.VMEM),
         cost_estimate=SMALL,
-        compiler_params=pltpu.CompilerParams(vmem_limit_bytes=32 << 20),
+        compiler_params=pltpu.CompilerParams(vmem_limit_bytes=room(*sides, wide)),
         name="combine",
     )(*sides, wide, *extra)
 
 
-def project_kernel(blocks, *refs):
+def project_kernel(blocks, rows, *refs):
     parts, weights = refs[:blocks], refs[blocks : blocks + QUAD]
     outs, total = refs[blocks + QUAD : -1], refs[-1]
-    rows = parts[0].shape[0]
     depth = 1024
     total[...] = jnp.zeros_like(total)
 
     @pl.loop(0, parts[0].shape[1] // depth)
     def _(i):
         span = pl.ds(pl.multiple_of(i * depth, depth), depth)
-        left = jnp.concatenate([p[:, span] for p in parts], axis=0)
+        left = jnp.concatenate([p[:rows, span] for p in parts], axis=0)
         right = jnp.concatenate([w[:, span] for w in weights], axis=0)
         total[...] += lax.dot_general(left, right, NT, preferred_element_type=jnp.float32)
 
+    width = total.shape[1]
     for b in range(blocks):
-        outs[b][...] = total[b * rows : (b + 1) * rows].astype(jnp.bfloat16)
-
-
-def project(parts, weights):
-    rows, width = parts[0].shape[0], QUAD * weights[0].shape[0]
+        for g in range(rows // SLAB):
+            top = b * rows + g * SLAB
+            outs[b][:, g * width : (g + 1) * width] = total[top : top + SLAB].astype(jnp.bfloat16)
+
+
+def project(parts, rows, weights):
+    width = QUAD * weights[0].shape[0]
     vmem = pl.BlockSpec(memory_space=pltpu.VMEM)
+    total = jax.ShapeDtypeStruct((rows * len(parts), width), jnp.float32)
     return pl.pallas_call(
-        functools.partial(project_kernel, len(parts)),
-        out_shape=[jax.ShapeDtypeStruct((rows, width), jnp.bfloat16)] * len(parts),
+        functools.partial(project_kernel, len(parts), rows),
+        out_shape=[jax.ShapeDtypeStruct((SLAB, rows // SLAB * width), jnp.bfloat16)] * len(parts),
         in_specs=[vmem] * (len(parts) + QUAD),
         out_specs=[vmem] * len(parts),
-        scratch_shapes=[pltpu.VMEM((rows * len(parts), width), jnp.float32)],
+        scratch_shapes=[pltpu.VMEM(total.shape, total.dtype)],
         cost_estimate=SMALL,
-        compiler_params=pltpu.CompilerParams(vmem_limit_bytes=40 << 20),
+        compiler_params=pltpu.CompilerParams(vmem_limit_bytes=room(*parts, *weights, total, total)),
         name="project",
     )(*parts, *weights)
 
@@ -110,7 +122,7 @@
         in_specs=[pl.BlockSpec(memory_space=pltpu.SMEM), vmem, vmem, vmem],
         out_specs=vmem,
         cost_estimate=SMALL,
-        compiler_params=pltpu.CompilerParams(vmem_limit_bytes=32 << 20),
+        compiler_params=pltpu.CompilerParams(vmem_limit_bytes=room(mine, mine, mine, mine, mine, over_y, rest)),
         name="assemble",
     )(here, mine, over_y, rest)
 
@@ -135,17 +147,6 @@
         return lax.ppermute(array, "expert", [(i, i ^ bit) for i in range(n)])
 
     weights = jnp.swapaxes(in_proj, 1, 2).reshape(owned * RANK, model_width)
-    half = weights.shape[0] // 2
-
-    width = queries.shape[1] // groups
-    lined = lax.dynamic_slice_in_dim(queries, group * width, width, axis=1)
-    lined = jnp.concatenate([lined, swap(lined, QUAD)], axis=0)
-    first = after(tokens, lined)
-    over_core = swap(weights, 1)
-    bit = 2 * QUAD
-    while bit < n:
-        lined = jnp.concatenate([lined, swap(lined, bit)], axis=0)
-        bit *= 2
 
     ways_home = []
     for s in range(1, planes):
@@ -173,50 +174,63 @@
     counts = jnp.broadcast_to(counts[:, None], (EX_DEV, RANK))
     repeated = jnp.concatenate([grad_side] * EX_DEV, axis=1)
     widely = jnp.repeat(member, RANK, axis=1)
-    wide = jnp.where(
-        widely[None], (gate[:, :, None] * repeated[None]).astype(jnp.bfloat16), jnp.zeros((), jnp.bfloat16)
-    )
-
-    over_y = swap(weights[:half], 2)
-    up, down = first, first
-    arrived, steps = [], []
-    for s in range(1, planes):
+    experts = QUAD * owned
+
+    def widen(part):
+        spread = (part[:, :, None] * repeated[None]).astype(jnp.bfloat16)
+        return jnp.where(widely[None], spread, jnp.zeros((), jnp.bfloat16))
+
+    wide, wide_late = widen(gate[:-experts]), widen(gate[-experts:])
+
+    over_y = swap(weights, 2)
+
+    width = queries.shape[1] // groups
+    lined = lax.dynamic_slice_in_dim(queries, group * width, width, axis=1)
+    lined = jnp.concatenate([lined, swap(lined, QUAD)], axis=0)
+
+    middle = (planes + 1) // 2
+    up, down = tokens, tokens
+    first = []
+    for s in range(1, middle):
+        up, down = move(up, [(p, p + 1) for p in range(s - 1, planes - 1)]), move(
+            down, [(p, p - 1) for p in range(1, planes - s + 1)]
+        )
+        first.extend([up, down])
+    over_core = swap(weights, 1)
+    lined = after(lined, wide, wide_late, *first)
+    bit = 2 * QUAD
+    while bit < n:
+        lined = jnp.concatenate([lined, swap(lined, bit)], axis=0)
+        bit *= 2
+
+    for s in range(middle, planes):
         up_hops = [(p, p + 1) for p in range(s - 1, planes - 1)]
         down_hops = [(p, p - 1) for p in range(1, planes - s + 1)]
-        if s == 2:
-            up, down = after(up, lined, wide), after(down, lined, wide)
+        if s == middle:
+            up, down = move(up, up_hops), move(down, down_hops)
+            up = down = up + down
+            across = swap(after(over_y, up), 1)
+            quad_weights = [weights, over_core, over_y, across]
+            lined = after(lined, up)
             ranged = [lined] + [
-                lax.ppermute(after(lined, over_y, up, down), "groups", [(g, (g + k) % groups) for g in range(groups)])
-                for k in range(1, groups)
+                lax.ppermute(lined, "groups", [(g, (g + k) % groups) for g in range(groups)]) for k in range(1, groups)
             ]
-        elif s == 3:
-            up, down = after(up, *ranged), after(down, *ranged)
-        if 2 * s > planes + 1:
+            own, *sides = project([tokens] + first + [up], token_count, quad_weights)
+            returned = [move(side, home) for side, home in zip(sides, ways_home)]
+            mine = jnp.concatenate(ranged, axis=1)
+            mine_over_y = swap(mine, 2)
+        else:
             up = down = move(up, up_hops + down_hops)
-        else:
-            up, down = move(up, up_hops), move(down, down_hops)
-            if 2 * s >= planes:
-                up = down = up + down
-        steps.append(up)
-        arrived.extend([up] if 2 * s >= planes else [up, down])
-
-    over_y_late = swap(after(weights[half:], arrived[0]), 2)
-    over_y_all = jnp.concatenate([over_y, over_y_late], axis=0)
-    across = swap(after(over_y_all, steps[1]), 1)
-    quad_weights = [weights, over_core, over_y_all, across]
-
-    experts = QUAD * owned
-    own, *sides = project([tokens] + arrived[:-1], quad_weights)
-    returned = [move(side, home) for side, home in zip(sides, ways_home[:-1])]
-    mine = after(jnp.concatenate(ranged, axis=1), over_y_all, steps[1])
-    mine_over_y = swap(mine, 2)
-    side = project([after(arrived[-1], *returned)], quad_weights)[0]
-    late = move(side, ways_home[-1])
-    early = combine([own] + returned, wide[:-experts])
-    rest = swap(after(jnp.concatenate([mine, mine_over_y], axis=0), side), 1)
+            wait = returned if s == planes - 1 else []
+            (side,) = project([after(up, *wait)], token_count, quad_weights)
+            returned.append(move(side, ways_home[len(returned)]))
+    late = returned.pop()
+    early = combine([own] + returned, wide)
+
+    rest = swap(after(jnp.concatenate([mine, mine_over_y], axis=0), late), 1)
     here = jnp.stack([plane, spot, group]).astype(jnp.int32)
     all_queries = assemble(here, mine, mine_over_y, rest, planes, groups)
-    sketches = combine([late], wide[-experts:], early, counts)
+    sketches = combine([late], wide_late, early, counts)
     sketches = sketches.reshape(EX_DEV, RANK * RANK)
     scores = lax.dot_general(sketches.astype(jnp.bfloat16), all_queries, NT, preferred_element_type=jnp.float32)
     return (sketches, scores)

time: 85.5 us -> 83.8 us (0.980)
  waiting for transfers between devices: 38.3 us -> 36.6 us
  local copies, waits for them, and re-layouts: 5.23 us -> 3.68 us
  other arithmetic: 2.38 us -> 3.76 us
    ppermute x8 -> x7, waiting for transfers between devices: 13.8 us -> 8 us  [swap(): return lax.ppermute(array, 'expert', [(i, i ^ bit) for i in range(n)])]
    ppermute x1, waiting for transfers between devices: 0.01 us -> 4.39 us  [shards(): lax.ppermute(lined, 'groups', [(g, (g + k) % groups) for g in range(group...]
    slice x3 -> x2, local copies, waits for them, and re-layouts: 2.4 us -> 0.01 us  [shards(): wide, wide_late = (widen(gate[:-experts]), widen(gate[-experts:]))]
    unnamed x21 -> x19, local copies, waits for them, and re-layouts: 1.13 us -> 2.14 us
    ppermute x8 -> x7, starting transfers between devices: 9.38 us -> 9.12 us  [swap(): return lax.ppermute(array, 'expert', [(i, i ^ bit) for i in range(n)])]
  transfers between devices with their start and end apart: 18 -> 17, of which waited for: 8 -> 10; matrix products, arithmetic and copies ran while one was open for 9% -> 8% of each run, Pallas kernels for 5% -> 7%
where the time goes in v7:
time: 83.8 us; the launch traced here: 83.2 us
  waiting for transfers between devices  36.6 us (44%)
  starting transfers between devices  29.1 us (35%)
  Pallas kernels  6.51 us (8%)
  other arithmetic  3.76 us (4%)
  local copies, waits for them, and re-layouts  3.68 us (4%)
  matrix products  2.58 us (3%)
  between operations  0.97 us (1%)
    ppermute x9, waiting for transfers between devices, move(): return lax.ppermute(array, 'expert', pairs)  24.2 us
    ppermute x9, starting transfers between devices, move(): return lax.ppermute(array, 'expert', pairs)  18.4 us
    ppermute x7, starting transfers between devices, swap(): return lax.ppermute(array, 'expert', [(i, i ^ bit) for i in range(n)])  9.12 us
    ppermute x7, waiting for transfers between devices, swap(): return lax.ppermute(array, 'expert', [(i, i ^ bit) for i in range(n)])  8 us
    pallas_call x2, Pallas kernels, project(): pl.pallas_call(functools.partial(project_kernel, len(parts), rows), out_s...  4.76 us
    ppermute x1, waiting for transfers between devices, shards(): lax.ppermute(lined, 'groups', [(g, (g + k) % groups) for g in range(group...  4.39 us
    unnamed x19, local copies, waits for them, and re-layouts  2.14 us
  transfers between devices with their start and end apart: 17, of which 10 were waited for; matrix products, arithmetic and copies ran while one was open for 8% of the time, Pallas kernels for 7%

profile of v7, /device:TPU:0, one launch (start us, length us, event | category | flops | bytes accessed | tf_op | source)
XLA Modules:
  0.0 83.2 jit_solution(16243173516588195026)
XLA Ops:
  0.7 5.1 %collective-permute-start = (bf16[64,4096]{1,0:T(8,128)(2,1)}, bf16[64,4096]{1,0:T(8,128)(2,1)S(1)}, u32[]{:S(2)}, u32[]{:S(2)}) collective-permute-start(bf16[64,4096]{1,0:T(8,128)(2,1)} %refs_0_.1), channel_id=1, source_target_pairs={{0,4},{1,5},{2,6},{3,7},{4,8},{5,9},{6,10},{7,11},{8,12},{9,13},{1... | collective-permute-start | bytes 1572872 | tf_op jit(solution)/shard_map/ppermute | solution.py:144
  5.8 1.3 %collective-permute-start.2 = (bf16[64,4096]{1,0:T(8,128)(2,1)}, bf16[64,4096]{1,0:T(8,128)(2,1)}, u32[]{:S(2)}, u32[]{:S(2)}) collective-permute-start(bf16[64,4096]{1,0:T(8,128)(2,1)} %refs_0_.1), channel_id=1, source_target_pairs={{4,0},{5,1},{6,2},{7,3},{8,4},{9,5},{10,6},{11,7},{12,8},{13,9},{1... | collective-permute-start | bytes 1572872 | tf_op jit(solution)/shard_map/ppermute | solution.py:144
  7.1 1.6 %collective-permute-start.6 = (bf16[128,4096]{1,0:T(8,128)(2,1)}, bf16[128,4096]{1,0:T(8,128)(2,1)S(1)}, u32[]{:S(2)}, u32[]{:S(2)}) collective-permute-start(bf16[128,4096]{1,0:T(8,128)(2,1)} %bitcast.16), channel_id=1, source_target_pairs={{0,2},{1,3},{2,0},{3,1},{4,6},{5,7},{6,4},{7,5},{8,10},{9,11},{10,... | collective-permute-start | bytes 3145736 | tf_op jit(solution)/shard_map/ppermute | solution.py:147
  8.6 0.8 %constant_dynamic-slice_fusion = bf16[16,2048]{1,0:T(8,128)(2,1)S(1)} fusion(bf16[16,4096]{1,0:T(8,128)(2,1)} %param.15, s32[]{:T(128)S(6)} %select_n.93), kind=kLoop, calls=%fused_computation.21 | loop fusion | bytes 131076 | tf_op jit(solution)/shard_map/dynamic_slice | solution.py:188
  9.5 2.6 %collective-permute-start.12 = (bf16[16,2048]{1,0:T(8,128)(2,1)S(1)}, bf16[16,2048]{1,0:T(8,128)(2,1)S(1)}, u32[]{:S(2)}, u32[]{:S(2)}) collective-permute-start(bf16[16,2048]{1,0:T(8,128)(2,1)S(1)} %constant_dynamic-slice_fusion), channel_id=1, source_target_pairs={{0,4},{1,5},{2,6},{3,7},{4,0},{5,1},{6,2},{7,3},{8,12},{9,13},{10,... | collective-permute-start | bytes 196616 | tf_op jit(solution)/shard_map/ppermute | solution.py:147
  12.1 0.1 stack.33
  12.3 0.1 add.55
  12.4 0.7 iota_compare_fusion
  13.2 1.3 %fusion.4 = f32[64,64]{1,0:T(8,128)S(1)} fusion(bf16[64,4096]{1,0:T(8,128)(2,1)S(1)} %copy-done, bf16[4096,64]{0,1:T(8,128)(2,1)} %param.14), kind=kOutput, calls=%fused_computation.22 | convolution fusion | flops 33554432 | bytes 1064960 | tf_op jit(solution)/shard_map/dot_general | solution.py:163
  14.6 0.1 select_n.89
  14.6 0.8 select_reduce_fusion
  15.5 0.1 broadcast_in_dim.70
  15.6 0.1 broadcast_in_dim.71
  15.8 0.1 pad_maximum_fusion.3
  15.9 0.3 fusion.refs_4_
  16.2 1.7 %collective-permute-done.refs_1_ = bf16[64,4096]{1,0:T(8,128)(2,1)S(1)} collective-permute-done((bf16[64,4096]{1,0:T(8,128)(2,1)}, bf16[64,4096]{1,0:T(8,128)(2,1)S(1)}, u32[]{:S(2)}, u32[]{:S(2)}) %collective-permute-start) | collective-permute-done | bytes 524320 | tf_op jit(solution)/shard_map/ppermute | solution.py:144
  17.9 0.7 collective-permute-start.1
  18.6 3.5 %collective-permute-done.2.refs_2_ = bf16[64,4096]{1,0:T(8,128)(2,1)} collective-permute-done((bf16[64,4096]{1,0:T(8,128)(2,1)}, bf16[64,4096]{1,0:T(8,128)(2,1)}, u32[]{:S(2)}, u32[]{:S(2)}) %collective-permute-start.2) | collective-permute-done | bytes 524320 | tf_op jit(solution)/shard_map/ppermute | solution.py:144
  22.1 1.3 %collective-permute-start.3 = (bf16[64,4096]{1,0:T(8,128)(2,1)}, bf16[64,4096]{1,0:T(8,128)(2,1)S(1)}, u32[]{:S(2)}, u32[]{:S(2)}) collective-permute-start(bf16[64,4096]{1,0:T(8,128)(2,1)} %collective-permute-done.2.refs_2_), channel_id=1, source_target_pairs={{4,0},{5,1},{6,2},{7,3},{8,4},{9,5},{10,6},{11,7},{20,16},{21,17},... | collective-permute-start | bytes 1572872 | tf_op jit(solution)/shard_map/ppermute | solution.py:144
  23.3 0.1 fusion.1.refs_1_
  23.5 3.2 %collective-permute-start.13 = (bf16[32,2048]{1,0:T(8,128)(2,1)S(1)}, bf16[32,2048]{1,0:T(8,128)(2,1)S(1)}, u32[]{:S(2)}, u32[]{:S(2)}) collective-permute-start(bf16[32,2048]{1,0:T(8,128)(2,1)S(1)} %pad_maximum_fusion.2), channel_id=1, source_target_pairs={{0,8},{1,9},{2,10},{3,11},{4,12},{5,13},{6,14},{7,15},{8,0},{9,1},... | collective-permute-start | bytes 393224 | tf_op jit(solution)/shard_map/ppermute | solution.py:147
  26.8 9.3 %collective-permute-done.3 = bf16[64,4096]{1,0:T(8,128)(2,1)S(1)} collective-permute-done((bf16[64,4096]{1,0:T(8,128)(2,1)}, bf16[64,4096]{1,0:T(8,128)(2,1)S(1)}, u32[]{:S(2)}, u32[]{:S(2)}) %collective-permute-start.3) | collective-permute-done | bytes 524320 | tf_op jit(solution)/shard_map/ppermute | solution.py:144
  36.1 0.1 add.49.refs_3_
  36.3 6.6 %collective-permute-done.13 = bf16[32,2048]{1,0:T(8,128)(2,1)S(1)} collective-permute-done((bf16[32,2048]{1,0:T(8,128)(2,1)S(1)}, bf16[32,2048]{1,0:T(8,128)(2,1)S(1)}, u32[]{:S(2)}, u32[]{:S(2)}) %collective-permute-start.13) | collective-permute-done | bytes 131104 | tf_op jit(solution)/shard_map/ppermute | solution.py:147
  42.9 1.6 %collective-permute-start.14 = (bf16[64,2048]{1,0:T(8,128)(2,1)S(1)}, bf16[64,2048]{1,0:T(8,128)(2,1)S(1)}, u32[]{:S(2)}, u32[]{:S(2)}) collective-permute-start(bf16[64,2048]{1,0:T(8,128)(2,1)S(1)} %pad_maximum_fusion.1), channel_id=1, source_target_pairs={{0,16},{16,0},{1,17},{17,1},{2,18},{18,2},{3,19},{19,3},{4,20},{20... | collective-permute-start | bytes 786440 | tf_op jit(solution)/shard_map/ppermute | solution.py:216
  44.5 1.3 %collective-permute-start.4 = (bf16[64,4096]{1,0:T(8,128)(2,1)S(1)}, bf16[64,4096]{1,0:T(8,128)(2,1)S(1)}, u32[]{:S(2)}, u32[]{:S(2)}) collective-permute-start(bf16[64,4096]{1,0:T(8,128)(2,1)S(1)} %add.49.refs_3_), channel_id=1, source_target_pairs={{8,12},{9,13},{10,14},{11,15},{4,0},{5,1},{6,2},{7,3},{24,28},{25,... | collective-permute-start | bytes 1572872 | tf_op jit(solution)/shard_map/ppermute | solution.py:144
  45.8 4.4 %collective-permute-done.14 = bf16[64,2048]{1,0:T(8,128)(2,1)S(1)} collective-permute-done((bf16[64,2048]{1,0:T(8,128)(2,1)S(1)}, bf16[64,2048]{1,0:T(8,128)(2,1)S(1)}, u32[]{:S(2)}, u32[]{:S(2)}) %collective-permute-start.14) | collective-permute-done | bytes 262176 | tf_op jit(solution)/shard_map/ppermute | solution.py:216
  50.2 1.6 %collective-permute-start.15 = (bf16[64,4096]{1,0:T(8,128)(2,1)S(1)}, bf16[64,4096]{1,0:T(8,128)(2,1)S(1)}, u32[]{:S(2)}, u32[]{:S(2)}) collective-permute-start(bf16[64,4096]{1,0:T(8,128)(2,1)S(1)} %constant_dynamic-update-slice_fusion.mine_ref), channel_id=1, source_target_pairs={{0,2},{1,3},{2,0},{3,1},{4,6},{5,7},{6,4},{7,5},{8,10},{9,11},{10,... | collective-permute-start | bytes 1572872 | tf_op jit(solution)/shard_map/ppermute | solution.py:147
  51.8 1.0 %copy-done.6 = bf16[64,4096]{1,0:T(8,128)(2,1)S(1)} copy-done((bf16[64,4096]{1,0:T(8,128)(2,1)S(1)}, bf16[64,4096]{1,0:T(8,128)(2,1)}, u32[]{:S(2)}) %copy-start.6) | copy-done | bytes 524312
  52.8 3.0 %project.2 = (bf16[16,2048]{1,0:T(8,128)(2,1)S(1)}, bf16[16,2048]{1,0:T(8,128)(2,1)S(1)}, bf16[16,2048]{1,0:T(8,128)(2,1)S(1)}, bf16[16,2048]{1,0:T(8,128)(2,1)S(1)}) custom-call(bf16[64,4096]{1,0:T(8,128)(2,1)S(1)} %copy-done.4, bf16[64,4096]{1,0:T(8,128)(2,1)S(1)} %copy-done.6, bf16[64,4096]{1,0:T(8,128)(2,1)} %collective-permute-done.2.refs_2_, ...), custom_call_target="tpu_custom_call" | custom-call | flops 1024 | bytes 1024 | tf_op jit(solution)/shard_map/project/pallas_call | solution.py:88
  55.8 1.3 %collective-permute-start.8 = (bf16[16,2048]{1,0:T(8,128)(2,1)S(1)}, bf16[16,2048]{1,0:T(8,128)(2,1)S(1)}, u32[]{:S(2)}, u32[]{:S(2)}) collective-permute-start(bf16[16,2048]{1,0:T(8,128)(2,1)S(1)} %get-tuple-element.12), channel_id=1, source_target_pairs={{4,0},{5,1},{6,2},{7,3},{8,4},{9,5},{10,6},{11,7},{12,8},{13,9},{1... | collective-permute-start | bytes 196616 | tf_op jit(solution)/shard_map/ppermute | solution.py:144
  57.1 4.5 %collective-permute-start.9 = (bf16[16,2048]{1,0:T(8,128)(2,1)S(1)}, bf16[16,2048]{1,0:T(8,128)(2,1)S(1)}, u32[]{:S(2)}, u32[]{:S(2)}) collective-permute-start(bf16[16,2048]{1,0:T(8,128)(2,1)S(1)} %get-tuple-element.13), channel_id=1, source_target_pairs={{0,4},{1,5},{2,6},{3,7},{4,8},{5,9},{6,10},{7,11},{8,12},{9,13},{1... | collective-permute-start | bytes 196616 | tf_op jit(solution)/shard_map/ppermute | solution.py:144
  61.7 0.1 collective-permute-start.10
  61.8 0.2 collective-permute-done.8.refs_1_
  62.0 1.6 %collective-permute-done.9.refs_2_ = bf16[16,2048]{1,0:T(8,128)(2,1)S(1)} collective-permute-done((bf16[16,2048]{1,0:T(8,128)(2,1)S(1)}, bf16[16,2048]{1,0:T(8,128)(2,1)S(1)}, u32[]{:S(2)}, u32[]{:S(2)}) %collective-permute-start.9) | collective-permute-done | bytes 65568 | tf_op jit(solution)/shard_map/ppermute | solution.py:144
  63.6 4.0 %collective-permute-done.10.refs_3_ = bf16[16,2048]{1,0:T(8,128)(2,1)S(1)} collective-permute-done((bf16[16,2048]{1,0:T(8,128)(2,1)S(1)}, bf16[16,2048]{1,0:T(8,128)(2,1)S(1)}, u32[]{:S(2)}, u32[]{:S(2)}) %collective-permute-start.10) | collective-permute-done | bytes 65568 | tf_op jit(solution)/shard_map/ppermute | solution.py:144
  67.6 1.8 %project.3 = bf16[16,2048]{1,0:T(8,128)(2,1)S(1)} custom-call(bf16[64,4096]{1,0:T(8,128)(2,1)S(1)} %collective-permute-done.4.refs_0_, bf16[128,4096]{1,0:T(8,128)(2,1)S(1)} %bitcast.19, bf16[128,4096]{1,0:T(8,128)(2,1)S(1)} %collective-permute-done.5.refs_5_.refs_2_, bf16[128,4096]{1,0:T(8,128)(2,1)S(1)} %collective-permute-done.6.refs_6_.refs_3_, ...), custom_call_target="tpu_custom_call" | custom-call | flops 1024 | bytes 1024 | tf_op jit(solution)/shard_map/project/pallas_call | solution.py:88
  69.4 2.8 %collective-permute-start.11 = (bf16[16,2048]{1,0:T(8,128)(2,1)S(1)}, bf16[16,2048]{1,0:T(8,128)(2,1)S(1)}, u32[]{:S(2)}, u32[]{:S(2)}) collective-permute-start(bf16[16,2048]{1,0:T(8,128)(2,1)S(1)} %project.3), channel_id=1, source_target_pairs={{12,0},{13,1},{14,2},{15,3},{0,12},{1,13},{2,14},{3,15},{28,16},{2... | collective-permute-start | bytes 196616 | tf_op jit(solution)/shard_map/ppermute | solution.py:144
  72.3 1.2 %pad_maximum_fusion = bf16[128,4096]{1,0:T(8,128)(2,1)} fusion(bf16[64,4096]{1,0:T(8,128)(2,1)S(1)} %collective-permute-done.15.over_y_ref, bf16[64,4096]{1,0:T(8,128)(2,1)S(1)} %constant_dynamic-update-slice_fusion.mine_ref), kind=kLoop, calls=%fused_computation.2 | loop fusion | flops 2097152 | bytes 2097152 | tf_op jit(solution)/shard_map/concatenate | solution.py:230
  73.4 3.9 %collective-permute-done.11.refs_0_ = bf16[16,2048]{1,0:T(8,128)(2,1)S(1)} collective-permute-done((bf16[16,2048]{1,0:T(8,128)(2,1)S(1)}, bf16[16,2048]{1,0:T(8,128)(2,1)S(1)}, u32[]{:S(2)}, u32[]{:S(2)}) %collective-permute-start.11) | collective-permute-done | bytes 65568 | tf_op jit(solution)/shard_map/ppermute | solution.py:144
  77.4 0.1 convert_reduce_fusion
  77.5 0.7 combine.2.refs_2_
  78.3 0.4 combine.3
  78.7 0.1 reshape.146
  78.8 1.4 %collective-permute-done.16.rest_ref = bf16[128,4096]{1,0:T(8,128)(2,1)S(1)} collective-permute-done((bf16[128,4096]{1,0:T(8,128)(2,1)}, bf16[128,4096]{1,0:T(8,128)(2,1)S(1)}, u32[]{:S(2)}, u32[]{:S(2)}) %collective-permute-start.16) | collective-permute-done | bytes 1048608 | tf_op jit(solution)/shard_map/ppermute | solution.py:147
  80.2 1.0 %copy-done.3 = bf16[64,4096]{1,0:T(8,128)(2,1)S(1)} copy-done((bf16[64,4096]{1,0:T(8,128)(2,1)S(1)}, bf16[64,4096]{1,0:T(8,128)(2,1)}, u32[]{:S(2)}) %copy-start.3) | copy-done | bytes 524312
  81.3 0.7 assemble.1
  82.0 1.3 %fusion.2 = f32[4,256]{1,0:T(4,128)} fusion(bf16[256,4096]{1,0:T(8,128)(2,1)S(1)} %assemble.1, f32[4,4096]{1,0:T(4,128)S(1)} %reshape.146), kind=kOutput, calls=%fused_computation.9 | convolution fusion | flops 8404992 | bytes 2166784 | tf_op jit(solution)/shard_map/dot_general | solution.py:235
  (39 shorter events, 0.5 us)
Async XLA Ops:
  0.6 12.5 %copy-start = (bf16[64,4096]{1,0:T(8,128)(2,1)S(1)}, bf16[64,4096]{1,0:T(8,128)(2,1)}, u32[]{:S(2)}) copy-start(bf16[64,4096]{1,0:T(8,128)(2,1)} %param.9) | copy-start | bytes 1572868
  0.6 26.1 %copy-start.1 = (bf16[2,4096,64]{1,2,0:T(8,128)(2,1)S(1)}, bf16[2,4096,64]{1,2,0:T(8,128)(2,1)}, u32[]{:S(2)}) copy-start(bf16[2,4096,64]{1,2,0:T(8,128)(2,1)} %param.13) | copy-start | bytes 3145732
  0.7 17.3 %collective-permute-start = (bf16[64,4096]{1,0:T(8,128)(2,1)}, bf16[64,4096]{1,0:T(8,128)(2,1)S(1)}, u32[]{:S(2)}, u32[]{:S(2)}) collective-permute-start(bf16[64,4096]{1,0:T(8,128)(2,1)} %refs_0_.1), channel_id=1, source_target_pairs={{0,4},{1,5},{2,6},{3,7},{4,8},{5,9},{6,10},{7,11},{8,12},{9,13},{1... | collective-permute-start | bytes 1572872 | tf_op jit(solution)/shard_map/ppermute | solution.py:144
  5.8 16.3 %collective-permute-start.2 = (bf16[64,4096]{1,0:T(8,128)(2,1)}, bf16[64,4096]{1,0:T(8,128)(2,1)}, u32[]{:S(2)}, u32[]{:S(2)}) collective-permute-start(bf16[64,4096]{1,0:T(8,128)(2,1)} %refs_0_.1), channel_id=1, source_target_pairs={{4,0},{5,1},{6,2},{7,3},{8,4},{9,5},{10,6},{11,7},{12,8},{13,9},{1... | collective-permute-start | bytes 1572872 | tf_op jit(solution)/shard_map/ppermute | solution.py:144
  7.1 29.2 %collective-permute-start.6 = (bf16[128,4096]{1,0:T(8,128)(2,1)}, bf16[128,4096]{1,0:T(8,128)(2,1)S(1)}, u32[]{:S(2)}, u32[]{:S(2)}) collective-permute-start(bf16[128,4096]{1,0:T(8,128)(2,1)} %bitcast.16), channel_id=1, source_target_pairs={{0,2},{1,3},{2,0},{3,1},{4,6},{5,7},{6,4},{7,5},{8,10},{9,11},{10,... | collective-permute-start | bytes 3145736 | tf_op jit(solution)/shard_map/ppermute | solution.py:147
  9.5 14.0 %collective-permute-start.12 = (bf16[16,2048]{1,0:T(8,128)(2,1)S(1)}, bf16[16,2048]{1,0:T(8,128)(2,1)S(1)}, u32[]{:S(2)}, u32[]{:S(2)}) collective-permute-start(bf16[16,2048]{1,0:T(8,128)(2,1)S(1)} %constant_dynamic-slice_fusion), channel_id=1, source_target_pairs={{0,4},{1,5},{2,6},{3,7},{4,0},{5,1},{6,2},{7,3},{8,12},{9,13},{10,... | collective-permute-start | bytes 196616 | tf_op jit(solution)/shard_map/ppermute | solution.py:147
  16.2 35.6 %copy-start.4 = (bf16[64,4096]{1,0:T(8,128)(2,1)S(1)}, bf16[64,4096]{1,0:T(8,128)(2,1)}, u32[]{:S(2)}) copy-start(bf16[64,4096]{1,0:T(8,128)(2,1)} %refs_0_.1) | copy-start | bytes 1572868
  17.9 26.6 %copy-start.5 = (bf16[64,4096]{1,0:T(8,128)(2,1)}, bf16[64,4096]{1,0:T(8,128)(2,1)S(1)}, u32[]{:S(2)}) copy-start(bf16[64,4096]{1,0:T(8,128)(2,1)S(1)} %collective-permute-done.refs_1_) | copy-start | bytes 1572868
  17.9 8.8 %collective-permute-start.1 = (bf16[64,4096]{1,0:T(8,128)(2,1)S(1)}, bf16[64,4096]{1,0:T(8,128)(2,1)S(1)}, u32[]{:S(2)}, u32[]{:S(2)}) collective-permute-start(bf16[64,4096]{1,0:T(8,128)(2,1)S(1)} %collective-permute-done.refs_1_), channel_id=1, source_target_pairs={{4,8},{5,9},{6,10},{7,11},{8,12},{9,13},{10,14},{11,15},{20,24},{2... | collective-permute-start | bytes 1572872 | tf_op jit(solution)/shard_map/ppermute | solution.py:144
  22.1 14.0 %collective-permute-start.3 = (bf16[64,4096]{1,0:T(8,128)(2,1)}, bf16[64,4096]{1,0:T(8,128)(2,1)S(1)}, u32[]{:S(2)}, u32[]{:S(2)}) collective-permute-start(bf16[64,4096]{1,0:T(8,128)(2,1)} %collective-permute-done.2.refs_2_), channel_id=1, source_target_pairs={{4,0},{5,1},{6,2},{7,3},{8,4},{9,5},{10,6},{11,7},{20,16},{21,17},... | collective-permute-start | bytes 1572872 | tf_op jit(solution)/shard_map/ppermute | solution.py:144
  23.5 19.4 %collective-permute-start.13 = (bf16[32,2048]{1,0:T(8,128)(2,1)S(1)}, bf16[32,2048]{1,0:T(8,128)(2,1)S(1)}, u32[]{:S(2)}, u32[]{:S(2)}) collective-permute-start(bf16[32,2048]{1,0:T(8,128)(2,1)S(1)} %pad_maximum_fusion.2), channel_id=1, source_target_pairs={{0,8},{1,9},{2,10},{3,11},{4,12},{5,13},{6,14},{7,15},{8,0},{9,1},... | collective-permute-start | bytes 393224 | tf_op jit(solution)/shard_map/ppermute | solution.py:147
  26.7 25.0 %collective-permute-start.5 = (bf16[128,4096]{1,0:T(8,128)(2,1)S(1)}, bf16[128,4096]{1,0:T(8,128)(2,1)S(1)}, u32[]{:S(2)}, u32[]{:S(2)}) collective-permute-start(bf16[128,4096]{1,0:T(8,128)(2,1)S(1)} %bitcast.17), channel_id=1, source_target_pairs={{0,1},{1,0},{2,3},{3,2},{4,5},{5,4},{6,7},{7,6},{8,9},{9,8},{10,11... | collective-permute-start | bytes 3145736 | tf_op jit(solution)/shard_map/ppermute | solution.py:147
  36.2 15.6 %collective-permute-start.7 = (bf16[128,4096]{1,0:T(8,128)(2,1)S(1)}, bf16[128,4096]{1,0:T(8,128)(2,1)S(1)}, u32[]{:S(2)}, u32[]{:S(2)}) collective-permute-start(bf16[128,4096]{1,0:T(8,128)(2,1)S(1)} %collective-permute-done.6.refs_6_.refs_3_), channel_id=1, source_target_pairs={{0,1},{1,0},{2,3},{3,2},{4,5},{5,4},{6,7},{7,6},{8,9},{9,8},{10,11... | collective-permute-start | bytes 3145736 | tf_op jit(solution)/shard_map/ppermute | solution.py:147
  42.9 7.3 %collective-permute-start.14 = (bf16[64,2048]{1,0:T(8,128)(2,1)S(1)}, bf16[64,2048]{1,0:T(8,128)(2,1)S(1)}, u32[]{:S(2)}, u32[]{:S(2)}) collective-permute-start(bf16[64,2048]{1,0:T(8,128)(2,1)S(1)} %pad_maximum_fusion.1), channel_id=1, source_target_pairs={{0,16},{16,0},{1,17},{17,1},{2,18},{18,2},{3,19},{19,3},{4,20},{20... | collective-permute-start | bytes 786440 | tf_op jit(solution)/shard_map/ppermute | solution.py:216
  44.5 17.3 %collective-permute-start.4 = (bf16[64,4096]{1,0:T(8,128)(2,1)S(1)}, bf16[64,4096]{1,0:T(8,128)(2,1)S(1)}, u32[]{:S(2)}, u32[]{:S(2)}) collective-permute-start(bf16[64,4096]{1,0:T(8,128)(2,1)S(1)} %add.49.refs_3_), channel_id=1, source_target_pairs={{8,12},{9,13},{10,14},{11,15},{4,0},{5,1},{6,2},{7,3},{24,28},{25,... | collective-permute-start | bytes 1572872 | tf_op jit(solution)/shard_map/ppermute | solution.py:144
  50.2 22.1 %collective-permute-start.15 = (bf16[64,4096]{1,0:T(8,128)(2,1)S(1)}, bf16[64,4096]{1,0:T(8,128)(2,1)S(1)}, u32[]{:S(2)}, u32[]{:S(2)}) collective-permute-start(bf16[64,4096]{1,0:T(8,128)(2,1)S(1)} %constant_dynamic-update-slice_fusion.mine_ref), channel_id=1, source_target_pairs={{0,2},{1,3},{2,0},{3,1},{4,6},{5,7},{6,4},{7,5},{8,10},{9,11},{10,... | collective-permute-start | bytes 1572872 | tf_op jit(solution)/shard_map/ppermute | solution.py:147
  51.8 1.0 %copy-start.6 = (bf16[64,4096]{1,0:T(8,128)(2,1)S(1)}, bf16[64,4096]{1,0:T(8,128)(2,1)}, u32[]{:S(2)}) copy-start(bf16[64,4096]{1,0:T(8,128)(2,1)} %copy-done.5) | copy-start | bytes 1572868
  55.8 6.2 %collective-permute-start.8 = (bf16[16,2048]{1,0:T(8,128)(2,1)S(1)}, bf16[16,2048]{1,0:T(8,128)(2,1)S(1)}, u32[]{:S(2)}, u32[]{:S(2)}) collective-permute-start(bf16[16,2048]{1,0:T(8,128)(2,1)S(1)} %get-tuple-element.12), channel_id=1, source_target_pairs={{4,0},{5,1},{6,2},{7,3},{8,4},{9,5},{10,6},{11,7},{12,8},{13,9},{1... | collective-permute-start | bytes 196616 | tf_op jit(solution)/shard_map/ppermute | solution.py:144
  57.1 6.4 %collective-permute-start.9 = (bf16[16,2048]{1,0:T(8,128)(2,1)S(1)}, bf16[16,2048]{1,0:T(8,128)(2,1)S(1)}, u32[]{:S(2)}, u32[]{:S(2)}) collective-permute-start(bf16[16,2048]{1,0:T(8,128)(2,1)S(1)} %get-tuple-element.13), channel_id=1, source_target_pairs={{0,4},{1,5},{2,6},{3,7},{4,8},{5,9},{6,10},{7,11},{8,12},{9,13},{1... | collective-permute-start | bytes 196616 | tf_op jit(solution)/shard_map/ppermute | solution.py:144
  61.7 5.9 %collective-permute-start.10 = (bf16[16,2048]{1,0:T(8,128)(2,1)S(1)}, bf16[16,2048]{1,0:T(8,128)(2,1)S(1)}, u32[]{:S(2)}, u32[]{:S(2)}) collective-permute-start(bf16[16,2048]{1,0:T(8,128)(2,1)S(1)} %get-tuple-element.14), channel_id=1, source_target_pairs={{8,0},{9,1},{10,2},{11,3},{12,4},{13,5},{14,6},{15,7},{0,8},{1,9},... | collective-permute-start | bytes 196616 | tf_op jit(solution)/shard_map/ppermute | solution.py:144
  69.4 8.1 %copy-start.8 = (s32[1,64]{1,0:T(1,128)S(1)}, s32[1,64]{1,0:T(1,128)}, u32[]{:S(2)}) copy-start(s32[1,64]{1,0:T(1,128)} %param.12) | copy-start | bytes 772
  69.4 8.0 %collective-permute-start.11 = (bf16[16,2048]{1,0:T(8,128)(2,1)S(1)}, bf16[16,2048]{1,0:T(8,128)(2,1)S(1)}, u32[]{:S(2)}, u32[]{:S(2)}) collective-permute-start(bf16[16,2048]{1,0:T(8,128)(2,1)S(1)} %project.3), channel_id=1, source_target_pairs={{12,0},{13,1},{14,2},{15,3},{0,12},{1,13},{2,14},{3,15},{28,16},{2... | collective-permute-start | bytes 196616 | tf_op jit(solution)/shard_map/ppermute | solution.py:144
  72.3 6.0 %copy-start.2 = (bf16[64,4096]{1,0:T(8,128)(2,1)}, bf16[64,4096]{1,0:T(8,128)(2,1)S(1)}, u32[]{:S(2)}) copy-start(bf16[64,4096]{1,0:T(8,128)(2,1)S(1)} %collective-permute-done.15.over_y_ref) | copy-start | bytes 1572868
  77.4 2.9 %collective-permute-start.16 = (bf16[128,4096]{1,0:T(8,128)(2,1)}, bf16[128,4096]{1,0:T(8,128)(2,1)S(1)}, u32[]{:S(2)}, u32[]{:S(2)}) collective-permute-start(bf16[128,4096]{1,0:T(8,128)(2,1)} %pad_maximum_fusion), channel_id=1, source_target_pairs={{0,1},{1,0},{2,3},{3,2},{4,5},{5,4},{6,7},{7,6},{8,9},{9,8},{10,11... | collective-permute-start | bytes 3145736 | tf_op jit(solution)/shard_map/ppermute | solution.py:147
  78.8 3.2 %copy-start.7 = (f32[4,4096]{1,0:T(4,128)}, f32[4,4096]{1,0:T(4,128)S(1)}, u32[]{:S(2)}) copy-start(f32[4,4096]{1,0:T(4,128)S(1)} %reshape.146) | copy-start | bytes 196612
  80.2 1.0 %copy-start.3 = (bf16[64,4096]{1,0:T(8,128)(2,1)S(1)}, bf16[64,4096]{1,0:T(8,128)(2,1)}, u32[]{:S(2)}) copy-start(bf16[64,4096]{1,0:T(8,128)(2,1)} %copy-done.2) | copy-start | bytes 1572868

commit v8 on v7

--- a/solution.py
+++ b/solution.py
@@ -208,7 +208,7 @@
         down_hops = [(p, p - 1) for p in range(1, planes - s + 1)]
         if s == middle:
             up, down = move(up, up_hops), move(down, down_hops)
-            up = down = up + down
+            up = down = up + after(down, lined)
             across = swap(after(over_y, up), 1)
             quad_weights = [weights, over_core, over_y, across]
             lined = after(lined, up)
@@ -217,7 +217,7 @@
             ]
             own, *sides = project([tokens] + first + [up], token_count, quad_weights)
             returned = [move(side, home) for side, home in zip(sides, ways_home)]
-            mine = jnp.concatenate(ranged, axis=1)
+            mine = jnp.concatenate(after(tuple(ranged), own), axis=1)
             mine_over_y = swap(mine, 2)
         else:
             up = down = move(up, up_hops + down_hops)

time: 83.8 us -> 82.4 us (0.983)
  waiting for transfers between devices: 36.6 us -> 34.1 us
  Pallas kernels: 6.51 us -> 8.25 us
  local copies, waits for them, and re-layouts: 3.68 us -> 2.66 us
    ppermute x9, waiting for transfers between devices: 24.2 us -> 14 us  [move(): return lax.ppermute(array, 'expert', pairs)]
    ppermute x7, waiting for transfers between devices: 8 us -> 17.7 us  [swap(): return lax.ppermute(array, 'expert', [(i, i ^ bit) for i in range(n)])]
    ppermute x1, waiting for transfers between devices: 4.39 us -> 2.34 us  [shards(): lax.ppermute(lined, 'groups', [(g, (g + k) % groups) for g in range(group...]
    pallas_call x2, Pallas kernels: 4.76 us -> 6.5 us  [project(): pl.pallas_call(functools.partial(project_kernel, len(parts), rows), out_s...]
    ppermute x9, starting transfers between devices: 18.4 us -> 19.5 us  [move(): return lax.ppermute(array, 'expert', pairs)]
    unnamed x19 -> x16, local copies, waits for them, and re-layouts: 2.14 us -> 1.11 us
  transfers between devices with their start and end apart: 17 -> 17, of which waited for: 10 -> 9; matrix products, arithmetic and copies ran while one was open for 8% -> 8% of each run, Pallas kernels for 7% -> 9%
where the time goes in v8:
time: 82.4 us; the launch traced here: 81.9 us
  waiting for transfers between devices  34.1 us (41%)
  starting transfers between devices  29.5 us (36%)
  Pallas kernels  8.25 us (10%)
  other arithmetic  3.85 us (5%)
  local copies, waits for them, and re-layouts  2.66 us (3%)
  matrix products  2.57 us (3%)
  between operations  1.01 us (1%)
    ppermute x9, starting transfers between devices, move(): return lax.ppermute(array, 'expert', pairs)  19.5 us
    ppermute x7, waiting for transfers between devices, swap(): return lax.ppermute(array, 'expert', [(i, i ^ bit) for i in range(n)])  17.7 us
    ppermute x9, waiting for transfers between devices, move(): return lax.ppermute(array, 'expert', pairs)  14 us
    ppermute x7, starting transfers between devices, swap(): return lax.ppermute(array, 'expert', [(i, i ^ bit) for i in range(n)])  8.41 us
    pallas_call x2, Pallas kernels, project(): pl.pallas_call(functools.partial(project_kernel, len(parts), rows), out_s...  6.5 us
    ppermute x1, waiting for transfers between devices, shards(): lax.ppermute(lined, 'groups', [(g, (g + k) % groups) for g in range(group...  2.34 us
  transfers between devices with their start and end apart: 17, of which 9 were waited for; matrix products, arithmetic and copies ran while one was open for 8% of the time, Pallas kernels for 9%

profile of v8, /device:TPU:0, one launch (start us, length us, event | category | flops | bytes accessed | tf_op | source)
XLA Modules:
  0.0 81.9 jit_solution(13680964398214364513)
XLA Ops:
  0.6 5.9 %collective-permute-start = (bf16[64,4096]{1,0:T(8,128)(2,1)}, bf16[64,4096]{1,0:T(8,128)(2,1)}, u32[]{:S(2)}, u32[]{:S(2)}) collective-permute-start(bf16[64,4096]{1,0:T(8,128)(2,1)} %refs_0_.1), channel_id=1, source_target_pairs={{0,4},{1,5},{2,6},{3,7},{4,8},{5,9},{6,10},{7,11},{8,12},{9,13},{1... | collective-permute-start | bytes 1572872 | tf_op jit(solution)/shard_map/ppermute | solution.py:144
  6.5 1.3 %collective-permute-start.2 = (bf16[64,4096]{1,0:T(8,128)(2,1)}, bf16[64,4096]{1,0:T(8,128)(2,1)}, u32[]{:S(2)}, u32[]{:S(2)}) collective-permute-start(bf16[64,4096]{1,0:T(8,128)(2,1)} %refs_0_.1), channel_id=1, source_target_pairs={{4,0},{5,1},{6,2},{7,3},{8,4},{9,5},{10,6},{11,7},{12,8},{13,9},{1... | collective-permute-start | bytes 1572872 | tf_op jit(solution)/shard_map/ppermute | solution.py:144
  7.8 0.1 collective-permute-start.7
  7.9 1.6 %collective-permute-start.8 = (bf16[128,4096]{1,0:T(8,128)(2,1)}, bf16[128,4096]{1,0:T(8,128)(2,1)}, u32[]{:S(2)}, u32[]{:S(2)}) collective-permute-start(bf16[128,4096]{1,0:T(8,128)(2,1)} %bitcast.17), channel_id=1, source_target_pairs={{0,2},{1,3},{2,0},{3,1},{4,6},{5,7},{6,4},{7,5},{8,10},{9,11},{10,... | collective-permute-start | bytes 3145736 | tf_op jit(solution)/shard_map/ppermute | solution.py:147
  9.5 0.8 %constant_dynamic-slice_fusion = bf16[16,2048]{1,0:T(8,128)(2,1)S(1)} fusion(bf16[16,4096]{1,0:T(8,128)(2,1)} %param.15, s32[]{:T(128)S(6)} %select_n.74), kind=kLoop, calls=%fused_computation.22 | loop fusion | bytes 131076 | tf_op jit(solution)/shard_map/dynamic_slice | solution.py:188
  10.3 2.6 %collective-permute-start.4 = (bf16[16,2048]{1,0:T(8,128)(2,1)S(1)}, bf16[16,2048]{1,0:T(8,128)(2,1)S(1)}, u32[]{:S(2)}, u32[]{:S(2)}) collective-permute-start(bf16[16,2048]{1,0:T(8,128)(2,1)S(1)} %constant_dynamic-slice_fusion), channel_id=1, source_target_pairs={{0,4},{1,5},{2,6},{3,7},{4,0},{5,1},{6,2},{7,3},{8,12},{9,13},{10,... | collective-permute-start | bytes 196616 | tf_op jit(solution)/shard_map/ppermute | solution.py:147
  13.0 0.1 stack.33
  13.2 0.1 add.55
  13.2 0.1 add_select_fusion
  13.3 0.1 select_n.90
  13.4 0.7 iota_compare_fusion
  14.2 1.3 %fusion.4 = f32[64,64]{1,0:T(8,128)S(1)} fusion(bf16[64,4096]{1,0:T(8,128)(2,1)S(1)} %copy-done, bf16[4096,64]{0,1:T(8,128)(2,1)} %param.14), kind=kOutput, calls=%fused_computation.23 | convolution fusion | flops 33554432 | bytes 1064960 | tf_op jit(solution)/shard_map/dot_general | solution.py:163
  15.5 0.9 %select_reduce_fusion = f32[40,64]{1,0:T(8,128)S(1)} fusion(f32[8,64]{1,0:T(8,128)} %bitcast.20, s32[8,64]{1,0:T(8,128)} %bitcast.21, s32[40]{0:T(128)S(1)} %select_n.90), kind=kLoop, calls=%fused_computation.5 | loop fusion | flops 58880 | bytes 14496 | tf_op jit(solution)/shard_map/reduce_sum | solution.py:168
  16.5 0.1 pad_maximum_fusion.2
  16.6 0.1 broadcast_in_dim.70
  16.7 0.1 broadcast_in_dim.71
  16.8 0.3 fusion.refs_4_
  17.2 0.1 fusion.1.refs_1_
  17.3 0.6 collective-permute-done.refs_1_
  17.9 0.7 collective-permute-start.1
  18.6 4.2 %collective-permute-done.2.refs_2_ = bf16[64,4096]{1,0:T(8,128)(2,1)} collective-permute-done((bf16[64,4096]{1,0:T(8,128)(2,1)}, bf16[64,4096]{1,0:T(8,128)(2,1)}, u32[]{:S(2)}, u32[]{:S(2)}) %collective-permute-start.2) | collective-permute-done | bytes 524320 | tf_op jit(solution)/shard_map/ppermute | solution.py:144
  22.8 1.3 %collective-permute-start.3 = (bf16[64,4096]{1,0:T(8,128)(2,1)}, bf16[64,4096]{1,0:T(8,128)(2,1)S(1)}, u32[]{:S(2)}, u32[]{:S(2)}) collective-permute-start(bf16[64,4096]{1,0:T(8,128)(2,1)} %collective-permute-done.2.refs_2_), channel_id=1, source_target_pairs={{4,0},{5,1},{6,2},{7,3},{8,4},{9,5},{10,6},{11,7},{20,16},{21,17},... | collective-permute-start | bytes 1572872 | tf_op jit(solution)/shard_map/ppermute | solution.py:144
  24.1 2.6 %collective-permute-start.5 = (bf16[32,2048]{1,0:T(8,128)(2,1)S(1)}, bf16[32,2048]{1,0:T(8,128)(2,1)S(1)}, u32[]{:S(2)}, u32[]{:S(2)}) collective-permute-start(bf16[32,2048]{1,0:T(8,128)(2,1)S(1)} %pad_maximum_fusion.1), channel_id=1, source_target_pairs={{0,8},{1,9},{2,10},{3,11},{4,12},{5,13},{6,14},{7,15},{8,0},{9,1},... | collective-permute-start | bytes 393224 | tf_op jit(solution)/shard_map/ppermute | solution.py:147
  26.7 16.3 %collective-permute-done.5 = bf16[32,2048]{1,0:T(8,128)(2,1)S(1)} collective-permute-done((bf16[32,2048]{1,0:T(8,128)(2,1)S(1)}, bf16[32,2048]{1,0:T(8,128)(2,1)S(1)}, u32[]{:S(2)}, u32[]{:S(2)}) %collective-permute-start.5) | collective-permute-done | bytes 131104 | tf_op jit(solution)/shard_map/ppermute | solution.py:147
  43.0 0.1 add.58.refs_3_
  43.2 1.6 %collective-permute-start.14 = (bf16[64,2048]{1,0:T(8,128)(2,1)S(1)}, bf16[64,2048]{1,0:T(8,128)(2,1)S(1)}, u32[]{:S(2)}, u32[]{:S(2)}) collective-permute-start(bf16[64,2048]{1,0:T(8,128)(2,1)S(1)} %constant_dynamic-update-slice_fusion), channel_id=1, source_target_pairs={{0,16},{16,0},{1,17},{17,1},{2,18},{18,2},{3,19},{19,3},{4,20},{20... | collective-permute-start | bytes 786440 | tf_op jit(solution)/shard_map/ppermute | solution.py:216
  44.8 1.3 %collective-permute-start.6 = (bf16[64,4096]{1,0:T(8,128)(2,1)S(1)}, bf16[64,4096]{1,0:T(8,128)(2,1)S(1)}, u32[]{:S(2)}, u32[]{:S(2)}) collective-permute-start(bf16[64,4096]{1,0:T(8,128)(2,1)S(1)} %add.58.refs_3_), channel_id=1, source_target_pairs={{8,12},{9,13},{10,14},{11,15},{4,0},{5,1},{6,2},{7,3},{24,28},{25,... | collective-permute-start | bytes 1572872 | tf_op jit(solution)/shard_map/ppermute | solution.py:144
  46.1 3.5 %project.2 = (bf16[16,2048]{1,0:T(8,128)(2,1)S(1)}, bf16[16,2048]{1,0:T(8,128)(2,1)S(1)}, bf16[16,2048]{1,0:T(8,128)(2,1)S(1)}, bf16[16,2048]{1,0:T(8,128)(2,1)S(1)}) custom-call(bf16[64,4096]{1,0:T(8,128)(2,1)S(1)} %copy-done.4, bf16[64,4096]{1,0:T(8,128)(2,1)} %collective-permute-done.refs_1_, bf16[64,4096]{1,0:T(8,128)(2,1)} %collective-permute-done.2.refs_2_, ...), custom_call_target="tpu_custom_call" | custom-call | flops 1024 | bytes 1024 | tf_op jit(solution)/shard_map/project/pallas_call | solution.py:88
  49.6 2.3 %collective-permute-done.14 = bf16[64,2048]{1,0:T(8,128)(2,1)S(1)} collective-permute-done((bf16[64,2048]{1,0:T(8,128)(2,1)S(1)}, bf16[64,2048]{1,0:T(8,128)(2,1)S(1)}, u32[]{:S(2)}, u32[]{:S(2)}) %collective-permute-start.14) | collective-permute-done | bytes 262176 | tf_op jit(solution)/shard_map/ppermute | solution.py:216
  52.0 1.5 %collective-permute-start.15 = (bf16[64,4096]{1,0:T(8,128)(2,1)S(1)}, bf16[64,4096]{1,0:T(8,128)(2,1)S(1)}, u32[]{:S(2)}, u32[]{:S(2)}) collective-permute-start(bf16[64,4096]{1,0:T(8,128)(2,1)S(1)} %constant_dynamic-update-slice_fusion.2.mine_ref), channel_id=1, source_target_pairs={{0,2},{1,3},{2,0},{3,1},{4,6},{5,7},{6,4},{7,5},{8,10},{9,11},{10,... | collective-permute-start | bytes 1572872 | tf_op jit(solution)/shard_map/ppermute | solution.py:147
  53.5 1.3 %collective-permute-start.10 = (bf16[16,2048]{1,0:T(8,128)(2,1)S(1)}, bf16[16,2048]{1,0:T(8,128)(2,1)S(1)}, u32[]{:S(2)}, u32[]{:S(2)}) collective-permute-start(bf16[16,2048]{1,0:T(8,128)(2,1)S(1)} %get-tuple-element.17), channel_id=1, source_target_pairs={{4,0},{5,1},{6,2},{7,3},{8,4},{9,5},{10,6},{11,7},{12,8},{13,9},{1... | collective-permute-start | bytes 196616 | tf_op jit(solution)/shard_map/ppermute | solution.py:144
  54.8 4.5 %collective-permute-start.11 = (bf16[16,2048]{1,0:T(8,128)(2,1)S(1)}, bf16[16,2048]{1,0:T(8,128)(2,1)S(1)}, u32[]{:S(2)}, u32[]{:S(2)}) collective-permute-start(bf16[16,2048]{1,0:T(8,128)(2,1)S(1)} %get-tuple-element.18), channel_id=1, source_target_pairs={{0,4},{1,5},{2,6},{3,7},{4,8},{5,9},{6,10},{7,11},{8,12},{9,13},{1... | collective-permute-start | bytes 196616 | tf_op jit(solution)/shard_map/ppermute | solution.py:144
  59.4 2.0 %collective-permute-done.6.refs_0_ = bf16[64,4096]{1,0:T(8,128)(2,1)S(1)} collective-permute-done((bf16[64,4096]{1,0:T(8,128)(2,1)S(1)}, bf16[64,4096]{1,0:T(8,128)(2,1)S(1)}, u32[]{:S(2)}, u32[]{:S(2)}) %collective-permute-start.6) | collective-permute-done | bytes 524320 | tf_op jit(solution)/shard_map/ppermute | solution.py:144
  61.4 0.8 collective-permute-done.10.refs_1_
  62.2 2.9 %collective-permute-done.12.refs_3_ = bf16[16,2048]{1,0:T(8,128)(2,1)S(1)} collective-permute-done((bf16[16,2048]{1,0:T(8,128)(2,1)S(1)}, bf16[16,2048]{1,0:T(8,128)(2,1)S(1)}, u32[]{:S(2)}, u32[]{:S(2)}) %collective-permute-start.12) | collective-permute-done | bytes 65568 | tf_op jit(solution)/shard_map/ppermute | solution.py:144
  65.0 3.0 %project.3 = bf16[16,2048]{1,0:T(8,128)(2,1)S(1)} custom-call(bf16[64,4096]{1,0:T(8,128)(2,1)S(1)} %collective-permute-done.6.refs_0_, bf16[128,4096]{1,0:T(8,128)(2,1)S(1)} %bitcast.19, bf16[128,4096]{1,0:T(8,128)(2,1)S(1)} %collective-permute-done.7.refs_5_.refs_2_, bf16[128,4096]{1,0:T(8,128)(2,1)} %collective-permute-done.8.refs_6_.refs_3_, ...), custom_call_target="tpu_custom_call" | custom-call | flops 1024 | bytes 1024 | tf_op jit(solution)/shard_map/project/pallas_call | solution.py:88
  68.1 3.2 %collective-permute-start.13 = (bf16[16,2048]{1,0:T(8,128)(2,1)S(1)}, bf16[16,2048]{1,0:T(8,128)(2,1)S(1)}, u32[]{:S(2)}, u32[]{:S(2)}) collective-permute-start(bf16[16,2048]{1,0:T(8,128)(2,1)S(1)} %project.3), channel_id=1, source_target_pairs={{12,0},{13,1},{14,2},{15,3},{0,12},{1,13},{2,14},{3,15},{28,16},{2... | collective-permute-start | bytes 196616 | tf_op jit(solution)/shard_map/ppermute | solution.py:144
  71.3 1.2 %pad_maximum_fusion = bf16[128,4096]{1,0:T(8,128)(2,1)} fusion(bf16[64,4096]{1,0:T(8,128)(2,1)S(1)} %collective-permute-done.15.over_y_ref, bf16[64,4096]{1,0:T(8,128)(2,1)S(1)} %constant_dynamic-update-slice_fusion.2.mine_ref), kind=kLoop, calls=%fused_computation.2 | loop fusion | flops 2097152 | bytes 2097152 | tf_op jit(solution)/shard_map/concatenate | solution.py:230
  72.4 3.6 %collective-permute-done.13.refs_0_ = bf16[16,2048]{1,0:T(8,128)(2,1)S(1)} collective-permute-done((bf16[16,2048]{1,0:T(8,128)(2,1)S(1)}, bf16[16,2048]{1,0:T(8,128)(2,1)S(1)}, u32[]{:S(2)}, u32[]{:S(2)}) %collective-permute-start.13) | collective-permute-done | bytes 65568 | tf_op jit(solution)/shard_map/ppermute | solution.py:144
  76.0 0.1 pad_add_fusion.here_ref
  76.1 0.1 convert_reduce_fusion
  76.2 0.7 combine.2.refs_2_
  77.0 0.4 combine.3
  77.3 0.1 reshape.146
  77.5 1.4 %collective-permute-done.16.rest_ref = bf16[128,4096]{1,0:T(8,128)(2,1)S(1)} collective-permute-done((bf16[128,4096]{1,0:T(8,128)(2,1)}, bf16[128,4096]{1,0:T(8,128)(2,1)S(1)}, u32[]{:S(2)}, u32[]{:S(2)}) %collective-permute-start.16) | collective-permute-done | bytes 1048608 | tf_op jit(solution)/shard_map/ppermute | solution.py:147
  78.9 1.0 %copy-done.3 = bf16[64,4096]{1,0:T(8,128)(2,1)S(1)} copy-done((bf16[64,4096]{1,0:T(8,128)(2,1)S(1)}, bf16[64,4096]{1,0:T(8,128)(2,1)}, u32[]{:S(2)}) %copy-start.3) | copy-done | bytes 524312
  79.9 0.7 assemble.1
  80.6 1.2 %fusion.2 = f32[4,256]{1,0:T(4,128)} fusion(bf16[256,4096]{1,0:T(8,128)(2,1)S(1)} %assemble.1, f32[4,4096]{1,0:T(4,128)S(1)} %reshape.146), kind=kOutput, calls=%fused_computation.8 | convolution fusion | flops 8404992 | bytes 2166784 | tf_op jit(solution)/shard_map/dot_general | solution.py:235
  (36 shorter events, 0.4 us)
Async XLA Ops:
  0.6 13.5 %copy-start = (bf16[64,4096]{1,0:T(8,128)(2,1)S(1)}, bf16[64,4096]{1,0:T(8,128)(2,1)}, u32[]{:S(2)}) copy-start(bf16[64,4096]{1,0:T(8,128)(2,1)} %param.9) | copy-start | bytes 1572868
  0.6 17.3 %collective-permute-start = (bf16[64,4096]{1,0:T(8,128)(2,1)}, bf16[64,4096]{1,0:T(8,128)(2,1)}, u32[]{:S(2)}, u32[]{:S(2)}) collective-permute-start(bf16[64,4096]{1,0:T(8,128)(2,1)} %refs_0_.1), channel_id=1, source_target_pairs={{0,4},{1,5},{2,6},{3,7},{4,8},{5,9},{6,10},{7,11},{8,12},{9,13},{1... | collective-permute-start | bytes 1572872 | tf_op jit(solution)/shard_map/ppermute | solution.py:144
  6.5 16.3 %collective-permute-start.2 = (bf16[64,4096]{1,0:T(8,128)(2,1)}, bf16[64,4096]{1,0:T(8,128)(2,1)}, u32[]{:S(2)}, u32[]{:S(2)}) collective-permute-start(bf16[64,4096]{1,0:T(8,128)(2,1)} %refs_0_.1), channel_id=1, source_target_pairs={{4,0},{5,1},{6,2},{7,3},{8,4},{9,5},{10,6},{11,7},{12,8},{13,9},{1... | collective-permute-start | bytes 1572872 | tf_op jit(solution)/shard_map/ppermute | solution.py:144
  7.8 38.3 %collective-permute-start.7 = (bf16[128,4096]{1,0:T(8,128)(2,1)}, bf16[128,4096]{1,0:T(8,128)(2,1)S(1)}, u32[]{:S(2)}, u32[]{:S(2)}) collective-permute-start(bf16[128,4096]{1,0:T(8,128)(2,1)} %bitcast.16), channel_id=1, source_target_pairs={{0,1},{1,0},{2,3},{3,2},{4,5},{5,4},{6,7},{7,6},{8,9},{9,8},{10,11... | collective-permute-start | bytes 3145736 | tf_op jit(solution)/shard_map/ppermute | solution.py:147
  7.9 35.2 %collective-permute-start.8 = (bf16[128,4096]{1,0:T(8,128)(2,1)}, bf16[128,4096]{1,0:T(8,128)(2,1)}, u32[]{:S(2)}, u32[]{:S(2)}) collective-permute-start(bf16[128,4096]{1,0:T(8,128)(2,1)} %bitcast.17), channel_id=1, source_target_pairs={{0,2},{1,3},{2,0},{3,1},{4,6},{5,7},{6,4},{7,5},{8,10},{9,11},{10,... | collective-permute-start | bytes 3145736 | tf_op jit(solution)/shard_map/ppermute | solution.py:147
  10.3 13.8 %collective-permute-start.4 = (bf16[16,2048]{1,0:T(8,128)(2,1)S(1)}, bf16[16,2048]{1,0:T(8,128)(2,1)S(1)}, u32[]{:S(2)}, u32[]{:S(2)}) collective-permute-start(bf16[16,2048]{1,0:T(8,128)(2,1)S(1)} %constant_dynamic-slice_fusion), channel_id=1, source_target_pairs={{0,4},{1,5},{2,6},{3,7},{4,0},{5,1},{6,2},{7,3},{8,12},{9,13},{10,... | collective-permute-start | bytes 196616 | tf_op jit(solution)/shard_map/ppermute | solution.py:147
  15.5 30.6 %copy-start.1 = (bf16[2,4096,64]{1,2,0:T(8,128)(2,1)S(1)}, bf16[2,4096,64]{1,2,0:T(8,128)(2,1)}, u32[]{:S(2)}) copy-start(bf16[2,4096,64]{1,2,0:T(8,128)(2,1)} %param.13) | copy-start | bytes 3145732
  15.5 30.6 %copy-start.4 = (bf16[64,4096]{1,0:T(8,128)(2,1)S(1)}, bf16[64,4096]{1,0:T(8,128)(2,1)}, u32[]{:S(2)}) copy-start(bf16[64,4096]{1,0:T(8,128)(2,1)} %refs_0_.1) | copy-start | bytes 1572868
  17.9 25.1 %collective-permute-start.1 = (bf16[64,4096]{1,0:T(8,128)(2,1)}, bf16[64,4096]{1,0:T(8,128)(2,1)S(1)}, u32[]{:S(2)}, u32[]{:S(2)}) collective-permute-start(bf16[64,4096]{1,0:T(8,128)(2,1)} %collective-permute-done.refs_1_), channel_id=1, source_target_pairs={{4,8},{5,9},{6,10},{7,11},{8,12},{9,13},{10,14},{11,15},{20,24},{2... | collective-permute-start | bytes 1572872 | tf_op jit(solution)/shard_map/ppermute | solution.py:144
  22.8 20.2 %collective-permute-start.3 = (bf16[64,4096]{1,0:T(8,128)(2,1)}, bf16[64,4096]{1,0:T(8,128)(2,1)S(1)}, u32[]{:S(2)}, u32[]{:S(2)}) collective-permute-start(bf16[64,4096]{1,0:T(8,128)(2,1)} %collective-permute-done.2.refs_2_), channel_id=1, source_target_pairs={{4,0},{5,1},{6,2},{7,3},{8,4},{9,5},{10,6},{11,7},{20,16},{21,17},... | collective-permute-start | bytes 1572872 | tf_op jit(solution)/shard_map/ppermute | solution.py:144
  24.1 18.8 %collective-permute-start.5 = (bf16[32,2048]{1,0:T(8,128)(2,1)S(1)}, bf16[32,2048]{1,0:T(8,128)(2,1)S(1)}, u32[]{:S(2)}, u32[]{:S(2)}) collective-permute-start(bf16[32,2048]{1,0:T(8,128)(2,1)S(1)} %pad_maximum_fusion.1), channel_id=1, source_target_pairs={{0,8},{1,9},{2,10},{3,11},{4,12},{5,13},{6,14},{7,15},{8,0},{9,1},... | collective-permute-start | bytes 393224 | tf_op jit(solution)/shard_map/ppermute | solution.py:147
  43.2 2.9 %collective-permute-start.9 = (bf16[128,4096]{1,0:T(8,128)(2,1)}, bf16[128,4096]{1,0:T(8,128)(2,1)S(1)}, u32[]{:S(2)}, u32[]{:S(2)}) collective-permute-start(bf16[128,4096]{1,0:T(8,128)(2,1)} %collective-permute-done.8.refs_6_.refs_3_), channel_id=1, source_target_pairs={{0,1},{1,0},{2,3},{3,2},{4,5},{5,4},{6,7},{7,6},{8,9},{9,8},{10,11... | collective-permute-start | bytes 3145736 | tf_op jit(solution)/shard_map/ppermute | solution.py:147
  43.2 8.7 %collective-permute-start.14 = (bf16[64,2048]{1,0:T(8,128)(2,1)S(1)}, bf16[64,2048]{1,0:T(8,128)(2,1)S(1)}, u32[]{:S(2)}, u32[]{:S(2)}) collective-permute-start(bf16[64,2048]{1,0:T(8,128)(2,1)S(1)} %constant_dynamic-update-slice_fusion), channel_id=1, source_target_pairs={{0,16},{16,0},{1,17},{17,1},{2,18},{18,2},{3,19},{19,3},{4,20},{20... | collective-permute-start | bytes 786440 | tf_op jit(solution)/shard_map/ppermute | solution.py:216
  44.8 16.6 %collective-permute-start.6 = (bf16[64,4096]{1,0:T(8,128)(2,1)S(1)}, bf16[64,4096]{1,0:T(8,128)(2,1)S(1)}, u32[]{:S(2)}, u32[]{:S(2)}) collective-permute-start(bf16[64,4096]{1,0:T(8,128)(2,1)S(1)} %add.58.refs_3_), channel_id=1, source_target_pairs={{8,12},{9,13},{10,14},{11,15},{4,0},{5,1},{6,2},{7,3},{24,28},{25,... | collective-permute-start | bytes 1572872 | tf_op jit(solution)/shard_map/ppermute | solution.py:144
  52.0 19.3 %collective-permute-start.15 = (bf16[64,4096]{1,0:T(8,128)(2,1)S(1)}, bf16[64,4096]{1,0:T(8,128)(2,1)S(1)}, u32[]{:S(2)}, u32[]{:S(2)}) collective-permute-start(bf16[64,4096]{1,0:T(8,128)(2,1)S(1)} %constant_dynamic-update-slice_fusion.2.mine_ref), channel_id=1, source_target_pairs={{0,2},{1,3},{2,0},{3,1},{4,6},{5,7},{6,4},{7,5},{8,10},{9,11},{10,... | collective-permute-start | bytes 1572872 | tf_op jit(solution)/shard_map/ppermute | solution.py:147
  53.5 8.7 %collective-permute-start.10 = (bf16[16,2048]{1,0:T(8,128)(2,1)S(1)}, bf16[16,2048]{1,0:T(8,128)(2,1)S(1)}, u32[]{:S(2)}, u32[]{:S(2)}) collective-permute-start(bf16[16,2048]{1,0:T(8,128)(2,1)S(1)} %get-tuple-element.17), channel_id=1, source_target_pairs={{4,0},{5,1},{6,2},{7,3},{8,4},{9,5},{10,6},{11,7},{12,8},{13,9},{1... | collective-permute-start | bytes 196616 | tf_op jit(solution)/shard_map/ppermute | solution.py:144
  54.8 7.4 %collective-permute-start.11 = (bf16[16,2048]{1,0:T(8,128)(2,1)S(1)}, bf16[16,2048]{1,0:T(8,128)(2,1)S(1)}, u32[]{:S(2)}, u32[]{:S(2)}) collective-permute-start(bf16[16,2048]{1,0:T(8,128)(2,1)S(1)} %get-tuple-element.18), channel_id=1, source_target_pairs={{0,4},{1,5},{2,6},{3,7},{4,8},{5,9},{6,10},{7,11},{8,12},{9,13},{1... | collective-permute-start | bytes 196616 | tf_op jit(solution)/shard_map/ppermute | solution.py:144
  59.3 5.7 %collective-permute-start.12 = (bf16[16,2048]{1,0:T(8,128)(2,1)S(1)}, bf16[16,2048]{1,0:T(8,128)(2,1)S(1)}, u32[]{:S(2)}, u32[]{:S(2)}) collective-permute-start(bf16[16,2048]{1,0:T(8,128)(2,1)S(1)} %get-tuple-element.19), channel_id=1, source_target_pairs={{8,0},{9,1},{10,2},{11,3},{12,4},{13,5},{14,6},{15,7},{0,8},{1,9},... | collective-permute-start | bytes 196616 | tf_op jit(solution)/shard_map/ppermute | solution.py:144
  68.1 8.1 %copy-start.6 = (s32[1,64]{1,0:T(1,128)S(1)}, s32[1,64]{1,0:T(1,128)}, u32[]{:S(2)}) copy-start(s32[1,64]{1,0:T(1,128)} %param.12) | copy-start | bytes 772
  68.1 8.0 %collective-permute-start.13 = (bf16[16,2048]{1,0:T(8,128)(2,1)S(1)}, bf16[16,2048]{1,0:T(8,128)(2,1)S(1)}, u32[]{:S(2)}, u32[]{:S(2)}) collective-permute-start(bf16[16,2048]{1,0:T(8,128)(2,1)S(1)} %project.3), channel_id=1, source_target_pairs={{12,0},{13,1},{14,2},{15,3},{0,12},{1,13},{2,14},{3,15},{28,16},{2... | collective-permute-start | bytes 196616 | tf_op jit(solution)/shard_map/ppermute | solution.py:144
  71.3 5.6 %copy-start.2 = (bf16[64,4096]{1,0:T(8,128)(2,1)}, bf16[64,4096]{1,0:T(8,128)(2,1)S(1)}, u32[]{:S(2)}) copy-start(bf16[64,4096]{1,0:T(8,128)(2,1)S(1)} %collective-permute-done.15.over_y_ref) | copy-start | bytes 1572868
  76.0 2.9 %collective-permute-start.16 = (bf16[128,4096]{1,0:T(8,128)(2,1)}, bf16[128,4096]{1,0:T(8,128)(2,1)S(1)}, u32[]{:S(2)}, u32[]{:S(2)}) collective-permute-start(bf16[128,4096]{1,0:T(8,128)(2,1)} %pad_maximum_fusion), channel_id=1, source_target_pairs={{0,1},{1,0},{2,3},{3,2},{4,5},{5,4},{6,7},{7,6},{8,9},{9,8},{10,11... | collective-permute-start | bytes 3145736 | tf_op jit(solution)/shard_map/ppermute | solution.py:147
  77.5 3.2 %copy-start.5 = (f32[4,4096]{1,0:T(4,128)}, f32[4,4096]{1,0:T(4,128)S(1)}, u32[]{:S(2)}) copy-start(f32[4,4096]{1,0:T(4,128)S(1)} %reshape.146) | copy-start | bytes 196612
  78.9 1.0 %copy-start.3 = (bf16[64,4096]{1,0:T(8,128)(2,1)S(1)}, bf16[64,4096]{1,0:T(8,128)(2,1)}, u32[]{:S(2)}) copy-start(bf16[64,4096]{1,0:T(8,128)(2,1)} %copy-done.2) | copy-start | bytes 1572868

commit v9 on v8

--- a/solution.py
+++ b/solution.py
@@ -97,14 +97,14 @@
     )(*parts, *weights)
 
 
-def assemble_kernel(planes, groups, here_ref, mine_ref, over_y_ref, rest_ref, out_ref):
+def assemble_kernel(order, groups, here_ref, mine_ref, over_y_ref, rest_ref, out_ref):
     span = mine_ref.shape[0]
-    rows, columns = span // planes, out_ref.shape[1] // groups
+    rows, columns = span // len(order), out_ref.shape[1] // groups
     sources = (mine_ref, rest_ref, over_y_ref, rest_ref)
     for rel in range(QUAD):
         base = span if rel == 3 else 0
-        for d in range(planes):
-            home = (here_ref[0] ^ d) * QUAD + (here_ref[1] ^ rel)
+        for d, other in enumerate(order):
+            home = (here_ref[0] ^ other) * QUAD + (here_ref[1] ^ rel)
             row = pl.multiple_of(home * rows, rows)
             for k in range(groups):
                 column = pl.multiple_of(lax.rem(here_ref[2] + (groups - k), groups) * columns, columns)
@@ -113,11 +113,11 @@
                 ]
 
 
-def assemble(here, mine, over_y, rest, planes, groups):
+def assemble(here, mine, over_y, rest, order, groups):
     span, width = mine.shape
     vmem = pl.BlockSpec(memory_space=pltpu.VMEM)
     return pl.pallas_call(
-        functools.partial(assemble_kernel, planes, groups),
+        functools.partial(assemble_kernel, order, groups),
         out_shape=jax.ShapeDtypeStruct((span * QUAD, width), mine.dtype),
         in_specs=[pl.BlockSpec(memory_space=pltpu.SMEM), vmem, vmem, vmem],
         out_specs=vmem,
@@ -186,7 +186,9 @@
 
     width = queries.shape[1] // groups
     lined = lax.dynamic_slice_in_dim(queries, group * width, width, axis=1)
-    lined = jnp.concatenate([lined, swap(lined, QUAD)], axis=0)
+    bit, order = planes // 2, [0]
+    lined = jnp.concatenate([lined, swap(lined, bit * QUAD)], axis=0)
+    order = order + [o ^ bit for o in order]
 
     middle = (planes + 1) // 2
     up, down = tokens, tokens
@@ -198,10 +200,11 @@
         first.extend([up, down])
     over_core = swap(weights, 1)
     lined = after(lined, wide, wide_late, *first)
-    bit = 2 * QUAD
-    while bit < n:
-        lined = jnp.concatenate([lined, swap(lined, bit)], axis=0)
-        bit *= 2
+    bit //= 2
+    while bit:
+        lined = jnp.concatenate([lined, swap(lined, bit * QUAD)], axis=0)
+        order = order + [o ^ bit for o in order]
+        bit //= 2
 
     for s in range(middle, planes):
         up_hops = [(p, p + 1) for p in range(s - 1, planes - 1)]
@@ -229,7 +232,7 @@
 
     rest = swap(after(jnp.concatenate([mine, mine_over_y], axis=0), late), 1)
     here = jnp.stack([plane, spot, group]).astype(jnp.int32)
-    all_queries = assemble(here, mine, mine_over_y, rest, planes, groups)
+    all_queries = assemble(here, mine, mine_over_y, rest, order, groups)
     sketches = combine([late], wide_late, early, counts)
     sketches = sketches.reshape(EX_DEV, RANK * RANK)
     scores = lax.dot_general(sketches.astype(jnp.bfloat16), all_queries, NT, preferred_element_type=jnp.float32)

time: 82.4 us -> 79 us (0.959)
  waiting for transfers between devices: 34.1 us -> 30.7 us
    ppermute x7, waiting for transfers between devices: 17.7 us -> 14.5 us  [swap(): return lax.ppermute(array, 'expert', [(i, i ^ bit) for i in range(n)])]
  transfers between devices with their start and end apart: 17 -> 17, of which waited for: 9 -> 10; matrix products, arithmetic and copies ran while one was open for 8% -> 9% of each run, Pallas kernels for 9% -> 10%
where the time goes in v9:
time: 79 us; the launch traced here: 78.5 us
  waiting for transfers between devices  30.7 us (39%)
  starting transfers between devices  29.5 us (37%)
  Pallas kernels  8.25 us (10%)
  other arithmetic  3.85 us (5%)
  local copies, waits for them, and re-layouts  2.66 us (3%)
  matrix products  2.58 us (3%)
  between operations  1 us (1%)
    ppermute x9, starting transfers between devices, move(): return lax.ppermute(array, 'expert', pairs)  19.5 us
    ppermute x7, waiting for transfers between devices, swap(): return lax.ppermute(array, 'expert', [(i, i ^ bit) for i in range(n)])  14.5 us
    ppermute x9, waiting for transfers between devices, move(): return lax.ppermute(array, 'expert', pairs)  13.8 us
    ppermute x7, starting transfers between devices, swap(): return lax.ppermute(array, 'expert', [(i, i ^ bit) for i in range(n)])  8.45 us
    pallas_call x2, Pallas kernels, project(): pl.pallas_call(functools.partial(project_kernel, len(parts), rows), out_s...  6.5 us
    ppermute x1, waiting for transfers between devices, shards(): lax.ppermute(lined, 'groups', [(g, (g + k) % groups) for g in range(group...  2.34 us
  transfers between devices with their start and end apart: 17, of which 10 were waited for; matrix products, arithmetic and copies ran while one was open for 9% of the time, Pallas kernels for 10%

profile of v9, /device:TPU:0, one launch (start us, length us, event | category | flops | bytes accessed | tf_op | source)
XLA Modules:
  0.0 78.5 jit_solution(7903385908949726403)
XLA Ops:
  0.6 5.9 %collective-permute-start = (bf16[64,4096]{1,0:T(8,128)(2,1)}, bf16[64,4096]{1,0:T(8,128)(2,1)}, u32[]{:S(2)}, u32[]{:S(2)}) collective-permute-start(bf16[64,4096]{1,0:T(8,128)(2,1)} %refs_0_.1), channel_id=1, source_target_pairs={{0,4},{1,5},{2,6},{3,7},{4,8},{5,9},{6,10},{7,11},{8,12},{9,13},{1... | collective-permute-start | bytes 1572872 | tf_op jit(solution)/shard_map/ppermute | solution.py:144
  6.5 1.3 %collective-permute-start.2 = (bf16[64,4096]{1,0:T(8,128)(2,1)}, bf16[64,4096]{1,0:T(8,128)(2,1)}, u32[]{:S(2)}, u32[]{:S(2)}) collective-permute-start(bf16[64,4096]{1,0:T(8,128)(2,1)} %refs_0_.1), channel_id=1, source_target_pairs={{4,0},{5,1},{6,2},{7,3},{8,4},{9,5},{10,6},{11,7},{12,8},{13,9},{1... | collective-permute-start | bytes 1572872 | tf_op jit(solution)/shard_map/ppermute | solution.py:144
  7.9 1.6 %collective-permute-start.8 = (bf16[128,4096]{1,0:T(8,128)(2,1)}, bf16[128,4096]{1,0:T(8,128)(2,1)}, u32[]{:S(2)}, u32[]{:S(2)}) collective-permute-start(bf16[128,4096]{1,0:T(8,128)(2,1)} %bitcast.17), channel_id=1, source_target_pairs={{0,2},{1,3},{2,0},{3,1},{4,6},{5,7},{6,4},{7,5},{8,10},{9,11},{10,... | collective-permute-start | bytes 3145736 | tf_op jit(solution)/shard_map/ppermute | solution.py:147
  9.5 0.8 %constant_dynamic-slice_fusion = bf16[16,2048]{1,0:T(8,128)(2,1)S(1)} fusion(bf16[16,4096]{1,0:T(8,128)(2,1)} %param.15, s32[]{:T(128)S(6)} %select_n.74), kind=kLoop, calls=%fused_computation.22 | loop fusion | bytes 131076 | tf_op jit(solution)/shard_map/dynamic_slice | solution.py:188
  10.3 2.9 %collective-permute-start.4 = (bf16[16,2048]{1,0:T(8,128)(2,1)S(1)}, bf16[16,2048]{1,0:T(8,128)(2,1)S(1)}, u32[]{:S(2)}, u32[]{:S(2)}) collective-permute-start(bf16[16,2048]{1,0:T(8,128)(2,1)S(1)} %constant_dynamic-slice_fusion), channel_id=1, source_target_pairs={{0,8},{1,9},{2,10},{3,11},{4,12},{5,13},{6,14},{7,15},{8,0},{9,1},... | collective-permute-start | bytes 196616 | tf_op jit(solution)/shard_map/ppermute | solution.py:147
  13.2 0.1 stack.33
  13.4 0.1 add.55
  13.5 0.1 add_select_fusion
  13.5 0.1 select_n.90
  13.6 0.7 iota_compare_fusion
  14.4 1.3 %fusion.4 = f32[64,64]{1,0:T(8,128)S(1)} fusion(bf16[64,4096]{1,0:T(8,128)(2,1)S(1)} %copy-done, bf16[4096,64]{0,1:T(8,128)(2,1)} %param.14), kind=kOutput, calls=%fused_computation.23 | convolution fusion | flops 33554432 | bytes 1064960 | tf_op jit(solution)/shard_map/dot_general | solution.py:163
  15.7 0.9 %select_reduce_fusion = f32[40,64]{1,0:T(8,128)S(1)} fusion(f32[8,64]{1,0:T(8,128)} %bitcast.20, s32[8,64]{1,0:T(8,128)} %bitcast.21, s32[40]{0:T(128)S(1)} %select_n.90), kind=kLoop, calls=%fused_computation.5 | loop fusion | flops 58880 | bytes 14496 | tf_op jit(solution)/shard_map/reduce_sum | solution.py:168
  16.7 0.1 pad_maximum_fusion.2
  16.8 0.1 broadcast_in_dim.70
  16.9 0.1 broadcast_in_dim.71
  17.1 0.3 fusion.refs_4_
  17.4 0.1 fusion.1.refs_1_
  17.5 0.4 collective-permute-done.refs_1_
  17.9 0.7 collective-permute-start.1
  18.6 4.2 %collective-permute-done.2.refs_2_ = bf16[64,4096]{1,0:T(8,128)(2,1)} collective-permute-done((bf16[64,4096]{1,0:T(8,128)(2,1)}, bf16[64,4096]{1,0:T(8,128)(2,1)}, u32[]{:S(2)}, u32[]{:S(2)}) %collective-permute-start.2) | collective-permute-done | bytes 524320 | tf_op jit(solution)/shard_map/ppermute | solution.py:144
  22.8 1.3 %collective-permute-start.3 = (bf16[64,4096]{1,0:T(8,128)(2,1)}, bf16[64,4096]{1,0:T(8,128)(2,1)S(1)}, u32[]{:S(2)}, u32[]{:S(2)}) collective-permute-start(bf16[64,4096]{1,0:T(8,128)(2,1)} %collective-permute-done.2.refs_2_), channel_id=1, source_target_pairs={{4,0},{5,1},{6,2},{7,3},{8,4},{9,5},{10,6},{11,7},{20,16},{21,17},... | collective-permute-start | bytes 1572872 | tf_op jit(solution)/shard_map/ppermute | solution.py:144
  24.1 0.9 %collective-permute-done.4 = bf16[16,2048]{1,0:T(8,128)(2,1)S(1)} collective-permute-done((bf16[16,2048]{1,0:T(8,128)(2,1)S(1)}, bf16[16,2048]{1,0:T(8,128)(2,1)S(1)}, u32[]{:S(2)}, u32[]{:S(2)}) %collective-permute-start.4) | collective-permute-done | bytes 65568 | tf_op jit(solution)/shard_map/ppermute | solution.py:147
  25.0 2.3 %collective-permute-start.5 = (bf16[32,2048]{1,0:T(8,128)(2,1)S(1)}, bf16[32,2048]{1,0:T(8,128)(2,1)S(1)}, u32[]{:S(2)}, u32[]{:S(2)}) collective-permute-start(bf16[32,2048]{1,0:T(8,128)(2,1)S(1)} %pad_maximum_fusion.1), channel_id=1, source_target_pairs={{0,4},{1,5},{2,6},{3,7},{4,0},{5,1},{6,2},{7,3},{8,12},{9,13},{10,... | collective-permute-start | bytes 393224 | tf_op jit(solution)/shard_map/ppermute | solution.py:147
  27.3 12.2 %collective-permute-done.5 = bf16[32,2048]{1,0:T(8,128)(2,1)S(1)} collective-permute-done((bf16[32,2048]{1,0:T(8,128)(2,1)S(1)}, bf16[32,2048]{1,0:T(8,128)(2,1)S(1)}, u32[]{:S(2)}, u32[]{:S(2)}) %collective-permute-start.5) | collective-permute-done | bytes 131104 | tf_op jit(solution)/shard_map/ppermute | solution.py:147
  39.5 0.1 add.58.refs_3_
  39.7 1.6 %collective-permute-start.14 = (bf16[64,2048]{1,0:T(8,128)(2,1)S(1)}, bf16[64,2048]{1,0:T(8,128)(2,1)S(1)}, u32[]{:S(2)}, u32[]{:S(2)}) collective-permute-start(bf16[64,2048]{1,0:T(8,128)(2,1)S(1)} %constant_dynamic-update-slice_fusion), channel_id=1, source_target_pairs={{0,16},{16,0},{1,17},{17,1},{2,18},{18,2},{3,19},{19,3},{4,20},{20... | collective-permute-start | bytes 786440 | tf_op jit(solution)/shard_map/ppermute | solution.py:219
  41.3 1.3 %collective-permute-start.6 = (bf16[64,4096]{1,0:T(8,128)(2,1)S(1)}, bf16[64,4096]{1,0:T(8,128)(2,1)S(1)}, u32[]{:S(2)}, u32[]{:S(2)}) collective-permute-start(bf16[64,4096]{1,0:T(8,128)(2,1)S(1)} %add.58.refs_3_), channel_id=1, source_target_pairs={{8,12},{9,13},{10,14},{11,15},{4,0},{5,1},{6,2},{7,3},{24,28},{25,... | collective-permute-start | bytes 1572872 | tf_op jit(solution)/shard_map/ppermute | solution.py:144
  42.6 3.5 %project.2 = (bf16[16,2048]{1,0:T(8,128)(2,1)S(1)}, bf16[16,2048]{1,0:T(8,128)(2,1)S(1)}, bf16[16,2048]{1,0:T(8,128)(2,1)S(1)}, bf16[16,2048]{1,0:T(8,128)(2,1)S(1)}) custom-call(bf16[64,4096]{1,0:T(8,128)(2,1)S(1)} %copy-done.4, bf16[64,4096]{1,0:T(8,128)(2,1)} %collective-permute-done.refs_1_, bf16[64,4096]{1,0:T(8,128)(2,1)} %collective-permute-done.2.refs_2_, ...), custom_call_target="tpu_custom_call" | custom-call | flops 1024 | bytes 1024 | tf_op jit(solution)/shard_map/project/pallas_call | solution.py:88
  46.1 2.3 %collective-permute-done.14 = bf16[64,2048]{1,0:T(8,128)(2,1)S(1)} collective-permute-done((bf16[64,2048]{1,0:T(8,128)(2,1)S(1)}, bf16[64,2048]{1,0:T(8,128)(2,1)S(1)}, u32[]{:S(2)}, u32[]{:S(2)}) %collective-permute-start.14) | collective-permute-done | bytes 262176 | tf_op jit(solution)/shard_map/ppermute | solution.py:219
  48.5 1.6 %collective-permute-start.15 = (bf16[64,4096]{1,0:T(8,128)(2,1)S(1)}, bf16[64,4096]{1,0:T(8,128)(2,1)S(1)}, u32[]{:S(2)}, u32[]{:S(2)}) collective-permute-start(bf16[64,4096]{1,0:T(8,128)(2,1)S(1)} %constant_dynamic-update-slice_fusion.2.mine_ref), channel_id=1, source_target_pairs={{0,2},{1,3},{2,0},{3,1},{4,6},{5,7},{6,4},{7,5},{8,10},{9,11},{10,... | collective-permute-start | bytes 1572872 | tf_op jit(solution)/shard_map/ppermute | solution.py:147
  50.1 1.3 %collective-permute-start.10 = (bf16[16,2048]{1,0:T(8,128)(2,1)S(1)}, bf16[16,2048]{1,0:T(8,128)(2,1)S(1)}, u32[]{:S(2)}, u32[]{:S(2)}) collective-permute-start(bf16[16,2048]{1,0:T(8,128)(2,1)S(1)} %get-tuple-element.17), channel_id=1, source_target_pairs={{4,0},{5,1},{6,2},{7,3},{8,4},{9,5},{10,6},{11,7},{12,8},{13,9},{1... | collective-permute-start | bytes 196616 | tf_op jit(solution)/shard_map/ppermute | solution.py:144
  51.4 4.5 %collective-permute-start.11 = (bf16[16,2048]{1,0:T(8,128)(2,1)S(1)}, bf16[16,2048]{1,0:T(8,128)(2,1)S(1)}, u32[]{:S(2)}, u32[]{:S(2)}) collective-permute-start(bf16[16,2048]{1,0:T(8,128)(2,1)S(1)} %get-tuple-element.18), channel_id=1, source_target_pairs={{0,4},{1,5},{2,6},{3,7},{4,8},{5,9},{6,10},{7,11},{8,12},{9,13},{1... | collective-permute-start | bytes 196616 | tf_op jit(solution)/shard_map/ppermute | solution.py:144
  56.0 1.9 %collective-permute-done.6.refs_0_ = bf16[64,4096]{1,0:T(8,128)(2,1)S(1)} collective-permute-done((bf16[64,4096]{1,0:T(8,128)(2,1)S(1)}, bf16[64,4096]{1,0:T(8,128)(2,1)S(1)}, u32[]{:S(2)}, u32[]{:S(2)}) %collective-permute-start.6) | collective-permute-done | bytes 524320 | tf_op jit(solution)/shard_map/ppermute | solution.py:144
  57.9 0.8 %collective-permute-done.10.refs_1_ = bf16[16,2048]{1,0:T(8,128)(2,1)S(1)} collective-permute-done((bf16[16,2048]{1,0:T(8,128)(2,1)S(1)}, bf16[16,2048]{1,0:T(8,128)(2,1)S(1)}, u32[]{:S(2)}, u32[]{:S(2)}) %collective-permute-start.10) | collective-permute-done | bytes 65568 | tf_op jit(solution)/shard_map/ppermute | solution.py:144
  58.7 3.0 %collective-permute-done.12.refs_3_ = bf16[16,2048]{1,0:T(8,128)(2,1)S(1)} collective-permute-done((bf16[16,2048]{1,0:T(8,128)(2,1)S(1)}, bf16[16,2048]{1,0:T(8,128)(2,1)S(1)}, u32[]{:S(2)}, u32[]{:S(2)}) %collective-permute-start.12) | collective-permute-done | bytes 65568 | tf_op jit(solution)/shard_map/ppermute | solution.py:144
  61.7 3.0 %project.3 = bf16[16,2048]{1,0:T(8,128)(2,1)S(1)} custom-call(bf16[64,4096]{1,0:T(8,128)(2,1)S(1)} %collective-permute-done.6.refs_0_, bf16[128,4096]{1,0:T(8,128)(2,1)S(1)} %bitcast.19, bf16[128,4096]{1,0:T(8,128)(2,1)S(1)} %collective-permute-done.7.refs_5_.refs_2_, bf16[128,4096]{1,0:T(8,128)(2,1)} %collective-permute-done.8.refs_6_.refs_3_, ...), custom_call_target="tpu_custom_call" | custom-call | flops 1024 | bytes 1024 | tf_op jit(solution)/shard_map/project/pallas_call | solution.py:88
  64.7 3.2 %collective-permute-start.13 = (bf16[16,2048]{1,0:T(8,128)(2,1)S(1)}, bf16[16,2048]{1,0:T(8,128)(2,1)S(1)}, u32[]{:S(2)}, u32[]{:S(2)}) collective-permute-start(bf16[16,2048]{1,0:T(8,128)(2,1)S(1)} %project.3), channel_id=1, source_target_pairs={{12,0},{13,1},{14,2},{15,3},{0,12},{1,13},{2,14},{3,15},{28,16},{2... | collective-permute-start | bytes 196616 | tf_op jit(solution)/shard_map/ppermute | solution.py:144
  67.9 1.2 %pad_maximum_fusion = bf16[128,4096]{1,0:T(8,128)(2,1)} fusion(bf16[64,4096]{1,0:T(8,128)(2,1)S(1)} %collective-permute-done.15.over_y_ref, bf16[64,4096]{1,0:T(8,128)(2,1)S(1)} %constant_dynamic-update-slice_fusion.2.mine_ref), kind=kLoop, calls=%fused_computation.2 | loop fusion | flops 2097152 | bytes 2097152 | tf_op jit(solution)/shard_map/concatenate | solution.py:233
  69.0 3.6 %collective-permute-done.13.refs_0_ = bf16[16,2048]{1,0:T(8,128)(2,1)S(1)} collective-permute-done((bf16[16,2048]{1,0:T(8,128)(2,1)S(1)}, bf16[16,2048]{1,0:T(8,128)(2,1)S(1)}, u32[]{:S(2)}, u32[]{:S(2)}) %collective-permute-start.13) | collective-permute-done | bytes 65568 | tf_op jit(solution)/shard_map/ppermute | solution.py:144
  72.7 0.1 pad_add_fusion.here_ref
  72.7 0.1 convert_reduce_fusion
  72.8 0.7 combine.2.refs_2_
  73.6 0.4 combine.3
  74.0 0.1 reshape.146
  74.1 1.4 %collective-permute-done.16.rest_ref = bf16[128,4096]{1,0:T(8,128)(2,1)S(1)} collective-permute-done((bf16[128,4096]{1,0:T(8,128)(2,1)}, bf16[128,4096]{1,0:T(8,128)(2,1)S(1)}, u32[]{:S(2)}, u32[]{:S(2)}) %collective-permute-start.16) | collective-permute-done | bytes 1048608 | tf_op jit(solution)/shard_map/ppermute | solution.py:147
  75.5 1.0 %copy-done.3 = bf16[64,4096]{1,0:T(8,128)(2,1)S(1)} copy-done((bf16[64,4096]{1,0:T(8,128)(2,1)S(1)}, bf16[64,4096]{1,0:T(8,128)(2,1)}, u32[]{:S(2)}) %copy-start.3) | copy-done | bytes 524312
  76.6 0.7 assemble.1
  77.3 1.2 %fusion.2 = f32[4,256]{1,0:T(4,128)} fusion(bf16[256,4096]{1,0:T(8,128)(2,1)S(1)} %assemble.1, f32[4,4096]{1,0:T(4,128)S(1)} %reshape.146), kind=kOutput, calls=%fused_computation.8 | convolution fusion | flops 8404992 | bytes 2166784 | tf_op jit(solution)/shard_map/dot_general | solution.py:238
  (36 shorter events, 0.5 us)
Async XLA Ops:
  0.6 13.7 %copy-start = (bf16[64,4096]{1,0:T(8,128)(2,1)S(1)}, bf16[64,4096]{1,0:T(8,128)(2,1)}, u32[]{:S(2)}) copy-start(bf16[64,4096]{1,0:T(8,128)(2,1)} %param.9) | copy-start | bytes 1572868
  0.6 17.3 %collective-permute-start = (bf16[64,4096]{1,0:T(8,128)(2,1)}, bf16[64,4096]{1,0:T(8,128)(2,1)}, u32[]{:S(2)}, u32[]{:S(2)}) collective-permute-start(bf16[64,4096]{1,0:T(8,128)(2,1)} %refs_0_.1), channel_id=1, source_target_pairs={{0,4},{1,5},{2,6},{3,7},{4,8},{5,9},{6,10},{7,11},{8,12},{9,13},{1... | collective-permute-start | bytes 1572872 | tf_op jit(solution)/shard_map/ppermute | solution.py:144
  6.5 16.3 %collective-permute-start.2 = (bf16[64,4096]{1,0:T(8,128)(2,1)}, bf16[64,4096]{1,0:T(8,128)(2,1)}, u32[]{:S(2)}, u32[]{:S(2)}) collective-permute-start(bf16[64,4096]{1,0:T(8,128)(2,1)} %refs_0_.1), channel_id=1, source_target_pairs={{4,0},{5,1},{6,2},{7,3},{8,4},{9,5},{10,6},{11,7},{12,8},{13,9},{1... | collective-permute-start | bytes 1572872 | tf_op jit(solution)/shard_map/ppermute | solution.py:144
  7.8 34.8 %collective-permute-start.7 = (bf16[128,4096]{1,0:T(8,128)(2,1)}, bf16[128,4096]{1,0:T(8,128)(2,1)S(1)}, u32[]{:S(2)}, u32[]{:S(2)}) collective-permute-start(bf16[128,4096]{1,0:T(8,128)(2,1)} %bitcast.16), channel_id=1, source_target_pairs={{0,1},{1,0},{2,3},{3,2},{4,5},{5,4},{6,7},{7,6},{8,9},{9,8},{10,11... | collective-permute-start | bytes 3145736 | tf_op jit(solution)/shard_map/ppermute | solution.py:147
  7.9 31.8 %collective-permute-start.8 = (bf16[128,4096]{1,0:T(8,128)(2,1)}, bf16[128,4096]{1,0:T(8,128)(2,1)}, u32[]{:S(2)}, u32[]{:S(2)}) collective-permute-start(bf16[128,4096]{1,0:T(8,128)(2,1)} %bitcast.17), channel_id=1, source_target_pairs={{0,2},{1,3},{2,0},{3,1},{4,6},{5,7},{6,4},{7,5},{8,10},{9,11},{10,... | collective-permute-start | bytes 3145736 | tf_op jit(solution)/shard_map/ppermute | solution.py:147
  10.3 14.7 %collective-permute-start.4 = (bf16[16,2048]{1,0:T(8,128)(2,1)S(1)}, bf16[16,2048]{1,0:T(8,128)(2,1)S(1)}, u32[]{:S(2)}, u32[]{:S(2)}) collective-permute-start(bf16[16,2048]{1,0:T(8,128)(2,1)S(1)} %constant_dynamic-slice_fusion), channel_id=1, source_target_pairs={{0,8},{1,9},{2,10},{3,11},{4,12},{5,13},{6,14},{7,15},{8,0},{9,1},... | collective-permute-start | bytes 196616 | tf_op jit(solution)/shard_map/ppermute | solution.py:147
  15.7 26.9 %copy-start.1 = (bf16[2,4096,64]{1,2,0:T(8,128)(2,1)S(1)}, bf16[2,4096,64]{1,2,0:T(8,128)(2,1)}, u32[]{:S(2)}) copy-start(bf16[2,4096,64]{1,2,0:T(8,128)(2,1)} %param.13) | copy-start | bytes 3145732
  15.7 26.9 %copy-start.4 = (bf16[64,4096]{1,0:T(8,128)(2,1)S(1)}, bf16[64,4096]{1,0:T(8,128)(2,1)}, u32[]{:S(2)}) copy-start(bf16[64,4096]{1,0:T(8,128)(2,1)} %refs_0_.1) | copy-start | bytes 1572868
  17.9 21.6 %collective-permute-start.1 = (bf16[64,4096]{1,0:T(8,128)(2,1)}, bf16[64,4096]{1,0:T(8,128)(2,1)S(1)}, u32[]{:S(2)}, u32[]{:S(2)}) collective-permute-start(bf16[64,4096]{1,0:T(8,128)(2,1)} %collective-permute-done.refs_1_), channel_id=1, source_target_pairs={{4,8},{5,9},{6,10},{7,11},{8,12},{9,13},{10,14},{11,15},{20,24},{2... | collective-permute-start | bytes 1572872 | tf_op jit(solution)/shard_map/ppermute | solution.py:144
  22.8 16.7 %collective-permute-start.3 = (bf16[64,4096]{1,0:T(8,128)(2,1)}, bf16[64,4096]{1,0:T(8,128)(2,1)S(1)}, u32[]{:S(2)}, u32[]{:S(2)}) collective-permute-start(bf16[64,4096]{1,0:T(8,128)(2,1)} %collective-permute-done.2.refs_2_), channel_id=1, source_target_pairs={{4,0},{5,1},{6,2},{7,3},{8,4},{9,5},{10,6},{11,7},{20,16},{21,17},... | collective-permute-start | bytes 1572872 | tf_op jit(solution)/shard_map/ppermute | solution.py:144
  25.0 14.4 %collective-permute-start.5 = (bf16[32,2048]{1,0:T(8,128)(2,1)S(1)}, bf16[32,2048]{1,0:T(8,128)(2,1)S(1)}, u32[]{:S(2)}, u32[]{:S(2)}) collective-permute-start(bf16[32,2048]{1,0:T(8,128)(2,1)S(1)} %pad_maximum_fusion.1), channel_id=1, source_target_pairs={{0,4},{1,5},{2,6},{3,7},{4,0},{5,1},{6,2},{7,3},{8,12},{9,13},{10,... | collective-permute-start | bytes 393224 | tf_op jit(solution)/shard_map/ppermute | solution.py:147
  39.7 2.9 %collective-permute-start.9 = (bf16[128,4096]{1,0:T(8,128)(2,1)}, bf16[128,4096]{1,0:T(8,128)(2,1)S(1)}, u32[]{:S(2)}, u32[]{:S(2)}) collective-permute-start(bf16[128,4096]{1,0:T(8,128)(2,1)} %collective-permute-done.8.refs_6_.refs_3_), channel_id=1, source_target_pairs={{0,1},{1,0},{2,3},{3,2},{4,5},{5,4},{6,7},{7,6},{8,9},{9,8},{10,11... | collective-permute-start | bytes 3145736 | tf_op jit(solution)/shard_map/ppermute | solution.py:147
  39.7 8.7 %collective-permute-start.14 = (bf16[64,2048]{1,0:T(8,128)(2,1)S(1)}, bf16[64,2048]{1,0:T(8,128)(2,1)S(1)}, u32[]{:S(2)}, u32[]{:S(2)}) collective-permute-start(bf16[64,2048]{1,0:T(8,128)(2,1)S(1)} %constant_dynamic-update-slice_fusion), channel_id=1, source_target_pairs={{0,16},{16,0},{1,17},{17,1},{2,18},{18,2},{3,19},{19,3},{4,20},{20... | collective-permute-start | bytes 786440 | tf_op jit(solution)/shard_map/ppermute | solution.py:219
  41.3 16.6 %collective-permute-start.6 = (bf16[64,4096]{1,0:T(8,128)(2,1)S(1)}, bf16[64,4096]{1,0:T(8,128)(2,1)S(1)}, u32[]{:S(2)}, u32[]{:S(2)}) collective-permute-start(bf16[64,4096]{1,0:T(8,128)(2,1)S(1)} %add.58.refs_3_), channel_id=1, source_target_pairs={{8,12},{9,13},{10,14},{11,15},{4,0},{5,1},{6,2},{7,3},{24,28},{25,... | collective-permute-start | bytes 1572872 | tf_op jit(solution)/shard_map/ppermute | solution.py:144
  48.5 19.4 %collective-permute-start.15 = (bf16[64,4096]{1,0:T(8,128)(2,1)S(1)}, bf16[64,4096]{1,0:T(8,128)(2,1)S(1)}, u32[]{:S(2)}, u32[]{:S(2)}) collective-permute-start(bf16[64,4096]{1,0:T(8,128)(2,1)S(1)} %constant_dynamic-update-slice_fusion.2.mine_ref), channel_id=1, source_target_pairs={{0,2},{1,3},{2,0},{3,1},{4,6},{5,7},{6,4},{7,5},{8,10},{9,11},{10,... | collective-permute-start | bytes 1572872 | tf_op jit(solution)/shard_map/ppermute | solution.py:147
  50.1 8.6 %collective-permute-start.10 = (bf16[16,2048]{1,0:T(8,128)(2,1)S(1)}, bf16[16,2048]{1,0:T(8,128)(2,1)S(1)}, u32[]{:S(2)}, u32[]{:S(2)}) collective-permute-start(bf16[16,2048]{1,0:T(8,128)(2,1)S(1)} %get-tuple-element.17), channel_id=1, source_target_pairs={{4,0},{5,1},{6,2},{7,3},{8,4},{9,5},{10,6},{11,7},{12,8},{13,9},{1... | collective-permute-start | bytes 196616 | tf_op jit(solution)/shard_map/ppermute | solution.py:144
  51.4 7.3 %collective-permute-start.11 = (bf16[16,2048]{1,0:T(8,128)(2,1)S(1)}, bf16[16,2048]{1,0:T(8,128)(2,1)S(1)}, u32[]{:S(2)}, u32[]{:S(2)}) collective-permute-start(bf16[16,2048]{1,0:T(8,128)(2,1)S(1)} %get-tuple-element.18), channel_id=1, source_target_pairs={{0,4},{1,5},{2,6},{3,7},{4,8},{5,9},{6,10},{7,11},{8,12},{9,13},{1... | collective-permute-start | bytes 196616 | tf_op jit(solution)/shard_map/ppermute | solution.py:144
  56.0 5.7 %collective-permute-start.12 = (bf16[16,2048]{1,0:T(8,128)(2,1)S(1)}, bf16[16,2048]{1,0:T(8,128)(2,1)S(1)}, u32[]{:S(2)}, u32[]{:S(2)}) collective-permute-start(bf16[16,2048]{1,0:T(8,128)(2,1)S(1)} %get-tuple-element.19), channel_id=1, source_target_pairs={{8,0},{9,1},{10,2},{11,3},{12,4},{13,5},{14,6},{15,7},{0,8},{1,9},... | collective-permute-start | bytes 196616 | tf_op jit(solution)/shard_map/ppermute | solution.py:144
  64.7 8.1 %copy-start.6 = (s32[1,64]{1,0:T(1,128)S(1)}, s32[1,64]{1,0:T(1,128)}, u32[]{:S(2)}) copy-start(s32[1,64]{1,0:T(1,128)} %param.12) | copy-start | bytes 772
  64.7 8.0 %collective-permute-start.13 = (bf16[16,2048]{1,0:T(8,128)(2,1)S(1)}, bf16[16,2048]{1,0:T(8,128)(2,1)S(1)}, u32[]{:S(2)}, u32[]{:S(2)}) collective-permute-start(bf16[16,2048]{1,0:T(8,128)(2,1)S(1)} %project.3), channel_id=1, source_target_pairs={{12,0},{13,1},{14,2},{15,3},{0,12},{1,13},{2,14},{3,15},{28,16},{2... | collective-permute-start | bytes 196616 | tf_op jit(solution)/shard_map/ppermute | solution.py:144
  67.9 5.6 %copy-start.2 = (bf16[64,4096]{1,0:T(8,128)(2,1)}, bf16[64,4096]{1,0:T(8,128)(2,1)S(1)}, u32[]{:S(2)}) copy-start(bf16[64,4096]{1,0:T(8,128)(2,1)S(1)} %collective-permute-done.15.over_y_ref) | copy-start | bytes 1572868
  72.7 2.9 %collective-permute-start.16 = (bf16[128,4096]{1,0:T(8,128)(2,1)}, bf16[128,4096]{1,0:T(8,128)(2,1)S(1)}, u32[]{:S(2)}, u32[]{:S(2)}) collective-permute-start(bf16[128,4096]{1,0:T(8,128)(2,1)} %pad_maximum_fusion), channel_id=1, source_target_pairs={{0,1},{1,0},{2,3},{3,2},{4,5},{5,4},{6,7},{7,6},{8,9},{9,8},{10,11... | collective-permute-start | bytes 3145736 | tf_op jit(solution)/shard_map/ppermute | solution.py:147
  74.1 3.2 %copy-start.5 = (f32[4,4096]{1,0:T(4,128)}, f32[4,4096]{1,0:T(4,128)S(1)}, u32[]{:S(2)}) copy-start(f32[4,4096]{1,0:T(4,128)S(1)} %reshape.146) | copy-start | bytes 196612
  75.5 1.0 %copy-start.3 = (bf16[64,4096]{1,0:T(8,128)(2,1)S(1)}, bf16[64,4096]{1,0:T(8,128)(2,1)}, u32[]{:S(2)}) copy-start(bf16[64,4096]{1,0:T(8,128)(2,1)} %copy-done.2) | copy-start | bytes 1572868

commit v10 on v9

--- a/solution.py
+++ b/solution.py
@@ -64,32 +64,37 @@
 def project_kernel(blocks, rows, *refs):
     parts, weights = refs[:blocks], refs[blocks : blocks + QUAD]
     outs, total = refs[blocks + QUAD : -1], refs[-1]
-    depth = 1024
-    total[...] = jnp.zeros_like(total)
-
-    @pl.loop(0, parts[0].shape[1] // depth)
-    def _(i):
-        span = pl.ds(pl.multiple_of(i * depth, depth), depth)
-        left = jnp.concatenate([p[:rows, span] for p in parts], axis=0)
-        right = jnp.concatenate([w[:, span] for w in weights], axis=0)
-        total[...] += lax.dot_general(left, right, NT, preferred_element_type=jnp.float32)
-
-    width = total.shape[1]
-    for b in range(blocks):
-        for g in range(rows // SLAB):
-            top = b * rows + g * SLAB
-            outs[b][:, g * width : (g + 1) * width] = total[top : top + SLAB].astype(jnp.bfloat16)
+    left = jnp.concatenate([p[...] for p in parts], axis=0)
+    right = jnp.concatenate([w[...] for w in weights], axis=0)
+    product = lax.dot_general(left, right, NT, preferred_element_type=jnp.float32)
+
+    @pl.when(pl.program_id(0) == 0)
+    def _():
+        total[...] = product
+
+    @pl.when(pl.program_id(0) > 0)
+    def _():
+        total[...] += product
+
+    @pl.when(pl.program_id(0) == pl.num_programs(0) - 1)
+    def _():
+        width = total.shape[1]
+        for b in range(blocks):
+            for g in range(rows // SLAB):
+                top = b * rows + g * SLAB
+                outs[b][:, g * width : (g + 1) * width] = total[top : top + SLAB].astype(jnp.bfloat16)
 
 
 def project(parts, rows, weights):
-    width = QUAD * weights[0].shape[0]
-    vmem = pl.BlockSpec(memory_space=pltpu.VMEM)
+    width, depth = QUAD * weights[0].shape[0], 1024
     total = jax.ShapeDtypeStruct((rows * len(parts), width), jnp.float32)
+    side = (SLAB, rows // SLAB * width)
     return pl.pallas_call(
         functools.partial(project_kernel, len(parts), rows),
-        out_shape=[jax.ShapeDtypeStruct((SLAB, rows // SLAB * width), jnp.bfloat16)] * len(parts),
-        in_specs=[vmem] * (len(parts) + QUAD),
-        out_specs=[vmem] * len(parts),
+        grid=(parts[0].shape[1] // depth,),
+        out_shape=[jax.ShapeDtypeStruct(side, jnp.bfloat16)] * len(parts),
+        in_specs=[pl.BlockSpec((a.shape[0], depth), lambda i: (0, i)) for a in (*parts, *weights)],
+        out_specs=[pl.BlockSpec(side, lambda i: (0, 0))] * len(parts),
         scratch_shapes=[pltpu.VMEM(total.shape, total.dtype)],
         cost_estimate=SMALL,
         compiler_params=pltpu.CompilerParams(vmem_limit_bytes=room(*parts, *weights, total, total)),
@@ -230,7 +235,7 @@
     late = returned.pop()
     early = combine([own] + returned, wide)
 
-    rest = swap(after(jnp.concatenate([mine, mine_over_y], axis=0), late), 1)
+    rest = swap(after(jnp.concatenate([mine, mine_over_y], axis=0), side), 1)
     here = jnp.stack([plane, spot, group]).astype(jnp.int32)
     all_queries = assemble(here, mine, mine_over_y, rest, order, groups)
     sketches = combine([late], wide_late, early, counts)

time: 79 us -> 79 us (level)
  waiting for transfers between devices: 30.7 us -> 29.4 us
  Pallas kernels: 8.25 us -> 9.15 us
    ppermute x7, waiting for transfers between devices: 14.5 us -> 13.1 us  [swap(): return lax.ppermute(array, 'expert', [(i, i ^ bit) for i in range(n)])]
    pallas_call x2, Pallas kernels: 6.5 us -> 7.41 us  [project(): pl.pallas_call(functools.partial(project_kernel, len(parts), rows), grid=...]
  transfers between devices with their start and end apart: 17 -> 17, of which waited for: 10 -> 9; matrix products, arithmetic and copies ran while one was open for 9% -> 7% of each run, Pallas kernels for 10% -> 11%
where the time goes in v10:
time: 79 us; the launch traced here: 78.4 us
  starting transfers between devices  29.7 us (38%)
  waiting for transfers between devices  29.4 us (37%)
  Pallas kernels  9.15 us (12%)
  other arithmetic  3.86 us (5%)
  local copies, waits for them, and re-layouts  2.68 us (3%)
  matrix products  2.58 us (3%)
  between operations  1.01 us (1%)
    ppermute x9, starting transfers between devices, move(): return lax.ppermute(array, 'expert', pairs)  19.7 us
    ppermute x9, waiting for transfers between devices, move(): return lax.ppermute(array, 'expert', pairs)  14.4 us
    ppermute x7, waiting for transfers between devices, swap(): return lax.ppermute(array, 'expert', [(i, i ^ bit) for i in range(n)])  13.1 us
    ppermute x7, starting transfers between devices, swap(): return lax.ppermute(array, 'expert', [(i, i ^ bit) for i in range(n)])  8.45 us
    pallas_call x2, Pallas kernels, project(): pl.pallas_call(functools.partial(project_kernel, len(parts), rows), grid=...  7.41 us
    ppermute x1, waiting for transfers between devices, shards(): lax.ppermute(lined, 'groups', [(g, (g + k) % groups) for g in range(group...  1.91 us
  transfers between devices with their start and end apart: 17, of which 9 were waited for; matrix products, arithmetic and copies ran while one was open for 7% of the time, Pallas kernels for 11%

profile of v10, /device:TPU:0, one launch (start us, length us, event | category | flops | bytes accessed | tf_op | source)
XLA Modules:
  0.0 78.4 jit_solution(11554945579942851572)
XLA Ops:
  0.6 5.9 %collective-permute-start = (bf16[64,4096]{1,0:T(8,128)(2,1)}, bf16[64,4096]{1,0:T(8,128)(2,1)}, u32[]{:S(2)}, u32[]{:S(2)}) collective-permute-start(bf16[64,4096]{1,0:T(8,128)(2,1)} %refs_0_.1), channel_id=1, source_target_pairs={{0,4},{1,5},{2,6},{3,7},{4,8},{5,9},{6,10},{7,11},{8,12},{9,13},{1... | collective-permute-start | bytes 1572872 | tf_op jit(solution)/shard_map/ppermute | solution.py:149
  6.5 1.3 %collective-permute-start.2 = (bf16[64,4096]{1,0:T(8,128)(2,1)}, bf16[64,4096]{1,0:T(8,128)(2,1)}, u32[]{:S(2)}, u32[]{:S(2)}) collective-permute-start(bf16[64,4096]{1,0:T(8,128)(2,1)} %refs_0_.1), channel_id=1, source_target_pairs={{4,0},{5,1},{6,2},{7,3},{8,4},{9,5},{10,6},{11,7},{12,8},{13,9},{1... | collective-permute-start | bytes 1572872 | tf_op jit(solution)/shard_map/ppermute | solution.py:149
  7.9 1.6 %collective-permute-start.8 = (bf16[128,4096]{1,0:T(8,128)(2,1)}, bf16[128,4096]{1,0:T(8,128)(2,1)}, u32[]{:S(2)}, u32[]{:S(2)}) collective-permute-start(bf16[128,4096]{1,0:T(8,128)(2,1)} %bitcast.17), channel_id=1, source_target_pairs={{0,2},{1,3},{2,0},{3,1},{4,6},{5,7},{6,4},{7,5},{8,10},{9,11},{10,... | collective-permute-start | bytes 3145736 | tf_op jit(solution)/shard_map/ppermute | solution.py:152
  9.5 0.8 %constant_dynamic-slice_fusion = bf16[16,2048]{1,0:T(8,128)(2,1)S(1)} fusion(bf16[16,4096]{1,0:T(8,128)(2,1)} %param.15, s32[]{:T(128)S(6)} %select_n.74), kind=kLoop, calls=%fused_computation.22 | loop fusion | bytes 131076 | tf_op jit(solution)/shard_map/dynamic_slice | solution.py:193
  10.3 2.9 %collective-permute-start.4 = (bf16[16,2048]{1,0:T(8,128)(2,1)S(1)}, bf16[16,2048]{1,0:T(8,128)(2,1)S(1)}, u32[]{:S(2)}, u32[]{:S(2)}) collective-permute-start(bf16[16,2048]{1,0:T(8,128)(2,1)S(1)} %constant_dynamic-slice_fusion), channel_id=1, source_target_pairs={{0,8},{1,9},{2,10},{3,11},{4,12},{5,13},{6,14},{7,15},{8,0},{9,1},... | collective-permute-start | bytes 196616 | tf_op jit(solution)/shard_map/ppermute | solution.py:152
  13.2 0.1 stack.33
  13.4 0.1 add.55
  13.5 0.1 add_select_fusion
  13.5 0.1 select_n.90
  13.6 0.7 iota_compare_fusion
  14.4 1.3 %fusion.4 = f32[64,64]{1,0:T(8,128)S(1)} fusion(bf16[64,4096]{1,0:T(8,128)(2,1)S(1)} %copy-done, bf16[4096,64]{0,1:T(8,128)(2,1)} %param.14), kind=kOutput, calls=%fused_computation.23 | convolution fusion | flops 33554432 | bytes 1064960 | tf_op jit(solution)/shard_map/dot_general | solution.py:168
  15.7 0.9 %select_reduce_fusion = f32[40,64]{1,0:T(8,128)S(1)} fusion(f32[8,64]{1,0:T(8,128)} %bitcast.20, s32[8,64]{1,0:T(8,128)} %bitcast.21, s32[40]{0:T(128)S(1)} %select_n.90), kind=kLoop, calls=%fused_computation.5 | loop fusion | flops 58880 | bytes 14496 | tf_op jit(solution)/shard_map/reduce_sum | solution.py:173
  16.7 0.1 pad_maximum_fusion.2
  16.8 0.1 broadcast_in_dim.70
  16.9 0.1 broadcast_in_dim.71
  17.1 0.3 fusion.refs_4_
  17.4 0.1 fusion.1.refs_1_
  17.5 0.4 collective-permute-done.refs_1_
  17.9 0.7 collective-permute-start.1
  18.6 4.2 %collective-permute-done.2.refs_2_ = bf16[64,4096]{1,0:T(8,128)(2,1)} collective-permute-done((bf16[64,4096]{1,0:T(8,128)(2,1)}, bf16[64,4096]{1,0:T(8,128)(2,1)}, u32[]{:S(2)}, u32[]{:S(2)}) %collective-permute-start.2) | collective-permute-done | bytes 524320 | tf_op jit(solution)/shard_map/ppermute | solution.py:149
  22.8 1.3 %collective-permute-start.3 = (bf16[64,4096]{1,0:T(8,128)(2,1)}, bf16[64,4096]{1,0:T(8,128)(2,1)S(1)}, u32[]{:S(2)}, u32[]{:S(2)}) collective-permute-start(bf16[64,4096]{1,0:T(8,128)(2,1)} %collective-permute-done.2.refs_2_), channel_id=1, source_target_pairs={{4,0},{5,1},{6,2},{7,3},{8,4},{9,5},{10,6},{11,7},{20,16},{21,17},... | collective-permute-start | bytes 1572872 | tf_op jit(solution)/shard_map/ppermute | solution.py:149
  24.1 0.9 %collective-permute-done.4 = bf16[16,2048]{1,0:T(8,128)(2,1)S(1)} collective-permute-done((bf16[16,2048]{1,0:T(8,128)(2,1)S(1)}, bf16[16,2048]{1,0:T(8,128)(2,1)S(1)}, u32[]{:S(2)}, u32[]{:S(2)}) %collective-permute-start.4) | collective-permute-done | bytes 65568 | tf_op jit(solution)/shard_map/ppermute | solution.py:152
  25.0 2.3 %collective-permute-start.5 = (bf16[32,2048]{1,0:T(8,128)(2,1)S(1)}, bf16[32,2048]{1,0:T(8,128)(2,1)S(1)}, u32[]{:S(2)}, u32[]{:S(2)}) collective-permute-start(bf16[32,2048]{1,0:T(8,128)(2,1)S(1)} %pad_maximum_fusion.1), channel_id=1, source_target_pairs={{0,4},{1,5},{2,6},{3,7},{4,0},{5,1},{6,2},{7,3},{8,12},{9,13},{10,... | collective-permute-start | bytes 393224 | tf_op jit(solution)/shard_map/ppermute | solution.py:152
  27.3 12.2 %collective-permute-done.5 = bf16[32,2048]{1,0:T(8,128)(2,1)S(1)} collective-permute-done((bf16[32,2048]{1,0:T(8,128)(2,1)S(1)}, bf16[32,2048]{1,0:T(8,128)(2,1)S(1)}, u32[]{:S(2)}, u32[]{:S(2)}) %collective-permute-start.5) | collective-permute-done | bytes 131104 | tf_op jit(solution)/shard_map/ppermute | solution.py:152
  39.5 0.1 add.58.refs_3_
  39.7 1.6 %collective-permute-start.14 = (bf16[64,2048]{1,0:T(8,128)(2,1)S(1)}, bf16[64,2048]{1,0:T(8,128)(2,1)S(1)}, u32[]{:S(2)}, u32[]{:S(2)}) collective-permute-start(bf16[64,2048]{1,0:T(8,128)(2,1)S(1)} %constant_dynamic-update-slice_fusion), channel_id=1, source_target_pairs={{0,16},{16,0},{1,17},{17,1},{2,18},{18,2},{3,19},{19,3},{4,20},{20... | collective-permute-start | bytes 786440 | tf_op jit(solution)/shard_map/ppermute | solution.py:224
  41.3 1.3 %collective-permute-start.6 = (bf16[64,4096]{1,0:T(8,128)(2,1)S(1)}, bf16[64,4096]{1,0:T(8,128)(2,1)S(1)}, u32[]{:S(2)}, u32[]{:S(2)}) collective-permute-start(bf16[64,4096]{1,0:T(8,128)(2,1)S(1)} %add.58.refs_3_), channel_id=1, source_target_pairs={{8,12},{9,13},{10,14},{11,15},{4,0},{5,1},{6,2},{7,3},{24,28},{25,... | collective-permute-start | bytes 1572872 | tf_op jit(solution)/shard_map/ppermute | solution.py:149
  42.6 3.9 %project.2 = (bf16[16,2048]{1,0:T(8,128)(2,1)S(1)}, bf16[16,2048]{1,0:T(8,128)(2,1)S(1)}, bf16[16,2048]{1,0:T(8,128)(2,1)S(1)}, bf16[16,2048]{1,0:T(8,128)(2,1)S(1)}) custom-call(bf16[64,4096]{1,0:T(8,128)(2,1)S(1)} %copy-done.4, bf16[64,4096]{1,0:T(8,128)(2,1)} %collective-permute-done.refs_1_, bf16[64,4096]{1,0:T(8,128)(2,1)} %collective-permute-done.2.refs_2_, ...), custom_call_target="tpu_custom_call" | custom-call | flops 1024 | bytes 1024 | tf_op jit(solution)/shard_map/project/pallas_call | solution.py:92
  46.6 1.9 %collective-permute-done.14 = bf16[64,2048]{1,0:T(8,128)(2,1)S(1)} collective-permute-done((bf16[64,2048]{1,0:T(8,128)(2,1)S(1)}, bf16[64,2048]{1,0:T(8,128)(2,1)S(1)}, u32[]{:S(2)}, u32[]{:S(2)}) %collective-permute-start.14) | collective-permute-done | bytes 262176 | tf_op jit(solution)/shard_map/ppermute | solution.py:224
  48.5 1.6 %collective-permute-start.15 = (bf16[64,4096]{1,0:T(8,128)(2,1)S(1)}, bf16[64,4096]{1,0:T(8,128)(2,1)S(1)}, u32[]{:S(2)}, u32[]{:S(2)}) collective-permute-start(bf16[64,4096]{1,0:T(8,128)(2,1)S(1)} %constant_dynamic-update-slice_fusion.2.mine_ref), channel_id=1, source_target_pairs={{0,2},{1,3},{2,0},{3,1},{4,6},{5,7},{6,4},{7,5},{8,10},{9,11},{10,... | collective-permute-start | bytes 1572872 | tf_op jit(solution)/shard_map/ppermute | solution.py:152
  50.1 1.3 %collective-permute-start.10 = (bf16[16,2048]{1,0:T(8,128)(2,1)S(1)}, bf16[16,2048]{1,0:T(8,128)(2,1)S(1)}, u32[]{:S(2)}, u32[]{:S(2)}) collective-permute-start(bf16[16,2048]{1,0:T(8,128)(2,1)S(1)} %get-tuple-element.17), channel_id=1, source_target_pairs={{4,0},{5,1},{6,2},{7,3},{8,4},{9,5},{10,6},{11,7},{12,8},{13,9},{1... | collective-permute-start | bytes 196616 | tf_op jit(solution)/shard_map/ppermute | solution.py:149
  51.4 4.5 %collective-permute-start.11 = (bf16[16,2048]{1,0:T(8,128)(2,1)S(1)}, bf16[16,2048]{1,0:T(8,128)(2,1)S(1)}, u32[]{:S(2)}, u32[]{:S(2)}) collective-permute-start(bf16[16,2048]{1,0:T(8,128)(2,1)S(1)} %get-tuple-element.18), channel_id=1, source_target_pairs={{0,4},{1,5},{2,6},{3,7},{4,8},{5,9},{6,10},{7,11},{8,12},{9,13},{1... | collective-permute-start | bytes 196616 | tf_op jit(solution)/shard_map/ppermute | solution.py:149
  56.0 0.3 collective-permute-start.12
  56.2 1.6 %collective-permute-done.6.refs_0_ = bf16[64,4096]{1,0:T(8,128)(2,1)S(1)} collective-permute-done((bf16[64,4096]{1,0:T(8,128)(2,1)S(1)}, bf16[64,4096]{1,0:T(8,128)(2,1)S(1)}, u32[]{:S(2)}, u32[]{:S(2)}) %collective-permute-start.6) | collective-permute-done | bytes 524320 | tf_op jit(solution)/shard_map/ppermute | solution.py:149
  57.9 1.2 %collective-permute-done.10.refs_1_ = bf16[16,2048]{1,0:T(8,128)(2,1)S(1)} collective-permute-done((bf16[16,2048]{1,0:T(8,128)(2,1)S(1)}, bf16[16,2048]{1,0:T(8,128)(2,1)S(1)}, u32[]{:S(2)}, u32[]{:S(2)}) %collective-permute-start.10) | collective-permute-done | bytes 65568 | tf_op jit(solution)/shard_map/ppermute | solution.py:149
  59.1 2.8 %collective-permute-done.12.refs_3_ = bf16[16,2048]{1,0:T(8,128)(2,1)S(1)} collective-permute-done((bf16[16,2048]{1,0:T(8,128)(2,1)S(1)}, bf16[16,2048]{1,0:T(8,128)(2,1)S(1)}, u32[]{:S(2)}, u32[]{:S(2)}) %collective-permute-start.12) | collective-permute-done | bytes 65568 | tf_op jit(solution)/shard_map/ppermute | solution.py:149
  61.9 3.5 %project.3 = bf16[16,2048]{1,0:T(8,128)(2,1)S(1)} custom-call(bf16[64,4096]{1,0:T(8,128)(2,1)S(1)} %collective-permute-done.6.refs_0_, bf16[128,4096]{1,0:T(8,128)(2,1)S(1)} %bitcast.19, bf16[128,4096]{1,0:T(8,128)(2,1)S(1)} %collective-permute-done.7.refs_5_.refs_2_, bf16[128,4096]{1,0:T(8,128)(2,1)} %collective-permute-done.8.refs_6_.refs_3_, ...), custom_call_target="tpu_custom_call" | custom-call | flops 1024 | bytes 1024 | tf_op jit(solution)/shard_map/project/pallas_call | solution.py:92
  65.4 1.2 %pad_maximum_fusion = bf16[128,4096]{1,0:T(8,128)(2,1)} fusion(bf16[64,4096]{1,0:T(8,128)(2,1)S(1)} %collective-permute-done.15.over_y_ref, bf16[64,4096]{1,0:T(8,128)(2,1)S(1)} %constant_dynamic-update-slice_fusion.2.mine_ref), kind=kLoop, calls=%fused_computation.2 | loop fusion | flops 2097152 | bytes 2097152 | tf_op jit(solution)/shard_map/concatenate | solution.py:238
  66.6 0.1 convert_reduce_fusion
  66.7 3.2 %collective-permute-start.13 = (bf16[16,2048]{1,0:T(8,128)(2,1)S(1)}, bf16[16,2048]{1,0:T(8,128)(2,1)S(1)}, u32[]{:S(2)}, u32[]{:S(2)}) collective-permute-start(bf16[16,2048]{1,0:T(8,128)(2,1)S(1)} %project.3), channel_id=1, source_target_pairs={{12,0},{13,1},{14,2},{15,3},{0,12},{1,13},{2,14},{3,15},{28,16},{2... | collective-permute-start | bytes 196616 | tf_op jit(solution)/shard_map/ppermute | solution.py:149
  69.9 0.1 pad_add_fusion.here_ref
  69.9 0.7 combine.2.refs_2_
  70.6 4.2 %collective-permute-done.13.refs_0_ = bf16[16,2048]{1,0:T(8,128)(2,1)S(1)} collective-permute-done((bf16[16,2048]{1,0:T(8,128)(2,1)S(1)}, bf16[16,2048]{1,0:T(8,128)(2,1)S(1)}, u32[]{:S(2)}, u32[]{:S(2)}) %collective-permute-start.13) | collective-permute-done | bytes 65568 | tf_op jit(solution)/shard_map/ppermute | solution.py:149
  74.9 0.4 combine.3
  75.3 0.1 reshape.146
  75.4 1.1 %copy-done.3 = bf16[64,4096]{1,0:T(8,128)(2,1)S(1)} copy-done((bf16[64,4096]{1,0:T(8,128)(2,1)S(1)}, bf16[64,4096]{1,0:T(8,128)(2,1)}, u32[]{:S(2)}) %copy-start.3) | copy-done | bytes 524312
  76.5 0.7 assemble.1
  77.2 1.2 %fusion.2 = f32[4,256]{1,0:T(4,128)} fusion(bf16[256,4096]{1,0:T(8,128)(2,1)S(1)} %assemble.1, f32[4,4096]{1,0:T(4,128)S(1)} %reshape.146), kind=kOutput, calls=%fused_computation.8 | convolution fusion | flops 8404992 | bytes 2166784 | tf_op jit(solution)/shard_map/dot_general | solution.py:243
  (36 shorter events, 0.4 us)
Async XLA Ops:
  0.6 13.7 %copy-start = (bf16[64,4096]{1,0:T(8,128)(2,1)S(1)}, bf16[64,4096]{1,0:T(8,128)(2,1)}, u32[]{:S(2)}) copy-start(bf16[64,4096]{1,0:T(8,128)(2,1)} %param.9) | copy-start | bytes 1572868
  0.6 17.3 %collective-permute-start = (bf16[64,4096]{1,0:T(8,128)(2,1)}, bf16[64,4096]{1,0:T(8,128)(2,1)}, u32[]{:S(2)}, u32[]{:S(2)}) collective-permute-start(bf16[64,4096]{1,0:T(8,128)(2,1)} %refs_0_.1), channel_id=1, source_target_pairs={{0,4},{1,5},{2,6},{3,7},{4,8},{5,9},{6,10},{7,11},{8,12},{9,13},{1... | collective-permute-start | bytes 1572872 | tf_op jit(solution)/shard_map/ppermute | solution.py:149
  6.5 16.3 %collective-permute-start.2 = (bf16[64,4096]{1,0:T(8,128)(2,1)}, bf16[64,4096]{1,0:T(8,128)(2,1)}, u32[]{:S(2)}, u32[]{:S(2)}) collective-permute-start(bf16[64,4096]{1,0:T(8,128)(2,1)} %refs_0_.1), channel_id=1, source_target_pairs={{4,0},{5,1},{6,2},{7,3},{8,4},{9,5},{10,6},{11,7},{12,8},{13,9},{1... | collective-permute-start | bytes 1572872 | tf_op jit(solution)/shard_map/ppermute | solution.py:149
  7.8 34.8 %collective-permute-start.7 = (bf16[128,4096]{1,0:T(8,128)(2,1)}, bf16[128,4096]{1,0:T(8,128)(2,1)S(1)}, u32[]{:S(2)}, u32[]{:S(2)}) collective-permute-start(bf16[128,4096]{1,0:T(8,128)(2,1)} %bitcast.16), channel_id=1, source_target_pairs={{0,1},{1,0},{2,3},{3,2},{4,5},{5,4},{6,7},{7,6},{8,9},{9,8},{10,11... | collective-permute-start | bytes 3145736 | tf_op jit(solution)/shard_map/ppermute | solution.py:152
  7.9 31.8 %collective-permute-start.8 = (bf16[128,4096]{1,0:T(8,128)(2,1)}, bf16[128,4096]{1,0:T(8,128)(2,1)}, u32[]{:S(2)}, u32[]{:S(2)}) collective-permute-start(bf16[128,4096]{1,0:T(8,128)(2,1)} %bitcast.17), channel_id=1, source_target_pairs={{0,2},{1,3},{2,0},{3,1},{4,6},{5,7},{6,4},{7,5},{8,10},{9,11},{10,... | collective-permute-start | bytes 3145736 | tf_op jit(solution)/shard_map/ppermute | solution.py:152
  10.3 14.7 %collective-permute-start.4 = (bf16[16,2048]{1,0:T(8,128)(2,1)S(1)}, bf16[16,2048]{1,0:T(8,128)(2,1)S(1)}, u32[]{:S(2)}, u32[]{:S(2)}) collective-permute-start(bf16[16,2048]{1,0:T(8,128)(2,1)S(1)} %constant_dynamic-slice_fusion), channel_id=1, source_target_pairs={{0,8},{1,9},{2,10},{3,11},{4,12},{5,13},{6,14},{7,15},{8,0},{9,1},... | collective-permute-start | bytes 196616 | tf_op jit(solution)/shard_map/ppermute | solution.py:152
  15.7 26.9 %copy-start.1 = (bf16[2,4096,64]{1,2,0:T(8,128)(2,1)S(1)}, bf16[2,4096,64]{1,2,0:T(8,128)(2,1)}, u32[]{:S(2)}) copy-start(bf16[2,4096,64]{1,2,0:T(8,128)(2,1)} %param.13) | copy-start | bytes 3145732
  15.7 26.9 %copy-start.4 = (bf16[64,4096]{1,0:T(8,128)(2,1)S(1)}, bf16[64,4096]{1,0:T(8,128)(2,1)}, u32[]{:S(2)}) copy-start(bf16[64,4096]{1,0:T(8,128)(2,1)} %refs_0_.1) | copy-start | bytes 1572868
  17.9 21.6 %collective-permute-start.1 = (bf16[64,4096]{1,0:T(8,128)(2,1)}, bf16[64,4096]{1,0:T(8,128)(2,1)S(1)}, u32[]{:S(2)}, u32[]{:S(2)}) collective-permute-start(bf16[64,4096]{1,0:T(8,128)(2,1)} %collective-permute-done.refs_1_), channel_id=1, source_target_pairs={{4,8},{5,9},{6,10},{7,11},{8,12},{9,13},{10,14},{11,15},{20,24},{2... | collective-permute-start | bytes 1572872 | tf_op jit(solution)/shard_map/ppermute | solution.py:149
  22.8 16.7 %collective-permute-start.3 = (bf16[64,4096]{1,0:T(8,128)(2,1)}, bf16[64,4096]{1,0:T(8,128)(2,1)S(1)}, u32[]{:S(2)}, u32[]{:S(2)}) collective-permute-start(bf16[64,4096]{1,0:T(8,128)(2,1)} %collective-permute-done.2.refs_2_), channel_id=1, source_target_pairs={{4,0},{5,1},{6,2},{7,3},{8,4},{9,5},{10,6},{11,7},{20,16},{21,17},... | collective-permute-start | bytes 1572872 | tf_op jit(solution)/shard_map/ppermute | solution.py:149
  25.0 14.4 %collective-permute-start.5 = (bf16[32,2048]{1,0:T(8,128)(2,1)S(1)}, bf16[32,2048]{1,0:T(8,128)(2,1)S(1)}, u32[]{:S(2)}, u32[]{:S(2)}) collective-permute-start(bf16[32,2048]{1,0:T(8,128)(2,1)S(1)} %pad_maximum_fusion.1), channel_id=1, source_target_pairs={{0,4},{1,5},{2,6},{3,7},{4,0},{5,1},{6,2},{7,3},{8,12},{9,13},{10,... | collective-permute-start | bytes 393224 | tf_op jit(solution)/shard_map/ppermute | solution.py:152
  39.7 2.9 %collective-permute-start.9 = (bf16[128,4096]{1,0:T(8,128)(2,1)}, bf16[128,4096]{1,0:T(8,128)(2,1)S(1)}, u32[]{:S(2)}, u32[]{:S(2)}) collective-permute-start(bf16[128,4096]{1,0:T(8,128)(2,1)} %collective-permute-done.8.refs_6_.refs_3_), channel_id=1, source_target_pairs={{0,1},{1,0},{2,3},{3,2},{4,5},{5,4},{6,7},{7,6},{8,9},{9,8},{10,11... | collective-permute-start | bytes 3145736 | tf_op jit(solution)/shard_map/ppermute | solution.py:152
  39.7 8.7 %collective-permute-start.14 = (bf16[64,2048]{1,0:T(8,128)(2,1)S(1)}, bf16[64,2048]{1,0:T(8,128)(2,1)S(1)}, u32[]{:S(2)}, u32[]{:S(2)}) collective-permute-start(bf16[64,2048]{1,0:T(8,128)(2,1)S(1)} %constant_dynamic-update-slice_fusion), channel_id=1, source_target_pairs={{0,16},{16,0},{1,17},{17,1},{2,18},{18,2},{3,19},{19,3},{4,20},{20... | collective-permute-start | bytes 786440 | tf_op jit(solution)/shard_map/ppermute | solution.py:224
  41.3 16.6 %collective-permute-start.6 = (bf16[64,4096]{1,0:T(8,128)(2,1)S(1)}, bf16[64,4096]{1,0:T(8,128)(2,1)S(1)}, u32[]{:S(2)}, u32[]{:S(2)}) collective-permute-start(bf16[64,4096]{1,0:T(8,128)(2,1)S(1)} %add.58.refs_3_), channel_id=1, source_target_pairs={{8,12},{9,13},{10,14},{11,15},{4,0},{5,1},{6,2},{7,3},{24,28},{25,... | collective-permute-start | bytes 1572872 | tf_op jit(solution)/shard_map/ppermute | solution.py:149
  48.5 16.9 %collective-permute-start.15 = (bf16[64,4096]{1,0:T(8,128)(2,1)S(1)}, bf16[64,4096]{1,0:T(8,128)(2,1)S(1)}, u32[]{:S(2)}, u32[]{:S(2)}) collective-permute-start(bf16[64,4096]{1,0:T(8,128)(2,1)S(1)} %constant_dynamic-update-slice_fusion.2.mine_ref), channel_id=1, source_target_pairs={{0,2},{1,3},{2,0},{3,1},{4,6},{5,7},{6,4},{7,5},{8,10},{9,11},{10,... | collective-permute-start | bytes 1572872 | tf_op jit(solution)/shard_map/ppermute | solution.py:152
  50.1 9.0 %collective-permute-start.10 = (bf16[16,2048]{1,0:T(8,128)(2,1)S(1)}, bf16[16,2048]{1,0:T(8,128)(2,1)S(1)}, u32[]{:S(2)}, u32[]{:S(2)}) collective-permute-start(bf16[16,2048]{1,0:T(8,128)(2,1)S(1)} %get-tuple-element.17), channel_id=1, source_target_pairs={{4,0},{5,1},{6,2},{7,3},{8,4},{9,5},{10,6},{11,7},{12,8},{13,9},{1... | collective-permute-start | bytes 196616 | tf_op jit(solution)/shard_map/ppermute | solution.py:149
  51.4 7.7 %collective-permute-start.11 = (bf16[16,2048]{1,0:T(8,128)(2,1)S(1)}, bf16[16,2048]{1,0:T(8,128)(2,1)S(1)}, u32[]{:S(2)}, u32[]{:S(2)}) collective-permute-start(bf16[16,2048]{1,0:T(8,128)(2,1)S(1)} %get-tuple-element.18), channel_id=1, source_target_pairs={{0,4},{1,5},{2,6},{3,7},{4,8},{5,9},{6,10},{7,11},{8,12},{9,13},{1... | collective-permute-start | bytes 196616 | tf_op jit(solution)/shard_map/ppermute | solution.py:149
  56.0 5.9 %collective-permute-start.12 = (bf16[16,2048]{1,0:T(8,128)(2,1)S(1)}, bf16[16,2048]{1,0:T(8,128)(2,1)S(1)}, u32[]{:S(2)}, u32[]{:S(2)}) collective-permute-start(bf16[16,2048]{1,0:T(8,128)(2,1)S(1)} %get-tuple-element.19), channel_id=1, source_target_pairs={{8,0},{9,1},{10,2},{11,3},{12,4},{13,5},{14,6},{15,7},{0,8},{1,9},... | collective-permute-start | bytes 196616 | tf_op jit(solution)/shard_map/ppermute | solution.py:149
  65.4 1.2 %copy-start.6 = (s32[1,64]{1,0:T(1,128)S(1)}, s32[1,64]{1,0:T(1,128)}, u32[]{:S(2)}) copy-start(s32[1,64]{1,0:T(1,128)} %param.12) | copy-start | bytes 772
  65.4 5.2 %copy-start.2 = (bf16[64,4096]{1,0:T(8,128)(2,1)}, bf16[64,4096]{1,0:T(8,128)(2,1)S(1)}, u32[]{:S(2)}) copy-start(bf16[64,4096]{1,0:T(8,128)(2,1)S(1)} %collective-permute-done.15.over_y_ref) | copy-start | bytes 1572868
  66.6 8.9 %collective-permute-start.16 = (bf16[128,4096]{1,0:T(8,128)(2,1)}, bf16[128,4096]{1,0:T(8,128)(2,1)S(1)}, u32[]{:S(2)}, u32[]{:S(2)}) collective-permute-start(bf16[128,4096]{1,0:T(8,128)(2,1)} %pad_maximum_fusion), channel_id=1, source_target_pairs={{0,1},{1,0},{2,3},{3,2},{4,5},{5,4},{6,7},{7,6},{8,9},{9,8},{10,11... | collective-permute-start | bytes 3145736 | tf_op jit(solution)/shard_map/ppermute | solution.py:152
  66.7 8.2 %collective-permute-start.13 = (bf16[16,2048]{1,0:T(8,128)(2,1)S(1)}, bf16[16,2048]{1,0:T(8,128)(2,1)S(1)}, u32[]{:S(2)}, u32[]{:S(2)}) collective-permute-start(bf16[16,2048]{1,0:T(8,128)(2,1)S(1)} %project.3), channel_id=1, source_target_pairs={{12,0},{13,1},{14,2},{15,3},{0,12},{1,13},{2,14},{3,15},{28,16},{2... | collective-permute-start | bytes 196616 | tf_op jit(solution)/shard_map/ppermute | solution.py:149
  75.4 1.8 %copy-start.5 = (f32[4,4096]{1,0:T(4,128)}, f32[4,4096]{1,0:T(4,128)S(1)}, u32[]{:S(2)}) copy-start(f32[4,4096]{1,0:T(4,128)S(1)} %reshape.146) | copy-start | bytes 196612
  75.4 1.1 %copy-start.3 = (bf16[64,4096]{1,0:T(8,128)(2,1)S(1)}, bf16[64,4096]{1,0:T(8,128)(2,1)}, u32[]{:S(2)}) copy-start(bf16[64,4096]{1,0:T(8,128)(2,1)} %copy-done.2) | copy-start | bytes 1572868

commit v11 on v9

--- a/solution.py
+++ b/solution.py
@@ -230,7 +230,7 @@
     late = returned.pop()
     early = combine([own] + returned, wide)
 
-    rest = swap(after(jnp.concatenate([mine, mine_over_y], axis=0), late), 1)
+    rest = swap(after(jnp.concatenate([mine, mine_over_y], axis=0), side), 1)
     here = jnp.stack([plane, spot, group]).astype(jnp.int32)
     all_queries = assemble(here, mine, mine_over_y, rest, order, groups)
     sketches = combine([late], wide_late, early, counts)

time: 79 us -> 78.3 us (level)
  waiting for transfers between devices: 30.7 us -> 29.9 us
    ppermute x7, waiting for transfers between devices: 14.5 us -> 13.1 us  [swap(): return lax.ppermute(array, 'expert', [(i, i ^ bit) for i in range(n)])]
  transfers between devices with their start and end apart: 17 -> 17, of which waited for: 10 -> 9; matrix products, arithmetic and copies ran while one was open for 9% -> 7% of each run, Pallas kernels for 10% -> 10%
where the time goes in v11:
time: 78.3 us; the launch traced here: 77.8 us
  waiting for transfers between devices  29.9 us (38%)
  starting transfers between devices  29.5 us (38%)
  Pallas kernels  8.25 us (11%)
  other arithmetic  3.86 us (5%)
  local copies, waits for them, and re-layouts  2.68 us (3%)
  matrix products  2.58 us (3%)
  between operations  1.02 us (1%)
    ppermute x9, starting transfers between devices, move(): return lax.ppermute(array, 'expert', pairs)  19.5 us
    ppermute x9, waiting for transfers between devices, move(): return lax.ppermute(array, 'expert', pairs)  14.5 us
    ppermute x7, waiting for transfers between devices, swap(): return lax.ppermute(array, 'expert', [(i, i ^ bit) for i in range(n)])  13.1 us
    ppermute x7, starting transfers between devices, swap(): return lax.ppermute(array, 'expert', [(i, i ^ bit) for i in range(n)])  8.45 us
    pallas_call x2, Pallas kernels, project(): pl.pallas_call(functools.partial(project_kernel, len(parts), rows), out_s...  6.5 us
    ppermute x1, waiting for transfers between devices, shards(): lax.ppermute(lined, 'groups', [(g, (g + k) % groups) for g in range(group...  2.34 us
  transfers between devices with their start and end apart: 17, of which 9 were waited for; matrix products, arithmetic and copies ran while one was open for 7% of the time, Pallas kernels for 10%

profile of v11, /device:TPU:0, one launch (start us, length us, event | category | flops | bytes accessed | tf_op | source)
XLA Modules:
  0.0 77.8 jit_solution(12489283769073453283)
XLA Ops:
  0.6 5.9 %collective-permute-start = (bf16[64,4096]{1,0:T(8,128)(2,1)}, bf16[64,4096]{1,0:T(8,128)(2,1)}, u32[]{:S(2)}, u32[]{:S(2)}) collective-permute-start(bf16[64,4096]{1,0:T(8,128)(2,1)} %refs_0_.1), channel_id=1, source_target_pairs={{0,4},{1,5},{2,6},{3,7},{4,8},{5,9},{6,10},{7,11},{8,12},{9,13},{1... | collective-permute-start | bytes 1572872 | tf_op jit(solution)/shard_map/ppermute | solution.py:144
  6.5 1.3 %collective-permute-start.2 = (bf16[64,4096]{1,0:T(8,128)(2,1)}, bf16[64,4096]{1,0:T(8,128)(2,1)}, u32[]{:S(2)}, u32[]{:S(2)}) collective-permute-start(bf16[64,4096]{1,0:T(8,128)(2,1)} %refs_0_.1), channel_id=1, source_target_pairs={{4,0},{5,1},{6,2},{7,3},{8,4},{9,5},{10,6},{11,7},{12,8},{13,9},{1... | collective-permute-start | bytes 1572872 | tf_op jit(solution)/shard_map/ppermute | solution.py:144
  7.8 0.1 collective-permute-start.7
  7.9 1.6 %collective-permute-start.8 = (bf16[128,4096]{1,0:T(8,128)(2,1)}, bf16[128,4096]{1,0:T(8,128)(2,1)}, u32[]{:S(2)}, u32[]{:S(2)}) collective-permute-start(bf16[128,4096]{1,0:T(8,128)(2,1)} %bitcast.17), channel_id=1, source_target_pairs={{0,2},{1,3},{2,0},{3,1},{4,6},{5,7},{6,4},{7,5},{8,10},{9,11},{10,... | collective-permute-start | bytes 3145736 | tf_op jit(solution)/shard_map/ppermute | solution.py:147
  9.5 0.8 %constant_dynamic-slice_fusion = bf16[16,2048]{1,0:T(8,128)(2,1)S(1)} fusion(bf16[16,4096]{1,0:T(8,128)(2,1)} %param.15, s32[]{:T(128)S(6)} %select_n.74), kind=kLoop, calls=%fused_computation.22 | loop fusion | bytes 131076 | tf_op jit(solution)/shard_map/dynamic_slice | solution.py:188
  10.3 2.9 %collective-permute-start.4 = (bf16[16,2048]{1,0:T(8,128)(2,1)S(1)}, bf16[16,2048]{1,0:T(8,128)(2,1)S(1)}, u32[]{:S(2)}, u32[]{:S(2)}) collective-permute-start(bf16[16,2048]{1,0:T(8,128)(2,1)S(1)} %constant_dynamic-slice_fusion), channel_id=1, source_target_pairs={{0,8},{1,9},{2,10},{3,11},{4,12},{5,13},{6,14},{7,15},{8,0},{9,1},... | collective-permute-start | bytes 196616 | tf_op jit(solution)/shard_map/ppermute | solution.py:147
  13.2 0.1 stack.33
  13.4 0.1 add.55
  13.5 0.1 add_select_fusion
  13.5 0.1 select_n.90
  13.6 0.7 iota_compare_fusion
  14.4 1.3 %fusion.4 = f32[64,64]{1,0:T(8,128)S(1)} fusion(bf16[64,4096]{1,0:T(8,128)(2,1)S(1)} %copy-done, bf16[4096,64]{0,1:T(8,128)(2,1)} %param.14), kind=kOutput, calls=%fused_computation.23 | convolution fusion | flops 33554432 | bytes 1064960 | tf_op jit(solution)/shard_map/dot_general | solution.py:163
  15.7 0.9 %select_reduce_fusion = f32[40,64]{1,0:T(8,128)S(1)} fusion(f32[8,64]{1,0:T(8,128)} %bitcast.20, s32[8,64]{1,0:T(8,128)} %bitcast.21, s32[40]{0:T(128)S(1)} %select_n.90), kind=kLoop, calls=%fused_computation.5 | loop fusion | flops 58880 | bytes 14496 | tf_op jit(solution)/shard_map/reduce_sum | solution.py:168
  16.7 0.1 pad_maximum_fusion.2
  16.8 0.1 broadcast_in_dim.70
  16.9 0.1 broadcast_in_dim.71
  17.1 0.3 fusion.refs_4_
  17.4 0.1 fusion.1.refs_1_
  17.5 0.4 collective-permute-done.refs_1_
  17.9 0.7 collective-permute-start.1
  18.6 4.2 %collective-permute-done.2.refs_2_ = bf16[64,4096]{1,0:T(8,128)(2,1)} collective-permute-done((bf16[64,4096]{1,0:T(8,128)(2,1)}, bf16[64,4096]{1,0:T(8,128)(2,1)}, u32[]{:S(2)}, u32[]{:S(2)}) %collective-permute-start.2) | collective-permute-done | bytes 524320 | tf_op jit(solution)/shard_map/ppermute | solution.py:144
  22.8 1.3 %collective-permute-start.3 = (bf16[64,4096]{1,0:T(8,128)(2,1)}, bf16[64,4096]{1,0:T(8,128)(2,1)S(1)}, u32[]{:S(2)}, u32[]{:S(2)}) collective-permute-start(bf16[64,4096]{1,0:T(8,128)(2,1)} %collective-permute-done.2.refs_2_), channel_id=1, source_target_pairs={{4,0},{5,1},{6,2},{7,3},{8,4},{9,5},{10,6},{11,7},{20,16},{21,17},... | collective-permute-start | bytes 1572872 | tf_op jit(solution)/shard_map/ppermute | solution.py:144
  24.1 0.9 %collective-permute-done.4 = bf16[16,2048]{1,0:T(8,128)(2,1)S(1)} collective-permute-done((bf16[16,2048]{1,0:T(8,128)(2,1)S(1)}, bf16[16,2048]{1,0:T(8,128)(2,1)S(1)}, u32[]{:S(2)}, u32[]{:S(2)}) %collective-permute-start.4) | collective-permute-done | bytes 65568 | tf_op jit(solution)/shard_map/ppermute | solution.py:147
  25.0 2.3 %collective-permute-start.5 = (bf16[32,2048]{1,0:T(8,128)(2,1)S(1)}, bf16[32,2048]{1,0:T(8,128)(2,1)S(1)}, u32[]{:S(2)}, u32[]{:S(2)}) collective-permute-start(bf16[32,2048]{1,0:T(8,128)(2,1)S(1)} %pad_maximum_fusion.1), channel_id=1, source_target_pairs={{0,4},{1,5},{2,6},{3,7},{4,0},{5,1},{6,2},{7,3},{8,12},{9,13},{10,... | collective-permute-start | bytes 393224 | tf_op jit(solution)/shard_map/ppermute | solution.py:147
  27.3 12.2 %collective-permute-done.5 = bf16[32,2048]{1,0:T(8,128)(2,1)S(1)} collective-permute-done((bf16[32,2048]{1,0:T(8,128)(2,1)S(1)}, bf16[32,2048]{1,0:T(8,128)(2,1)S(1)}, u32[]{:S(2)}, u32[]{:S(2)}) %collective-permute-start.5) | collective-permute-done | bytes 131104 | tf_op jit(solution)/shard_map/ppermute | solution.py:147
  39.5 0.1 add.58.refs_3_
  39.7 1.6 %collective-permute-start.14 = (bf16[64,2048]{1,0:T(8,128)(2,1)S(1)}, bf16[64,2048]{1,0:T(8,128)(2,1)S(1)}, u32[]{:S(2)}, u32[]{:S(2)}) collective-permute-start(bf16[64,2048]{1,0:T(8,128)(2,1)S(1)} %constant_dynamic-update-slice_fusion), channel_id=1, source_target_pairs={{0,16},{16,0},{1,17},{17,1},{2,18},{18,2},{3,19},{19,3},{4,20},{20... | collective-permute-start | bytes 786440 | tf_op jit(solution)/shard_map/ppermute | solution.py:219
  41.3 1.3 %collective-permute-start.6 = (bf16[64,4096]{1,0:T(8,128)(2,1)S(1)}, bf16[64,4096]{1,0:T(8,128)(2,1)S(1)}, u32[]{:S(2)}, u32[]{:S(2)}) collective-permute-start(bf16[64,4096]{1,0:T(8,128)(2,1)S(1)} %add.58.refs_3_), channel_id=1, source_target_pairs={{8,12},{9,13},{10,14},{11,15},{4,0},{5,1},{6,2},{7,3},{24,28},{25,... | collective-permute-start | bytes 1572872 | tf_op jit(solution)/shard_map/ppermute | solution.py:144
  42.6 3.5 %project.2 = (bf16[16,2048]{1,0:T(8,128)(2,1)S(1)}, bf16[16,2048]{1,0:T(8,128)(2,1)S(1)}, bf16[16,2048]{1,0:T(8,128)(2,1)S(1)}, bf16[16,2048]{1,0:T(8,128)(2,1)S(1)}) custom-call(bf16[64,4096]{1,0:T(8,128)(2,1)S(1)} %copy-done.4, bf16[64,4096]{1,0:T(8,128)(2,1)} %collective-permute-done.refs_1_, bf16[64,4096]{1,0:T(8,128)(2,1)} %collective-permute-done.2.refs_2_, ...), custom_call_target="tpu_custom_call" | custom-call | flops 1024 | bytes 1024 | tf_op jit(solution)/shard_map/project/pallas_call | solution.py:88
  46.1 2.3 %collective-permute-done.14 = bf16[64,2048]{1,0:T(8,128)(2,1)S(1)} collective-permute-done((bf16[64,2048]{1,0:T(8,128)(2,1)S(1)}, bf16[64,2048]{1,0:T(8,128)(2,1)S(1)}, u32[]{:S(2)}, u32[]{:S(2)}) %collective-permute-start.14) | collective-permute-done | bytes 262176 | tf_op jit(solution)/shard_map/ppermute | solution.py:219
  48.5 1.6 %collective-permute-start.15 = (bf16[64,4096]{1,0:T(8,128)(2,1)S(1)}, bf16[64,4096]{1,0:T(8,128)(2,1)S(1)}, u32[]{:S(2)}, u32[]{:S(2)}) collective-permute-start(bf16[64,4096]{1,0:T(8,128)(2,1)S(1)} %constant_dynamic-update-slice_fusion.2.mine_ref), channel_id=1, source_target_pairs={{0,2},{1,3},{2,0},{3,1},{4,6},{5,7},{6,4},{7,5},{8,10},{9,11},{10,... | collective-permute-start | bytes 1572872 | tf_op jit(solution)/shard_map/ppermute | solution.py:147
  50.1 1.3 %collective-permute-start.10 = (bf16[16,2048]{1,0:T(8,128)(2,1)S(1)}, bf16[16,2048]{1,0:T(8,128)(2,1)S(1)}, u32[]{:S(2)}, u32[]{:S(2)}) collective-permute-start(bf16[16,2048]{1,0:T(8,128)(2,1)S(1)} %get-tuple-element.17), channel_id=1, source_target_pairs={{4,0},{5,1},{6,2},{7,3},{8,4},{9,5},{10,6},{11,7},{12,8},{13,9},{1... | collective-permute-start | bytes 196616 | tf_op jit(solution)/shard_map/ppermute | solution.py:144
  51.4 4.5 %collective-permute-start.11 = (bf16[16,2048]{1,0:T(8,128)(2,1)S(1)}, bf16[16,2048]{1,0:T(8,128)(2,1)S(1)}, u32[]{:S(2)}, u32[]{:S(2)}) collective-permute-start(bf16[16,2048]{1,0:T(8,128)(2,1)S(1)} %get-tuple-element.18), channel_id=1, source_target_pairs={{0,4},{1,5},{2,6},{3,7},{4,8},{5,9},{6,10},{7,11},{8,12},{9,13},{1... | collective-permute-start | bytes 196616 | tf_op jit(solution)/shard_map/ppermute | solution.py:144
  56.0 1.9 %collective-permute-done.6.refs_0_ = bf16[64,4096]{1,0:T(8,128)(2,1)S(1)} collective-permute-done((bf16[64,4096]{1,0:T(8,128)(2,1)S(1)}, bf16[64,4096]{1,0:T(8,128)(2,1)S(1)}, u32[]{:S(2)}, u32[]{:S(2)}) %collective-permute-start.6) | collective-permute-done | bytes 524320 | tf_op jit(solution)/shard_map/ppermute | solution.py:144
  57.9 0.8 %collective-permute-done.10.refs_1_ = bf16[16,2048]{1,0:T(8,128)(2,1)S(1)} collective-permute-done((bf16[16,2048]{1,0:T(8,128)(2,1)S(1)}, bf16[16,2048]{1,0:T(8,128)(2,1)S(1)}, u32[]{:S(2)}, u32[]{:S(2)}) %collective-permute-start.10) | collective-permute-done | bytes 65568 | tf_op jit(solution)/shard_map/ppermute | solution.py:144
  58.7 3.0 %collective-permute-done.12.refs_3_ = bf16[16,2048]{1,0:T(8,128)(2,1)S(1)} collective-permute-done((bf16[16,2048]{1,0:T(8,128)(2,1)S(1)}, bf16[16,2048]{1,0:T(8,128)(2,1)S(1)}, u32[]{:S(2)}, u32[]{:S(2)}) %collective-permute-start.12) | collective-permute-done | bytes 65568 | tf_op jit(solution)/shard_map/ppermute | solution.py:144
  61.7 3.0 %project.3 = bf16[16,2048]{1,0:T(8,128)(2,1)S(1)} custom-call(bf16[64,4096]{1,0:T(8,128)(2,1)S(1)} %collective-permute-done.6.refs_0_, bf16[128,4096]{1,0:T(8,128)(2,1)S(1)} %bitcast.19, bf16[128,4096]{1,0:T(8,128)(2,1)S(1)} %collective-permute-done.7.refs_5_.refs_2_, bf16[128,4096]{1,0:T(8,128)(2,1)} %collective-permute-done.8.refs_6_.refs_3_, ...), custom_call_target="tpu_custom_call" | custom-call | flops 1024 | bytes 1024 | tf_op jit(solution)/shard_map/project/pallas_call | solution.py:88
  64.7 1.2 %pad_maximum_fusion = bf16[128,4096]{1,0:T(8,128)(2,1)} fusion(bf16[64,4096]{1,0:T(8,128)(2,1)S(1)} %collective-permute-done.15.over_y_ref, bf16[64,4096]{1,0:T(8,128)(2,1)S(1)} %constant_dynamic-update-slice_fusion.2.mine_ref), kind=kLoop, calls=%fused_computation.2 | loop fusion | flops 2097152 | bytes 2097152 | tf_op jit(solution)/shard_map/concatenate | solution.py:233
  65.9 0.1 convert_reduce_fusion
  66.0 3.2 %collective-permute-start.13 = (bf16[16,2048]{1,0:T(8,128)(2,1)S(1)}, bf16[16,2048]{1,0:T(8,128)(2,1)S(1)}, u32[]{:S(2)}, u32[]{:S(2)}) collective-permute-start(bf16[16,2048]{1,0:T(8,128)(2,1)S(1)} %project.3), channel_id=1, source_target_pairs={{12,0},{13,1},{14,2},{15,3},{0,12},{1,13},{2,14},{3,15},{28,16},{2... | collective-permute-start | bytes 196616 | tf_op jit(solution)/shard_map/ppermute | solution.py:144
  69.1 0.1 pad_add_fusion.here_ref
  69.2 0.7 combine.2.refs_2_
  69.9 4.2 %collective-permute-done.13.refs_0_ = bf16[16,2048]{1,0:T(8,128)(2,1)S(1)} collective-permute-done((bf16[16,2048]{1,0:T(8,128)(2,1)S(1)}, bf16[16,2048]{1,0:T(8,128)(2,1)S(1)}, u32[]{:S(2)}, u32[]{:S(2)}) %collective-permute-start.13) | collective-permute-done | bytes 65568 | tf_op jit(solution)/shard_map/ppermute | solution.py:144
  74.2 0.4 combine.3
  74.6 0.1 reshape.146
  74.7 1.1 %copy-done.3 = bf16[64,4096]{1,0:T(8,128)(2,1)S(1)} copy-done((bf16[64,4096]{1,0:T(8,128)(2,1)S(1)}, bf16[64,4096]{1,0:T(8,128)(2,1)}, u32[]{:S(2)}) %copy-start.3) | copy-done | bytes 524312
  75.8 0.7 assemble.1
  76.5 1.2 %fusion.2 = f32[4,256]{1,0:T(4,128)} fusion(bf16[256,4096]{1,0:T(8,128)(2,1)S(1)} %assemble.1, f32[4,4096]{1,0:T(4,128)S(1)} %reshape.146), kind=kOutput, calls=%fused_computation.8 | convolution fusion | flops 8404992 | bytes 2166784 | tf_op jit(solution)/shard_map/dot_general | solution.py:238
  (36 shorter events, 0.4 us)
Async XLA Ops:
  0.6 13.7 %copy-start = (bf16[64,4096]{1,0:T(8,128)(2,1)S(1)}, bf16[64,4096]{1,0:T(8,128)(2,1)}, u32[]{:S(2)}) copy-start(bf16[64,4096]{1,0:T(8,128)(2,1)} %param.9) | copy-start | bytes 1572868
  0.6 17.3 %collective-permute-start = (bf16[64,4096]{1,0:T(8,128)(2,1)}, bf16[64,4096]{1,0:T(8,128)(2,1)}, u32[]{:S(2)}, u32[]{:S(2)}) collective-permute-start(bf16[64,4096]{1,0:T(8,128)(2,1)} %refs_0_.1), channel_id=1, source_target_pairs={{0,4},{1,5},{2,6},{3,7},{4,8},{5,9},{6,10},{7,11},{8,12},{9,13},{1... | collective-permute-start | bytes 1572872 | tf_op jit(solution)/shard_map/ppermute | solution.py:144
  6.5 16.3 %collective-permute-start.2 = (bf16[64,4096]{1,0:T(8,128)(2,1)}, bf16[64,4096]{1,0:T(8,128)(2,1)}, u32[]{:S(2)}, u32[]{:S(2)}) collective-permute-start(bf16[64,4096]{1,0:T(8,128)(2,1)} %refs_0_.1), channel_id=1, source_target_pairs={{4,0},{5,1},{6,2},{7,3},{8,4},{9,5},{10,6},{11,7},{12,8},{13,9},{1... | collective-permute-start | bytes 1572872 | tf_op jit(solution)/shard_map/ppermute | solution.py:144
  7.8 34.8 %collective-permute-start.7 = (bf16[128,4096]{1,0:T(8,128)(2,1)}, bf16[128,4096]{1,0:T(8,128)(2,1)S(1)}, u32[]{:S(2)}, u32[]{:S(2)}) collective-permute-start(bf16[128,4096]{1,0:T(8,128)(2,1)} %bitcast.16), channel_id=1, source_target_pairs={{0,1},{1,0},{2,3},{3,2},{4,5},{5,4},{6,7},{7,6},{8,9},{9,8},{10,11... | collective-permute-start | bytes 3145736 | tf_op jit(solution)/shard_map/ppermute | solution.py:147
  7.9 31.8 %collective-permute-start.8 = (bf16[128,4096]{1,0:T(8,128)(2,1)}, bf16[128,4096]{1,0:T(8,128)(2,1)}, u32[]{:S(2)}, u32[]{:S(2)}) collective-permute-start(bf16[128,4096]{1,0:T(8,128)(2,1)} %bitcast.17), channel_id=1, source_target_pairs={{0,2},{1,3},{2,0},{3,1},{4,6},{5,7},{6,4},{7,5},{8,10},{9,11},{10,... | collective-permute-start | bytes 3145736 | tf_op jit(solution)/shard_map/ppermute | solution.py:147
  10.3 14.7 %collective-permute-start.4 = (bf16[16,2048]{1,0:T(8,128)(2,1)S(1)}, bf16[16,2048]{1,0:T(8,128)(2,1)S(1)}, u32[]{:S(2)}, u32[]{:S(2)}) collective-permute-start(bf16[16,2048]{1,0:T(8,128)(2,1)S(1)} %constant_dynamic-slice_fusion), channel_id=1, source_target_pairs={{0,8},{1,9},{2,10},{3,11},{4,12},{5,13},{6,14},{7,15},{8,0},{9,1},... | collective-permute-start | bytes 196616 | tf_op jit(solution)/shard_map/ppermute | solution.py:147
  15.7 26.9 %copy-start.1 = (bf16[2,4096,64]{1,2,0:T(8,128)(2,1)S(1)}, bf16[2,4096,64]{1,2,0:T(8,128)(2,1)}, u32[]{:S(2)}) copy-start(bf16[2,4096,64]{1,2,0:T(8,128)(2,1)} %param.13) | copy-start | bytes 3145732
  15.7 26.9 %copy-start.4 = (bf16[64,4096]{1,0:T(8,128)(2,1)S(1)}, bf16[64,4096]{1,0:T(8,128)(2,1)}, u32[]{:S(2)}) copy-start(bf16[64,4096]{1,0:T(8,128)(2,1)} %refs_0_.1) | copy-start | bytes 1572868
  17.9 21.6 %collective-permute-start.1 = (bf16[64,4096]{1,0:T(8,128)(2,1)}, bf16[64,4096]{1,0:T(8,128)(2,1)S(1)}, u32[]{:S(2)}, u32[]{:S(2)}) collective-permute-start(bf16[64,4096]{1,0:T(8,128)(2,1)} %collective-permute-done.refs_1_), channel_id=1, source_target_pairs={{4,8},{5,9},{6,10},{7,11},{8,12},{9,13},{10,14},{11,15},{20,24},{2... | collective-permute-start | bytes 1572872 | tf_op jit(solution)/shard_map/ppermute | solution.py:144
  22.8 16.7 %collective-permute-start.3 = (bf16[64,4096]{1,0:T(8,128)(2,1)}, bf16[64,4096]{1,0:T(8,128)(2,1)S(1)}, u32[]{:S(2)}, u32[]{:S(2)}) collective-permute-start(bf16[64,4096]{1,0:T(8,128)(2,1)} %collective-permute-done.2.refs_2_), channel_id=1, source_target_pairs={{4,0},{5,1},{6,2},{7,3},{8,4},{9,5},{10,6},{11,7},{20,16},{21,17},... | collective-permute-start | bytes 1572872 | tf_op jit(solution)/shard_map/ppermute | solution.py:144
  25.0 14.4 %collective-permute-start.5 = (bf16[32,2048]{1,0:T(8,128)(2,1)S(1)}, bf16[32,2048]{1,0:T(8,128)(2,1)S(1)}, u32[]{:S(2)}, u32[]{:S(2)}) collective-permute-start(bf16[32,2048]{1,0:T(8,128)(2,1)S(1)} %pad_maximum_fusion.1), channel_id=1, source_target_pairs={{0,4},{1,5},{2,6},{3,7},{4,0},{5,1},{6,2},{7,3},{8,12},{9,13},{10,... | collective-permute-start | bytes 393224 | tf_op jit(solution)/shard_map/ppermute | solution.py:147
  39.7 2.9 %collective-permute-start.9 = (bf16[128,4096]{1,0:T(8,128)(2,1)}, bf16[128,4096]{1,0:T(8,128)(2,1)S(1)}, u32[]{:S(2)}, u32[]{:S(2)}) collective-permute-start(bf16[128,4096]{1,0:T(8,128)(2,1)} %collective-permute-done.8.refs_6_.refs_3_), channel_id=1, source_target_pairs={{0,1},{1,0},{2,3},{3,2},{4,5},{5,4},{6,7},{7,6},{8,9},{9,8},{10,11... | collective-permute-start | bytes 3145736 | tf_op jit(solution)/shard_map/ppermute | solution.py:147
  39.7 8.7 %collective-permute-start.14 = (bf16[64,2048]{1,0:T(8,128)(2,1)S(1)}, bf16[64,2048]{1,0:T(8,128)(2,1)S(1)}, u32[]{:S(2)}, u32[]{:S(2)}) collective-permute-start(bf16[64,2048]{1,0:T(8,128)(2,1)S(1)} %constant_dynamic-update-slice_fusion), channel_id=1, source_target_pairs={{0,16},{16,0},{1,17},{17,1},{2,18},{18,2},{3,19},{19,3},{4,20},{20... | collective-permute-start | bytes 786440 | tf_op jit(solution)/shard_map/ppermute | solution.py:219
  41.3 16.6 %collective-permute-start.6 = (bf16[64,4096]{1,0:T(8,128)(2,1)S(1)}, bf16[64,4096]{1,0:T(8,128)(2,1)S(1)}, u32[]{:S(2)}, u32[]{:S(2)}) collective-permute-start(bf16[64,4096]{1,0:T(8,128)(2,1)S(1)} %add.58.refs_3_), channel_id=1, source_target_pairs={{8,12},{9,13},{10,14},{11,15},{4,0},{5,1},{6,2},{7,3},{24,28},{25,... | collective-permute-start | bytes 1572872 | tf_op jit(solution)/shard_map/ppermute | solution.py:144
  48.5 16.2 %collective-permute-start.15 = (bf16[64,4096]{1,0:T(8,128)(2,1)S(1)}, bf16[64,4096]{1,0:T(8,128)(2,1)S(1)}, u32[]{:S(2)}, u32[]{:S(2)}) collective-permute-start(bf16[64,4096]{1,0:T(8,128)(2,1)S(1)} %constant_dynamic-update-slice_fusion.2.mine_ref), channel_id=1, source_target_pairs={{0,2},{1,3},{2,0},{3,1},{4,6},{5,7},{6,4},{7,5},{8,10},{9,11},{10,... | collective-permute-start | bytes 1572872 | tf_op jit(solution)/shard_map/ppermute | solution.py:147
  50.1 8.6 %collective-permute-start.10 = (bf16[16,2048]{1,0:T(8,128)(2,1)S(1)}, bf16[16,2048]{1,0:T(8,128)(2,1)S(1)}, u32[]{:S(2)}, u32[]{:S(2)}) collective-permute-start(bf16[16,2048]{1,0:T(8,128)(2,1)S(1)} %get-tuple-element.17), channel_id=1, source_target_pairs={{4,0},{5,1},{6,2},{7,3},{8,4},{9,5},{10,6},{11,7},{12,8},{13,9},{1... | collective-permute-start | bytes 196616 | tf_op jit(solution)/shard_map/ppermute | solution.py:144
  51.4 7.3 %collective-permute-start.11 = (bf16[16,2048]{1,0:T(8,128)(2,1)S(1)}, bf16[16,2048]{1,0:T(8,128)(2,1)S(1)}, u32[]{:S(2)}, u32[]{:S(2)}) collective-permute-start(bf16[16,2048]{1,0:T(8,128)(2,1)S(1)} %get-tuple-element.18), channel_id=1, source_target_pairs={{0,4},{1,5},{2,6},{3,7},{4,8},{5,9},{6,10},{7,11},{8,12},{9,13},{1... | collective-permute-start | bytes 196616 | tf_op jit(solution)/shard_map/ppermute | solution.py:144
  56.0 5.7 %collective-permute-start.12 = (bf16[16,2048]{1,0:T(8,128)(2,1)S(1)}, bf16[16,2048]{1,0:T(8,128)(2,1)S(1)}, u32[]{:S(2)}, u32[]{:S(2)}) collective-permute-start(bf16[16,2048]{1,0:T(8,128)(2,1)S(1)} %get-tuple-element.19), channel_id=1, source_target_pairs={{8,0},{9,1},{10,2},{11,3},{12,4},{13,5},{14,6},{15,7},{0,8},{1,9},... | collective-permute-start | bytes 196616 | tf_op jit(solution)/shard_map/ppermute | solution.py:144
  64.7 1.2 %copy-start.6 = (s32[1,64]{1,0:T(1,128)S(1)}, s32[1,64]{1,0:T(1,128)}, u32[]{:S(2)}) copy-start(s32[1,64]{1,0:T(1,128)} %param.12) | copy-start | bytes 772
  64.7 5.2 %copy-start.2 = (bf16[64,4096]{1,0:T(8,128)(2,1)}, bf16[64,4096]{1,0:T(8,128)(2,1)S(1)}, u32[]{:S(2)}) copy-start(bf16[64,4096]{1,0:T(8,128)(2,1)S(1)} %collective-permute-done.15.over_y_ref) | copy-start | bytes 1572868
  65.9 8.9 %collective-permute-start.16 = (bf16[128,4096]{1,0:T(8,128)(2,1)}, bf16[128,4096]{1,0:T(8,128)(2,1)S(1)}, u32[]{:S(2)}, u32[]{:S(2)}) collective-permute-start(bf16[128,4096]{1,0:T(8,128)(2,1)} %pad_maximum_fusion), channel_id=1, source_target_pairs={{0,1},{1,0},{2,3},{3,2},{4,5},{5,4},{6,7},{7,6},{8,9},{9,8},{10,11... | collective-permute-start | bytes 3145736 | tf_op jit(solution)/shard_map/ppermute | solution.py:147
  66.0 8.2 %collective-permute-start.13 = (bf16[16,2048]{1,0:T(8,128)(2,1)S(1)}, bf16[16,2048]{1,0:T(8,128)(2,1)S(1)}, u32[]{:S(2)}, u32[]{:S(2)}) collective-permute-start(bf16[16,2048]{1,0:T(8,128)(2,1)S(1)} %project.3), channel_id=1, source_target_pairs={{12,0},{13,1},{14,2},{15,3},{0,12},{1,13},{2,14},{3,15},{28,16},{2... | collective-permute-start | bytes 196616 | tf_op jit(solution)/shard_map/ppermute | solution.py:144
  74.7 1.8 %copy-start.5 = (f32[4,4096]{1,0:T(4,128)}, f32[4,4096]{1,0:T(4,128)S(1)}, u32[]{:S(2)}) copy-start(f32[4,4096]{1,0:T(4,128)S(1)} %reshape.146) | copy-start | bytes 196612
  74.7 1.1 %copy-start.3 = (bf16[64,4096]{1,0:T(8,128)(2,1)S(1)}, bf16[64,4096]{1,0:T(8,128)(2,1)}, u32[]{:S(2)}) copy-start(bf16[64,4096]{1,0:T(8,128)(2,1)} %copy-done.2) | copy-start | bytes 1572868

commit v12 on v11

--- a/solution.py
+++ b/solution.py
@@ -233,7 +233,7 @@
     rest = swap(after(jnp.concatenate([mine, mine_over_y], axis=0), side), 1)
     here = jnp.stack([plane, spot, group]).astype(jnp.int32)
     all_queries = assemble(here, mine, mine_over_y, rest, order, groups)
-    sketches = combine([late], wide_late, early, counts)
+    sketches = combine([late], after(wide_late, all_queries), early, counts)
     sketches = sketches.reshape(EX_DEV, RANK * RANK)
     scores = lax.dot_general(sketches.astype(jnp.bfloat16), all_queries, NT, preferred_element_type=jnp.float32)
     return (sketches, scores)

time: 78.3 us -> 75.9 us (0.969)
  waiting for transfers between devices: 29.9 us -> 23.3 us
  starting transfers between devices: 29.5 us -> 35.5 us
  other arithmetic: 3.86 us -> 2.79 us
    ppermute x7, waiting for transfers between devices: 13.1 us -> 9.4 us  [swap(): return lax.ppermute(array, 'expert', [(i, i ^ bit) for i in range(n)])]
    ppermute x9, starting transfers between devices: 19.5 us -> 22.5 us  [move(): return lax.ppermute(array, 'expert', pairs)]
    ppermute x7, starting transfers between devices: 8.45 us -> 11.4 us  [swap(): return lax.ppermute(array, 'expert', [(i, i ^ bit) for i in range(n)])]
    ppermute x9, waiting for transfers between devices: 14.5 us -> 11.5 us  [move(): return lax.ppermute(array, 'expert', pairs)]
    concatenate x1, other arithmetic: 1.15 us -> 0.09 us  [shards(): rest = swap(after(jnp.concatenate([mine, mine_over_y], axis=0), side), 1)]
  transfers between devices with their start and end apart: 17 -> 17, of which waited for: 9 -> 7; matrix products, arithmetic and copies ran while one was open for 7% -> 7% of each run, Pallas kernels for 10% -> 10%
where the time goes in v12:
time: 75.9 us; the launch traced here: 75.4 us
  starting transfers between devices  35.5 us (47%)
  waiting for transfers between devices  23.3 us (31%)
  Pallas kernels  8.25 us (11%)
  other arithmetic  2.79 us (4%)
  matrix products  2.58 us (3%)
  local copies, waits for them, and re-layouts  2.08 us (3%)
  between operations  0.99 us (1%)
    ppermute x9, starting transfers between devices, move(): return lax.ppermute(array, 'expert', pairs)  22.5 us
    ppermute x9, waiting for transfers between devices, move(): return lax.ppermute(array, 'expert', pairs)  11.5 us
    ppermute x7, starting transfers between devices, swap(): return lax.ppermute(array, 'expert', [(i, i ^ bit) for i in range(n)])  11.4 us
    ppermute x7, waiting for transfers between devices, swap(): return lax.ppermute(array, 'expert', [(i, i ^ bit) for i in range(n)])  9.4 us
    pallas_call x2, Pallas kernels, project(): pl.pallas_call(functools.partial(project_kernel, len(parts), rows), out_s...  6.5 us
    ppermute x1, waiting for transfers between devices, shards(): lax.ppermute(lined, 'groups', [(g, (g + k) % groups) for g in range(group...  2.35 us
    ppermute x1, starting transfers between devices, shards(): lax.ppermute(lined, 'groups', [(g, (g + k) % groups) for g in range(group...  1.56 us
  transfers between devices with their start and end apart: 17, of which 7 were waited for; matrix products, arithmetic and copies ran while one was open for 7% of the time, Pallas kernels for 10%

profile of v12, /device:TPU:0, one launch (start us, length us, event | category | flops | bytes accessed | tf_op | source)
XLA Modules:
  0.0 75.4 jit_solution(14089975028506956346)
XLA Ops:
  0.6 5.9 %collective-permute-start = (bf16[64,4096]{1,0:T(8,128)(2,1)}, bf16[64,4096]{1,0:T(8,128)(2,1)}, u32[]{:S(2)}, u32[]{:S(2)}) collective-permute-start(bf16[64,4096]{1,0:T(8,128)(2,1)} %refs_0_.1), channel_id=1, source_target_pairs={{0,4},{1,5},{2,6},{3,7},{4,8},{5,9},{6,10},{7,11},{8,12},{9,13},{1... | collective-permute-start | bytes 1572872 | tf_op jit(solution)/shard_map/ppermute | solution.py:144
  6.5 1.3 %collective-permute-start.2 = (bf16[64,4096]{1,0:T(8,128)(2,1)}, bf16[64,4096]{1,0:T(8,128)(2,1)}, u32[]{:S(2)}, u32[]{:S(2)}) collective-permute-start(bf16[64,4096]{1,0:T(8,128)(2,1)} %refs_0_.1), channel_id=1, source_target_pairs={{4,0},{5,1},{6,2},{7,3},{8,4},{9,5},{10,6},{11,7},{12,8},{13,9},{1... | collective-permute-start | bytes 1572872 | tf_op jit(solution)/shard_map/ppermute | solution.py:144
  7.8 1.6 %collective-permute-start.8 = (bf16[128,4096]{1,0:T(8,128)(2,1)}, bf16[128,4096]{1,0:T(8,128)(2,1)S(1)}, u32[]{:S(2)}, u32[]{:S(2)}) collective-permute-start(bf16[128,4096]{1,0:T(8,128)(2,1)} %bitcast.16), channel_id=1, source_target_pairs={{0,2},{1,3},{2,0},{3,1},{4,6},{5,7},{6,4},{7,5},{8,10},{9,11},{10,... | collective-permute-start | bytes 3145736 | tf_op jit(solution)/shard_map/ppermute | solution.py:147
  9.4 0.8 %constant_dynamic-slice_fusion = bf16[16,2048]{1,0:T(8,128)(2,1)S(1)} fusion(bf16[16,4096]{1,0:T(8,128)(2,1)} %param.15, s32[]{:T(128)S(6)} %select_n.74), kind=kLoop, calls=%fused_computation.22 | loop fusion | bytes 131076 | tf_op jit(solution)/shard_map/dynamic_slice | solution.py:188
  10.3 2.9 %collective-permute-start.4 = (bf16[16,2048]{1,0:T(8,128)(2,1)S(1)}, bf16[16,2048]{1,0:T(8,128)(2,1)S(1)}, u32[]{:S(2)}, u32[]{:S(2)}) collective-permute-start(bf16[16,2048]{1,0:T(8,128)(2,1)S(1)} %constant_dynamic-slice_fusion), channel_id=1, source_target_pairs={{0,8},{1,9},{2,10},{3,11},{4,12},{5,13},{6,14},{7,15},{8,0},{9,1},... | collective-permute-start | bytes 196616 | tf_op jit(solution)/shard_map/ppermute | solution.py:147
  13.1 0.1 stack.33
  13.2 0.1 iota_add_fusion
  13.3 0.1 add.55
  13.4 0.1 add_select_fusion
  13.5 0.1 select_n.90
  13.5 0.7 iota_compare_fusion
  14.3 1.3 %fusion.4 = f32[64,64]{1,0:T(8,128)S(1)} fusion(bf16[64,4096]{1,0:T(8,128)(2,1)S(1)} %copy-done, bf16[4096,64]{0,1:T(8,128)(2,1)} %param.14), kind=kOutput, calls=%fused_computation.23 | convolution fusion | flops 33554432 | bytes 1064960 | tf_op jit(solution)/shard_map/dot_general | solution.py:163
  15.6 0.9 %select_reduce_fusion = f32[40,64]{1,0:T(8,128)S(1)} fusion(f32[8,64]{1,0:T(8,128)} %bitcast.20, s32[8,64]{1,0:T(8,128)} %bitcast.21, s32[40]{0:T(128)S(1)} %select_n.90), kind=kLoop, calls=%fused_computation.5 | loop fusion | flops 58880 | bytes 14496 | tf_op jit(solution)/shard_map/reduce_sum | solution.py:168
  16.6 0.1 pad_maximum_fusion.2
  16.7 0.1 broadcast_in_dim.70
  16.9 0.1 broadcast_in_dim.71
  17.0 0.3 fusion.refs_4_
  17.3 0.1 fusion.1.refs_1_
  17.5 5.4 %collective-permute-done.2.refs_2_ = bf16[64,4096]{1,0:T(8,128)(2,1)} collective-permute-done((bf16[64,4096]{1,0:T(8,128)(2,1)}, bf16[64,4096]{1,0:T(8,128)(2,1)}, u32[]{:S(2)}, u32[]{:S(2)}) %collective-permute-start.2) | collective-permute-done | bytes 524320 | tf_op jit(solution)/shard_map/ppermute | solution.py:144
  22.8 1.3 %collective-permute-start.3 = (bf16[64,4096]{1,0:T(8,128)(2,1)}, bf16[64,4096]{1,0:T(8,128)(2,1)S(1)}, u32[]{:S(2)}, u32[]{:S(2)}) collective-permute-start(bf16[64,4096]{1,0:T(8,128)(2,1)} %collective-permute-done.2.refs_2_), channel_id=1, source_target_pairs={{4,0},{5,1},{6,2},{7,3},{8,4},{9,5},{10,6},{11,7},{20,16},{21,17},... | collective-permute-start | bytes 1572872 | tf_op jit(solution)/shard_map/ppermute | solution.py:144
  24.1 0.7 collective-permute-start.1
  24.8 0.2 collective-permute-done.4
  25.0 5.3 %collective-permute-start.5 = (bf16[32,2048]{1,0:T(8,128)(2,1)S(1)}, bf16[32,2048]{1,0:T(8,128)(2,1)S(1)}, u32[]{:S(2)}, u32[]{:S(2)}) collective-permute-start(bf16[32,2048]{1,0:T(8,128)(2,1)S(1)} %pad_maximum_fusion.1), channel_id=1, source_target_pairs={{0,4},{1,5},{2,6},{3,7},{4,0},{5,1},{6,2},{7,3},{8,12},{9,13},{10,... | collective-permute-start | bytes 393224 | tf_op jit(solution)/shard_map/ppermute | solution.py:147
  30.3 9.2 %collective-permute-done.5 = bf16[32,2048]{1,0:T(8,128)(2,1)S(1)} collective-permute-done((bf16[32,2048]{1,0:T(8,128)(2,1)S(1)}, bf16[32,2048]{1,0:T(8,128)(2,1)S(1)}, u32[]{:S(2)}, u32[]{:S(2)}) %collective-permute-start.5) | collective-permute-done | bytes 131104 | tf_op jit(solution)/shard_map/ppermute | solution.py:147
  39.5 0.1 add.58.refs_3_
  39.7 0.1 collective-permute-start.9
  39.8 1.6 %collective-permute-start.14 = (bf16[64,2048]{1,0:T(8,128)(2,1)S(1)}, bf16[64,2048]{1,0:T(8,128)(2,1)S(1)}, u32[]{:S(2)}, u32[]{:S(2)}) collective-permute-start(bf16[64,2048]{1,0:T(8,128)(2,1)S(1)} %constant_dynamic-update-slice_fusion), channel_id=1, source_target_pairs={{0,16},{16,0},{1,17},{17,1},{2,18},{18,2},{3,19},{19,3},{4,20},{20... | collective-permute-start | bytes 786440 | tf_op jit(solution)/shard_map/ppermute | solution.py:219
  41.3 1.3 %collective-permute-start.6 = (bf16[64,4096]{1,0:T(8,128)(2,1)S(1)}, bf16[64,4096]{1,0:T(8,128)(2,1)S(1)}, u32[]{:S(2)}, u32[]{:S(2)}) collective-permute-start(bf16[64,4096]{1,0:T(8,128)(2,1)S(1)} %add.58.refs_3_), channel_id=1, source_target_pairs={{8,12},{9,13},{10,14},{11,15},{4,0},{5,1},{6,2},{7,3},{24,28},{25,... | collective-permute-start | bytes 1572872 | tf_op jit(solution)/shard_map/ppermute | solution.py:144
  42.6 3.5 %project.2 = (bf16[16,2048]{1,0:T(8,128)(2,1)S(1)}, bf16[16,2048]{1,0:T(8,128)(2,1)S(1)}, bf16[16,2048]{1,0:T(8,128)(2,1)S(1)}, bf16[16,2048]{1,0:T(8,128)(2,1)S(1)}) custom-call(bf16[64,4096]{1,0:T(8,128)(2,1)S(1)} %copy-done.2, bf16[64,4096]{1,0:T(8,128)(2,1)} %collective-permute-done.refs_1_, bf16[64,4096]{1,0:T(8,128)(2,1)} %collective-permute-done.2.refs_2_, ...), custom_call_target="tpu_custom_call" | custom-call | flops 1024 | bytes 1024 | tf_op jit(solution)/shard_map/project/pallas_call | solution.py:88
  46.1 2.3 %collective-permute-done.14 = bf16[64,2048]{1,0:T(8,128)(2,1)S(1)} collective-permute-done((bf16[64,2048]{1,0:T(8,128)(2,1)S(1)}, bf16[64,2048]{1,0:T(8,128)(2,1)S(1)}, u32[]{:S(2)}, u32[]{:S(2)}) %collective-permute-start.14) | collective-permute-done | bytes 262176 | tf_op jit(solution)/shard_map/ppermute | solution.py:219
  48.5 1.6 %collective-permute-start.15 = (bf16[64,4096]{1,0:T(8,128)(2,1)S(1)}, bf16[64,4096]{1,0:T(8,128)(2,1)S(1)}, u32[]{:S(2)}, u32[]{:S(2)}) collective-permute-start(bf16[64,4096]{1,0:T(8,128)(2,1)S(1)} %constant_dynamic-update-slice_fusion.2.mine_ref), channel_id=1, source_target_pairs={{0,2},{1,3},{2,0},{3,1},{4,6},{5,7},{6,4},{7,5},{8,10},{9,11},{10,... | collective-permute-start | bytes 1572872 | tf_op jit(solution)/shard_map/ppermute | solution.py:147
  50.1 1.3 %collective-permute-start.10 = (bf16[16,2048]{1,0:T(8,128)(2,1)S(1)}, bf16[16,2048]{1,0:T(8,128)(2,1)S(1)}, u32[]{:S(2)}, u32[]{:S(2)}) collective-permute-start(bf16[16,2048]{1,0:T(8,128)(2,1)S(1)} %get-tuple-element.18), channel_id=1, source_target_pairs={{4,0},{5,1},{6,2},{7,3},{8,4},{9,5},{10,6},{11,7},{12,8},{13,9},{1... | collective-permute-start | bytes 196616 | tf_op jit(solution)/shard_map/ppermute | solution.py:144
  51.4 4.5 %collective-permute-start.11 = (bf16[16,2048]{1,0:T(8,128)(2,1)S(1)}, bf16[16,2048]{1,0:T(8,128)(2,1)S(1)}, u32[]{:S(2)}, u32[]{:S(2)}) collective-permute-start(bf16[16,2048]{1,0:T(8,128)(2,1)S(1)} %get-tuple-element.19), channel_id=1, source_target_pairs={{0,4},{1,5},{2,6},{3,7},{4,8},{5,9},{6,10},{7,11},{8,12},{9,13},{1... | collective-permute-start | bytes 196616 | tf_op jit(solution)/shard_map/ppermute | solution.py:144
  56.0 2.6 %collective-permute-start.12 = (bf16[16,2048]{1,0:T(8,128)(2,1)S(1)}, bf16[16,2048]{1,0:T(8,128)(2,1)S(1)}, u32[]{:S(2)}, u32[]{:S(2)}) collective-permute-start(bf16[16,2048]{1,0:T(8,128)(2,1)S(1)} %get-tuple-element.20), channel_id=1, source_target_pairs={{8,0},{9,1},{10,2},{11,3},{12,4},{13,5},{14,6},{15,7},{0,8},{1,9},... | collective-permute-start | bytes 196616 | tf_op jit(solution)/shard_map/ppermute | solution.py:144
  58.5 0.8 collective-permute-done.10.refs_1_
  59.3 2.6 %collective-permute-done.12.refs_3_ = bf16[16,2048]{1,0:T(8,128)(2,1)S(1)} collective-permute-done((bf16[16,2048]{1,0:T(8,128)(2,1)S(1)}, bf16[16,2048]{1,0:T(8,128)(2,1)S(1)}, u32[]{:S(2)}, u32[]{:S(2)}) %collective-permute-start.12) | collective-permute-done | bytes 65568 | tf_op jit(solution)/shard_map/ppermute | solution.py:144
  61.9 3.0 %project.3 = bf16[16,2048]{1,0:T(8,128)(2,1)S(1)} custom-call(bf16[64,4096]{1,0:T(8,128)(2,1)S(1)} %collective-permute-done.6.refs_0_, bf16[128,4096]{1,0:T(8,128)(2,1)S(1)} %bitcast.19, bf16[128,4096]{1,0:T(8,128)(2,1)} %collective-permute-done.7.refs_5_.refs_2_, bf16[128,4096]{1,0:T(8,128)(2,1)S(1)} %collective-permute-done.8.refs_6_.refs_3_, ...), custom_call_target="tpu_custom_call" | custom-call | flops 1024 | bytes 1024 | tf_op jit(solution)/shard_map/project/pallas_call | solution.py:88
  64.9 0.1 pad_maximum_fusion
  65.1 0.5 copy-done.4
  65.6 0.1 convert_reduce_fusion
  65.7 3.7 %collective-permute-start.13 = (bf16[16,2048]{1,0:T(8,128)(2,1)S(1)}, bf16[16,2048]{1,0:T(8,128)(2,1)S(1)}, u32[]{:S(2)}, u32[]{:S(2)}) collective-permute-start(bf16[16,2048]{1,0:T(8,128)(2,1)S(1)} %project.3), channel_id=1, source_target_pairs={{12,0},{13,1},{14,2},{15,3},{0,12},{1,13},{2,14},{3,15},{28,16},{2... | collective-permute-start | bytes 196616 | tf_op jit(solution)/shard_map/ppermute | solution.py:144
  69.3 0.1 pad_add_fusion.here_ref
  69.4 0.7 combine.2.refs_2_
  70.1 0.7 assemble.1
  70.8 2.8 %collective-permute-done.13.refs_0_ = bf16[16,2048]{1,0:T(8,128)(2,1)S(1)} collective-permute-done((bf16[16,2048]{1,0:T(8,128)(2,1)S(1)}, bf16[16,2048]{1,0:T(8,128)(2,1)S(1)}, u32[]{:S(2)}, u32[]{:S(2)}) %collective-permute-start.13) | collective-permute-done | bytes 65568 | tf_op jit(solution)/shard_map/ppermute | solution.py:144
  73.7 0.4 combine.3
  74.1 0.1 reshape.146
  74.2 1.2 %fusion.2 = f32[4,256]{1,0:T(4,128)} fusion(bf16[256,4096]{1,0:T(8,128)(2,1)S(1)} %assemble.1, f32[4,4096]{1,0:T(4,128)S(1)} %reshape.146), kind=kOutput, calls=%fused_computation.8 | convolution fusion | flops 8404992 | bytes 2166784 | tf_op jit(solution)/shard_map/dot_general | solution.py:238
  (32 shorter events, 0.3 us)
Async XLA Ops:
  0.6 13.6 %copy-start = (bf16[64,4096]{1,0:T(8,128)(2,1)S(1)}, bf16[64,4096]{1,0:T(8,128)(2,1)}, u32[]{:S(2)}) copy-start(bf16[64,4096]{1,0:T(8,128)(2,1)} %param.9) | copy-start | bytes 1572868
  0.6 23.5 %collective-permute-start = (bf16[64,4096]{1,0:T(8,128)(2,1)}, bf16[64,4096]{1,0:T(8,128)(2,1)}, u32[]{:S(2)}, u32[]{:S(2)}) collective-permute-start(bf16[64,4096]{1,0:T(8,128)(2,1)} %refs_0_.1), channel_id=1, source_target_pairs={{0,4},{1,5},{2,6},{3,7},{4,8},{5,9},{6,10},{7,11},{8,12},{9,13},{1... | collective-permute-start | bytes 1572872 | tf_op jit(solution)/shard_map/ppermute | solution.py:144
  6.5 16.3 %collective-permute-start.2 = (bf16[64,4096]{1,0:T(8,128)(2,1)}, bf16[64,4096]{1,0:T(8,128)(2,1)}, u32[]{:S(2)}, u32[]{:S(2)}) collective-permute-start(bf16[64,4096]{1,0:T(8,128)(2,1)} %refs_0_.1), channel_id=1, source_target_pairs={{4,0},{5,1},{6,2},{7,3},{8,4},{9,5},{10,6},{11,7},{12,8},{13,9},{1... | collective-permute-start | bytes 1572872 | tf_op jit(solution)/shard_map/ppermute | solution.py:144
  7.8 31.8 %collective-permute-start.8 = (bf16[128,4096]{1,0:T(8,128)(2,1)}, bf16[128,4096]{1,0:T(8,128)(2,1)S(1)}, u32[]{:S(2)}, u32[]{:S(2)}) collective-permute-start(bf16[128,4096]{1,0:T(8,128)(2,1)} %bitcast.16), channel_id=1, source_target_pairs={{0,2},{1,3},{2,0},{3,1},{4,6},{5,7},{6,4},{7,5},{8,10},{9,11},{10,... | collective-permute-start | bytes 3145736 | tf_op jit(solution)/shard_map/ppermute | solution.py:147
  9.4 33.2 %collective-permute-start.7 = (bf16[128,4096]{1,0:T(8,128)(2,1)}, bf16[128,4096]{1,0:T(8,128)(2,1)}, u32[]{:S(2)}, u32[]{:S(2)}) collective-permute-start(bf16[128,4096]{1,0:T(8,128)(2,1)} %bitcast.17), channel_id=1, source_target_pairs={{0,1},{1,0},{2,3},{3,2},{4,5},{5,4},{6,7},{7,6},{8,9},{9,8},{10,11... | collective-permute-start | bytes 3145736 | tf_op jit(solution)/shard_map/ppermute | solution.py:147
  10.3 14.8 %collective-permute-start.4 = (bf16[16,2048]{1,0:T(8,128)(2,1)S(1)}, bf16[16,2048]{1,0:T(8,128)(2,1)S(1)}, u32[]{:S(2)}, u32[]{:S(2)}) collective-permute-start(bf16[16,2048]{1,0:T(8,128)(2,1)S(1)} %constant_dynamic-slice_fusion), channel_id=1, source_target_pairs={{0,8},{1,9},{2,10},{3,11},{4,12},{5,13},{6,14},{7,15},{8,0},{9,1},... | collective-permute-start | bytes 196616 | tf_op jit(solution)/shard_map/ppermute | solution.py:147
  15.6 27.0 %copy-start.1 = (bf16[2,4096,64]{1,2,0:T(8,128)(2,1)S(1)}, bf16[2,4096,64]{1,2,0:T(8,128)(2,1)}, u32[]{:S(2)}) copy-start(bf16[2,4096,64]{1,2,0:T(8,128)(2,1)} %param.13) | copy-start | bytes 3145732
  15.6 27.0 %copy-start.2 = (bf16[64,4096]{1,0:T(8,128)(2,1)S(1)}, bf16[64,4096]{1,0:T(8,128)(2,1)}, u32[]{:S(2)}) copy-start(bf16[64,4096]{1,0:T(8,128)(2,1)} %refs_0_.1) | copy-start | bytes 1572868
  22.8 16.7 %collective-permute-start.3 = (bf16[64,4096]{1,0:T(8,128)(2,1)}, bf16[64,4096]{1,0:T(8,128)(2,1)S(1)}, u32[]{:S(2)}, u32[]{:S(2)}) collective-permute-start(bf16[64,4096]{1,0:T(8,128)(2,1)} %collective-permute-done.2.refs_2_), channel_id=1, source_target_pairs={{4,0},{5,1},{6,2},{7,3},{8,4},{9,5},{10,6},{11,7},{20,16},{21,17},... | collective-permute-start | bytes 1572872 | tf_op jit(solution)/shard_map/ppermute | solution.py:144
  24.1 15.4 %collective-permute-start.1 = (bf16[64,4096]{1,0:T(8,128)(2,1)}, bf16[64,4096]{1,0:T(8,128)(2,1)S(1)}, u32[]{:S(2)}, u32[]{:S(2)}) collective-permute-start(bf16[64,4096]{1,0:T(8,128)(2,1)} %collective-permute-done.refs_1_), channel_id=1, source_target_pairs={{4,8},{5,9},{6,10},{7,11},{8,12},{9,13},{10,14},{11,15},{20,24},{2... | collective-permute-start | bytes 1572872 | tf_op jit(solution)/shard_map/ppermute | solution.py:144
  25.0 14.4 %collective-permute-start.5 = (bf16[32,2048]{1,0:T(8,128)(2,1)S(1)}, bf16[32,2048]{1,0:T(8,128)(2,1)S(1)}, u32[]{:S(2)}, u32[]{:S(2)}) collective-permute-start(bf16[32,2048]{1,0:T(8,128)(2,1)S(1)} %pad_maximum_fusion.1), channel_id=1, source_target_pairs={{0,4},{1,5},{2,6},{3,7},{4,0},{5,1},{6,2},{7,3},{8,12},{9,13},{10,... | collective-permute-start | bytes 393224 | tf_op jit(solution)/shard_map/ppermute | solution.py:147
  39.7 2.9 %collective-permute-start.9 = (bf16[128,4096]{1,0:T(8,128)(2,1)S(1)}, bf16[128,4096]{1,0:T(8,128)(2,1)S(1)}, u32[]{:S(2)}, u32[]{:S(2)}) collective-permute-start(bf16[128,4096]{1,0:T(8,128)(2,1)S(1)} %collective-permute-done.8.refs_6_.refs_3_), channel_id=1, source_target_pairs={{0,1},{1,0},{2,3},{3,2},{4,5},{5,4},{6,7},{7,6},{8,9},{9,8},{10,11... | collective-permute-start | bytes 3145736 | tf_op jit(solution)/shard_map/ppermute | solution.py:147
  39.8 8.7 %collective-permute-start.14 = (bf16[64,2048]{1,0:T(8,128)(2,1)S(1)}, bf16[64,2048]{1,0:T(8,128)(2,1)S(1)}, u32[]{:S(2)}, u32[]{:S(2)}) collective-permute-start(bf16[64,2048]{1,0:T(8,128)(2,1)S(1)} %constant_dynamic-update-slice_fusion), channel_id=1, source_target_pairs={{0,16},{16,0},{1,17},{17,1},{2,18},{18,2},{3,19},{19,3},{4,20},{20... | collective-permute-start | bytes 786440 | tf_op jit(solution)/shard_map/ppermute | solution.py:219
  41.3 17.2 %collective-permute-start.6 = (bf16[64,4096]{1,0:T(8,128)(2,1)S(1)}, bf16[64,4096]{1,0:T(8,128)(2,1)S(1)}, u32[]{:S(2)}, u32[]{:S(2)}) collective-permute-start(bf16[64,4096]{1,0:T(8,128)(2,1)S(1)} %add.58.refs_3_), channel_id=1, source_target_pairs={{8,12},{9,13},{10,14},{11,15},{4,0},{5,1},{6,2},{7,3},{24,28},{25,... | collective-permute-start | bytes 1572872 | tf_op jit(solution)/shard_map/ppermute | solution.py:144
  48.5 16.4 %collective-permute-start.15 = (bf16[64,4096]{1,0:T(8,128)(2,1)S(1)}, bf16[64,4096]{1,0:T(8,128)(2,1)S(1)}, u32[]{:S(2)}, u32[]{:S(2)}) collective-permute-start(bf16[64,4096]{1,0:T(8,128)(2,1)S(1)} %constant_dynamic-update-slice_fusion.2.mine_ref), channel_id=1, source_target_pairs={{0,2},{1,3},{2,0},{3,1},{4,6},{5,7},{6,4},{7,5},{8,10},{9,11},{10,... | collective-permute-start | bytes 1572872 | tf_op jit(solution)/shard_map/ppermute | solution.py:147
  50.1 9.2 %collective-permute-start.10 = (bf16[16,2048]{1,0:T(8,128)(2,1)S(1)}, bf16[16,2048]{1,0:T(8,128)(2,1)S(1)}, u32[]{:S(2)}, u32[]{:S(2)}) collective-permute-start(bf16[16,2048]{1,0:T(8,128)(2,1)S(1)} %get-tuple-element.18), channel_id=1, source_target_pairs={{4,0},{5,1},{6,2},{7,3},{8,4},{9,5},{10,6},{11,7},{12,8},{13,9},{1... | collective-permute-start | bytes 196616 | tf_op jit(solution)/shard_map/ppermute | solution.py:144
  51.4 7.9 %collective-permute-start.11 = (bf16[16,2048]{1,0:T(8,128)(2,1)S(1)}, bf16[16,2048]{1,0:T(8,128)(2,1)S(1)}, u32[]{:S(2)}, u32[]{:S(2)}) collective-permute-start(bf16[16,2048]{1,0:T(8,128)(2,1)S(1)} %get-tuple-element.19), channel_id=1, source_target_pairs={{0,4},{1,5},{2,6},{3,7},{4,8},{5,9},{6,10},{7,11},{8,12},{9,13},{1... | collective-permute-start | bytes 196616 | tf_op jit(solution)/shard_map/ppermute | solution.py:144
  56.0 5.9 %collective-permute-start.12 = (bf16[16,2048]{1,0:T(8,128)(2,1)S(1)}, bf16[16,2048]{1,0:T(8,128)(2,1)S(1)}, u32[]{:S(2)}, u32[]{:S(2)}) collective-permute-start(bf16[16,2048]{1,0:T(8,128)(2,1)S(1)} %get-tuple-element.20), channel_id=1, source_target_pairs={{8,0},{9,1},{10,2},{11,3},{12,4},{13,5},{14,6},{15,7},{0,8},{1,9},... | collective-permute-start | bytes 196616 | tf_op jit(solution)/shard_map/ppermute | solution.py:144
  64.9 0.7 copy-start.4
  65.0 5.1 %collective-permute-start.16 = (bf16[128,4096]{1,0:T(8,128)(2,1)S(1)}, bf16[128,4096]{1,0:T(8,128)(2,1)S(1)}, u32[]{:S(2)}, u32[]{:S(2)}) collective-permute-start(bf16[128,4096]{1,0:T(8,128)(2,1)S(1)} %pad_maximum_fusion), channel_id=1, source_target_pairs={{0,1},{1,0},{2,3},{3,2},{4,5},{5,4},{6,7},{7,6},{8,9},{9,8},{10,11... | collective-permute-start | bytes 3145736 | tf_op jit(solution)/shard_map/ppermute | solution.py:147
  65.7 8.0 %collective-permute-start.13 = (bf16[16,2048]{1,0:T(8,128)(2,1)S(1)}, bf16[16,2048]{1,0:T(8,128)(2,1)S(1)}, u32[]{:S(2)}, u32[]{:S(2)}) collective-permute-start(bf16[16,2048]{1,0:T(8,128)(2,1)S(1)} %project.3), channel_id=1, source_target_pairs={{12,0},{13,1},{14,2},{15,3},{0,12},{1,13},{2,14},{3,15},{28,16},{2... | collective-permute-start | bytes 196616 | tf_op jit(solution)/shard_map/ppermute | solution.py:144
  74.2 1.3 %copy-start.3 = (f32[4,4096]{1,0:T(4,128)}, f32[4,4096]{1,0:T(4,128)S(1)}, u32[]{:S(2)}) copy-start(f32[4,4096]{1,0:T(4,128)S(1)} %reshape.146) | copy-start | bytes 196612

commit v13 on v12

--- a/solution.py
+++ b/solution.py
@@ -222,15 +222,16 @@
             returned = [move(side, home) for side, home in zip(sides, ways_home)]
             mine = jnp.concatenate(after(tuple(ranged), own), axis=1)
             mine_over_y = swap(mine, 2)
+            both = jnp.concatenate([mine, mine_over_y], axis=0)
         else:
             up = down = move(up, up_hops + down_hops)
-            wait = returned if s == planes - 1 else []
+            wait = [*returned, both] if s == planes - 1 else []
             (side,) = project([after(up, *wait)], token_count, quad_weights)
             returned.append(move(side, ways_home[len(returned)]))
     late = returned.pop()
     early = combine([own] + returned, wide)
 
-    rest = swap(after(jnp.concatenate([mine, mine_over_y], axis=0), side), 1)
+    rest = swap(after(both, side), 1)
     here = jnp.stack([plane, spot, group]).astype(jnp.int32)
     all_queries = assemble(here, mine, mine_over_y, rest, order, groups)
     sketches = combine([late], after(wide_late, all_queries), early, counts)

time: 75.9 us -> 81.8 us (1.078)
  starting transfers between devices: 35.5 us -> 39.7 us
  waiting for transfers between devices: 23.3 us -> 25.4 us
    ppermute x9, starting transfers between devices: 22.5 us -> 26.7 us  [move(): return lax.ppermute(array, 'expert', pairs)]
    ppermute x7, waiting for transfers between devices: 9.4 us -> 10.5 us  [swap(): return lax.ppermute(array, 'expert', [(i, i ^ bit) for i in range(n)])]
    ppermute x9, waiting for transfers between devices: 11.5 us -> 12.4 us  [move(): return lax.ppermute(array, 'expert', pairs)]
  transfers between devices with their start and end apart: 17 -> 17, of which waited for: 7 -> 8; matrix products, arithmetic and copies ran while one was open for 7% -> 7% of each run, Pallas kernels for 10% -> 6%
where the time goes in v13:
time: 81.8 us; the launch traced here: 81.3 us
  starting transfers between devices  39.7 us (49%)
  waiting for transfers between devices  25.4 us (31%)
  Pallas kernels  8.24 us (10%)
  other arithmetic  2.79 us (3%)
  matrix products  2.58 us (3%)
  local copies, waits for them, and re-layouts  1.62 us (2%)
  between operations  0.97 us (1%)
    ppermute x9, starting transfers between devices, move(): return lax.ppermute(array, 'expert', pairs)  26.7 us
    ppermute x9, waiting for transfers between devices, move(): return lax.ppermute(array, 'expert', pairs)  12.4 us
    ppermute x7, starting transfers between devices, swap(): return lax.ppermute(array, 'expert', [(i, i ^ bit) for i in range(n)])  11.4 us
    ppermute x7, waiting for transfers between devices, swap(): return lax.ppermute(array, 'expert', [(i, i ^ bit) for i in range(n)])  10.5 us
    pallas_call x2, Pallas kernels, project(): pl.pallas_call(functools.partial(project_kernel, len(parts), rows), out_s...  6.5 us
    ppermute x1, waiting for transfers between devices, shards(): lax.ppermute(lined, 'groups', [(g, (g + k) % groups) for g in range(group...  2.58 us
  transfers between devices with their start and end apart: 17, of which 8 were waited for; matrix products, arithmetic and copies ran while one was open for 7% of the time, Pallas kernels for 6%

profile of v13, /device:TPU:0, one launch (start us, length us, event | category | flops | bytes accessed | tf_op | source)
XLA Modules:
  0.0 81.3 jit_solution(12479209393445145360)
XLA Ops:
  0.6 5.9 %collective-permute-start = (bf16[64,4096]{1,0:T(8,128)(2,1)}, bf16[64,4096]{1,0:T(8,128)(2,1)}, u32[]{:S(2)}, u32[]{:S(2)}) collective-permute-start(bf16[64,4096]{1,0:T(8,128)(2,1)} %refs_0_.1), channel_id=1, source_target_pairs={{0,4},{1,5},{2,6},{3,7},{4,8},{5,9},{6,10},{7,11},{8,12},{9,13},{1... | collective-permute-start | bytes 1572872 | tf_op jit(solution)/shard_map/ppermute | solution.py:144
  6.5 1.3 %collective-permute-start.2 = (bf16[64,4096]{1,0:T(8,128)(2,1)}, bf16[64,4096]{1,0:T(8,128)(2,1)}, u32[]{:S(2)}, u32[]{:S(2)}) collective-permute-start(bf16[64,4096]{1,0:T(8,128)(2,1)} %refs_0_.1), channel_id=1, source_target_pairs={{4,0},{5,1},{6,2},{7,3},{8,4},{9,5},{10,6},{11,7},{12,8},{13,9},{1... | collective-permute-start | bytes 1572872 | tf_op jit(solution)/shard_map/ppermute | solution.py:144
  7.8 1.6 %collective-permute-start.8 = (bf16[128,4096]{1,0:T(8,128)(2,1)}, bf16[128,4096]{1,0:T(8,128)(2,1)S(1)}, u32[]{:S(2)}, u32[]{:S(2)}) collective-permute-start(bf16[128,4096]{1,0:T(8,128)(2,1)} %bitcast.16), channel_id=1, source_target_pairs={{0,2},{1,3},{2,0},{3,1},{4,6},{5,7},{6,4},{7,5},{8,10},{9,11},{10,... | collective-permute-start | bytes 3145736 | tf_op jit(solution)/shard_map/ppermute | solution.py:147
  9.4 0.8 %constant_dynamic-slice_fusion = bf16[16,2048]{1,0:T(8,128)(2,1)S(1)} fusion(bf16[16,4096]{1,0:T(8,128)(2,1)} %param.15, s32[]{:T(128)S(6)} %select_n.74), kind=kLoop, calls=%fused_computation.22 | loop fusion | bytes 131076 | tf_op jit(solution)/shard_map/dynamic_slice | solution.py:188
  10.3 2.9 %collective-permute-start.4 = (bf16[16,2048]{1,0:T(8,128)(2,1)S(1)}, bf16[16,2048]{1,0:T(8,128)(2,1)S(1)}, u32[]{:S(2)}, u32[]{:S(2)}) collective-permute-start(bf16[16,2048]{1,0:T(8,128)(2,1)S(1)} %constant_dynamic-slice_fusion), channel_id=1, source_target_pairs={{0,8},{1,9},{2,10},{3,11},{4,12},{5,13},{6,14},{7,15},{8,0},{9,1},... | collective-permute-start | bytes 196616 | tf_op jit(solution)/shard_map/ppermute | solution.py:147
  13.1 0.1 stack.33
  13.2 0.1 iota_add_fusion
  13.3 0.1 add.55
  13.4 0.1 add_select_fusion
  13.5 0.1 select_n.90
  13.5 0.7 iota_compare_fusion
  14.3 1.3 %fusion.4 = f32[64,64]{1,0:T(8,128)S(1)} fusion(bf16[64,4096]{1,0:T(8,128)(2,1)S(1)} %copy-done, bf16[4096,64]{0,1:T(8,128)(2,1)} %param.14), kind=kOutput, calls=%fused_computation.23 | convolution fusion | flops 33554432 | bytes 1064960 | tf_op jit(solution)/shard_map/dot_general | solution.py:163
  15.6 0.9 %select_reduce_fusion = f32[40,64]{1,0:T(8,128)S(1)} fusion(f32[8,64]{1,0:T(8,128)} %bitcast.20, s32[8,64]{1,0:T(8,128)} %bitcast.21, s32[40]{0:T(128)S(1)} %select_n.90), kind=kLoop, calls=%fused_computation.5 | loop fusion | flops 58880 | bytes 14496 | tf_op jit(solution)/shard_map/reduce_sum | solution.py:168
  16.6 0.1 pad_maximum_fusion.2
  16.7 0.1 broadcast_in_dim.70
  16.9 0.1 broadcast_in_dim.71
  17.0 0.3 fusion.refs_4_
  17.3 0.1 fusion.1.refs_1_
  17.5 5.4 %collective-permute-done.2.refs_2_ = bf16[64,4096]{1,0:T(8,128)(2,1)} collective-permute-done((bf16[64,4096]{1,0:T(8,128)(2,1)}, bf16[64,4096]{1,0:T(8,128)(2,1)}, u32[]{:S(2)}, u32[]{:S(2)}) %collective-permute-start.2) | collective-permute-done | bytes 524320 | tf_op jit(solution)/shard_map/ppermute | solution.py:144
  22.8 1.3 %collective-permute-start.3 = (bf16[64,4096]{1,0:T(8,128)(2,1)}, bf16[64,4096]{1,0:T(8,128)(2,1)S(1)}, u32[]{:S(2)}, u32[]{:S(2)}) collective-permute-start(bf16[64,4096]{1,0:T(8,128)(2,1)} %collective-permute-done.2.refs_2_), channel_id=1, source_target_pairs={{4,0},{5,1},{6,2},{7,3},{8,4},{9,5},{10,6},{11,7},{20,16},{21,17},... | collective-permute-start | bytes 1572872 | tf_op jit(solution)/shard_map/ppermute | solution.py:144
  24.1 0.7 collective-permute-start.1
  24.8 0.2 collective-permute-done.4
  25.0 5.3 %collective-permute-start.5 = (bf16[32,2048]{1,0:T(8,128)(2,1)S(1)}, bf16[32,2048]{1,0:T(8,128)(2,1)S(1)}, u32[]{:S(2)}, u32[]{:S(2)}) collective-permute-start(bf16[32,2048]{1,0:T(8,128)(2,1)S(1)} %pad_maximum_fusion.1), channel_id=1, source_target_pairs={{0,4},{1,5},{2,6},{3,7},{4,0},{5,1},{6,2},{7,3},{8,12},{9,13},{10,... | collective-permute-start | bytes 393224 | tf_op jit(solution)/shard_map/ppermute | solution.py:147
  30.3 9.2 %collective-permute-done.5 = bf16[32,2048]{1,0:T(8,128)(2,1)S(1)} collective-permute-done((bf16[32,2048]{1,0:T(8,128)(2,1)S(1)}, bf16[32,2048]{1,0:T(8,128)(2,1)S(1)}, u32[]{:S(2)}, u32[]{:S(2)}) %collective-permute-start.5) | collective-permute-done | bytes 131104 | tf_op jit(solution)/shard_map/ppermute | solution.py:147
  39.5 0.1 add.58.refs_3_
  39.7 0.1 collective-permute-start.9
  39.8 1.6 %collective-permute-start.13 = (bf16[64,2048]{1,0:T(8,128)(2,1)S(1)}, bf16[64,2048]{1,0:T(8,128)(2,1)S(1)}, u32[]{:S(2)}, u32[]{:S(2)}) collective-permute-start(bf16[64,2048]{1,0:T(8,128)(2,1)S(1)} %constant_dynamic-update-slice_fusion), channel_id=1, source_target_pairs={{0,16},{16,0},{1,17},{17,1},{2,18},{18,2},{3,19},{19,3},{4,20},{20... | collective-permute-start | bytes 786440 | tf_op jit(solution)/shard_map/ppermute | solution.py:219
  41.3 1.1 %collective-permute-done.9.refs_7_.refs_4_ = bf16[128,4096]{1,0:T(8,128)(2,1)S(1)} collective-permute-done((bf16[128,4096]{1,0:T(8,128)(2,1)S(1)}, bf16[128,4096]{1,0:T(8,128)(2,1)S(1)}, u32[]{:S(2)}, u32[]{:S(2)}) %collective-permute-start.9) | collective-permute-done | bytes 1048608 | tf_op jit(solution)/shard_map/ppermute | solution.py:147
  42.4 3.5 %project.2 = (bf16[16,2048]{1,0:T(8,128)(2,1)S(1)}, bf16[16,2048]{1,0:T(8,128)(2,1)S(1)}, bf16[16,2048]{1,0:T(8,128)(2,1)S(1)}, bf16[16,2048]{1,0:T(8,128)(2,1)S(1)}) custom-call(bf16[64,4096]{1,0:T(8,128)(2,1)S(1)} %copy-done.2, bf16[64,4096]{1,0:T(8,128)(2,1)} %collective-permute-done.refs_1_, bf16[64,4096]{1,0:T(8,128)(2,1)} %collective-permute-done.2.refs_2_, ...), custom_call_target="tpu_custom_call" | custom-call | flops 1024 | bytes 1024 | tf_op jit(solution)/shard_map/project/pallas_call | solution.py:88
  45.9 2.6 %collective-permute-done.13 = bf16[64,2048]{1,0:T(8,128)(2,1)S(1)} collective-permute-done((bf16[64,2048]{1,0:T(8,128)(2,1)S(1)}, bf16[64,2048]{1,0:T(8,128)(2,1)S(1)}, u32[]{:S(2)}, u32[]{:S(2)}) %collective-permute-start.13) | collective-permute-done | bytes 262176 | tf_op jit(solution)/shard_map/ppermute | solution.py:219
  48.5 1.6 %collective-permute-start.14 = (bf16[64,4096]{1,0:T(8,128)(2,1)S(1)}, bf16[64,4096]{1,0:T(8,128)(2,1)S(1)}, u32[]{:S(2)}, u32[]{:S(2)}) collective-permute-start(bf16[64,4096]{1,0:T(8,128)(2,1)S(1)} %constant_dynamic-update-slice_fusion.2.mine_ref), channel_id=1, source_target_pairs={{0,2},{1,3},{2,0},{3,1},{4,6},{5,7},{6,4},{7,5},{8,10},{9,11},{10,... | collective-permute-start | bytes 1572872 | tf_op jit(solution)/shard_map/ppermute | solution.py:147
  50.1 1.3 %collective-permute-start.6 = (bf16[64,4096]{1,0:T(8,128)(2,1)S(1)}, bf16[64,4096]{1,0:T(8,128)(2,1)S(1)}, u32[]{:S(2)}, u32[]{:S(2)}) collective-permute-start(bf16[64,4096]{1,0:T(8,128)(2,1)S(1)} %add.58.refs_3_), channel_id=1, source_target_pairs={{8,12},{9,13},{10,14},{11,15},{4,0},{5,1},{6,2},{7,3},{24,28},{25,... | collective-permute-start | bytes 1572872 | tf_op jit(solution)/shard_map/ppermute | solution.py:144
  51.4 1.3 %collective-permute-start.10 = (bf16[16,2048]{1,0:T(8,128)(2,1)S(1)}, bf16[16,2048]{1,0:T(8,128)(2,1)S(1)}, u32[]{:S(2)}, u32[]{:S(2)}) collective-permute-start(bf16[16,2048]{1,0:T(8,128)(2,1)S(1)} %get-tuple-element.18), channel_id=1, source_target_pairs={{4,0},{5,1},{6,2},{7,3},{8,4},{9,5},{10,6},{11,7},{12,8},{13,9},{1... | collective-permute-start | bytes 196616 | tf_op jit(solution)/shard_map/ppermute | solution.py:144
  52.7 5.2 %collective-permute-start.11 = (bf16[16,2048]{1,0:T(8,128)(2,1)S(1)}, bf16[16,2048]{1,0:T(8,128)(2,1)S(1)}, u32[]{:S(2)}, u32[]{:S(2)}) collective-permute-start(bf16[16,2048]{1,0:T(8,128)(2,1)S(1)} %get-tuple-element.19), channel_id=1, source_target_pairs={{0,4},{1,5},{2,6},{3,7},{4,8},{5,9},{6,10},{7,11},{8,12},{9,13},{1... | collective-permute-start | bytes 196616 | tf_op jit(solution)/shard_map/ppermute | solution.py:144
  57.9 4.3 %collective-permute-start.12 = (bf16[16,2048]{1,0:T(8,128)(2,1)S(1)}, bf16[16,2048]{1,0:T(8,128)(2,1)S(1)}, u32[]{:S(2)}, u32[]{:S(2)}) collective-permute-start(bf16[16,2048]{1,0:T(8,128)(2,1)S(1)} %get-tuple-element.20), channel_id=1, source_target_pairs={{8,0},{9,1},{10,2},{11,3},{12,4},{13,5},{14,6},{15,7},{0,8},{1,9},... | collective-permute-start | bytes 196616 | tf_op jit(solution)/shard_map/ppermute | solution.py:144
  62.2 0.1 pad_maximum_fusion
  62.3 5.0 %collective-permute-done.6.refs_0_ = bf16[64,4096]{1,0:T(8,128)(2,1)S(1)} collective-permute-done((bf16[64,4096]{1,0:T(8,128)(2,1)S(1)}, bf16[64,4096]{1,0:T(8,128)(2,1)S(1)}, u32[]{:S(2)}, u32[]{:S(2)}) %collective-permute-start.6) | collective-permute-done | bytes 524320 | tf_op jit(solution)/shard_map/ppermute | solution.py:144
  67.3 0.7 collective-permute-done.10.refs_1_
  68.0 3.0 %project.3 = bf16[16,2048]{1,0:T(8,128)(2,1)S(1)} custom-call(bf16[64,4096]{1,0:T(8,128)(2,1)S(1)} %collective-permute-done.6.refs_0_, bf16[128,4096]{1,0:T(8,128)(2,1)S(1)} %bitcast.19, bf16[128,4096]{1,0:T(8,128)(2,1)} %collective-permute-done.7.refs_5_.refs_2_, bf16[128,4096]{1,0:T(8,128)(2,1)S(1)} %collective-permute-done.8.refs_6_.refs_3_, ...), custom_call_target="tpu_custom_call" | custom-call | flops 1024 | bytes 1024 | tf_op jit(solution)/shard_map/project/pallas_call | solution.py:88
  71.1 0.1 convert_reduce_fusion
  71.2 5.5 %collective-permute-start.15 = (bf16[16,2048]{1,0:T(8,128)(2,1)S(1)}, bf16[16,2048]{1,0:T(8,128)(2,1)S(1)}, u32[]{:S(2)}, u32[]{:S(2)}) collective-permute-start(bf16[16,2048]{1,0:T(8,128)(2,1)S(1)} %project.3), channel_id=1, source_target_pairs={{12,0},{13,1},{14,2},{15,3},{0,12},{1,13},{2,14},{3,15},{28,16},{2... | collective-permute-start | bytes 196616 | tf_op jit(solution)/shard_map/ppermute | solution.py:144
  76.8 0.1 pad_add_fusion.here_ref
  76.8 0.7 combine.2.refs_2_
  77.6 0.7 assemble.1
  78.2 1.3 %collective-permute-done.15.refs_0_ = bf16[16,2048]{1,0:T(8,128)(2,1)S(1)} collective-permute-done((bf16[16,2048]{1,0:T(8,128)(2,1)S(1)}, bf16[16,2048]{1,0:T(8,128)(2,1)S(1)}, u32[]{:S(2)}, u32[]{:S(2)}) %collective-permute-start.15) | collective-permute-done | bytes 65568 | tf_op jit(solution)/shard_map/ppermute | solution.py:144
  79.6 0.4 combine.3
  79.9 0.1 reshape.146
  80.1 1.2 %fusion.2 = f32[4,256]{1,0:T(4,128)} fusion(bf16[256,4096]{1,0:T(8,128)(2,1)S(1)} %assemble.1, f32[4,4096]{1,0:T(4,128)S(1)} %reshape.146), kind=kOutput, calls=%fused_computation.8 | convolution fusion | flops 8404992 | bytes 2166784 | tf_op jit(solution)/shard_map/dot_general | solution.py:239
  (32 shorter events, 0.3 us)
Async XLA Ops:
  0.6 13.6 %copy-start = (bf16[64,4096]{1,0:T(8,128)(2,1)S(1)}, bf16[64,4096]{1,0:T(8,128)(2,1)}, u32[]{:S(2)}) copy-start(bf16[64,4096]{1,0:T(8,128)(2,1)} %param.9) | copy-start | bytes 1572868
  0.6 23.5 %collective-permute-start = (bf16[64,4096]{1,0:T(8,128)(2,1)}, bf16[64,4096]{1,0:T(8,128)(2,1)}, u32[]{:S(2)}, u32[]{:S(2)}) collective-permute-start(bf16[64,4096]{1,0:T(8,128)(2,1)} %refs_0_.1), channel_id=1, source_target_pairs={{0,4},{1,5},{2,6},{3,7},{4,8},{5,9},{6,10},{7,11},{8,12},{9,13},{1... | collective-permute-start | bytes 1572872 | tf_op jit(solution)/shard_map/ppermute | solution.py:144
  6.5 16.3 %collective-permute-start.2 = (bf16[64,4096]{1,0:T(8,128)(2,1)}, bf16[64,4096]{1,0:T(8,128)(2,1)}, u32[]{:S(2)}, u32[]{:S(2)}) collective-permute-start(bf16[64,4096]{1,0:T(8,128)(2,1)} %refs_0_.1), channel_id=1, source_target_pairs={{4,0},{5,1},{6,2},{7,3},{8,4},{9,5},{10,6},{11,7},{12,8},{13,9},{1... | collective-permute-start | bytes 1572872 | tf_op jit(solution)/shard_map/ppermute | solution.py:144
  7.8 31.8 %collective-permute-start.8 = (bf16[128,4096]{1,0:T(8,128)(2,1)}, bf16[128,4096]{1,0:T(8,128)(2,1)S(1)}, u32[]{:S(2)}, u32[]{:S(2)}) collective-permute-start(bf16[128,4096]{1,0:T(8,128)(2,1)} %bitcast.16), channel_id=1, source_target_pairs={{0,2},{1,3},{2,0},{3,1},{4,6},{5,7},{6,4},{7,5},{8,10},{9,11},{10,... | collective-permute-start | bytes 3145736 | tf_op jit(solution)/shard_map/ppermute | solution.py:147
  9.4 31.9 %collective-permute-start.7 = (bf16[128,4096]{1,0:T(8,128)(2,1)}, bf16[128,4096]{1,0:T(8,128)(2,1)}, u32[]{:S(2)}, u32[]{:S(2)}) collective-permute-start(bf16[128,4096]{1,0:T(8,128)(2,1)} %bitcast.17), channel_id=1, source_target_pairs={{0,1},{1,0},{2,3},{3,2},{4,5},{5,4},{6,7},{7,6},{8,9},{9,8},{10,11... | collective-permute-start | bytes 3145736 | tf_op jit(solution)/shard_map/ppermute | solution.py:147
  10.3 14.8 %collective-permute-start.4 = (bf16[16,2048]{1,0:T(8,128)(2,1)S(1)}, bf16[16,2048]{1,0:T(8,128)(2,1)S(1)}, u32[]{:S(2)}, u32[]{:S(2)}) collective-permute-start(bf16[16,2048]{1,0:T(8,128)(2,1)S(1)} %constant_dynamic-slice_fusion), channel_id=1, source_target_pairs={{0,8},{1,9},{2,10},{3,11},{4,12},{5,13},{6,14},{7,15},{8,0},{9,1},... | collective-permute-start | bytes 196616 | tf_op jit(solution)/shard_map/ppermute | solution.py:147
  15.6 26.8 %copy-start.1 = (bf16[2,4096,64]{1,2,0:T(8,128)(2,1)S(1)}, bf16[2,4096,64]{1,2,0:T(8,128)(2,1)}, u32[]{:S(2)}) copy-start(bf16[2,4096,64]{1,2,0:T(8,128)(2,1)} %param.13) | copy-start | bytes 3145732
  15.6 26.8 %copy-start.2 = (bf16[64,4096]{1,0:T(8,128)(2,1)S(1)}, bf16[64,4096]{1,0:T(8,128)(2,1)}, u32[]{:S(2)}) copy-start(bf16[64,4096]{1,0:T(8,128)(2,1)} %refs_0_.1) | copy-start | bytes 1572868
  22.8 16.7 %collective-permute-start.3 = (bf16[64,4096]{1,0:T(8,128)(2,1)}, bf16[64,4096]{1,0:T(8,128)(2,1)S(1)}, u32[]{:S(2)}, u32[]{:S(2)}) collective-permute-start(bf16[64,4096]{1,0:T(8,128)(2,1)} %collective-permute-done.2.refs_2_), channel_id=1, source_target_pairs={{4,0},{5,1},{6,2},{7,3},{8,4},{9,5},{10,6},{11,7},{20,16},{21,17},... | collective-permute-start | bytes 1572872 | tf_op jit(solution)/shard_map/ppermute | solution.py:144
  24.1 15.4 %collective-permute-start.1 = (bf16[64,4096]{1,0:T(8,128)(2,1)}, bf16[64,4096]{1,0:T(8,128)(2,1)S(1)}, u32[]{:S(2)}, u32[]{:S(2)}) collective-permute-start(bf16[64,4096]{1,0:T(8,128)(2,1)} %collective-permute-done.refs_1_), channel_id=1, source_target_pairs={{4,8},{5,9},{6,10},{7,11},{8,12},{9,13},{10,14},{11,15},{20,24},{2... | collective-permute-start | bytes 1572872 | tf_op jit(solution)/shard_map/ppermute | solution.py:144
  25.0 14.4 %collective-permute-start.5 = (bf16[32,2048]{1,0:T(8,128)(2,1)S(1)}, bf16[32,2048]{1,0:T(8,128)(2,1)S(1)}, u32[]{:S(2)}, u32[]{:S(2)}) collective-permute-start(bf16[32,2048]{1,0:T(8,128)(2,1)S(1)} %pad_maximum_fusion.1), channel_id=1, source_target_pairs={{0,4},{1,5},{2,6},{3,7},{4,0},{5,1},{6,2},{7,3},{8,12},{9,13},{10,... | collective-permute-start | bytes 393224 | tf_op jit(solution)/shard_map/ppermute | solution.py:147
  39.7 2.7 %collective-permute-start.9 = (bf16[128,4096]{1,0:T(8,128)(2,1)S(1)}, bf16[128,4096]{1,0:T(8,128)(2,1)S(1)}, u32[]{:S(2)}, u32[]{:S(2)}) collective-permute-start(bf16[128,4096]{1,0:T(8,128)(2,1)S(1)} %collective-permute-done.8.refs_6_.refs_3_), channel_id=1, source_target_pairs={{0,1},{1,0},{2,3},{3,2},{4,5},{5,4},{6,7},{7,6},{8,9},{9,8},{10,11... | collective-permute-start | bytes 3145736 | tf_op jit(solution)/shard_map/ppermute | solution.py:147
  39.8 8.7 %collective-permute-start.13 = (bf16[64,2048]{1,0:T(8,128)(2,1)S(1)}, bf16[64,2048]{1,0:T(8,128)(2,1)S(1)}, u32[]{:S(2)}, u32[]{:S(2)}) collective-permute-start(bf16[64,2048]{1,0:T(8,128)(2,1)S(1)} %constant_dynamic-update-slice_fusion), channel_id=1, source_target_pairs={{0,16},{16,0},{1,17},{17,1},{2,18},{18,2},{3,19},{19,3},{4,20},{20... | collective-permute-start | bytes 786440 | tf_op jit(solution)/shard_map/ppermute | solution.py:219
  48.5 13.6 %collective-permute-start.14 = (bf16[64,4096]{1,0:T(8,128)(2,1)S(1)}, bf16[64,4096]{1,0:T(8,128)(2,1)S(1)}, u32[]{:S(2)}, u32[]{:S(2)}) collective-permute-start(bf16[64,4096]{1,0:T(8,128)(2,1)S(1)} %constant_dynamic-update-slice_fusion.2.mine_ref), channel_id=1, source_target_pairs={{0,2},{1,3},{2,0},{3,1},{4,6},{5,7},{6,4},{7,5},{8,10},{9,11},{10,... | collective-permute-start | bytes 1572872 | tf_op jit(solution)/shard_map/ppermute | solution.py:147
  50.1 17.2 %collective-permute-start.6 = (bf16[64,4096]{1,0:T(8,128)(2,1)S(1)}, bf16[64,4096]{1,0:T(8,128)(2,1)S(1)}, u32[]{:S(2)}, u32[]{:S(2)}) collective-permute-start(bf16[64,4096]{1,0:T(8,128)(2,1)S(1)} %add.58.refs_3_), channel_id=1, source_target_pairs={{8,12},{9,13},{10,14},{11,15},{4,0},{5,1},{6,2},{7,3},{24,28},{25,... | collective-permute-start | bytes 1572872 | tf_op jit(solution)/shard_map/ppermute | solution.py:144
  51.4 16.6 %collective-permute-start.10 = (bf16[16,2048]{1,0:T(8,128)(2,1)S(1)}, bf16[16,2048]{1,0:T(8,128)(2,1)S(1)}, u32[]{:S(2)}, u32[]{:S(2)}) collective-permute-start(bf16[16,2048]{1,0:T(8,128)(2,1)S(1)} %get-tuple-element.18), channel_id=1, source_target_pairs={{4,0},{5,1},{6,2},{7,3},{8,4},{9,5},{10,6},{11,7},{12,8},{13,9},{1... | collective-permute-start | bytes 196616 | tf_op jit(solution)/shard_map/ppermute | solution.py:144
  52.7 15.3 %collective-permute-start.11 = (bf16[16,2048]{1,0:T(8,128)(2,1)S(1)}, bf16[16,2048]{1,0:T(8,128)(2,1)S(1)}, u32[]{:S(2)}, u32[]{:S(2)}) collective-permute-start(bf16[16,2048]{1,0:T(8,128)(2,1)S(1)} %get-tuple-element.19), channel_id=1, source_target_pairs={{0,4},{1,5},{2,6},{3,7},{4,8},{5,9},{6,10},{7,11},{8,12},{9,13},{1... | collective-permute-start | bytes 196616 | tf_op jit(solution)/shard_map/ppermute | solution.py:144
  57.9 10.1 %collective-permute-start.12 = (bf16[16,2048]{1,0:T(8,128)(2,1)S(1)}, bf16[16,2048]{1,0:T(8,128)(2,1)S(1)}, u32[]{:S(2)}, u32[]{:S(2)}) collective-permute-start(bf16[16,2048]{1,0:T(8,128)(2,1)S(1)} %get-tuple-element.20), channel_id=1, source_target_pairs={{8,0},{9,1},{10,2},{11,3},{12,4},{13,5},{14,6},{15,7},{0,8},{1,9},... | collective-permute-start | bytes 196616 | tf_op jit(solution)/shard_map/ppermute | solution.py:144
  62.3 8.9 %copy-start.4 = (s32[1,64]{1,0:T(1,128)S(1)}, s32[1,64]{1,0:T(1,128)}, u32[]{:S(2)}) copy-start(s32[1,64]{1,0:T(1,128)} %param.12) | copy-start | bytes 772
  71.0 6.5 %collective-permute-start.16 = (bf16[128,4096]{1,0:T(8,128)(2,1)S(1)}, bf16[128,4096]{1,0:T(8,128)(2,1)S(1)}, u32[]{:S(2)}, u32[]{:S(2)}) collective-permute-start(bf16[128,4096]{1,0:T(8,128)(2,1)S(1)} %pad_maximum_fusion), channel_id=1, source_target_pairs={{0,1},{1,0},{2,3},{3,2},{4,5},{5,4},{6,7},{7,6},{8,9},{9,8},{10,11... | collective-permute-start | bytes 3145736 | tf_op jit(solution)/shard_map/ppermute | solution.py:147
  71.2 8.3 %collective-permute-start.15 = (bf16[16,2048]{1,0:T(8,128)(2,1)S(1)}, bf16[16,2048]{1,0:T(8,128)(2,1)S(1)}, u32[]{:S(2)}, u32[]{:S(2)}) collective-permute-start(bf16[16,2048]{1,0:T(8,128)(2,1)S(1)} %project.3), channel_id=1, source_target_pairs={{12,0},{13,1},{14,2},{15,3},{0,12},{1,13},{2,14},{3,15},{28,16},{2... | collective-permute-start | bytes 196616 | tf_op jit(solution)/shard_map/ppermute | solution.py:144
  80.1 1.3 %copy-start.3 = (f32[4,4096]{1,0:T(4,128)}, f32[4,4096]{1,0:T(4,128)S(1)}, u32[]{:S(2)}) copy-start(f32[4,4096]{1,0:T(4,128)S(1)} %reshape.146) | copy-start | bytes 196612
